TPU v7x, 128 devices: a whole 4x4x4 slice. The times are simulated.
128 devices in a mesh: dp: 8 (over x, core), fsdp: 16 (over z, y).
Axes of the slice: x: 4, y: 4, z: 4, core: 2. Of those that a mesh axis runs over, the one named last changes fastest.
Arguments:
- replica_grads: bfloat16 [8, 2048, 16384], P('dp', 'fsdp'), may hold values from -240 to 240
- owners: int32 [8, 16], P('dp'), may hold values from 0 to 31, as said below
- left_factor: float32 [8, 32, 512, 512], P('dp', 'fsdp'), may hold values from -30 to 30
- right_factor: float32 [8, 32, 512, 512], P('dp', 'fsdp'), may hold values from -30 to 30
- left_basis: float32 [8, 32, 512, 512], P('dp', 'fsdp'), may hold values from -0.25 to 0.25
- right_basis: float32 [8, 32, 512, 512], P('dp', 'fsdp'), may hold values from -0.25 to 0.25
- first_moment: float32 [8, 32, 512, 512], P('dp', 'fsdp'), may hold values from -2 to 2
- second_moment: float32 [8, 32, 512, 512], P('dp', 'fsdp'), may hold values from 0.1 to 2
Outputs:
- update: bfloat16 [2048, 16384], P('fsdp', 'dp')
- new_left: float32 [8, 32, 512, 512], P('dp', 'fsdp')
- new_right: float32 [8, 32, 512, 512], P('dp', 'fsdp')
- new_first: float32 [8, 32, 512, 512], P('dp', 'fsdp')
- new_second: float32 [8, 32, 512, 512], P('dp', 'fsdp')
Inputs may be any that keep to these rules, and one draw needn't show every extreme that they name: owners[d, b] = o * 2 + s names slot s of owner o along fsdp within replica group d; the entries of one row are distinct, and in every row some owner has all 2 of its slots named.
All inputs are finite; a program needn't handle non-finite values.
Results may differ from a plain program's by a relative error of at most 0.012.
Values may be sent and summed in bfloat16 or wider, within the bound.
No kernel may reach another device: no remote copies, remote signals or barrier semaphores. Data moves between devices by JAX's collectives and lax.ppermute only.
A program may use at most 128 MiB of HBM per device.

v0:
```python
import jax
import jax.numpy as jnp
from jax import lax
from jax.experimental import pallas as pl
from jax.experimental.pallas import tpu as pltpu
from jax.sharding import PartitionSpec as P

f32 = jnp.float32
bf16 = jnp.bfloat16
SMEM = pltpu.MemorySpace.SMEM
VMEM = pltpu.MemorySpace.VMEM
HBM = pltpu.MemorySpace.HBM
LANES = 128


def in_hbm(*arrays):
    return [pltpu.with_memory_space_constraint(a, HBM) for a in arrays]


def split3(value):
    head, rest = split(value)
    mid, tail = split(value - head.astype(f32))
    return head, mid, tail


def split(value):
    head = value.astype(bf16)
    return head, (value - head.astype(f32)).astype(bf16)


def mm(a, b, dims=((1,), (0,))):
    return lax.dot_general(a, b, (dims, ((), ())), preferred_element_type=f32)


def mm3(a, b, dims=((1,), (0,))):
    return mm(a[0], b[0], dims) + (mm(a[0], b[1], dims) + mm(a[1], b[0], dims))


def prepare_body(left_ref, right_ref, first_ref, lt_h, lt_l, l_h, r_h, r_l, rot_ref):
    left = left_ref[0]
    left_t = left.T
    left_t_split = split(left_t)
    right_split = split(right_ref[0])
    lt_h[0], lt_l[0] = left_t_split
    l_h[0] = left.astype(bf16)
    r_h[0], r_l[0] = right_split
    half = mm3(left_t_split, split(first_ref[0]))
    rot_ref[0] = 0.9 * mm3(split(half), right_split)


def prepare(left_basis, right_basis, first_moment):
    slots, n, _ = left_basis.shape
    block = pl.BlockSpec((1, n, n), lambda s: (s, 0, 0))
    half = HBM((slots, n, n), bf16)
    return pl.pallas_call(
        prepare_body,
        grid=(slots,),
        in_specs=[block] * 3,
        out_specs=[block] * 6,
        out_shape=[half] * 5 + [HBM((slots, n, n), f32)],
        compiler_params=pltpu.CompilerParams(vmem_limit_bytes=32 << 20),
        cost_estimate=pl.CostEstimate(
            flops=slots * 12 * n**3, bytes_accessed=slots * 26 * n * n, transcendentals=0
        ),
        name="prepare",
    )(*in_hbm(left_basis, right_basis, first_moment))


def local(body, arrays, out_shape, name, limit=8 << 20):
    return pl.pallas_call(
        body,
        in_specs=[pl.BlockSpec(memory_space=SMEM)]
        + [pl.BlockSpec(memory_space=VMEM)] * (len(arrays) - 1),
        out_specs=jax.tree.map(lambda _: pl.BlockSpec(memory_space=VMEM), out_shape),
        out_shape=out_shape,
        compiler_params=pltpu.CompilerParams(vmem_limit_bytes=limit),
        name=name,
    )(*arrays)


def dispatch_body(table, *refs):
    *srcs, dst, square = refs
    n = dst.shape[2]
    bands = len(srcs)
    width = srcs[0].shape[1] - LANES
    cols = width // n
    z = table[0, bands * cols]
    total = jnp.zeros(square.shape, f32)
    for j, src in enumerate(srcs):
        band = lax.rem(z + bands - j, bands)
        for c in range(cols):
            dst[table[0, band * cols + c]] = src[:, c * n : (c + 1) * n]
        terms = src[:, width:].astype(f32)
        for t in range(3):
            total = total + terms[8 * t : 8 * t + 8]
    square[...] = total


def collect_body(table, src, *dsts):
    n = src.shape[2]
    bands = len(dsts)
    cols = dsts[0].shape[1] // n
    z = table[0, bands * cols]
    for j, dst in enumerate(dsts):
        band = lax.rem(z + j, bands)
        for c in range(cols):
            dst[:, c * n : (c + 1) * n] = src[table[0, band * cols + c]]


def put_body(table, *refs):
    *srcs, dst = refs
    bands = len(srcs)
    z = table[0, table.shape[1] - 1]
    for j, src in enumerate(srcs):
        dst[lax.rem(z + bands - j, bands)] = src[...]


def plus_body(table, *refs):
    total = refs[0][...]
    for ref in refs[1:-1]:
        total = total + ref[...]
    refs[-1][...] = total


def slabs(place, src, core, dst, sems, steps, chips, width):
    return [
        pltpu.make_async_copy(
            src.at[
                :,
                pl.ds(
                    pl.multiple_of((2 * lax.rem(place[0] + j, chips) + core) * width, width),
                    width,
                ),
            ],
            dst.at[i],
            sems.at[i],
        )
        for i, j in enumerate(steps)
    ]


def pick(place, grads, steps, width):
    rows, columns = grads.shape
    chips = columns // width // 2

    def body(place, src, dst, sems):
        copies = slabs(place, src, 1 - place[1], dst, sems, steps, chips, width)
        for c in copies:
            c.start()
        for c in copies:
            c.wait()

    return pl.pallas_call(
        body,
        in_specs=[pl.BlockSpec(memory_space=SMEM), pl.BlockSpec(memory_space=HBM)],
        out_specs=pl.BlockSpec(memory_space=VMEM),
        out_shape=jax.ShapeDtypeStruct((len(steps), rows, width), bf16),
        scratch_shapes=[pltpu.SemaphoreType.DMA((len(steps),))],
        compiler_params=pltpu.CompilerParams(vmem_limit_bytes=4 << 20),
        name="pick",
    )(place, *in_hbm(grads))


def pair(body, place, grads, other, steps, width, outs, name):
    rows, columns = grads.shape
    chips = columns // width // 2
    low = rows // 2

    def run(place, src, far, *refs):
        *outs, near, sems = refs
        copies = slabs(place, src, place[1], near, sems, steps, chips, width)
        for c in copies:
            c.start()

        def total(i, a):
            if a == 0:
                copies[i].wait()
            part = slice(a * low, (a + 1) * low)
            return near[i, part].astype(f32) + far[i, part].astype(f32)

        body(total, low, *outs)

    return pl.pallas_call(
        run,
        in_specs=[
            pl.BlockSpec(memory_space=SMEM),
            pl.BlockSpec(memory_space=HBM),
            pl.BlockSpec(memory_space=VMEM),
        ],
        out_specs=[pl.BlockSpec(memory_space=VMEM)] * len(outs),
        out_shape=[jax.ShapeDtypeStruct(shape, kind) for shape, kind in outs],
        scratch_shapes=[
            pltpu.VMEM((len(steps), rows, width), bf16),
            pltpu.SemaphoreType.DMA((len(steps),)),
        ],
        compiler_params=pltpu.CompilerParams(vmem_limit_bytes=8 << 20),
        name=name,
    )(place, *in_hbm(grads), other)


def far_body(total, low, to_right, to_left):
    to_right[...] = total(0, 0).astype(bf16)
    to_left[...] = total(0, 1).astype(bf16)


def near_body(total, low, to_right, to_left, keep_right, keep_left, own):
    keep_right[...] = total(0, 0)
    to_right[...] = total(0, 1).astype(bf16)
    to_left[...] = total(1, 0).astype(bf16)
    keep_left[...] = total(1, 1)
    for a in range(2):
        own[a * low : (a + 1) * low] = total(2, a)


def relay(place, kept, arrived):
    def body(place, kept, arrived, out):
        out[...] = (kept[...] + arrived[...].astype(f32)).astype(bf16)

    out = jax.ShapeDtypeStruct(kept.shape, bf16)
    return local(body, (place, kept, arrived), out, "relay")


def finish(place, own, left_direct, right_direct, left_sum, right_sum, bands):
    rows, width = own.shape
    low = rows // 2
    piece = rows // bands

    def body(place, own, left_direct, right_direct, left_sum, right_sum, *outs):
        total = jnp.zeros((8, LANES), f32)
        for q in range(bands):
            near, far = (left_sum, right_direct) if q * piece < low else (left_direct, right_sum)
            part = slice(q * piece % low, q * piece % low + piece)
            value = own[q * piece : (q + 1) * piece] + (
                near[part].astype(f32) + far[part].astype(f32)
            )
            step = lax.rem(q - place[2] + bands, bands)
            rounded = value.astype(bf16)
            for j in range(bands):

                @pl.when(step == j)
                def _():
                    outs[j][:, :width] = rounded

            by_row = jnp.sum((value * value).reshape(piece // 8, 8, width), axis=0)
            for c in range(width // LANES):
                total = total + by_row[:, c * LANES : (c + 1) * LANES]
        terms = [t.astype(f32) for t in split3(total)]
        terms.append(jnp.zeros((piece - 24, LANES), f32))
        terms = jnp.concatenate(terms, axis=0).astype(bf16)
        for out in outs:
            out[:, width:] = terms

    arrays = [place, own, left_direct, right_direct, left_sum, right_sum]
    out = [jax.ShapeDtypeStruct((piece, width + LANES), bf16)] * bands
    return local(body, arrays, out, "finish", 12 << 20)


def sum_over_replicas(place, grads, bands):
    size = lax.axis_size("dp")
    rows, columns = grads.shape
    width = columns // size
    half = (rows // 2, width)
    swap = [(d, d ^ 1) for d in range(size)]
    up = [(d, (d + 2) % size) for d in range(size)]
    down = [(d, (d - 2) % size) for d in range(size)]
    other = lax.ppermute(pick(place, grads, (2,), width), "dp", swap)
    others = lax.ppermute(pick(place, grads, (1, 3, 0), width), "dp", swap)
    to_right, to_left = pair(
        far_body, place, grads, other, (2,), width, [(half, bf16)] * 2, "pair_far"
    )
    left_far = lax.ppermute(to_right, "dp", up)
    right_far = lax.ppermute(to_left, "dp", down)
    outs = [(half, bf16)] * 2 + [(half, f32)] * 2 + [((rows, width), f32)]
    to_right, to_left, keep_right, keep_left, own = pair(
        near_body, place, grads, others, (1, 3, 0), width, outs, "pair_near"
    )
    left_direct = lax.ppermute(to_right, "dp", up)
    right_direct = lax.ppermute(to_left, "dp", down)
    left_sum = lax.ppermute(relay(place, keep_right, left_far), "dp", up)
    right_sum = lax.ppermute(relay(place, keep_left, right_far), "dp", down)
    return own, left_direct, right_direct, left_sum, right_sum


def exchange(arrays, steps):
    order = sorted(range(1, len(arrays)), key=lambda j: -min(j, len(arrays) - j))
    got = {0: arrays[0]}
    for j in order:
        got[j] = lax.ppermute(arrays[j], *steps[j - 1])
    return [got[j] for j in range(len(arrays))]


def add_up(place, value, steps):
    arrived = [lax.ppermute(value, axis, perm) for axis, perm in steps]
    return local(plus_body, [place, value] + arrived, jax.ShapeDtypeStruct(value.shape, f32), "plus")


def assemble(pieces_ref, slot, bands):
    senders = pieces_ref.shape[0]
    per = senders // bands
    return jnp.concatenate(
        [pieces_ref[z * per + y, slot] for y in range(per) for z in range(bands)], axis=0
    )


def is_named(table, slot):
    named = table[0, 0] == slot
    for b in range(1, table.shape[1]):
        named = jnp.logical_or(named, table[0, b] == slot)
    return named


def clip_of(square, entries):
    total = jnp.sum(jnp.sum(square[...], axis=0, keepdims=True), axis=1, keepdims=True)
    return jnp.minimum(1.0, 1.0 / jnp.sqrt(total / entries + 1e-06))


def direction_body(
    bands, entries, table, me, square, pieces, second, *refs
):
    states, (out, second_out), scratch = refs[:6], refs[6:8], refs[8:]
    *bufs, old, new, sems, out_sems = scratch
    slots = second.shape[0]
    sources = (*states[:2], *states[3:5], states[5], second, states[2])
    targets = (*bufs[:2], *bufs[3:5], bufs[5], old, bufs[2])
    copies = [
        [
            pltpu.make_async_copy(src.at[s], dst.at[s], sems.at[s, i])
            for i, (src, dst) in enumerate(zip(sources, targets))
        ]
        for s in range(slots)
    ]
    for group in copies:
        for c in group:
            c.start()
    lt_h, lt_l, l_h, r_h, r_l, rot = bufs
    scale = clip_of(square, entries)
    senders, rows, n = pieces.shape[0], pieces.shape[2], pieces.shape[3]
    per = senders // bands
    for s in range(slots):
        wait = [c.wait for c in copies[s]]
        block = assemble(pieces, s, bands)
        wait[0]()
        wait[1]()
        half = mm(lt_h[s], block) + mm(lt_l[s], block)
        wait[2]()
        wait[3]()
        rotated = mm3(split(half), (r_h[s], r_l[s])) * scale
        wait[4]()
        wait[5]()
        value = 0.95 * old[s] + 0.05 * rotated * rotated
        step = (rot[s] + 0.1 * rotated) / (jnp.sqrt(value) + 1e-08)
        named = is_named(table, me[0] * slots + s)
        new[s] = jnp.where(named, value, old[s])
        pltpu.make_async_copy(new.at[s], second_out.at[s], out_sems.at[s]).start()
        wait[6]()
        back = mm(l_h[s], step.astype(bf16))
        update = mm(back.astype(bf16), r_h[s], ((1,), (1,))).astype(bf16)
        for y in range(per):
            for z in range(bands):
                row = (y * bands + z) * rows
                out[z * per + y, s] = update[row : row + rows]
    for s in range(slots):
        pltpu.make_async_copy(new.at[s], second_out.at[s], out_sems.at[s]).wait()


def direction(table, me, square, pieces, prepared, second, bands, entries):
    slots, n, _ = second.shape
    scalar = pl.BlockSpec(memory_space=SMEM)
    whole = pl.BlockSpec(memory_space=VMEM)
    far = pl.BlockSpec(memory_space=HBM)

    def body(*refs):
        direction_body(bands, entries, *refs)

    return pl.pallas_call(
        body,
        in_specs=[scalar] * 2 + [whole] * 2 + [far] * 7,
        out_specs=[whole, far],
        out_shape=[
            jax.ShapeDtypeStruct(pieces.shape, bf16),
            HBM(second.shape, f32),
        ],
        scratch_shapes=[pltpu.VMEM((slots, n, n), bf16)] * 5
        + [pltpu.VMEM((slots, n, n), f32)] * 3
        + [pltpu.SemaphoreType.DMA((slots, 7)), pltpu.SemaphoreType.DMA((slots,))],
        compiler_params=pltpu.CompilerParams(vmem_limit_bytes=32 << 20),
        name="direction",
    )(table, me, square, pieces, *in_hbm(second, *prepared))


def factors_body(bands, entries, table, me, clip, pieces, left, right, first, left_out, right_out, first_out):
    slot = me[0] * pl.num_programs(0) + pl.program_id(0)
    scale = clip_of(clip, entries)
    s = assemble(pieces, pl.program_id(0), bands)
    named = is_named(table, slot)
    square = 0.1 * scale * scale
    left_out[0] = jnp.where(named, 0.9 * left[0] + square * mm(s, s, ((1,), (1,))), left[0])
    right_out[0] = jnp.where(named, 0.9 * right[0] + square * mm(s.T, s), right[0])
    first_out[0] = jnp.where(named, 0.9 * first[0] + (0.1 * scale) * s.astype(f32), first[0])


def factors(table, me, clip, pieces, left, right, first, bands, entries):
    slots, n, _ = left.shape
    block = pl.BlockSpec((1, n, n), lambda s: (s, 0, 0))
    scalar = pl.BlockSpec(memory_space=SMEM)
    whole = pl.BlockSpec(memory_space=VMEM)

    def body(*refs):
        factors_body(bands, entries, *refs)

    return pl.pallas_call(
        body,
        grid=(slots,),
        in_specs=[scalar] * 2 + [whole] * 2 + [block] * 3,
        out_specs=[block] * 3,
        out_shape=[HBM(left.shape, f32)] * 3,
        compiler_params=pltpu.CompilerParams(vmem_limit_bytes=32 << 20),
        cost_estimate=pl.CostEstimate(
            flops=slots * 4 * n**3, bytes_accessed=slots * 26 * n * n, transcendentals=0
        ),
        name="factors",
    )(table, me, clip, pieces, *in_hbm(left, right, first))


def per_device(
    replica_grads,
    owners,
    left_factor,
    right_factor,
    left_basis,
    right_basis,
    first_moment,
    second_moment,
):
    rows_dev = replica_grads.shape[1]
    shards = lax.axis_size("fsdp")
    slots, n = left_factor.shape[1:3]
    per_band = n // rows_dev
    bands = shards // per_band
    dp = lax.axis_size("dp")
    dp_me = lax.axis_index("dp").astype(jnp.int32)
    me = lax.axis_index("fsdp").astype(jnp.int32)
    place = jnp.stack([dp_me // 2, dp_me % 2, me // per_band])
    table = jnp.concatenate([owners, (me // per_band).reshape(1, 1)], axis=1)
    me = me.reshape(1)
    core = [("dp", [(d, d ^ 1) for d in range(dp)])]
    along_x = [("dp", [(d, (d + 2 * h) % dp) for d in range(dp)]) for h in range(1, dp // 2)]
    along_y = [
        ("fsdp", [(i, i // per_band * per_band + (i + h) % per_band) for i in range(shards)])
        for h in range(1, per_band)
    ]
    along_z = [
        ("fsdp", [(i, (i + h * per_band) % shards) for i in range(shards)])
        for h in range(1, bands)
    ]
    prepared = prepare(left_basis[0], right_basis[0], first_moment[0])
    parts = sum_over_replicas(place, replica_grads[0], bands)
    parts, prepared = lax.optimization_barrier((parts, prepared))
    sums = finish(place, *parts, bands)
    rows = sums[0].shape[0]
    width = sums[0].shape[1] - LANES
    cols = width // n
    entries = rows_dev * shards * replica_grads.shape[2]
    spread = exchange(sums, along_z)
    out = [
        jax.ShapeDtypeStruct((shards * slots, rows, n), bf16),
        jax.ShapeDtypeStruct((8, LANES), f32),
    ]
    sent, square = local(dispatch_body, [table, *spread], out, "dispatch")
    pieces = lax.all_to_all(
        sent.reshape(shards, slots, rows, n), "fsdp", split_axis=0, concat_axis=0, tiled=True
    )
    for steps in (core, along_x, along_y):
        square = add_up(place, square, steps)
    update, second_new = direction(
        owners, me, square, pieces, prepared, second_moment[0], bands, entries
    )
    back = lax.all_to_all(update, "fsdp", split_axis=0, concat_axis=0, tiled=True)
    new = factors(
        owners, me, square, pieces, left_factor[0], right_factor[0], first_moment[0], bands, entries
    )
    back, new = lax.optimization_barrier((back, new))
    left_new, right_new, first_new = new
    out = [jax.ShapeDtypeStruct((rows, width), bf16)] * bands
    mine = local(collect_body, [table, back.reshape(shards * slots, rows, n)], out, "collect")
    out = jax.ShapeDtypeStruct((bands, rows, width), bf16)
    result = local(put_body, [table, *exchange(mine, along_z)], out, "put").reshape(rows_dev, width)
    return (result, left_new[None], right_new[None], first_new[None], second_new[None])


def solution(mesh):
    state = P("dp", "fsdp", None, None)
    return jax.shard_map(
        per_device,
        mesh=mesh,
        in_specs=(P("dp", "fsdp", None), P("dp", None)) + (state,) * 6,
        out_specs=(P("fsdp", "dp"),) + (state,) * 4,
        check_vma=False,
    )
```

profile of v0, /device:TPU:0, one launch (start us, length us, event | category | flops | bytes accessed | tf_op | source)
XLA Modules:
  0.0 109.2 jit_solution(6039645821209056786)
XLA Ops:
  0.7 1.9 %pick.2 = bf16[3,128,2048]{2,1,0:T(8,128)(2,1)S(1)} custom-call(s32[3]{0:T(128)S(1)} %pad_add_fusion.1.place.table, bf16[128,16384]{1,0:T(8,128)(2,1)} %bitcast.20), custom_call_target="tpu_custom_call" | custom-call | tf_op jit(solution)/shard_map/pick/pallas_call | solution.py:153
  2.8 1.6 %pick.3 = bf16[1,128,2048]{2,1,0:T(8,128)(2,1)S(1)} custom-call(s32[3]{0:T(128)S(1)} %pad_add_fusion.1.place.table, bf16[128,16384]{1,0:T(8,128)(2,1)} %bitcast.21), custom_call_target="tpu_custom_call" | custom-call | tf_op jit(solution)/shard_map/pick/pallas_call | solution.py:153
  4.4 0.6 collective-permute-start.3
  5.0 2.0 %collective-permute-done.3.far = bf16[1,128,2048]{2,1,0:T(8,128)(2,1)S(1)} collective-permute-done((bf16[1,128,2048]{2,1,0:T(8,128)(2,1)S(1)}, bf16[1,128,2048]{2,1,0:T(8,128)(2,1)S(1)}, u32[]{:S(2)}, u32[]{:S(2)}) %collective-permute-start.3) | collective-permute-done | bytes 524320 | tf_op jit(solution)/shard_map/ppermute | solution.py:266
  6.9 1.7 %pair_far.1 = (bf16[64,2048]{1,0:T(8,128)(2,1)S(1)}, bf16[64,2048]{1,0:T(8,128)(2,1)S(1)}) custom-call(s32[3]{0:T(128)S(1)} %pad_add_fusion.1.place.table, bf16[128,16384]{1,0:T(8,128)(2,1)} %bitcast.22, bf16[1,128,2048]{2,1,0:T(8,128)(2,1)S(1)} %collective-permute-done.3.far), custom_call_target="tpu_custom_call" | custom-call | tf_op jit(solution)/shard_map/pair_far/pallas_call | solution.py:183
  8.7 1.6 %collective-permute-start.4 = (bf16[64,2048]{1,0:T(8,128)(2,1)S(1)}, bf16[64,2048]{1,0:T(8,128)(2,1)S(1)}, u32[]{:S(2)}, u32[]{:S(2)}) collective-permute-start(bf16[64,2048]{1,0:T(8,128)(2,1)S(1)} %get-tuple-element.52), channel_id=1, source_target_pairs={{0,32},{16,48},{32,64},{48,80},{64,96},{80,112},{96,0},{112,16},{1... | collective-permute-start | bytes 786440 | tf_op jit(solution)/shard_map/ppermute | solution.py:271
  10.3 1.7 %collective-permute-start.6 = (bf16[64,2048]{1,0:T(8,128)(2,1)S(1)}, bf16[64,2048]{1,0:T(8,128)(2,1)S(1)}, u32[]{:S(2)}, u32[]{:S(2)}) collective-permute-start(bf16[64,2048]{1,0:T(8,128)(2,1)S(1)} %get-tuple-element.54), channel_id=1, source_target_pairs={{0,96},{16,112},{32,0},{48,16},{64,32},{80,48},{96,64},{112,80},{1... | collective-permute-start | bytes 786440 | tf_op jit(solution)/shard_map/ppermute | solution.py:272
  12.0 2.1 %pair_near.1 = (bf16[64,2048]{1,0:T(8,128)(2,1)S(1)}, bf16[64,2048]{1,0:T(8,128)(2,1)S(1)}, f32[64,2048]{1,0:T(8,128)S(1)}, f32[64,2048]{1,0:T(8,128)S(1)}, f32[128,2048]{1,0:T(8,128)S(1)}) custom-call(s32[3]{0:T(128)S(1)} %pad_add_fusion.1.place.table, bf16[128,16384]{1,0:T(8,128)(2,1)} %bitcast.23, bf16[3,128,2048]{2,1,0:T(8,128)(2,1)S(1)} %collective-permute-done.far), custom_call_target="tpu_custom_call" | custom-call | tf_op jit(solution)/shard_map/pair_near/pallas_call | solution.py:183
  14.1 0.4 collective-permute-start.1
  14.5 2.9 %collective-permute-start.2 = (bf16[64,2048]{1,0:T(8,128)(2,1)S(1)}, bf16[64,2048]{1,0:T(8,128)(2,1)S(1)}, u32[]{:S(2)}, u32[]{:S(2)}) collective-permute-start(bf16[64,2048]{1,0:T(8,128)(2,1)S(1)} %get-tuple-element.50), channel_id=1, source_target_pairs={{0,96},{16,112},{32,0},{48,16},{64,32},{80,48},{96,64},{112,80},{1... | collective-permute-start | bytes 786440 | tf_op jit(solution)/shard_map/ppermute | solution.py:278
  17.4 1.6 %collective-permute-done.4.arrived = bf16[64,2048]{1,0:T(8,128)(2,1)S(1)} collective-permute-done((bf16[64,2048]{1,0:T(8,128)(2,1)S(1)}, bf16[64,2048]{1,0:T(8,128)(2,1)S(1)}, u32[]{:S(2)}, u32[]{:S(2)}) %collective-permute-start.4) | collective-permute-done | bytes 262176 | tf_op jit(solution)/shard_map/ppermute | solution.py:271
  19.0 0.6 relay.2
  19.6 0.5 collective-permute-start.5
  20.1 0.6 relay.3
  20.7 2.9 %collective-permute-start.7 = (bf16[64,2048]{1,0:T(8,128)(2,1)S(1)}, bf16[64,2048]{1,0:T(8,128)(2,1)S(1)}, u32[]{:S(2)}, u32[]{:S(2)}) collective-permute-start(bf16[64,2048]{1,0:T(8,128)(2,1)S(1)} %relay.3), channel_id=1, source_target_pairs={{0,96},{16,112},{32,0},{48,16},{64,32},{80,48},{96,64},{112,80},{1... | collective-permute-start | bytes 786440 | tf_op jit(solution)/shard_map/ppermute | solution.py:280
  23.6 6.9 %prepare.1 = (bf16[2,512,512]{2,1,0:T(8,128)(2,1)}, bf16[2,512,512]{2,1,0:T(8,128)(2,1)}, bf16[2,512,512]{2,1,0:T(8,128)(2,1)}, bf16[2,512,512]{2,1,0:T(8,128)(2...) custom-call(f32[2,512,512]{2,1,0:T(8,128)} %bitcast.30, f32[2,512,512]{2,1,0:T(8,128)} %bitcast.31, ...), custom_call_target="tpu_custom_call" | custom-call | flops 3221225472 | bytes 13631488 | tf_op jit(solution)/shard_map/prepare/pallas_call | solution.py:55
  30.5 0.9 finish.1
  31.4 2.0 %collective-permute-start.8 = (bf16[32,2176]{1,0:T(8,128)(2,1)S(1)}, bf16[32,2176]{1,0:T(8,128)(2,1)S(1)}, u32[]{:S(2)}, u32[]{:S(2)}) collective-permute-start(bf16[32,2176]{1,0:T(8,128)(2,1)S(1)} %get-tuple-element.67), channel_id=1, source_target_pairs={{0,4},{1,5},{2,6},{3,7},{4,8},{5,9},{6,10},{7,11},{8,12},{9,13},{1... | collective-permute-start | bytes 417800 | tf_op jit(solution)/shard_map/ppermute | solution.py:288
  33.4 3.6 %collective-permute-start.9 = (bf16[32,2176]{1,0:T(8,128)(2,1)S(1)}, bf16[32,2176]{1,0:T(8,128)(2,1)S(1)}, u32[]{:S(2)}, u32[]{:S(2)}) collective-permute-start(bf16[32,2176]{1,0:T(8,128)(2,1)S(1)} %get-tuple-element.68), channel_id=1, source_target_pairs={{0,8},{1,9},{2,10},{3,11},{4,12},{5,13},{6,14},{7,15},{8,0},{9,1},... | collective-permute-start | bytes 417800 | tf_op jit(solution)/shard_map/ppermute | solution.py:288
  37.0 1.0 collective-permute-start.10
  38.1 2.0 %collective-permute-done.8.refs_1_ = bf16[32,2176]{1,0:T(8,128)(2,1)S(1)} collective-permute-done((bf16[32,2176]{1,0:T(8,128)(2,1)S(1)}, bf16[32,2176]{1,0:T(8,128)(2,1)S(1)}, u32[]{:S(2)}, u32[]{:S(2)}) %collective-permute-start.8) | collective-permute-done | bytes 139296 | tf_op jit(solution)/shard_map/ppermute | solution.py:288
  40.1 2.0 %collective-permute-done.9.refs_2_ = bf16[32,2176]{1,0:T(8,128)(2,1)S(1)} collective-permute-done((bf16[32,2176]{1,0:T(8,128)(2,1)S(1)}, bf16[32,2176]{1,0:T(8,128)(2,1)S(1)}, u32[]{:S(2)}, u32[]{:S(2)}) %collective-permute-start.9) | collective-permute-done | bytes 139296 | tf_op jit(solution)/shard_map/ppermute | solution.py:288
  42.1 1.6 %dispatch.1 = (bf16[32,32,512]{2,1,0:T(8,128)(2,1)}, f32[8,128]{1,0:T(8,128)S(1)}) custom-call(s32[1,17]{1,0:T(1,128)S(1)} %pad_add_fusion.table, bf16[32,2176]{1,0:T(8,128)(2,1)S(1)} %get-tuple-element.66.refs_0_, bf16[32,2176]{1,0:T(8,128)(2,1)S(1)} %collective-permute-done.8.refs_1_, bf16[32,2176]{1,0:T(8,128)(2,1)S(1)} %collective-permute-done.9.refs_2_, ...), custom_call_target="tpu_custom_call" | custom-call | tf_op jit(solution)/shard_map/dispatch/pallas_call | solution.py:70
  43.7 6.6 %all-to-all-start = ((bf16[16,2,32,512]{3,2,1,0:T(8,128)(2,1)}), bf16[16,2,32,512]{3,2,1,0:T(8,128)(2,1)S(1)}, u32[]{:S(2)}, u32[]{:S(2)}) async-start(bf16[16,2,32,512]{3,2,1,0:T(8,128)(2,1)} %bitcast.9), calls=%async_computation | async-start | bytes 2097152 | tf_op jit(solution)/shard_map/all_to_all | solution.py:470
  50.3 1.2 %collective-permute-done.11.refs_1_ = f32[8,128]{1,0:T(8,128)S(1)} collective-permute-done((f32[8,128]{1,0:T(8,128)S(1)}, f32[8,128]{1,0:T(8,128)S(1)}, u32[]{:S(2)}, u32[]{:S(2)}) %collective-permute-start.11) | collective-permute-done | bytes 4128 | tf_op jit(solution)/shard_map/ppermute | solution.py:293
  51.5 0.5 plus.3.refs_0_
  52.0 2.1 %collective-permute-start.14 = (f32[8,128]{1,0:T(8,128)S(1)}, f32[8,128]{1,0:T(8,128)S(1)}, u32[]{:S(2)}, u32[]{:S(2)}) collective-permute-start(f32[8,128]{1,0:T(8,128)S(1)} %plus.3.refs_0_), channel_id=1, source_target_pairs={{0,96},{16,112},{32,0},{48,16},{64,32},{80,48},{96,64},{112,80},{1... | collective-permute-start | bytes 12296 | tf_op jit(solution)/shard_map/ppermute | solution.py:293
  54.2 0.7 collective-permute-start.13
  54.9 0.6 collective-permute-start.12
  55.7 3.6 %collective-permute-done.13.refs_2_ = f32[8,128]{1,0:T(8,128)S(1)} collective-permute-done((f32[8,128]{1,0:T(8,128)S(1)}, f32[8,128]{1,0:T(8,128)S(1)}, u32[]{:S(2)}, u32[]{:S(2)}) %collective-permute-start.13) | collective-permute-done | bytes 4128 | tf_op jit(solution)/shard_map/ppermute | solution.py:293
  59.3 0.4 collective-permute-done.12.refs_1_
  59.7 0.5 plus.4.refs_0_
  60.2 3.1 %collective-permute-start.17 = (f32[8,128]{1,0:T(8,128)S(1)}, f32[8,128]{1,0:T(8,128)S(1)}, u32[]{:S(2)}, u32[]{:S(2)}) collective-permute-start(f32[8,128]{1,0:T(8,128)S(1)} %plus.4.refs_0_), channel_id=1, source_target_pairs={{0,3},{1,0},{2,1},{3,2},{4,7},{5,4},{6,5},{7,6},{8,11},{9,8},{10,9... | collective-permute-start | bytes 12296 | tf_op jit(solution)/shard_map/ppermute | solution.py:293
  63.4 0.9 collective-permute-start.16
  64.2 0.9 collective-permute-start.15
  65.1 3.4 %collective-permute-done.16.refs_2_ = f32[8,128]{1,0:T(8,128)S(1)} collective-permute-done((f32[8,128]{1,0:T(8,128)S(1)}, f32[8,128]{1,0:T(8,128)S(1)}, u32[]{:S(2)}, u32[]{:S(2)}) %collective-permute-start.16) | collective-permute-done | bytes 4128 | tf_op jit(solution)/shard_map/ppermute | solution.py:293
  68.5 0.6 collective-permute-done.15.refs_1_
  69.0 0.5 plus.5.refs_2_
  69.6 9.2 %direction.1 = (bf16[16,2,32,512]{3,2,1,0:T(8,128)(2,1)}, f32[2,512,512]{2,1,0:T(8,128)}) custom-call(s32[1,16]{1,0:T(1,128)S(1)} %copy-done, s32[1]{0:T(128)} %bitcast.1.refs_1_, f32[8,128]{1,0:T(8,128)S(1)} %plus.5.refs_2_, bf16[16,2,32,512]{3,2,1,0:T(8,128)(2,1)S(1)} %all-to-all-done.refs_3_, f32[2,512,512]{2,1,0:T(8,128)} %bitcast.24, ...), custom_call_target="tpu_custom_call" | custom-call | tf_op jit(solution)/shard_map/direction/pallas_call | solution.py:375
  78.8 5.3 %all-to-all-start.1 = ((bf16[16,2,32,512]{3,2,1,0:T(8,128)(2,1)}), bf16[16,2,32,512]{3,2,1,0:T(8,128)(2,1)S(1)}, u32[]{:S(2)}, u32[]{:S(2)}) async-start(bf16[16,2,32,512]{3,2,1,0:T(8,128)(2,1)} %get-tuple-element.78), calls=%async_computation.1 | async-start | bytes 2097152 | tf_op jit(solution)/shard_map/all_to_all | solution.py:478
  84.0 5.3 %factors.1 = (f32[2,512,512]{2,1,0:T(8,128)}, f32[2,512,512]{2,1,0:T(8,128)}, f32[2,512,512]{2,1,0:T(8,128)}) custom-call(s32[1,16]{1,0:T(1,128)S(1)} %copy-done, s32[1]{0:T(128)} %bitcast.1.refs_1_, f32[8,128]{1,0:T(8,128)S(1)} %plus.5.refs_2_, bf16[16,2,32,512]{3,2,1,0:T(8,128)(2,1)S(1)} %all-to-all-done.refs_3_, f32[2,512,512]{2,1,0:T(8,128)} %bitcast.27, ...), custom_call_target="tpu_custom_call" | custom-call | flops 1073741824 | bytes 13631488 | tf_op jit(solution)/shard_map/factors/pallas_call | solution.py:411
  89.4 9.4 %all-to-all-done.1 = bf16[16,2,32,512]{3,2,1,0:T(8,128)(2,1)S(1)} async-done(((bf16[16,2,32,512]{3,2,1,0:T(8,128)(2,1)}), bf16[16,2,32,512]{3,2,1,0:T(8,128)(2,1)S(1)}, u32[]{:S(2)}, u32[]{:S(2)}) %all-to-all-start.1) | async-done | bytes 1048608 | tf_op jit(solution)/shard_map/all_to_all | solution.py:478
  98.7 0.6 collect.1
  99.4 2.7 %collective-permute-start.19 = (bf16[32,2048]{1,0:T(8,128)(2,1)S(1)}, bf16[32,2048]{1,0:T(8,128)(2,1)S(1)}, u32[]{:S(2)}, u32[]{:S(2)}) collective-permute-start(bf16[32,2048]{1,0:T(8,128)(2,1)S(1)} %get-tuple-element.85), channel_id=1, source_target_pairs={{0,8},{1,9},{2,10},{3,11},{4,12},{5,13},{6,14},{7,15},{8,0},{9,1},... | collective-permute-start | bytes 393224 | tf_op jit(solution)/shard_map/ppermute | solution.py:288
  102.1 0.9 collective-permute-start.20
  103.1 3.9 %collective-permute-done.18.refs_1_ = bf16[32,2048]{1,0:T(8,128)(2,1)S(1)} collective-permute-done((bf16[32,2048]{1,0:T(8,128)(2,1)S(1)}, bf16[32,2048]{1,0:T(8,128)(2,1)S(1)}, u32[]{:S(2)}, u32[]{:S(2)}) %collective-permute-start.18) | collective-permute-done | bytes 131104 | tf_op jit(solution)/shard_map/ppermute | solution.py:288
  107.0 0.9 collective-permute-done.20.refs_3_
  107.8 1.4 %put.1 = bf16[4,32,2048]{2,1,0:T(8,128)(2,1)} custom-call(s32[1,17]{1,0:T(1,128)S(1)} %pad_add_fusion.table, bf16[32,2048]{1,0:T(8,128)(2,1)S(1)} %get-tuple-element.83.refs_0_, bf16[32,2048]{1,0:T(8,128)(2,1)S(1)} %collective-permute-done.18.refs_1_, bf16[32,2048]{1,0:T(8,128)(2,1)S(1)} %collective-permute-done.19.refs_2_, ...), custom_call_target="tpu_custom_call" | custom-call | tf_op jit(solution)/shard_map/put/pallas_call | solution.py:70
  (18 shorter events, 0.7 us)
Async XLA Ops:
  2.7 9.3 %collective-permute-start = (bf16[3,128,2048]{2,1,0:T(8,128)(2,1)S(1)}, bf16[3,128,2048]{2,1,0:T(8,128)(2,1)S(1)}, u32[]{:S(2)}, u32[]{:S(2)}) collective-permute-start(bf16[3,128,2048]{2,1,0:T(8,128)(2,1)S(1)} %pick.2), channel_id=1, source_target_pairs={{0,16},{16,0},{32,48},{48,32},{64,80},{80,64},{96,112},{112,96},{1... | collective-permute-start | bytes 4718600 | tf_op jit(solution)/shard_map/ppermute | solution.py:267
  4.4 2.5 %collective-permute-start.3 = (bf16[1,128,2048]{2,1,0:T(8,128)(2,1)S(1)}, bf16[1,128,2048]{2,1,0:T(8,128)(2,1)S(1)}, u32[]{:S(2)}, u32[]{:S(2)}) collective-permute-start(bf16[1,128,2048]{2,1,0:T(8,128)(2,1)S(1)} %pick.3), channel_id=1, source_target_pairs={{0,16},{16,0},{32,48},{48,32},{64,80},{80,64},{96,112},{112,96},{1... | collective-permute-start | bytes 1572872 | tf_op jit(solution)/shard_map/ppermute | solution.py:266
  8.7 10.3 %collective-permute-start.4 = (bf16[64,2048]{1,0:T(8,128)(2,1)S(1)}, bf16[64,2048]{1,0:T(8,128)(2,1)S(1)}, u32[]{:S(2)}, u32[]{:S(2)}) collective-permute-start(bf16[64,2048]{1,0:T(8,128)(2,1)S(1)} %get-tuple-element.52), channel_id=1, source_target_pairs={{0,32},{16,48},{32,64},{48,80},{64,96},{80,112},{96,0},{112,16},{1... | collective-permute-start | bytes 786440 | tf_op jit(solution)/shard_map/ppermute | solution.py:271
  10.3 9.8 %collective-permute-start.6 = (bf16[64,2048]{1,0:T(8,128)(2,1)S(1)}, bf16[64,2048]{1,0:T(8,128)(2,1)S(1)}, u32[]{:S(2)}, u32[]{:S(2)}) collective-permute-start(bf16[64,2048]{1,0:T(8,128)(2,1)S(1)} %get-tuple-element.54), channel_id=1, source_target_pairs={{0,96},{16,112},{32,0},{48,16},{64,32},{80,48},{96,64},{112,80},{1... | collective-permute-start | bytes 786440 | tf_op jit(solution)/shard_map/ppermute | solution.py:272
  14.1 16.4 %collective-permute-start.1 = (bf16[64,2048]{1,0:T(8,128)(2,1)S(1)}, bf16[64,2048]{1,0:T(8,128)(2,1)S(1)}, u32[]{:S(2)}, u32[]{:S(2)}) collective-permute-start(bf16[64,2048]{1,0:T(8,128)(2,1)S(1)} %get-tuple-element.49), channel_id=1, source_target_pairs={{0,32},{16,48},{32,64},{48,80},{64,96},{80,112},{96,0},{112,16},{1... | collective-permute-start | bytes 786440 | tf_op jit(solution)/shard_map/ppermute | solution.py:277
  14.5 16.0 %collective-permute-start.2 = (bf16[64,2048]{1,0:T(8,128)(2,1)S(1)}, bf16[64,2048]{1,0:T(8,128)(2,1)S(1)}, u32[]{:S(2)}, u32[]{:S(2)}) collective-permute-start(bf16[64,2048]{1,0:T(8,128)(2,1)S(1)} %get-tuple-element.50), channel_id=1, source_target_pairs={{0,96},{16,112},{32,0},{48,16},{64,32},{80,48},{96,64},{112,80},{1... | collective-permute-start | bytes 786440 | tf_op jit(solution)/shard_map/ppermute | solution.py:278
  19.6 10.9 %collective-permute-start.5 = (bf16[64,2048]{1,0:T(8,128)(2,1)S(1)}, bf16[64,2048]{1,0:T(8,128)(2,1)S(1)}, u32[]{:S(2)}, u32[]{:S(2)}) collective-permute-start(bf16[64,2048]{1,0:T(8,128)(2,1)S(1)} %relay.2), channel_id=1, source_target_pairs={{0,32},{16,48},{32,64},{48,80},{64,96},{80,112},{96,0},{112,16},{1... | collective-permute-start | bytes 786440 | tf_op jit(solution)/shard_map/ppermute | solution.py:279
  20.7 9.8 %collective-permute-start.7 = (bf16[64,2048]{1,0:T(8,128)(2,1)S(1)}, bf16[64,2048]{1,0:T(8,128)(2,1)S(1)}, u32[]{:S(2)}, u32[]{:S(2)}) collective-permute-start(bf16[64,2048]{1,0:T(8,128)(2,1)S(1)} %relay.3), channel_id=1, source_target_pairs={{0,96},{16,112},{32,0},{48,16},{64,32},{80,48},{96,64},{112,80},{1... | collective-permute-start | bytes 786440 | tf_op jit(solution)/shard_map/ppermute | solution.py:280
  30.4 7.6 %copy-start = (s32[1,16]{1,0:T(1,128)S(1)}, s32[1,16]{1,0:T(1,128)}, u32[]{:S(2)}) copy-start(s32[1,16]{1,0:T(1,128)} %refs_0_.3) | copy-start | bytes 196
  31.4 8.7 %collective-permute-start.8 = (bf16[32,2176]{1,0:T(8,128)(2,1)S(1)}, bf16[32,2176]{1,0:T(8,128)(2,1)S(1)}, u32[]{:S(2)}, u32[]{:S(2)}) collective-permute-start(bf16[32,2176]{1,0:T(8,128)(2,1)S(1)} %get-tuple-element.67), channel_id=1, source_target_pairs={{0,4},{1,5},{2,6},{3,7},{4,8},{5,9},{6,10},{7,11},{8,12},{9,13},{1... | collective-permute-start | bytes 417800 | tf_op jit(solution)/shard_map/ppermute | solution.py:288
  33.4 8.6 %collective-permute-start.9 = (bf16[32,2176]{1,0:T(8,128)(2,1)S(1)}, bf16[32,2176]{1,0:T(8,128)(2,1)S(1)}, u32[]{:S(2)}, u32[]{:S(2)}) collective-permute-start(bf16[32,2176]{1,0:T(8,128)(2,1)S(1)} %get-tuple-element.68), channel_id=1, source_target_pairs={{0,8},{1,9},{2,10},{3,11},{4,12},{5,13},{6,14},{7,15},{8,0},{9,1},... | collective-permute-start | bytes 417800 | tf_op jit(solution)/shard_map/ppermute | solution.py:288
  37.0 5.1 %collective-permute-start.10 = (bf16[32,2176]{1,0:T(8,128)(2,1)S(1)}, bf16[32,2176]{1,0:T(8,128)(2,1)S(1)}, u32[]{:S(2)}, u32[]{:S(2)}) collective-permute-start(bf16[32,2176]{1,0:T(8,128)(2,1)S(1)} %get-tuple-element.69), channel_id=1, source_target_pairs={{0,12},{1,13},{2,14},{3,15},{4,0},{5,1},{6,2},{7,3},{8,4},{9,5},{1... | collective-permute-start | bytes 417800 | tf_op jit(solution)/shard_map/ppermute | solution.py:288
  43.7 25.9 %all-to-all-start = ((bf16[16,2,32,512]{3,2,1,0:T(8,128)(2,1)}), bf16[16,2,32,512]{3,2,1,0:T(8,128)(2,1)S(1)}, u32[]{:S(2)}, u32[]{:S(2)}) async-start(bf16[16,2,32,512]{3,2,1,0:T(8,128)(2,1)} %bitcast.9), calls=%async_computation | async-start | bytes 2097152 | tf_op jit(solution)/shard_map/all_to_all | solution.py:470
  50.2 1.2 %collective-permute-start.11 = (f32[8,128]{1,0:T(8,128)S(1)}, f32[8,128]{1,0:T(8,128)S(1)}, u32[]{:S(2)}, u32[]{:S(2)}) collective-permute-start(f32[8,128]{1,0:T(8,128)S(1)} %get-tuple-element.70.refs_0_), channel_id=1, source_target_pairs={{0,16},{16,0},{32,48},{48,32},{64,80},{80,64},{96,112},{112,96},{1... | collective-permute-start | bytes 12296 | tf_op jit(solution)/shard_map/ppermute | solution.py:293
  52.0 3.7 %collective-permute-start.14 = (f32[8,128]{1,0:T(8,128)S(1)}, f32[8,128]{1,0:T(8,128)S(1)}, u32[]{:S(2)}, u32[]{:S(2)}) collective-permute-start(f32[8,128]{1,0:T(8,128)S(1)} %plus.3.refs_0_), channel_id=1, source_target_pairs={{0,96},{16,112},{32,0},{48,16},{64,32},{80,48},{96,64},{112,80},{1... | collective-permute-start | bytes 12296 | tf_op jit(solution)/shard_map/ppermute | solution.py:293
  54.2 5.1 %collective-permute-start.13 = (f32[8,128]{1,0:T(8,128)S(1)}, f32[8,128]{1,0:T(8,128)S(1)}, u32[]{:S(2)}, u32[]{:S(2)}) collective-permute-start(f32[8,128]{1,0:T(8,128)S(1)} %plus.3.refs_0_), channel_id=1, source_target_pairs={{0,64},{16,80},{32,96},{48,112},{64,0},{80,16},{96,32},{112,48},{1... | collective-permute-start | bytes 12296 | tf_op jit(solution)/shard_map/ppermute | solution.py:293
  54.9 4.8 %collective-permute-start.12 = (f32[8,128]{1,0:T(8,128)S(1)}, f32[8,128]{1,0:T(8,128)S(1)}, u32[]{:S(2)}, u32[]{:S(2)}) collective-permute-start(f32[8,128]{1,0:T(8,128)S(1)} %plus.3.refs_0_), channel_id=1, source_target_pairs={{0,32},{16,48},{32,64},{48,80},{64,96},{80,112},{96,0},{112,16},{1... | collective-permute-start | bytes 12296 | tf_op jit(solution)/shard_map/ppermute | solution.py:293
  60.2 4.8 %collective-permute-start.17 = (f32[8,128]{1,0:T(8,128)S(1)}, f32[8,128]{1,0:T(8,128)S(1)}, u32[]{:S(2)}, u32[]{:S(2)}) collective-permute-start(f32[8,128]{1,0:T(8,128)S(1)} %plus.4.refs_0_), channel_id=1, source_target_pairs={{0,3},{1,0},{2,1},{3,2},{4,7},{5,4},{6,5},{7,6},{8,11},{9,8},{10,9... | collective-permute-start | bytes 12296 | tf_op jit(solution)/shard_map/ppermute | solution.py:293
  63.4 5.1 %collective-permute-start.16 = (f32[8,128]{1,0:T(8,128)S(1)}, f32[8,128]{1,0:T(8,128)S(1)}, u32[]{:S(2)}, u32[]{:S(2)}) collective-permute-start(f32[8,128]{1,0:T(8,128)S(1)} %plus.4.refs_0_), channel_id=1, source_target_pairs={{0,2},{1,3},{2,0},{3,1},{4,6},{5,7},{6,4},{7,5},{8,10},{9,11},{10,... | collective-permute-start | bytes 12296 | tf_op jit(solution)/shard_map/ppermute | solution.py:293
  64.2 4.8 %collective-permute-start.15 = (f32[8,128]{1,0:T(8,128)S(1)}, f32[8,128]{1,0:T(8,128)S(1)}, u32[]{:S(2)}, u32[]{:S(2)}) collective-permute-start(f32[8,128]{1,0:T(8,128)S(1)} %plus.4.refs_0_), channel_id=1, source_target_pairs={{0,1},{1,2},{2,3},{3,0},{4,5},{5,6},{6,7},{7,4},{8,9},{9,10},{10,1... | collective-permute-start | bytes 12296 | tf_op jit(solution)/shard_map/ppermute | solution.py:293
  78.8 20.0 %all-to-all-start.1 = ((bf16[16,2,32,512]{3,2,1,0:T(8,128)(2,1)}), bf16[16,2,32,512]{3,2,1,0:T(8,128)(2,1)S(1)}, u32[]{:S(2)}, u32[]{:S(2)}) async-start(bf16[16,2,32,512]{3,2,1,0:T(8,128)(2,1)} %get-tuple-element.78), calls=%async_computation.1 | async-start | bytes 2097152 | tf_op jit(solution)/shard_map/all_to_all | solution.py:478
  99.3 7.7 %collective-permute-start.18 = (bf16[32,2048]{1,0:T(8,128)(2,1)S(1)}, bf16[32,2048]{1,0:T(8,128)(2,1)S(1)}, u32[]{:S(2)}, u32[]{:S(2)}) collective-permute-start(bf16[32,2048]{1,0:T(8,128)(2,1)S(1)} %get-tuple-element.84), channel_id=1, source_target_pairs={{0,4},{1,5},{2,6},{3,7},{4,8},{5,9},{6,10},{7,11},{8,12},{9,13},{1... | collective-permute-start | bytes 393224 | tf_op jit(solution)/shard_map/ppermute | solution.py:288
  99.4 7.6 %collective-permute-start.19 = (bf16[32,2048]{1,0:T(8,128)(2,1)S(1)}, bf16[32,2048]{1,0:T(8,128)(2,1)S(1)}, u32[]{:S(2)}, u32[]{:S(2)}) collective-permute-start(bf16[32,2048]{1,0:T(8,128)(2,1)S(1)} %get-tuple-element.85), channel_id=1, source_target_pairs={{0,8},{1,9},{2,10},{3,11},{4,12},{5,13},{6,14},{7,15},{8,0},{9,1},... | collective-permute-start | bytes 393224 | tf_op jit(solution)/shard_map/ppermute | solution.py:288
  102.1 5.7 %collective-permute-start.20 = (bf16[32,2048]{1,0:T(8,128)(2,1)S(1)}, bf16[32,2048]{1,0:T(8,128)(2,1)S(1)}, u32[]{:S(2)}, u32[]{:S(2)}) collective-permute-start(bf16[32,2048]{1,0:T(8,128)(2,1)S(1)} %get-tuple-element.86), channel_id=1, source_target_pairs={{0,12},{1,13},{2,14},{3,15},{4,0},{5,1},{6,2},{7,3},{8,4},{9,5},{1... | collective-permute-start | bytes 393224 | tf_op jit(solution)/shard_map/ppermute | solution.py:288
where the time goes:
time: 110 us; the launch traced here: 109 us
  starting transfers between devices  41.2 us (37%)
  Pallas kernels  35.9 us (33%)
  waiting for transfers between devices  31.1 us (28%)
    ppermute x6, starting transfers between devices, exchange(): got[j] = lax.ppermute(arrays[j], *steps[j - 1])  10.4 us
    all_to_all x1, waiting for transfers between devices, per_device(): lax.all_to_all(update, 'fsdp', split_axis=0, concat_axis=0, tiled=True)  9.37 us
    ppermute x7, waiting for transfers between devices, add_up(): arrived = [lax.ppermute(value, axis, perm) for axis, perm in steps]  9.34 us
    pallas_call x1, Pallas kernels, direction(): pl.pallas_call(body, in_specs=[scalar] * 2 + [whole] * 2 + [far] * 7, out...  9.16 us
    ppermute x6, waiting for transfers between devices, exchange(): got[j] = lax.ppermute(arrays[j], *steps[j - 1])  8.76 us
    ppermute x7, starting transfers between devices, add_up(): arrived = [lax.ppermute(value, axis, perm) for axis, perm in steps]  8.33 us
    pallas_call x9, Pallas kernels, local(): pl.pallas_call(body, in_specs=[pl.BlockSpec(memory_space=SMEM)] + [pl.Blo...  7.23 us
    pallas_call x1, Pallas kernels, prepare(): pl.pallas_call(prepare_body, grid=(slots,), in_specs=[block] * 3, out_spe...  6.87 us
  transfers between devices with their start and end apart: 23, of which 13 were waited for; matrix products, arithmetic and copies ran while one was open for 0% of the time, Pallas kernels for 19%

commit v1 on v0

v1 whole, which is shorter than its diff:
```python
import jax
import jax.numpy as jnp
from jax import lax
from jax.experimental import pallas as pl
from jax.experimental.pallas import tpu as pltpu
from jax.sharding import PartitionSpec as P

f32 = jnp.float32
bf16 = jnp.bfloat16
SMEM = pltpu.MemorySpace.SMEM
VMEM = pltpu.MemorySpace.VMEM
HBM = pltpu.MemorySpace.HBM
LANES = 128


def in_hbm(*arrays):
    return [pltpu.with_memory_space_constraint(a, HBM) for a in arrays]


def split3(value):
    head, rest = split(value)
    mid, tail = split(value - head.astype(f32))
    return head, mid, tail


def split(value):
    head = value.astype(bf16)
    return head, (value - head.astype(f32)).astype(bf16)


def mm(a, b, dims=((1,), (0,))):
    return lax.dot_general(a, b, (dims, ((), ())), preferred_element_type=f32)


def tiles(count, size=32):
    return [slice(r, r + size) for r in range(0, count, size)]


def prepare_body(left_ref, right_ref, first_ref, lt_ref, l_ref, r_ref, rot_ref, half, product):
    n = left_ref.shape[1]
    for rows in tiles(n, LANES):
        head, tail = split(left_ref[0, rows].T)
        lt_ref[0, :n, rows] = head
        lt_ref[0, n:, rows] = tail
    for rows in tiles(n):
        l_ref[0, rows] = left_ref[0, rows].astype(bf16)
        head, tail = split(right_ref[0, rows])
        r_ref[0, rows, :n] = head
        r_ref[0, rows, n:] = tail
        half[rows] = first_ref[0, rows].astype(bf16)
    product[...] = mm(lt_ref[0], half[...])
    for rows, more in zip(tiles(n), tiles(2 * n)[n // 32 :]):
        half[rows] = (product[rows] + product[more]).astype(bf16)
    right = r_ref[0]
    rot_ref[0] = 0.9 * (mm(half[...], right[:, :n]) + mm(half[...], right[:, n:]))


def prepare(left_basis, right_basis, first_moment):
    slots, n, _ = left_basis.shape
    block = pl.BlockSpec((1, n, n), lambda s: (s, 0, 0))
    return pl.pallas_call(
        prepare_body,
        grid=(slots,),
        in_specs=[block] * 3,
        out_specs=[
            pl.BlockSpec((1, 2 * n, n), lambda s: (s, 0, 0)),
            block,
            pl.BlockSpec((1, n, 2 * n), lambda s: (s, 0, 0)),
            block,
        ],
        out_shape=[
            HBM((slots, 2 * n, n), bf16),
            HBM((slots, n, n), bf16),
            HBM((slots, n, 2 * n), bf16),
            HBM((slots, n, n), f32),
        ],
        scratch_shapes=[pltpu.VMEM((n, n), bf16), pltpu.VMEM((2 * n, n), f32)],
        compiler_params=pltpu.CompilerParams(vmem_limit_bytes=24 << 20),
        cost_estimate=pl.CostEstimate(
            flops=slots * 8 * n**3, bytes_accessed=slots * 26 * n * n, transcendentals=0
        ),
        name="prepare",
    )(*in_hbm(left_basis, right_basis, first_moment))


def local(body, arrays, out_shape, name, limit=8 << 20):
    return pl.pallas_call(
        body,
        in_specs=[pl.BlockSpec(memory_space=SMEM)]
        + [pl.BlockSpec(memory_space=VMEM)] * (len(arrays) - 1),
        out_specs=jax.tree.map(
            lambda _: pl.BlockSpec(memory_space=VMEM), out_shape, is_leaf=lambda o: hasattr(o, "shape")
        ),
        out_shape=out_shape,
        compiler_params=pltpu.CompilerParams(vmem_limit_bytes=limit),
        name=name,
    )(*arrays)


def dispatch_body(table, *refs):
    *squares, dst = refs[4:]
    srcs = refs[:4]
    n = dst.shape[2]
    rows, width = srcs[0].shape
    bands = len(srcs)
    cols = width // n
    slots = (dst.shape[1] - 8) // rows
    z = table[0, bands * cols]
    for j, src in enumerate(srcs):
        band = lax.rem(z + bands - j, bands)
        for c in range(cols):
            slot = table[0, band * cols + c]
            row = pl.multiple_of(lax.rem(slot, slots) * rows, rows)
            dst[slot // slots, pl.ds(row, rows)] = src[:, c * n : (c + 1) * n]
    total = squares[0][...]
    for square in squares[1:]:
        total = total + square[...]
    terms = [t.astype(f32) for t in split3(total)]
    terms.append(jnp.zeros((8, n - 3 * LANES), f32))
    terms = jnp.concatenate(terms, axis=1).astype(bf16)
    for o in range(dst.shape[0]):
        dst[o, slots * rows :] = terms


def collect_body(table, src, *dsts):
    n = src.shape[2]
    bands = len(dsts)
    cols = dsts[0].shape[1] // n
    z = table[0, bands * cols]
    for j, dst in enumerate(dsts):
        band = lax.rem(z + j, bands)
        for c in range(cols):
            dst[:, c * n : (c + 1) * n] = src[table[0, band * cols + c]]


def put_body(table, *refs):
    *srcs, dst = refs
    bands = len(srcs)
    z = table[0, table.shape[1] - 1]
    for j, src in enumerate(srcs):
        dst[lax.rem(z + bands - j, bands)] = src[...]


def plus_body(place, a, b, out):
    out[...] = a[...] + b[...]


def load(place, grads, width):
    rows, columns = grads.shape
    chips = columns // width // 2
    groups = ((2,), (1, 3, 0))

    def body(place, src, *refs):
        *dsts, sems = refs
        copies = []
        for i, dst in enumerate(dsts):
            core = 1 - place[1] if i < 2 else place[1]
            for k, j in enumerate(groups[i % 2]):
                slab = 2 * lax.rem(place[0] + j, chips) + core
                columns = pl.ds(pl.multiple_of(slab * width, width), width)
                copies.append(
                    pltpu.make_async_copy(src.at[:, columns], dst.at[k], sems.at[len(copies)])
                )
        for c in copies:
            c.start()
        for c in copies:
            c.wait()

    return pl.pallas_call(
        body,
        in_specs=[pl.BlockSpec(memory_space=SMEM), pl.BlockSpec(memory_space=HBM)],
        out_specs=[pl.BlockSpec(memory_space=VMEM)] * 4,
        out_shape=[VMEM((len(g), rows, width), bf16) for g in groups * 2],
        scratch_shapes=[pltpu.SemaphoreType.DMA((2 * chips,))],
        compiler_params=pltpu.CompilerParams(vmem_limit_bytes=2 << 20),
        name="load",
    )(place, *in_hbm(grads))


def pair(body, place, near, far, outs, name):
    low = near.shape[1] // 2

    def run(place, near, far, *outs):
        def total(i, a):
            part = slice(a * low, (a + 1) * low)
            return near[i, part].astype(f32) + far[i, part].astype(f32)

        body(total, low, *outs)

    out = [jax.ShapeDtypeStruct(shape, kind) for shape, kind in outs]
    return local(run, [place, near, far], out, name)


def far_body(total, low, to_right, to_left):
    to_right[...] = total(0, 0).astype(bf16)
    to_left[...] = total(0, 1).astype(bf16)


def near_body(total, low, to_right, to_left, keep_right, keep_left, own):
    keep_right[...] = total(0, 0)
    to_right[...] = total(0, 1).astype(bf16)
    to_left[...] = total(1, 0).astype(bf16)
    keep_left[...] = total(1, 1)
    for a in range(2):
        own[a * low : (a + 1) * low] = total(2, a)


def relay(place, kept, arrived):
    def body(place, kept, arrived, out):
        out[...] = (kept[...] + arrived[...].astype(f32)).astype(bf16)

    out = jax.ShapeDtypeStruct(kept.shape, bf16)
    return local(body, (place, kept, arrived), out, "relay")


def finish(place, own, left_direct, right_direct, left_sum, right_sum, bands):
    rows, width = own.shape
    low = rows // 2
    piece = rows // bands

    def body(place, own, left_direct, right_direct, left_sum, right_sum, *refs):
        *outs, square = refs
        total = jnp.zeros((8, LANES), f32)
        for q in range(bands):
            near, far = (left_sum, right_direct) if q * piece < low else (left_direct, right_sum)
            part = slice(q * piece % low, q * piece % low + piece)
            value = own[q * piece : (q + 1) * piece] + (
                near[part].astype(f32) + far[part].astype(f32)
            )
            step = lax.rem(q - place[2] + bands, bands)
            rounded = value.astype(bf16)
            for j in range(bands):

                @pl.when(step == j)
                def _():
                    outs[j][...] = rounded

            by_row = jnp.sum((value * value).reshape(piece // 8, 8, width), axis=0)
            for c in range(width // LANES):
                total = total + by_row[:, c * LANES : (c + 1) * LANES]
        square[...] = total

    arrays = [place, own, left_direct, right_direct, left_sum, right_sum]
    out = [jax.ShapeDtypeStruct((piece, width), bf16)] * bands
    out.append(jax.ShapeDtypeStruct((8, LANES), f32))
    return local(body, arrays, out, "finish", 12 << 20)


def sum_over_replicas(place, grads, bands):
    size = lax.axis_size("dp")
    rows, columns = grads.shape
    width = columns // size
    half = (rows // 2, width)
    swap = [(d, d ^ 1) for d in range(size)]
    up = [(d, (d + 2) % size) for d in range(size)]
    down = [(d, (d - 2) % size) for d in range(size)]
    far_there, near_there, far_here, near_here = load(place, grads, width)
    other = lax.ppermute(far_there, "dp", swap)
    other, near_there = lax.optimization_barrier((other, near_there))
    others = lax.ppermute(near_there, "dp", swap)
    to_right, to_left = pair(far_body, place, far_here, other, [(half, bf16)] * 2, "pair_far")
    left_far = lax.ppermute(to_right, "dp", up)
    right_far = lax.ppermute(to_left, "dp", down)
    outs = [(half, bf16)] * 2 + [(half, f32)] * 2 + [((rows, width), f32)]
    to_right, to_left, keep_right, keep_left, own = pair(
        near_body, place, near_here, others, outs, "pair_near"
    )
    left_direct = lax.ppermute(to_right, "dp", up)
    right_direct = lax.ppermute(to_left, "dp", down)
    left_sum = lax.ppermute(relay(place, keep_right, left_far), "dp", up)
    right_sum = lax.ppermute(relay(place, keep_left, right_far), "dp", down)
    return own, left_direct, right_direct, left_sum, right_sum


def exchange(arrays, steps):
    order = sorted(range(1, len(arrays)), key=lambda j: -min(j, len(arrays) - j))
    got = {0: arrays[0]}
    for j in order:
        got[j] = lax.ppermute(arrays[j], *steps[j - 1])
    return [got[j] for j in range(len(arrays))]


def assemble(pieces, slot, rows, bands):
    per = pieces.shape[0] // bands
    part = pl.ds(slot * rows, rows)
    return jnp.concatenate(
        [pieces[z * per + y, part] for y in range(per) for z in range(bands)], axis=0
    )


def is_named(table, slot):
    named = table[0, 0] == slot
    for b in range(1, table.shape[1]):
        named = jnp.logical_or(named, table[0, b] == slot)
    return named


def clip_of(pieces, entries):
    total = jnp.zeros((8, pieces.shape[2]), f32)
    for sender in range(pieces.shape[0]):
        total = total + pieces[sender, pieces.shape[1] - 8 :].astype(f32)
    total = jnp.sum(jnp.sum(total, axis=0, keepdims=True), axis=1, keepdims=True)
    return jnp.minimum(1.0, 1.0 / jnp.sqrt(total / entries + 1e-06))


def direction_body(bands, entries, table, me, pieces, second, *refs):
    lt_src, l_src, r_src, rot_src, out, second_out = refs[:6]
    lt, left, right, rot, old, new, half, product, step, sems, out_sems = refs[6:]
    slots, n, _ = second.shape
    sources, targets = (lt_src, r_src, rot_src, second, l_src), (lt, right, rot, old, left)
    copies = [
        [
            pltpu.make_async_copy(src.at[s], dst.at[s], sems.at[s, i])
            for i, (src, dst) in enumerate(zip(sources, targets))
        ]
        for s in range(slots)
    ]
    for group in copies:
        for c in group:
            c.start()
    scale = clip_of(pieces, entries)
    senders = pieces.shape[0]
    rows = n // senders
    per = senders // bands
    for s in range(slots):
        block = assemble(pieces, s, rows, bands)
        copies[s][0].wait()
        product[...] = mm(lt[s], block)
        for r, more in zip(tiles(n), tiles(2 * n)[n // 32 :]):
            half[r] = (product[r] + product[more]).astype(bf16)
        copies[s][1].wait()
        product[:n] = mm(half[...], right[s, :, :n])
        product[n:] = mm(half[...], right[s, :, n:])
        copies[s][2].wait()
        copies[s][3].wait()
        named = is_named(table, me[0] * slots + s)
        for r, more in zip(tiles(n), tiles(2 * n)[n // 32 :]):
            rotated = (product[r] + product[more]) * scale
            before = old[s, r]
            value = 0.95 * before + 0.05 * rotated * rotated
            new[s, r] = jnp.where(named, value, before)
            turned = rot[s, r] + 0.1 * rotated
            step[r] = (turned / (jnp.sqrt(value) + 1e-08)).astype(bf16)
        pltpu.make_async_copy(new.at[s], second_out.at[s], out_sems.at[s]).start()
        copies[s][4].wait()
        half[...] = mm(left[s], step[...]).astype(bf16)
        update = mm(half[...], right[s, :, :n], ((1,), (1,))).astype(bf16)
        for y in range(per):
            for z in range(bands):
                row = (y * bands + z) * rows
                out[z * per + y, s] = update[row : row + rows]
    for s in range(slots):
        pltpu.make_async_copy(new.at[s], second_out.at[s], out_sems.at[s]).wait()


def direction(table, me, pieces, prepared, second, bands, entries):
    slots, n, _ = second.shape
    senders = pieces.shape[0]
    scalar = pl.BlockSpec(memory_space=SMEM)
    whole = pl.BlockSpec(memory_space=VMEM)
    far = pl.BlockSpec(memory_space=HBM)

    def body(*refs):
        direction_body(bands, entries, *refs)

    return pl.pallas_call(
        body,
        in_specs=[scalar] * 2 + [whole] + [far] * 5,
        out_specs=[whole, far],
        out_shape=[
            jax.ShapeDtypeStruct((senders, slots, n // senders, n), bf16),
            HBM(second.shape, f32),
        ],
        scratch_shapes=[
            pltpu.VMEM((slots, 2 * n, n), bf16),
            pltpu.VMEM((slots, n, n), bf16),
            pltpu.VMEM((slots, n, 2 * n), bf16),
            pltpu.VMEM((slots, n, n), f32),
            pltpu.VMEM((slots, n, n), f32),
            pltpu.VMEM((slots, n, n), f32),
            pltpu.VMEM((n, n), bf16),
            pltpu.VMEM((2 * n, n), f32),
            pltpu.VMEM((n, n), bf16),
            pltpu.SemaphoreType.DMA((slots, 5)),
            pltpu.SemaphoreType.DMA((slots,)),
        ],
        compiler_params=pltpu.CompilerParams(vmem_limit_bytes=32 << 20),
        name="direction",
    )(table, me, pieces, *in_hbm(second, *prepared))


def factors_body(bands, entries, table, me, pieces, left, right, first, left_out, right_out, first_out):
    slot = me[0] * pl.num_programs(0) + pl.program_id(0)
    scale = clip_of(pieces, entries)
    s = assemble(pieces, pl.program_id(0), left.shape[1] // pieces.shape[0], bands)
    named = is_named(table, slot)
    square = 0.1 * scale * scale
    left_out[0] = jnp.where(named, 0.9 * left[0] + square * mm(s, s, ((1,), (1,))), left[0])
    right_out[0] = jnp.where(named, 0.9 * right[0] + square * mm(s.T, s), right[0])
    first_out[0] = jnp.where(named, 0.9 * first[0] + (0.1 * scale) * s.astype(f32), first[0])


def factors(table, me, pieces, left, right, first, bands, entries):
    slots, n, _ = left.shape
    block = pl.BlockSpec((1, n, n), lambda s: (s, 0, 0))
    scalar = pl.BlockSpec(memory_space=SMEM)
    whole = pl.BlockSpec(memory_space=VMEM)

    def body(*refs):
        factors_body(bands, entries, *refs)

    return pl.pallas_call(
        body,
        grid=(slots,),
        in_specs=[scalar] * 2 + [whole] + [block] * 3,
        out_specs=[block] * 3,
        out_shape=[HBM(left.shape, f32)] * 3,
        compiler_params=pltpu.CompilerParams(vmem_limit_bytes=32 << 20),
        cost_estimate=pl.CostEstimate(
            flops=slots * 4 * n**3, bytes_accessed=slots * 26 * n * n, transcendentals=0
        ),
        name="factors",
    )(table, me, pieces, *in_hbm(left, right, first))


def per_device(
    replica_grads,
    owners,
    left_factor,
    right_factor,
    left_basis,
    right_basis,
    first_moment,
    second_moment,
):
    rows_dev = replica_grads.shape[1]
    shards = lax.axis_size("fsdp")
    slots, n = left_factor.shape[1:3]
    per_band = n // rows_dev
    bands = shards // per_band
    dp = lax.axis_size("dp")
    dp_me = lax.axis_index("dp").astype(jnp.int32)
    me = lax.axis_index("fsdp").astype(jnp.int32)
    place = jnp.stack([dp_me // 2, dp_me % 2, me // per_band])
    table = jnp.concatenate([owners, (me // per_band).reshape(1, 1)], axis=1)
    me = me.reshape(1)
    core = ("dp", [(d, d ^ 1) for d in range(dp)])
    along_x = [("dp", [(d, (d + 2 * h) % dp) for d in range(dp)]) for h in range(1, dp // 2)]
    along_z = [
        ("fsdp", [(i, (i + h * per_band) % shards) for i in range(shards)])
        for h in range(1, bands)
    ]
    parts = sum_over_replicas(place, replica_grads[0], bands)
    prepared = prepare(left_basis[0], right_basis[0], first_moment[0])
    parts, prepared = lax.optimization_barrier((parts, prepared))
    *sums, square = finish(place, *parts, bands)
    rows, width = sums[0].shape
    cols = width // n
    entries = rows_dev * shards * replica_grads.shape[2]
    spread = exchange(sums, along_z)
    out = jax.ShapeDtypeStruct((8, LANES), f32)
    square = local(plus_body, [place, square, lax.ppermute(square, *core)], out, "plus")
    squares = [square] + [lax.ppermute(square, *step) for step in along_x]
    out = jax.ShapeDtypeStruct((shards, slots * rows + 8, n), bf16)
    sent = local(dispatch_body, [table, *spread, *squares], out, "dispatch")
    pieces = lax.all_to_all(sent, "fsdp", split_axis=0, concat_axis=0, tiled=True)
    update, second_new = direction(
        owners, me, pieces, prepared, second_moment[0], bands, entries
    )
    back = lax.all_to_all(update, "fsdp", split_axis=0, concat_axis=0, tiled=True)
    back, pieces = lax.optimization_barrier((back, pieces))
    new = factors(
        owners, me, pieces, left_factor[0], right_factor[0], first_moment[0], bands, entries
    )
    left_new, right_new, first_new = new
    out = [jax.ShapeDtypeStruct((rows, width), bf16)] * bands
    mine = local(collect_body, [table, back.reshape(shards * slots, rows, n)], out, "collect")
    out = jax.ShapeDtypeStruct((bands, rows, width), bf16)
    result = local(put_body, [table, *exchange(mine, along_z)], out, "put").reshape(rows_dev, width)
    return (result, left_new[None], right_new[None], first_new[None], second_new[None])


def solution(mesh):
    state = P("dp", "fsdp", None, None)
    return jax.shard_map(
        per_device,
        mesh=mesh,
        in_specs=(P("dp", "fsdp", None), P("dp", None)) + (state,) * 6,
        out_specs=(P("fsdp", "dp"),) + (state,) * 4,
        check_vma=False,
    )
```

time: 110 us -> 106 us (0.964)
  blocking collectives: 0 us -> 40.1 us
  waiting for transfers between devices: 31.1 us -> 10.9 us
  starting transfers between devices: 41.2 us -> 24.6 us
  Pallas kernels: 35.9 us -> 28.9 us
    all_to_all x0 -> x2, blocking collectives: none -> 40.1 us  [the longest x1 22.4 us: per_device(): lax.all_to_all(sent, 'fsdp', split_axis=0, concat_axis=0, tiled=True)]
    all_to_all x2 -> x0, starting transfers between devices: 11.8 us -> none  [the longest x1 6.58 us: per_device(): lax.all_to_all(sent.reshape(shards, slots, rows, n), 'fsdp', split_axis=0...]
    all_to_all x2 -> x0, waiting for transfers between devices: 9.37 us -> none  [the longest x1 9.37 us: per_device(): lax.all_to_all(update, 'fsdp', split_axis=0, concat_axis=0, tiled=True)]
    ppermute x6, waiting for transfers between devices: 8.76 us -> 0.02 us  [exchange(): got[j] = lax.ppermute(arrays[j], *steps[j - 1])]
    pallas_call x6 -> x3, Pallas kernels: 21.8 us -> 15.7 us  [the longest x1 7.64 us: direction(): pl.pallas_call(body, in_specs=[scalar] * 2 + [whole] + [far] * 5, out_spe...]
    ppermute x9 -> x6, starting transfers between devices: 8.99 us -> 4.38 us  [the longest x3 4.16 us: per_device(): squares = [square] + [lax.ppermute(square, *step) for step in along_x]]
    ppermute x9 -> x6, waiting for transfers between devices: 11.3 us -> 7.97 us  [the longest x3 4.91 us: per_device(): squares = [square] + [lax.ppermute(square, *step) for step in along_x]]
    ppermute x1, waiting for transfers between devices: 1.65 us -> 2.92 us  [sum_over_replicas(): left_far = lax.ppermute(to_right, 'dp', up)]
  transfers between devices with their start and end apart: 23 -> 18, of which waited for: 13 -> 6; matrix products, arithmetic and copies ran while one was open for 0% -> 0% of each run, Pallas kernels for 19% -> 14%
where the time goes in v1:
time: 106 us
  blocking collectives  40.1 us (38%)
  Pallas kernels  28.9 us (27%)
  starting transfers between devices  24.6 us (23%)
  waiting for transfers between devices  10.9 us (10%)
    all_to_all x1, blocking collectives, per_device(): lax.all_to_all(sent, 'fsdp', split_axis=0, concat_axis=0, tiled=True)  22.4 us
    all_to_all x1, blocking collectives, per_device(): lax.all_to_all(update, 'fsdp', split_axis=0, concat_axis=0, tiled=True)  17.7 us
    ppermute x6, starting transfers between devices, exchange(): got[j] = lax.ppermute(arrays[j], *steps[j - 1])  10.3 us
    pallas_call x1, Pallas kernels, direction(): pl.pallas_call(body, in_specs=[scalar] * 2 + [whole] + [far] * 5, out_spe...  7.64 us
    pallas_call x9, Pallas kernels, local(): pl.pallas_call(body, in_specs=[pl.BlockSpec(memory_space=SMEM)] + [pl.Blo...  6.8 us
    pallas_call x1, Pallas kernels, prepare(): pl.pallas_call(prepare_body, grid=(slots,), in_specs=[block] * 3, out_spe...  6.35 us
    pallas_call x1, Pallas kernels, factors(): pl.pallas_call(body, grid=(slots,), in_specs=[scalar] * 2 + [whole] + [bl...  5.33 us
    ppermute x3, waiting for transfers between devices, per_device(): squares = [square] + [lax.ppermute(square, *step) for step in along_x]  4.91 us
  transfers between devices with their start and end apart: 18, of which 6 were waited for; matrix products, arithmetic and copies ran while one was open for 0% of the time, Pallas kernels for 14%

profile of v1, /device:TPU:0, one launch (start us, length us, event | category | flops | bytes accessed | tf_op | source)
XLA Modules:
  0.0 105.5 jit_solution(18056262611054068210)
XLA Ops:
  0.7 0.1 pad_add_fusion.1.place
  0.7 2.8 %load.1 = (bf16[1,128,2048]{2,1,0:T(8,128)(2,1)S(1)}, bf16[3,128,2048]{2,1,0:T(8,128)(2,1)S(1)}, bf16[1,128,2048]{2,1,0:T(8,128)(2,1)S(1)}, bf16[3,128,2048]{2,1,0:T(8,128)(2,1)S(1)}) custom-call(s32[3]{0:T(128)S(1)} %pad_add_fusion.1.place, bf16[128,16384]{1,0:T(8,128)(2,1)} %bitcast.19), custom_call_target="tpu_custom_call" | custom-call | tf_op jit(solution)/shard_map/load/pallas_call | solution.py:169
  3.5 0.1 collective-permute-start
  3.6 1.9 %collective-permute-done.far = bf16[1,128,2048]{2,1,0:T(8,128)(2,1)S(1)} collective-permute-done((bf16[1,128,2048]{2,1,0:T(8,128)(2,1)S(1)}, bf16[1,128,2048]{2,1,0:T(8,128)(2,1)S(1)}, u32[]{:S(2)}, u32[]{:S(2)}) %collective-permute-start) | collective-permute-done | bytes 524320 | tf_op jit(solution)/shard_map/ppermute | solution.py:258
  5.5 0.1 collective-permute-start.1
  5.7 0.7 pair_far.1
  6.3 1.7 %collective-permute-start.4 = (bf16[64,2048]{1,0:T(8,128)(2,1)S(1)}, bf16[64,2048]{1,0:T(8,128)(2,1)S(1)}, u32[]{:S(2)}, u32[]{:S(2)}) collective-permute-start(bf16[64,2048]{1,0:T(8,128)(2,1)S(1)} %get-tuple-element.57), channel_id=1, source_target_pairs={{0,32},{16,48},{32,64},{48,80},{64,96},{80,112},{96,0},{112,16},{1... | collective-permute-start | bytes 786440 | tf_op jit(solution)/shard_map/ppermute | solution.py:262
  8.0 1.7 %collective-permute-start.6 = (bf16[64,2048]{1,0:T(8,128)(2,1)S(1)}, bf16[64,2048]{1,0:T(8,128)(2,1)S(1)}, u32[]{:S(2)}, u32[]{:S(2)}) collective-permute-start(bf16[64,2048]{1,0:T(8,128)(2,1)S(1)} %get-tuple-element.59), channel_id=1, source_target_pairs={{0,96},{16,112},{32,0},{48,16},{64,32},{80,48},{96,64},{112,80},{1... | collective-permute-start | bytes 786440 | tf_op jit(solution)/shard_map/ppermute | solution.py:263
  9.6 0.0 collective-permute-done.1.far
  9.6 0.9 pair_near.1
  10.5 0.9 collective-permute-start.2
  11.4 2.4 %collective-permute-start.3 = (bf16[64,2048]{1,0:T(8,128)(2,1)S(1)}, bf16[64,2048]{1,0:T(8,128)(2,1)S(1)}, u32[]{:S(2)}, u32[]{:S(2)}) collective-permute-start(bf16[64,2048]{1,0:T(8,128)(2,1)S(1)} %get-tuple-element.53), channel_id=1, source_target_pairs={{0,96},{16,112},{32,0},{48,16},{64,32},{80,48},{96,64},{112,80},{1... | collective-permute-start | bytes 786440 | tf_op jit(solution)/shard_map/ppermute | solution.py:269
  13.8 2.9 %collective-permute-done.4.arrived = bf16[64,2048]{1,0:T(8,128)(2,1)S(1)} collective-permute-done((bf16[64,2048]{1,0:T(8,128)(2,1)S(1)}, bf16[64,2048]{1,0:T(8,128)(2,1)S(1)}, u32[]{:S(2)}, u32[]{:S(2)}) %collective-permute-start.4) | collective-permute-done | bytes 262176 | tf_op jit(solution)/shard_map/ppermute | solution.py:262
  16.7 0.6 relay.2
  17.3 0.4 collective-permute-start.5
  17.8 0.0 collective-permute-done.6.arrived
  17.8 0.6 relay.3
  18.4 2.9 %collective-permute-start.7 = (bf16[64,2048]{1,0:T(8,128)(2,1)S(1)}, bf16[64,2048]{1,0:T(8,128)(2,1)S(1)}, u32[]{:S(2)}, u32[]{:S(2)}) collective-permute-start(bf16[64,2048]{1,0:T(8,128)(2,1)S(1)} %relay.3), channel_id=1, source_target_pairs={{0,96},{16,112},{32,0},{48,16},{64,32},{80,48},{96,64},{112,80},{1... | collective-permute-start | bytes 786440 | tf_op jit(solution)/shard_map/ppermute | solution.py:271
  21.3 6.4 %prepare.1 = (bf16[2,1024,512]{2,1,0:T(8,128)(2,1)}, bf16[2,512,512]{2,1,0:T(8,128)(2,1)}, bf16[2,512,1024]{2,1,0:T(8,128)(2,1)}, f32[2,512,512]{2,1,0:T(8,128)}) custom-call(f32[2,512,512]{2,1,0:T(8,128)} %bitcast.26, f32[2,512,512]{2,1,0:T(8,128)} %bitcast.27, f32[2,512,512]{2,1,0:T(8,128)} %bitcast.21), custom_call_target="tpu_custom_call" | custom-call | flops 2147483648 | bytes 13631488 | tf_op jit(solution)/shard_map/prepare/pallas_call | solution.py:61
  27.7 0.0 collective-permute-done.2.left_direct
  27.7 0.0 collective-permute-done.3.right_direct
  27.7 0.0 collective-permute-done.5.left_sum
  27.7 0.0 collective-permute-done.7.right_sum
  27.7 0.9 finish.1
  28.6 2.1 %collective-permute-start.8 = (bf16[32,2048]{1,0:T(8,128)(2,1)S(1)}, bf16[32,2048]{1,0:T(8,128)(2,1)S(1)}, u32[]{:S(2)}, u32[]{:S(2)}) collective-permute-start(bf16[32,2048]{1,0:T(8,128)(2,1)S(1)} %get-tuple-element.70), channel_id=1, source_target_pairs={{0,4},{1,5},{2,6},{3,7},{4,8},{5,9},{6,10},{7,11},{8,12},{9,13},{1... | collective-permute-start | bytes 393224 | tf_op jit(solution)/shard_map/ppermute | solution.py:279
  30.7 3.6 %collective-permute-start.9 = (bf16[32,2048]{1,0:T(8,128)(2,1)S(1)}, bf16[32,2048]{1,0:T(8,128)(2,1)S(1)}, u32[]{:S(2)}, u32[]{:S(2)}) collective-permute-start(bf16[32,2048]{1,0:T(8,128)(2,1)S(1)} %get-tuple-element.71), channel_id=1, source_target_pairs={{0,8},{1,9},{2,10},{3,11},{4,12},{5,13},{6,14},{7,15},{8,0},{9,1},... | collective-permute-start | bytes 393224 | tf_op jit(solution)/shard_map/ppermute | solution.py:279
  34.3 1.0 collective-permute-start.10
  35.3 0.0 collective-permute-start.11
  35.3 1.2 %collective-permute-done.11.b = f32[8,128]{1,0:T(8,128)S(1)} collective-permute-done((f32[8,128]{1,0:T(8,128)S(1)}, f32[8,128]{1,0:T(8,128)S(1)}, u32[]{:S(2)}, u32[]{:S(2)}) %collective-permute-start.11) | collective-permute-done | bytes 4128 | tf_op jit(solution)/shard_map/ppermute | solution.py:462
  36.4 0.5 plus.1.refs_4_
  37.0 2.7 %collective-permute-start.14 = (f32[8,128]{1,0:T(8,128)S(1)}, f32[8,128]{1,0:T(8,128)S(1)}, u32[]{:S(2)}, u32[]{:S(2)}) collective-permute-start(f32[8,128]{1,0:T(8,128)S(1)} %plus.1.refs_4_), channel_id=1, source_target_pairs={{0,96},{16,112},{32,0},{48,16},{64,32},{80,48},{96,64},{112,80},{1... | collective-permute-start | bytes 12296 | tf_op jit(solution)/shard_map/ppermute | solution.py:463
  39.7 0.6 collective-permute-start.13
  40.3 0.7 collective-permute-done.14.refs_7_
  41.1 0.8 collective-permute-start.12
  41.9 0.1 pad_add_fusion.table
  41.9 2.9 %collective-permute-done.13.refs_6_ = f32[8,128]{1,0:T(8,128)S(1)} collective-permute-done((f32[8,128]{1,0:T(8,128)S(1)}, f32[8,128]{1,0:T(8,128)S(1)}, u32[]{:S(2)}, u32[]{:S(2)}) %collective-permute-start.13) | collective-permute-done | bytes 4128 | tf_op jit(solution)/shard_map/ppermute | solution.py:463
  44.8 1.3 %collective-permute-done.12.refs_5_ = f32[8,128]{1,0:T(8,128)S(1)} collective-permute-done((f32[8,128]{1,0:T(8,128)S(1)}, f32[8,128]{1,0:T(8,128)S(1)}, u32[]{:S(2)}, u32[]{:S(2)}) %collective-permute-start.12) | collective-permute-done | bytes 4128 | tf_op jit(solution)/shard_map/ppermute | solution.py:463
  46.1 0.7 dispatch.1
  46.9 22.4 %all_to_all.10.refs_2_ = bf16[16,72,512]{2,1,0:T(8,128)(2,1)S(1)} all-to-all(bf16[16,72,512]{2,1,0:T(8,128)(2,1)S(1)} %dispatch.1), channel_id=1, replica_groups=mesh['dp'=8,'fsdp'=16] {'fsdp'}, dimensions={0} | all-to-all | bytes 2359296 | tf_op jit(solution)/shard_map/all_to_all | solution.py:466
  69.3 7.6 %direction.1 = (bf16[16,2,32,512]{3,2,1,0:T(8,128)(2,1)S(1)}, f32[2,512,512]{2,1,0:T(8,128)}) custom-call(s32[1,16]{1,0:T(1,128)S(1)} %copy-done, s32[1]{0:T(128)} %bitcast.1.refs_1_, bf16[16,72,512]{2,1,0:T(8,128)(2,1)S(1)} %all_to_all.10.refs_2_, f32[2,512,512]{2,1,0:T(8,128)} %bitcast.20, bf16[2,1024,512]{2,1,0:T(8,128)(2,1)} %get-tuple-element.74.refs_4_, ...), custom_call_target="tpu_custom_call" | custom-call | tf_op jit(solution)/shard_map/direction/pallas_call | solution.py:366
  76.9 17.7 %all_to_all.11 = bf16[16,2,32,512]{3,2,1,0:T(8,128)(2,1)S(1)} all-to-all(bf16[16,2,32,512]{3,2,1,0:T(8,128)(2,1)S(1)} %get-tuple-element.78), channel_id=1, replica_groups=mesh['dp'=8,'fsdp'=16] {'fsdp'}, dimensions={0} | all-to-all | bytes 2097152 | tf_op jit(solution)/shard_map/all_to_all | solution.py:470
  94.6 0.6 collect.1
  95.2 0.1 collective-permute-start.15
  95.3 2.4 %collective-permute-start.16 = (bf16[32,2048]{1,0:T(8,128)(2,1)S(1)}, bf16[32,2048]{1,0:T(8,128)(2,1)S(1)}, u32[]{:S(2)}, u32[]{:S(2)}) collective-permute-start(bf16[32,2048]{1,0:T(8,128)(2,1)S(1)} %get-tuple-element.82), channel_id=1, source_target_pairs={{0,8},{1,9},{2,10},{3,11},{4,12},{5,13},{6,14},{7,15},{8,0},{9,1},... | collective-permute-start | bytes 393224 | tf_op jit(solution)/shard_map/ppermute | solution.py:279
  97.7 1.1 %collective-permute-start.17 = (bf16[32,2048]{1,0:T(8,128)(2,1)S(1)}, bf16[32,2048]{1,0:T(8,128)(2,1)S(1)}, u32[]{:S(2)}, u32[]{:S(2)}) collective-permute-start(bf16[32,2048]{1,0:T(8,128)(2,1)S(1)} %get-tuple-element.83), channel_id=1, source_target_pairs={{0,12},{1,13},{2,14},{3,15},{4,0},{5,1},{6,2},{7,3},{8,4},{9,5},{1... | collective-permute-start | bytes 393224 | tf_op jit(solution)/shard_map/ppermute | solution.py:279
  98.8 5.3 %factors.1 = (f32[2,512,512]{2,1,0:T(8,128)}, f32[2,512,512]{2,1,0:T(8,128)}, f32[2,512,512]{2,1,0:T(8,128)}) custom-call(s32[1,16]{1,0:T(1,128)S(1)} %copy-done, s32[1]{0:T(128)} %bitcast.1.refs_1_, bf16[16,72,512]{2,1,0:T(8,128)(2,1)S(1)} %all_to_all.10.refs_2_, f32[2,512,512]{2,1,0:T(8,128)} %bitcast.23, f32[2,512,512]{2,1,0:T(8,128)} %bitcast.24, ...), custom_call_target="tpu_custom_call" | custom-call | flops 1073741824 | bytes 13631488 | tf_op jit(solution)/shard_map/factors/pallas_call | solution.py:412
  104.1 0.0 collective-permute-done.16.refs_2_
  104.2 1.4 %put.1 = bf16[4,32,2048]{2,1,0:T(8,128)(2,1)} custom-call(s32[1,17]{1,0:T(1,128)S(1)} %pad_add_fusion.table, bf16[32,2048]{1,0:T(8,128)(2,1)S(1)} %get-tuple-element.80.refs_0_, bf16[32,2048]{1,0:T(8,128)(2,1)S(1)} %collective-permute-done.15.refs_1_, bf16[32,2048]{1,0:T(8,128)(2,1)S(1)} %collective-permute-done.16.refs_2_, ...), custom_call_target="tpu_custom_call" | custom-call | tf_op jit(solution)/shard_map/put/pallas_call | solution.py:87
  (7 shorter events, 0.0 us)
Async XLA Ops:
  3.5 2.0 %collective-permute-start = (bf16[1,128,2048]{2,1,0:T(8,128)(2,1)S(1)}, bf16[1,128,2048]{2,1,0:T(8,128)(2,1)S(1)}, u32[]{:S(2)}, u32[]{:S(2)}) collective-permute-start(bf16[1,128,2048]{2,1,0:T(8,128)(2,1)S(1)} %get-tuple-element.48), channel_id=1, source_target_pairs={{0,16},{16,0},{32,48},{48,32},{64,80},{80,64},{96,112},{112,96},{1... | collective-permute-start | bytes 1572872 | tf_op jit(solution)/shard_map/ppermute | solution.py:258
  5.5 4.1 %collective-permute-start.1 = (bf16[3,128,2048]{2,1,0:T(8,128)(2,1)S(1)}, bf16[3,128,2048]{2,1,0:T(8,128)(2,1)S(1)}, u32[]{:S(2)}, u32[]{:S(2)}) collective-permute-start(bf16[3,128,2048]{2,1,0:T(8,128)(2,1)S(1)} %get-tuple-element.50), channel_id=1, source_target_pairs={{0,16},{16,0},{32,48},{48,32},{64,80},{80,64},{96,112},{112,96},{1... | collective-permute-start | bytes 4718600 | tf_op jit(solution)/shard_map/ppermute | solution.py:260
  6.3 10.4 %collective-permute-start.4 = (bf16[64,2048]{1,0:T(8,128)(2,1)S(1)}, bf16[64,2048]{1,0:T(8,128)(2,1)S(1)}, u32[]{:S(2)}, u32[]{:S(2)}) collective-permute-start(bf16[64,2048]{1,0:T(8,128)(2,1)S(1)} %get-tuple-element.57), channel_id=1, source_target_pairs={{0,32},{16,48},{32,64},{48,80},{64,96},{80,112},{96,0},{112,16},{1... | collective-permute-start | bytes 786440 | tf_op jit(solution)/shard_map/ppermute | solution.py:262
  8.0 9.8 %collective-permute-start.6 = (bf16[64,2048]{1,0:T(8,128)(2,1)S(1)}, bf16[64,2048]{1,0:T(8,128)(2,1)S(1)}, u32[]{:S(2)}, u32[]{:S(2)}) collective-permute-start(bf16[64,2048]{1,0:T(8,128)(2,1)S(1)} %get-tuple-element.59), channel_id=1, source_target_pairs={{0,96},{16,112},{32,0},{48,16},{64,32},{80,48},{96,64},{112,80},{1... | collective-permute-start | bytes 786440 | tf_op jit(solution)/shard_map/ppermute | solution.py:263
  10.5 17.1 %collective-permute-start.2 = (bf16[64,2048]{1,0:T(8,128)(2,1)S(1)}, bf16[64,2048]{1,0:T(8,128)(2,1)S(1)}, u32[]{:S(2)}, u32[]{:S(2)}) collective-permute-start(bf16[64,2048]{1,0:T(8,128)(2,1)S(1)} %get-tuple-element.52), channel_id=1, source_target_pairs={{0,32},{16,48},{32,64},{48,80},{64,96},{80,112},{96,0},{112,16},{1... | collective-permute-start | bytes 786440 | tf_op jit(solution)/shard_map/ppermute | solution.py:268
  11.4 16.2 %collective-permute-start.3 = (bf16[64,2048]{1,0:T(8,128)(2,1)S(1)}, bf16[64,2048]{1,0:T(8,128)(2,1)S(1)}, u32[]{:S(2)}, u32[]{:S(2)}) collective-permute-start(bf16[64,2048]{1,0:T(8,128)(2,1)S(1)} %get-tuple-element.53), channel_id=1, source_target_pairs={{0,96},{16,112},{32,0},{48,16},{64,32},{80,48},{96,64},{112,80},{1... | collective-permute-start | bytes 786440 | tf_op jit(solution)/shard_map/ppermute | solution.py:269
  17.3 10.3 %collective-permute-start.5 = (bf16[64,2048]{1,0:T(8,128)(2,1)S(1)}, bf16[64,2048]{1,0:T(8,128)(2,1)S(1)}, u32[]{:S(2)}, u32[]{:S(2)}) collective-permute-start(bf16[64,2048]{1,0:T(8,128)(2,1)S(1)} %relay.2), channel_id=1, source_target_pairs={{0,32},{16,48},{32,64},{48,80},{64,96},{80,112},{96,0},{112,16},{1... | collective-permute-start | bytes 786440 | tf_op jit(solution)/shard_map/ppermute | solution.py:270
  18.4 9.3 %collective-permute-start.7 = (bf16[64,2048]{1,0:T(8,128)(2,1)S(1)}, bf16[64,2048]{1,0:T(8,128)(2,1)S(1)}, u32[]{:S(2)}, u32[]{:S(2)}) collective-permute-start(bf16[64,2048]{1,0:T(8,128)(2,1)S(1)} %relay.3), channel_id=1, source_target_pairs={{0,96},{16,112},{32,0},{48,16},{64,32},{80,48},{96,64},{112,80},{1... | collective-permute-start | bytes 786440 | tf_op jit(solution)/shard_map/ppermute | solution.py:271
  27.7 14.2 %copy-start = (s32[1,16]{1,0:T(1,128)S(1)}, s32[1,16]{1,0:T(1,128)}, u32[]{:S(2)}) copy-start(s32[1,16]{1,0:T(1,128)} %refs_0_.3) | copy-start | bytes 196
  28.6 17.5 %collective-permute-start.8 = (bf16[32,2048]{1,0:T(8,128)(2,1)S(1)}, bf16[32,2048]{1,0:T(8,128)(2,1)S(1)}, u32[]{:S(2)}, u32[]{:S(2)}) collective-permute-start(bf16[32,2048]{1,0:T(8,128)(2,1)S(1)} %get-tuple-element.70), channel_id=1, source_target_pairs={{0,4},{1,5},{2,6},{3,7},{4,8},{5,9},{6,10},{7,11},{8,12},{9,13},{1... | collective-permute-start | bytes 393224 | tf_op jit(solution)/shard_map/ppermute | solution.py:279
  30.7 15.5 %collective-permute-start.9 = (bf16[32,2048]{1,0:T(8,128)(2,1)S(1)}, bf16[32,2048]{1,0:T(8,128)(2,1)S(1)}, u32[]{:S(2)}, u32[]{:S(2)}) collective-permute-start(bf16[32,2048]{1,0:T(8,128)(2,1)S(1)} %get-tuple-element.71), channel_id=1, source_target_pairs={{0,8},{1,9},{2,10},{3,11},{4,12},{5,13},{6,14},{7,15},{8,0},{9,1},... | collective-permute-start | bytes 393224 | tf_op jit(solution)/shard_map/ppermute | solution.py:279
  34.3 11.9 %collective-permute-start.10 = (bf16[32,2048]{1,0:T(8,128)(2,1)S(1)}, bf16[32,2048]{1,0:T(8,128)(2,1)S(1)}, u32[]{:S(2)}, u32[]{:S(2)}) collective-permute-start(bf16[32,2048]{1,0:T(8,128)(2,1)S(1)} %get-tuple-element.72), channel_id=1, source_target_pairs={{0,12},{1,13},{2,14},{3,15},{4,0},{5,1},{6,2},{7,3},{8,4},{9,5},{1... | collective-permute-start | bytes 393224 | tf_op jit(solution)/shard_map/ppermute | solution.py:279
  35.3 1.2 %collective-permute-start.11 = (f32[8,128]{1,0:T(8,128)S(1)}, f32[8,128]{1,0:T(8,128)S(1)}, u32[]{:S(2)}, u32[]{:S(2)}) collective-permute-start(f32[8,128]{1,0:T(8,128)S(1)} %get-tuple-element.73.a), channel_id=1, source_target_pairs={{0,16},{16,0},{32,48},{48,32},{64,80},{80,64},{96,112},{112,96},{1... | collective-permute-start | bytes 12296 | tf_op jit(solution)/shard_map/ppermute | solution.py:462
  37.0 4.1 %collective-permute-start.14 = (f32[8,128]{1,0:T(8,128)S(1)}, f32[8,128]{1,0:T(8,128)S(1)}, u32[]{:S(2)}, u32[]{:S(2)}) collective-permute-start(f32[8,128]{1,0:T(8,128)S(1)} %plus.1.refs_4_), channel_id=1, source_target_pairs={{0,96},{16,112},{32,0},{48,16},{64,32},{80,48},{96,64},{112,80},{1... | collective-permute-start | bytes 12296 | tf_op jit(solution)/shard_map/ppermute | solution.py:463
  39.7 5.1 %collective-permute-start.13 = (f32[8,128]{1,0:T(8,128)S(1)}, f32[8,128]{1,0:T(8,128)S(1)}, u32[]{:S(2)}, u32[]{:S(2)}) collective-permute-start(f32[8,128]{1,0:T(8,128)S(1)} %plus.1.refs_4_), channel_id=1, source_target_pairs={{0,64},{16,80},{32,96},{48,112},{64,0},{80,16},{96,32},{112,48},{1... | collective-permute-start | bytes 12296 | tf_op jit(solution)/shard_map/ppermute | solution.py:463
  41.1 5.1 %collective-permute-start.12 = (f32[8,128]{1,0:T(8,128)S(1)}, f32[8,128]{1,0:T(8,128)S(1)}, u32[]{:S(2)}, u32[]{:S(2)}) collective-permute-start(f32[8,128]{1,0:T(8,128)S(1)} %plus.1.refs_4_), channel_id=1, source_target_pairs={{0,32},{16,48},{32,64},{48,80},{64,96},{80,112},{96,0},{112,16},{1... | collective-permute-start | bytes 12296 | tf_op jit(solution)/shard_map/ppermute | solution.py:463
  95.2 8.9 %collective-permute-start.15 = (bf16[32,2048]{1,0:T(8,128)(2,1)S(1)}, bf16[32,2048]{1,0:T(8,128)(2,1)S(1)}, u32[]{:S(2)}, u32[]{:S(2)}) collective-permute-start(bf16[32,2048]{1,0:T(8,128)(2,1)S(1)} %get-tuple-element.81), channel_id=1, source_target_pairs={{0,4},{1,5},{2,6},{3,7},{4,8},{5,9},{6,10},{7,11},{8,12},{9,13},{1... | collective-permute-start | bytes 393224 | tf_op jit(solution)/shard_map/ppermute | solution.py:279
  95.3 8.9 %collective-permute-start.16 = (bf16[32,2048]{1,0:T(8,128)(2,1)S(1)}, bf16[32,2048]{1,0:T(8,128)(2,1)S(1)}, u32[]{:S(2)}, u32[]{:S(2)}) collective-permute-start(bf16[32,2048]{1,0:T(8,128)(2,1)S(1)} %get-tuple-element.82), channel_id=1, source_target_pairs={{0,8},{1,9},{2,10},{3,11},{4,12},{5,13},{6,14},{7,15},{8,0},{9,1},... | collective-permute-start | bytes 393224 | tf_op jit(solution)/shard_map/ppermute | solution.py:279
  97.7 6.5 %collective-permute-start.17 = (bf16[32,2048]{1,0:T(8,128)(2,1)S(1)}, bf16[32,2048]{1,0:T(8,128)(2,1)S(1)}, u32[]{:S(2)}, u32[]{:S(2)}) collective-permute-start(bf16[32,2048]{1,0:T(8,128)(2,1)S(1)} %get-tuple-element.83), channel_id=1, source_target_pairs={{0,12},{1,13},{2,14},{3,15},{4,0},{5,1},{6,2},{7,3},{8,4},{9,5},{1... | collective-permute-start | bytes 393224 | tf_op jit(solution)/shard_map/ppermute | solution.py:279

commit v2 on v1

--- a/solution.py
+++ b/solution.py
@@ -98,8 +98,7 @@
 
 
 def dispatch_body(table, *refs):
-    *squares, dst = refs[4:]
-    srcs = refs[:4]
+    *srcs, squares, dst = refs
     n = dst.shape[2]
     rows, width = srcs[0].shape
     bands = len(srcs)
@@ -112,9 +111,9 @@
             slot = table[0, band * cols + c]
             row = pl.multiple_of(lax.rem(slot, slots) * rows, rows)
             dst[slot // slots, pl.ds(row, rows)] = src[:, c * n : (c + 1) * n]
-    total = squares[0][...]
-    for square in squares[1:]:
-        total = total + square[...]
+    total = squares[0]
+    for i in range(1, squares.shape[0]):
+        total = total + squares[i]
     terms = [t.astype(f32) for t in split3(total)]
     terms.append(jnp.zeros((8, n - 3 * LANES), f32))
     terms = jnp.concatenate(terms, axis=1).astype(bf16)
@@ -133,16 +132,31 @@
             dst[:, c * n : (c + 1) * n] = src[table[0, band * cols + c]]
 
 
-def put_body(table, *refs):
-    *srcs, dst = refs
-    bands = len(srcs)
-    z = table[0, table.shape[1] - 1]
-    for j, src in enumerate(srcs):
-        dst[lax.rem(z + bands - j, bands)] = src[...]
-
-
-def plus_body(place, a, b, out):
-    out[...] = a[...] + b[...]
+def put(table, arrays):
+    bands = len(arrays)
+    rows, width = arrays[0].shape
+
+    def body(table, *refs):
+        *srcs, dst, sems = refs
+        z = table[0, table.shape[1] - 1]
+        copies = [
+            pltpu.make_async_copy(src, dst.at[lax.rem(z + bands - j, bands)], sems.at[j])
+            for j, src in enumerate(srcs)
+        ]
+        for c in copies:
+            c.start()
+        for c in copies:
+            c.wait()
+
+    return pl.pallas_call(
+        body,
+        in_specs=[pl.BlockSpec(memory_space=SMEM)] + [pl.BlockSpec(memory_space=VMEM)] * bands,
+        out_specs=pl.BlockSpec(memory_space=HBM),
+        out_shape=HBM((bands, rows, width), bf16),
+        scratch_shapes=[pltpu.SemaphoreType.DMA((bands,))],
+        compiler_params=pltpu.CompilerParams(vmem_limit_bytes=2 << 20),
+        name="put",
+    )(table, *arrays)
 
 
 def load(place, grads, width):
@@ -213,13 +227,13 @@
     return local(body, (place, kept, arrived), out, "relay")
 
 
-def finish(place, own, left_direct, right_direct, left_sum, right_sum, bands):
+def finish(place, own, left_direct, right_direct, left_sum, right_sum, bands, copies):
     rows, width = own.shape
     low = rows // 2
     piece = rows // bands
 
     def body(place, own, left_direct, right_direct, left_sum, right_sum, *refs):
-        *outs, square = refs
+        *outs, squares = refs
         total = jnp.zeros((8, LANES), f32)
         for q in range(bands):
             near, far = (left_sum, right_direct) if q * piece < low else (left_direct, right_sum)
@@ -238,11 +252,12 @@
             by_row = jnp.sum((value * value).reshape(piece // 8, 8, width), axis=0)
             for c in range(width // LANES):
                 total = total + by_row[:, c * LANES : (c + 1) * LANES]
-        square[...] = total
+        for i in range(squares.shape[0]):
+            squares[i] = total
 
     arrays = [place, own, left_direct, right_direct, left_sum, right_sum]
     out = [jax.ShapeDtypeStruct((piece, width), bf16)] * bands
-    out.append(jax.ShapeDtypeStruct((8, LANES), f32))
+    out.append(jax.ShapeDtypeStruct((copies, 8, LANES), f32))
     return local(body, arrays, out, "finish", 12 << 20)
 
 
@@ -444,8 +459,6 @@
     place = jnp.stack([dp_me // 2, dp_me % 2, me // per_band])
     table = jnp.concatenate([owners, (me // per_band).reshape(1, 1)], axis=1)
     me = me.reshape(1)
-    core = ("dp", [(d, d ^ 1) for d in range(dp)])
-    along_x = [("dp", [(d, (d + 2 * h) % dp) for d in range(dp)]) for h in range(1, dp // 2)]
     along_z = [
         ("fsdp", [(i, (i + h * per_band) % shards) for i in range(shards)])
         for h in range(1, bands)
@@ -453,16 +466,14 @@
     parts = sum_over_replicas(place, replica_grads[0], bands)
     prepared = prepare(left_basis[0], right_basis[0], first_moment[0])
     parts, prepared = lax.optimization_barrier((parts, prepared))
-    *sums, square = finish(place, *parts, bands)
+    *sums, squares = finish(place, *parts, bands, dp)
     rows, width = sums[0].shape
     cols = width // n
     entries = rows_dev * shards * replica_grads.shape[2]
     spread = exchange(sums, along_z)
-    out = jax.ShapeDtypeStruct((8, LANES), f32)
-    square = local(plus_body, [place, square, lax.ppermute(square, *core)], out, "plus")
-    squares = [square] + [lax.ppermute(square, *step) for step in along_x]
+    squares = lax.all_to_all(squares, "dp", split_axis=0, concat_axis=0, tiled=True)
     out = jax.ShapeDtypeStruct((shards, slots * rows + 8, n), bf16)
-    sent = local(dispatch_body, [table, *spread, *squares], out, "dispatch")
+    sent = local(dispatch_body, [table, *spread, squares], out, "dispatch")
     pieces = lax.all_to_all(sent, "fsdp", split_axis=0, concat_axis=0, tiled=True)
     update, second_new = direction(
         owners, me, pieces, prepared, second_moment[0], bands, entries
@@ -475,8 +486,7 @@
     left_new, right_new, first_new = new
     out = [jax.ShapeDtypeStruct((rows, width), bf16)] * bands
     mine = local(collect_body, [table, back.reshape(shards * slots, rows, n)], out, "collect")
-    out = jax.ShapeDtypeStruct((bands, rows, width), bf16)
-    result = local(put_body, [table, *exchange(mine, along_z)], out, "put").reshape(rows_dev, width)
+    result = put(table, exchange(mine, along_z)).reshape(rows_dev, width)
     return (result, left_new[None], right_new[None], first_new[None], second_new[None])
 
 

time: 106 us -> 107 us (level)
  blocking collectives: 40.1 us -> 42.7 us
    ppermute x4 -> x0, waiting for transfers between devices: 6.07 us -> none  [the longest x3 4.91 us: per_device(): squares = [square] + [lax.ppermute(square, *step) for step in along_x]]
    all_to_all x0 -> x1, waiting for transfers between devices: none -> 5.37 us  [per_device(): lax.all_to_all(squares, 'dp', split_axis=0, concat_axis=0, tiled=True)]
    ppermute x4 -> x0, starting transfers between devices: 4.16 us -> none  [the longest x3 4.16 us: per_device(): squares = [square] + [lax.ppermute(square, *step) for step in along_x]]
    all_to_all x0 -> x1, starting transfers between devices: none -> 3.95 us  [per_device(): lax.all_to_all(squares, 'dp', split_axis=0, concat_axis=0, tiled=True)]
    all_to_all x1, blocking collectives: 17.7 us -> 19.3 us  [per_device(): lax.all_to_all(update, 'fsdp', split_axis=0, concat_axis=0, tiled=True)]
    pallas_call x0 -> x1, Pallas kernels: none -> 1.37 us  [put(): pl.pallas_call(body, in_specs=[pl.BlockSpec(memory_space=SMEM)] + [pl.Blo...]
    pallas_call x9 -> x7, Pallas kernels: 6.8 us -> 5.49 us  [local(): pl.pallas_call(body, in_specs=[pl.BlockSpec(memory_space=SMEM)] + [pl.Blo...]
  transfers between devices with their start and end apart: 18 -> 15, of which waited for: 6 -> 3; matrix products, arithmetic and copies ran while one was open for 0% -> 0% of each run, Pallas kernels for 14% -> 13%
where the time goes in v2:
time: 107 us
  blocking collectives  42.7 us (40%)
  Pallas kernels  29 us (27%)
  starting transfers between devices  24.3 us (23%)
  waiting for transfers between devices  10.2 us (10%)
    all_to_all x1, blocking collectives, per_device(): lax.all_to_all(sent, 'fsdp', split_axis=0, concat_axis=0, tiled=True)  23.3 us
    all_to_all x1, blocking collectives, per_device(): lax.all_to_all(update, 'fsdp', split_axis=0, concat_axis=0, tiled=True)  19.3 us
    ppermute x6, starting transfers between devices, exchange(): got[j] = lax.ppermute(arrays[j], *steps[j - 1])  10.1 us
    pallas_call x1, Pallas kernels, direction(): pl.pallas_call(body, in_specs=[scalar] * 2 + [whole] + [far] * 5, out_spe...  7.64 us
    pallas_call x1, Pallas kernels, prepare(): pl.pallas_call(prepare_body, grid=(slots,), in_specs=[block] * 3, out_spe...  6.35 us
    pallas_call x7, Pallas kernels, local(): pl.pallas_call(body, in_specs=[pl.BlockSpec(memory_space=SMEM)] + [pl.Blo...  5.49 us
    all_to_all x1, waiting for transfers between devices, per_device(): lax.all_to_all(squares, 'dp', split_axis=0, concat_axis=0, tiled=True)  5.37 us
    pallas_call x1, Pallas kernels, factors(): pl.pallas_call(body, grid=(slots,), in_specs=[scalar] * 2 + [whole] + [bl...  5.35 us
  transfers between devices with their start and end apart: 15, of which 3 were waited for; matrix products, arithmetic and copies ran while one was open for 0% of the time, Pallas kernels for 13%

profile of v2, /device:TPU:0, one launch (start us, length us, event | category | flops | bytes accessed | tf_op | source)
XLA Modules:
  0.0 107.1 jit_solution(2667855968363987945)
XLA Ops:
  0.7 0.1 pad_add_fusion.1.place
  0.7 2.8 %load.1 = (bf16[1,128,2048]{2,1,0:T(8,128)(2,1)S(1)}, bf16[3,128,2048]{2,1,0:T(8,128)(2,1)S(1)}, bf16[1,128,2048]{2,1,0:T(8,128)(2,1)S(1)}, bf16[3,128,2048]{2,1,0:T(8,128)(2,1)S(1)}) custom-call(s32[3]{0:T(128)S(1)} %pad_add_fusion.1.place, bf16[128,16384]{1,0:T(8,128)(2,1)} %bitcast.19), custom_call_target="tpu_custom_call" | custom-call | tf_op jit(solution)/shard_map/load/pallas_call | solution.py:183
  3.5 0.1 collective-permute-start
  3.6 1.9 %collective-permute-done.far = bf16[1,128,2048]{2,1,0:T(8,128)(2,1)S(1)} collective-permute-done((bf16[1,128,2048]{2,1,0:T(8,128)(2,1)S(1)}, bf16[1,128,2048]{2,1,0:T(8,128)(2,1)S(1)}, u32[]{:S(2)}, u32[]{:S(2)}) %collective-permute-start) | collective-permute-done | bytes 524320 | tf_op jit(solution)/shard_map/ppermute | solution.py:273
  5.5 0.1 collective-permute-start.1
  5.7 0.7 pair_far.1
  6.3 1.7 %collective-permute-start.4 = (bf16[64,2048]{1,0:T(8,128)(2,1)S(1)}, bf16[64,2048]{1,0:T(8,128)(2,1)S(1)}, u32[]{:S(2)}, u32[]{:S(2)}) collective-permute-start(bf16[64,2048]{1,0:T(8,128)(2,1)S(1)} %get-tuple-element.57), channel_id=1, source_target_pairs={{0,32},{16,48},{32,64},{48,80},{64,96},{80,112},{96,0},{112,16},{1... | collective-permute-start | bytes 786440 | tf_op jit(solution)/shard_map/ppermute | solution.py:277
  8.0 1.7 %collective-permute-start.6 = (bf16[64,2048]{1,0:T(8,128)(2,1)S(1)}, bf16[64,2048]{1,0:T(8,128)(2,1)S(1)}, u32[]{:S(2)}, u32[]{:S(2)}) collective-permute-start(bf16[64,2048]{1,0:T(8,128)(2,1)S(1)} %get-tuple-element.59), channel_id=1, source_target_pairs={{0,96},{16,112},{32,0},{48,16},{64,32},{80,48},{96,64},{112,80},{1... | collective-permute-start | bytes 786440 | tf_op jit(solution)/shard_map/ppermute | solution.py:278
  9.6 0.0 collective-permute-done.1.far
  9.6 0.9 pair_near.1
  10.5 0.9 collective-permute-start.2
  11.4 2.4 %collective-permute-start.3 = (bf16[64,2048]{1,0:T(8,128)(2,1)S(1)}, bf16[64,2048]{1,0:T(8,128)(2,1)S(1)}, u32[]{:S(2)}, u32[]{:S(2)}) collective-permute-start(bf16[64,2048]{1,0:T(8,128)(2,1)S(1)} %get-tuple-element.53), channel_id=1, source_target_pairs={{0,96},{16,112},{32,0},{48,16},{64,32},{80,48},{96,64},{112,80},{1... | collective-permute-start | bytes 786440 | tf_op jit(solution)/shard_map/ppermute | solution.py:284
  13.8 2.9 %collective-permute-done.4.arrived = bf16[64,2048]{1,0:T(8,128)(2,1)S(1)} collective-permute-done((bf16[64,2048]{1,0:T(8,128)(2,1)S(1)}, bf16[64,2048]{1,0:T(8,128)(2,1)S(1)}, u32[]{:S(2)}, u32[]{:S(2)}) %collective-permute-start.4) | collective-permute-done | bytes 262176 | tf_op jit(solution)/shard_map/ppermute | solution.py:277
  16.7 0.6 relay.2
  17.3 0.4 collective-permute-start.5
  17.8 0.0 collective-permute-done.6.arrived
  17.8 0.6 relay.3
  18.4 2.9 %collective-permute-start.7 = (bf16[64,2048]{1,0:T(8,128)(2,1)S(1)}, bf16[64,2048]{1,0:T(8,128)(2,1)S(1)}, u32[]{:S(2)}, u32[]{:S(2)}) collective-permute-start(bf16[64,2048]{1,0:T(8,128)(2,1)S(1)} %relay.3), channel_id=1, source_target_pairs={{0,96},{16,112},{32,0},{48,16},{64,32},{80,48},{96,64},{112,80},{1... | collective-permute-start | bytes 786440 | tf_op jit(solution)/shard_map/ppermute | solution.py:286
  21.3 6.4 %prepare.1 = (bf16[2,1024,512]{2,1,0:T(8,128)(2,1)}, bf16[2,512,512]{2,1,0:T(8,128)(2,1)}, bf16[2,512,1024]{2,1,0:T(8,128)(2,1)}, f32[2,512,512]{2,1,0:T(8,128)}) custom-call(f32[2,512,512]{2,1,0:T(8,128)} %bitcast.26, f32[2,512,512]{2,1,0:T(8,128)} %bitcast.27, f32[2,512,512]{2,1,0:T(8,128)} %bitcast.21), custom_call_target="tpu_custom_call" | custom-call | flops 2147483648 | bytes 13631488 | tf_op jit(solution)/shard_map/prepare/pallas_call | solution.py:61
  27.7 0.0 copy-start
  27.7 0.0 collective-permute-done.2.left_direct
  27.7 0.0 collective-permute-done.3.right_direct
  27.7 0.0 collective-permute-done.5.left_sum
  27.7 0.0 collective-permute-done.7.right_sum
  27.7 1.5 %finish.1 = (bf16[32,2048]{1,0:T(8,128)(2,1)S(1)}, bf16[32,2048]{1,0:T(8,128)(2,1)S(1)}, bf16[32,2048]{1,0:T(8,128)(2,1)S(1)}, bf16[32,2048]{1,0:T(8,128)(2,1)S(1)}, f32[8,8,128]{2,1,0:T(8,128)}) custom-call(s32[3]{0:T(128)S(1)} %pad_add_fusion.1.place, f32[128,2048]{1,0:T(8,128)S(1)} %get-tuple-element.64.own, ...), custom_call_target="tpu_custom_call" | custom-call | tf_op jit(solution)/shard_map/finish/pallas_call | solution.py:87
  29.2 2.0 %collective-permute-start.8 = (bf16[32,2048]{1,0:T(8,128)(2,1)S(1)}, bf16[32,2048]{1,0:T(8,128)(2,1)S(1)}, u32[]{:S(2)}, u32[]{:S(2)}) collective-permute-start(bf16[32,2048]{1,0:T(8,128)(2,1)S(1)} %get-tuple-element.70), channel_id=1, source_target_pairs={{0,4},{1,5},{2,6},{3,7},{4,8},{5,9},{6,10},{7,11},{8,12},{9,13},{1... | collective-permute-start | bytes 393224 | tf_op jit(solution)/shard_map/ppermute | solution.py:294
  31.2 3.6 %collective-permute-start.9 = (bf16[32,2048]{1,0:T(8,128)(2,1)S(1)}, bf16[32,2048]{1,0:T(8,128)(2,1)S(1)}, u32[]{:S(2)}, u32[]{:S(2)}) collective-permute-start(bf16[32,2048]{1,0:T(8,128)(2,1)S(1)} %get-tuple-element.71), channel_id=1, source_target_pairs={{0,8},{1,9},{2,10},{3,11},{4,12},{5,13},{6,14},{7,15},{8,0},{9,1},... | collective-permute-start | bytes 393224 | tf_op jit(solution)/shard_map/ppermute | solution.py:294
  34.8 1.0 collective-permute-start.10
  35.8 3.9 %all-to-all-start = ((f32[8,8,128]{2,1,0:T(8,128)}), f32[8,8,128]{2,1,0:T(8,128)S(1)}, u32[]{:S(2)}, u32[]{:S(2)}) async-start(f32[8,8,128]{2,1,0:T(8,128)} %get-tuple-element.73), calls=%async_computation | async-start | bytes 65536 | tf_op jit(solution)/shard_map/all_to_all | solution.py:474
  39.8 0.0 copy-done
  39.8 0.1 pad_add_fusion.table
  39.8 5.4 %all-to-all-done.refs_4_ = f32[8,8,128]{2,1,0:T(8,128)S(1)} async-done(((f32[8,8,128]{2,1,0:T(8,128)}), f32[8,8,128]{2,1,0:T(8,128)S(1)}, u32[]{:S(2)}, u32[]{:S(2)}) %all-to-all-start) | async-done | bytes 32800 | tf_op jit(solution)/shard_map/all_to_all | solution.py:474
  45.2 0.0 collective-permute-done.8.refs_1_
  45.2 0.0 collective-permute-done.9.refs_2_
  45.2 0.0 collective-permute-done.10.refs_3_
  45.2 0.7 dispatch.1
  45.9 23.3 %all_to_all.15.refs_2_ = bf16[16,72,512]{2,1,0:T(8,128)(2,1)S(1)} all-to-all(bf16[16,72,512]{2,1,0:T(8,128)(2,1)S(1)} %dispatch.1), channel_id=1, replica_groups=mesh['dp'=8,'fsdp'=16] {'fsdp'}, dimensions={0} | all-to-all | bytes 2359296 | tf_op jit(solution)/shard_map/all_to_all | solution.py:477
  69.2 7.6 %direction.1 = (bf16[16,2,32,512]{3,2,1,0:T(8,128)(2,1)S(1)}, f32[2,512,512]{2,1,0:T(8,128)}) custom-call(s32[1,16]{1,0:T(1,128)S(1)} %copy-done, s32[1]{0:T(128)} %bitcast.1.refs_1_, bf16[16,72,512]{2,1,0:T(8,128)(2,1)S(1)} %all_to_all.15.refs_2_, f32[2,512,512]{2,1,0:T(8,128)} %bitcast.20, bf16[2,1024,512]{2,1,0:T(8,128)(2,1)} %get-tuple-element.74.refs_4_, ...), custom_call_target="tpu_custom_call" | custom-call | tf_op jit(solution)/shard_map/direction/pallas_call | solution.py:381
  76.9 19.3 %all_to_all.16 = bf16[16,2,32,512]{3,2,1,0:T(8,128)(2,1)S(1)} all-to-all(bf16[16,2,32,512]{3,2,1,0:T(8,128)(2,1)S(1)} %get-tuple-element.78), channel_id=1, replica_groups=mesh['dp'=8,'fsdp'=16] {'fsdp'}, dimensions={0} | all-to-all | bytes 2097152 | tf_op jit(solution)/shard_map/all_to_all | solution.py:481
  96.2 0.6 collect.1
  96.8 0.1 collective-permute-start.11
  96.9 2.4 %collective-permute-start.12 = (bf16[32,2048]{1,0:T(8,128)(2,1)S(1)}, bf16[32,2048]{1,0:T(8,128)(2,1)S(1)}, u32[]{:S(2)}, u32[]{:S(2)}) collective-permute-start(bf16[32,2048]{1,0:T(8,128)(2,1)S(1)} %get-tuple-element.82), channel_id=1, source_target_pairs={{0,8},{1,9},{2,10},{3,11},{4,12},{5,13},{6,14},{7,15},{8,0},{9,1},... | collective-permute-start | bytes 393224 | tf_op jit(solution)/shard_map/ppermute | solution.py:294
  99.3 1.1 %collective-permute-start.13 = (bf16[32,2048]{1,0:T(8,128)(2,1)S(1)}, bf16[32,2048]{1,0:T(8,128)(2,1)S(1)}, u32[]{:S(2)}, u32[]{:S(2)}) collective-permute-start(bf16[32,2048]{1,0:T(8,128)(2,1)S(1)} %get-tuple-element.83), channel_id=1, source_target_pairs={{0,12},{1,13},{2,14},{3,15},{4,0},{5,1},{6,2},{7,3},{8,4},{9,5},{1... | collective-permute-start | bytes 393224 | tf_op jit(solution)/shard_map/ppermute | solution.py:294
  100.4 5.3 %factors.1 = (f32[2,512,512]{2,1,0:T(8,128)}, f32[2,512,512]{2,1,0:T(8,128)}, f32[2,512,512]{2,1,0:T(8,128)}) custom-call(s32[1,16]{1,0:T(1,128)S(1)} %copy-done, s32[1]{0:T(128)} %bitcast.1.refs_1_, bf16[16,72,512]{2,1,0:T(8,128)(2,1)S(1)} %all_to_all.15.refs_2_, f32[2,512,512]{2,1,0:T(8,128)} %bitcast.23, f32[2,512,512]{2,1,0:T(8,128)} %bitcast.24, ...), custom_call_target="tpu_custom_call" | custom-call | flops 1073741824 | bytes 13631488 | tf_op jit(solution)/shard_map/factors/pallas_call | solution.py:427
  105.7 0.0 collective-permute-done.11.refs_1_
  105.7 0.0 collective-permute-done.12.refs_2_
  105.7 0.0 collective-permute-done.13.refs_3_
  105.8 1.4 %put.1 = bf16[4,32,2048]{2,1,0:T(8,128)(2,1)} custom-call(s32[1,17]{1,0:T(1,128)S(1)} %pad_add_fusion.table, bf16[32,2048]{1,0:T(8,128)(2,1)S(1)} %get-tuple-element.80.refs_0_, bf16[32,2048]{1,0:T(8,128)(2,1)S(1)} %collective-permute-done.11.refs_1_, bf16[32,2048]{1,0:T(8,128)(2,1)S(1)} %collective-permute-done.12.refs_2_, ...), custom_call_target="tpu_custom_call" | custom-call | tf_op jit(solution)/shard_map/put/pallas_call | solution.py:151
Async XLA Ops:
  3.5 2.0 %collective-permute-start = (bf16[1,128,2048]{2,1,0:T(8,128)(2,1)S(1)}, bf16[1,128,2048]{2,1,0:T(8,128)(2,1)S(1)}, u32[]{:S(2)}, u32[]{:S(2)}) collective-permute-start(bf16[1,128,2048]{2,1,0:T(8,128)(2,1)S(1)} %get-tuple-element.48), channel_id=1, source_target_pairs={{0,16},{16,0},{32,48},{48,32},{64,80},{80,64},{96,112},{112,96},{1... | collective-permute-start | bytes 1572872 | tf_op jit(solution)/shard_map/ppermute | solution.py:273
  5.5 4.1 %collective-permute-start.1 = (bf16[3,128,2048]{2,1,0:T(8,128)(2,1)S(1)}, bf16[3,128,2048]{2,1,0:T(8,128)(2,1)S(1)}, u32[]{:S(2)}, u32[]{:S(2)}) collective-permute-start(bf16[3,128,2048]{2,1,0:T(8,128)(2,1)S(1)} %get-tuple-element.50), channel_id=1, source_target_pairs={{0,16},{16,0},{32,48},{48,32},{64,80},{80,64},{96,112},{112,96},{1... | collective-permute-start | bytes 4718600 | tf_op jit(solution)/shard_map/ppermute | solution.py:275
  6.3 10.4 %collective-permute-start.4 = (bf16[64,2048]{1,0:T(8,128)(2,1)S(1)}, bf16[64,2048]{1,0:T(8,128)(2,1)S(1)}, u32[]{:S(2)}, u32[]{:S(2)}) collective-permute-start(bf16[64,2048]{1,0:T(8,128)(2,1)S(1)} %get-tuple-element.57), channel_id=1, source_target_pairs={{0,32},{16,48},{32,64},{48,80},{64,96},{80,112},{96,0},{112,16},{1... | collective-permute-start | bytes 786440 | tf_op jit(solution)/shard_map/ppermute | solution.py:277
  8.0 9.8 %collective-permute-start.6 = (bf16[64,2048]{1,0:T(8,128)(2,1)S(1)}, bf16[64,2048]{1,0:T(8,128)(2,1)S(1)}, u32[]{:S(2)}, u32[]{:S(2)}) collective-permute-start(bf16[64,2048]{1,0:T(8,128)(2,1)S(1)} %get-tuple-element.59), channel_id=1, source_target_pairs={{0,96},{16,112},{32,0},{48,16},{64,32},{80,48},{96,64},{112,80},{1... | collective-permute-start | bytes 786440 | tf_op jit(solution)/shard_map/ppermute | solution.py:278
  10.5 17.1 %collective-permute-start.2 = (bf16[64,2048]{1,0:T(8,128)(2,1)S(1)}, bf16[64,2048]{1,0:T(8,128)(2,1)S(1)}, u32[]{:S(2)}, u32[]{:S(2)}) collective-permute-start(bf16[64,2048]{1,0:T(8,128)(2,1)S(1)} %get-tuple-element.52), channel_id=1, source_target_pairs={{0,32},{16,48},{32,64},{48,80},{64,96},{80,112},{96,0},{112,16},{1... | collective-permute-start | bytes 786440 | tf_op jit(solution)/shard_map/ppermute | solution.py:283
  11.4 16.2 %collective-permute-start.3 = (bf16[64,2048]{1,0:T(8,128)(2,1)S(1)}, bf16[64,2048]{1,0:T(8,128)(2,1)S(1)}, u32[]{:S(2)}, u32[]{:S(2)}) collective-permute-start(bf16[64,2048]{1,0:T(8,128)(2,1)S(1)} %get-tuple-element.53), channel_id=1, source_target_pairs={{0,96},{16,112},{32,0},{48,16},{64,32},{80,48},{96,64},{112,80},{1... | collective-permute-start | bytes 786440 | tf_op jit(solution)/shard_map/ppermute | solution.py:284
  17.3 10.3 %collective-permute-start.5 = (bf16[64,2048]{1,0:T(8,128)(2,1)S(1)}, bf16[64,2048]{1,0:T(8,128)(2,1)S(1)}, u32[]{:S(2)}, u32[]{:S(2)}) collective-permute-start(bf16[64,2048]{1,0:T(8,128)(2,1)S(1)} %relay.2), channel_id=1, source_target_pairs={{0,32},{16,48},{32,64},{48,80},{64,96},{80,112},{96,0},{112,16},{1... | collective-permute-start | bytes 786440 | tf_op jit(solution)/shard_map/ppermute | solution.py:285
  18.4 9.3 %collective-permute-start.7 = (bf16[64,2048]{1,0:T(8,128)(2,1)S(1)}, bf16[64,2048]{1,0:T(8,128)(2,1)S(1)}, u32[]{:S(2)}, u32[]{:S(2)}) collective-permute-start(bf16[64,2048]{1,0:T(8,128)(2,1)S(1)} %relay.3), channel_id=1, source_target_pairs={{0,96},{16,112},{32,0},{48,16},{64,32},{80,48},{96,64},{112,80},{1... | collective-permute-start | bytes 786440 | tf_op jit(solution)/shard_map/ppermute | solution.py:286
  27.7 12.1 %copy-start = (s32[1,16]{1,0:T(1,128)S(1)}, s32[1,16]{1,0:T(1,128)}, u32[]{:S(2)}) copy-start(s32[1,16]{1,0:T(1,128)} %refs_0_.3) | copy-start | bytes 196
  29.2 16.0 %collective-permute-start.8 = (bf16[32,2048]{1,0:T(8,128)(2,1)S(1)}, bf16[32,2048]{1,0:T(8,128)(2,1)S(1)}, u32[]{:S(2)}, u32[]{:S(2)}) collective-permute-start(bf16[32,2048]{1,0:T(8,128)(2,1)S(1)} %get-tuple-element.70), channel_id=1, source_target_pairs={{0,4},{1,5},{2,6},{3,7},{4,8},{5,9},{6,10},{7,11},{8,12},{9,13},{1... | collective-permute-start | bytes 393224 | tf_op jit(solution)/shard_map/ppermute | solution.py:294
  31.2 14.0 %collective-permute-start.9 = (bf16[32,2048]{1,0:T(8,128)(2,1)S(1)}, bf16[32,2048]{1,0:T(8,128)(2,1)S(1)}, u32[]{:S(2)}, u32[]{:S(2)}) collective-permute-start(bf16[32,2048]{1,0:T(8,128)(2,1)S(1)} %get-tuple-element.71), channel_id=1, source_target_pairs={{0,8},{1,9},{2,10},{3,11},{4,12},{5,13},{6,14},{7,15},{8,0},{9,1},... | collective-permute-start | bytes 393224 | tf_op jit(solution)/shard_map/ppermute | solution.py:294
  34.8 10.4 %collective-permute-start.10 = (bf16[32,2048]{1,0:T(8,128)(2,1)S(1)}, bf16[32,2048]{1,0:T(8,128)(2,1)S(1)}, u32[]{:S(2)}, u32[]{:S(2)}) collective-permute-start(bf16[32,2048]{1,0:T(8,128)(2,1)S(1)} %get-tuple-element.72), channel_id=1, source_target_pairs={{0,12},{1,13},{2,14},{3,15},{4,0},{5,1},{6,2},{7,3},{8,4},{9,5},{1... | collective-permute-start | bytes 393224 | tf_op jit(solution)/shard_map/ppermute | solution.py:294
  35.8 9.4 %all-to-all-start = ((f32[8,8,128]{2,1,0:T(8,128)}), f32[8,8,128]{2,1,0:T(8,128)S(1)}, u32[]{:S(2)}, u32[]{:S(2)}) async-start(f32[8,8,128]{2,1,0:T(8,128)} %get-tuple-element.73), calls=%async_computation | async-start | bytes 65536 | tf_op jit(solution)/shard_map/all_to_all | solution.py:474
  96.8 8.9 %collective-permute-start.11 = (bf16[32,2048]{1,0:T(8,128)(2,1)S(1)}, bf16[32,2048]{1,0:T(8,128)(2,1)S(1)}, u32[]{:S(2)}, u32[]{:S(2)}) collective-permute-start(bf16[32,2048]{1,0:T(8,128)(2,1)S(1)} %get-tuple-element.81), channel_id=1, source_target_pairs={{0,4},{1,5},{2,6},{3,7},{4,8},{5,9},{6,10},{7,11},{8,12},{9,13},{1... | collective-permute-start | bytes 393224 | tf_op jit(solution)/shard_map/ppermute | solution.py:294
  96.9 8.8 %collective-permute-start.12 = (bf16[32,2048]{1,0:T(8,128)(2,1)S(1)}, bf16[32,2048]{1,0:T(8,128)(2,1)S(1)}, u32[]{:S(2)}, u32[]{:S(2)}) collective-permute-start(bf16[32,2048]{1,0:T(8,128)(2,1)S(1)} %get-tuple-element.82), channel_id=1, source_target_pairs={{0,8},{1,9},{2,10},{3,11},{4,12},{5,13},{6,14},{7,15},{8,0},{9,1},... | collective-permute-start | bytes 393224 | tf_op jit(solution)/shard_map/ppermute | solution.py:294
  99.3 6.5 %collective-permute-start.13 = (bf16[32,2048]{1,0:T(8,128)(2,1)S(1)}, bf16[32,2048]{1,0:T(8,128)(2,1)S(1)}, u32[]{:S(2)}, u32[]{:S(2)}) collective-permute-start(bf16[32,2048]{1,0:T(8,128)(2,1)S(1)} %get-tuple-element.83), channel_id=1, source_target_pairs={{0,12},{1,13},{2,14},{3,15},{4,0},{5,1},{6,2},{7,3},{8,4},{9,5},{1... | collective-permute-start | bytes 393224 | tf_op jit(solution)/shard_map/ppermute | solution.py:294

commit v3 on v1

v3 whole, which is shorter than its diff:
```python
import jax
import jax.numpy as jnp
from jax import lax
from jax.experimental import pallas as pl
from jax.experimental.pallas import tpu as pltpu
from jax.sharding import PartitionSpec as P

f32 = jnp.float32
bf16 = jnp.bfloat16
SMEM = pltpu.MemorySpace.SMEM
VMEM = pltpu.MemorySpace.VMEM
HBM = pltpu.MemorySpace.HBM
LANES = 128


def in_hbm(*arrays):
    return [pltpu.with_memory_space_constraint(a, HBM) for a in arrays]


def split3(value):
    head, rest = split(value)
    mid, tail = split(value - head.astype(f32))
    return head, mid, tail


def split(value):
    head = value.astype(bf16)
    return head, (value - head.astype(f32)).astype(bf16)


def mm(a, b, dims=((1,), (0,))):
    return lax.dot_general(a, b, (dims, ((), ())), preferred_element_type=f32)


def tiles(count, size=32):
    return [slice(r, r + size) for r in range(0, count, size)]


def prepare_body(
    left_src, right_src, first_src, lt_dst, l_dst, r_dst, rot_dst, *scratch
):
    left, right, first, lt, low, head, rot, lt_both, half, tail, product, sems, out_sems = scratch
    slots, n, _ = left.shape
    pairs = ((left_src, left), (first_src, first), (right_src, right))
    copies = [
        [
            pltpu.make_async_copy(src.at[s], dst.at[s], sems.at[s, i])
            for i, (src, dst) in enumerate(pairs)
        ]
        for s in range(slots)
    ]
    for group in copies:
        for c in group:
            c.start()
    pairs = ((lt, lt_dst), (low, l_dst), (head, r_dst), (rot, rot_dst))
    outs = [
        [
            pltpu.make_async_copy(src.at[s], dst.at[s], out_sems.at[s, i])
            for i, (src, dst) in enumerate(pairs)
        ]
        for s in range(slots)
    ]
    for s in range(slots):
        copies[s][0].wait()
        for rows in tiles(n, LANES):
            above, below = split(left[s, rows].T)
            lt[s, :, rows] = above
            lt_both[:n, rows] = above
            lt_both[n:, rows] = below
        outs[s][0].start()
        for rows in tiles(n):
            low[s, rows] = left[s, rows].astype(bf16)
        outs[s][1].start()
        copies[s][1].wait()
        for rows in tiles(n):
            half[rows] = first[s, rows].astype(bf16)
        product[...] = mm(lt_both[...], half[...])
        copies[s][2].wait()
        for rows, more in zip(tiles(n), tiles(2 * n)[n // 32 :]):
            half[rows] = (product[rows] + product[more]).astype(bf16)
            head[s, rows], tail[rows] = split(right[s, rows])
        outs[s][2].start()
        rot[s] = 0.9 * (mm(half[...], head[s]) + mm(half[...], tail[...]))
        outs[s][3].start()
    for group in outs:
        for c in group:
            c.wait()


def prepare(left_basis, right_basis, first_moment):
    slots, n, _ = left_basis.shape
    far = pl.BlockSpec(memory_space=HBM)
    return pl.pallas_call(
        prepare_body,
        in_specs=[far] * 3,
        out_specs=[far] * 4,
        out_shape=[HBM((slots, n, n), bf16)] * 3 + [HBM((slots, n, n), f32)],
        scratch_shapes=[pltpu.VMEM((slots, n, n), f32)] * 3
        + [pltpu.VMEM((slots, n, n), bf16)] * 3
        + [
            pltpu.VMEM((slots, n, n), f32),
            pltpu.VMEM((2 * n, n), bf16),
            pltpu.VMEM((n, n), bf16),
            pltpu.VMEM((n, n), bf16),
            pltpu.VMEM((2 * n, n), f32),
            pltpu.SemaphoreType.DMA((slots, 3)),
            pltpu.SemaphoreType.DMA((slots, 4)),
        ],
        compiler_params=pltpu.CompilerParams(vmem_limit_bytes=24 << 20),
        cost_estimate=pl.CostEstimate(
            flops=slots * 8 * n**3, bytes_accessed=slots * 22 * n * n, transcendentals=0
        ),
        name="prepare",
    )(*in_hbm(left_basis, right_basis, first_moment))


def local(body, arrays, out_shape, name, limit=8 << 20, cost=None):
    return pl.pallas_call(
        body,
        in_specs=[pl.BlockSpec(memory_space=SMEM)]
        + [pl.BlockSpec(memory_space=VMEM)] * (len(arrays) - 1),
        out_specs=jax.tree.map(
            lambda _: pl.BlockSpec(memory_space=VMEM), out_shape, is_leaf=lambda o: hasattr(o, "shape")
        ),
        out_shape=out_shape,
        compiler_params=pltpu.CompilerParams(vmem_limit_bytes=limit),
        cost_estimate=cost,
        name=name,
    )(*arrays)


def dispatch_body(table, *refs):
    *srcs, dst, square = refs
    n = dst.shape[2]
    bands = len(srcs)
    width = srcs[0].shape[1] - LANES
    cols = width // n
    z = table[0, bands * cols]
    total = jnp.zeros(square.shape, f32)
    for j, src in enumerate(srcs):
        band = lax.rem(z + bands - j, bands)
        for c in range(cols):
            dst[table[0, band * cols + c]] = src[:, c * n : (c + 1) * n]
        terms = src[:, width:].astype(f32)
        for t in range(3):
            total = total + terms[8 * t : 8 * t + 8]
    square[...] = total


def collect_body(table, src, *dsts):
    n = src.shape[2]
    bands = len(dsts)
    cols = dsts[0].shape[1] // n
    z = table[0, bands * cols]
    for j, dst in enumerate(dsts):
        band = lax.rem(z + j, bands)
        for c in range(cols):
            dst[:, c * n : (c + 1) * n] = src[table[0, band * cols + c]]


def put_body(table, *refs):
    *srcs, dst = refs
    bands = len(srcs)
    z = table[0, table.shape[1] - 1]
    for j, src in enumerate(srcs):
        dst[lax.rem(z + bands - j, bands)] = src[...]


def plus_body(place, *refs):
    total = refs[0][...]
    for ref in refs[1:-1]:
        total = total + ref[...]
    refs[-1][...] = total


def load(place, grads, width):
    rows, columns = grads.shape
    chips = columns // width // 2
    groups = ((2,), (1, 3, 0))

    def body(place, src, *refs):
        *dsts, sems = refs
        copies = []
        for i, dst in enumerate(dsts):
            core = 1 - place[1] if i < 2 else place[1]
            for k, j in enumerate(groups[i % 2]):
                slab = 2 * lax.rem(place[0] + j, chips) + core
                columns = pl.ds(pl.multiple_of(slab * width, width), width)
                copies.append(
                    pltpu.make_async_copy(src.at[:, columns], dst.at[k], sems.at[len(copies)])
                )
        for c in copies:
            c.start()
        for c in copies:
            c.wait()

    return pl.pallas_call(
        body,
        in_specs=[pl.BlockSpec(memory_space=SMEM), pl.BlockSpec(memory_space=HBM)],
        out_specs=[pl.BlockSpec(memory_space=VMEM)] * 4,
        out_shape=[VMEM((len(g), rows, width), bf16) for g in groups * 2],
        scratch_shapes=[pltpu.SemaphoreType.DMA((2 * chips,))],
        compiler_params=pltpu.CompilerParams(vmem_limit_bytes=2 << 20),
        name="load",
    )(place, *in_hbm(grads))


def pair(body, place, near, far, outs, name):
    low = near.shape[1] // 2

    def run(place, near, far, *outs):
        def total(i, a):
            part = slice(a * low, (a + 1) * low)
            return near[i, part].astype(f32) + far[i, part].astype(f32)

        body(total, low, *outs)

    out = [jax.ShapeDtypeStruct(shape, kind) for shape, kind in outs]
    return local(run, [place, near, far], out, name)


def far_body(total, low, to_right, to_left):
    to_right[...] = total(0, 0).astype(bf16)
    to_left[...] = total(0, 1).astype(bf16)


def near_body(total, low, to_right, to_left, keep_right, keep_left, own):
    keep_right[...] = total(0, 0)
    to_right[...] = total(0, 1).astype(bf16)
    to_left[...] = total(1, 0).astype(bf16)
    keep_left[...] = total(1, 1)
    for a in range(2):
        own[a * low : (a + 1) * low] = total(2, a)


def relay(place, kept, arrived):
    def body(place, kept, arrived, out):
        out[...] = (kept[...] + arrived[...].astype(f32)).astype(bf16)

    out = jax.ShapeDtypeStruct(kept.shape, bf16)
    return local(body, (place, kept, arrived), out, "relay")


def direct_body(place, own, left_direct, right_direct, out):
    low = left_direct.shape[0]
    out[:low] = own[:low] + right_direct[...].astype(f32)
    out[low:] = own[low:] + left_direct[...].astype(f32)


def finish(place, own, left_sum, right_sum, bands):
    rows, width = own.shape
    low = rows // 2
    piece = rows // bands

    def body(place, own, left_sum, right_sum, *outs):
        total = jnp.zeros((8, LANES), f32)
        for q in range(bands):
            relayed = left_sum if q * piece < low else right_sum
            part = slice(q * piece % low, q * piece % low + piece)
            value = own[q * piece : (q + 1) * piece] + relayed[part].astype(f32)
            step = lax.rem(q - place[2] + bands, bands)
            rounded = value.astype(bf16)
            for j in range(bands):

                @pl.when(step == j)
                def _():
                    outs[j][:, :width] = rounded

            by_row = jnp.sum((value * value).reshape(piece // 8, 8, width), axis=0)
            for c in range(width // LANES):
                total = total + by_row[:, c * LANES : (c + 1) * LANES]
        terms = [t.astype(f32) for t in split3(total)]
        terms.append(jnp.zeros((piece - 24, LANES), f32))
        terms = jnp.concatenate(terms, axis=0).astype(bf16)
        for out in outs:
            out[:, width:] = terms

    arrays = [place, own, left_sum, right_sum]
    out = [jax.ShapeDtypeStruct((piece, width + LANES), bf16)] * bands
    return local(body, arrays, out, "finish", 12 << 20)


def sum_over_replicas(place, grads, bands):
    size = lax.axis_size("dp")
    rows, columns = grads.shape
    width = columns // size
    half = (rows // 2, width)
    swap = [(d, d ^ 1) for d in range(size)]
    up = [(d, (d + 2) % size) for d in range(size)]
    down = [(d, (d - 2) % size) for d in range(size)]
    far_there, near_there, far_here, near_here = load(place, grads, width)
    other = lax.ppermute(far_there, "dp", swap)
    other, near_there = lax.optimization_barrier((other, near_there))
    others = lax.ppermute(near_there, "dp", swap)
    to_right, to_left = pair(far_body, place, far_here, other, [(half, bf16)] * 2, "pair_far")
    left_far = lax.ppermute(to_right, "dp", up)
    right_far = lax.ppermute(to_left, "dp", down)
    outs = [(half, bf16)] * 2 + [(half, f32)] * 2 + [((rows, width), f32)]
    to_right, to_left, keep_right, keep_left, own = pair(
        near_body, place, near_here, others, outs, "pair_near"
    )
    left_direct = lax.ppermute(to_right, "dp", up)
    right_direct = lax.ppermute(to_left, "dp", down)
    left_sum = lax.ppermute(relay(place, keep_right, left_far), "dp", up)
    right_sum = lax.ppermute(relay(place, keep_left, right_far), "dp", down)
    out = jax.ShapeDtypeStruct((rows, width), f32)
    own = local(direct_body, [place, own, left_direct, right_direct], out, "direct", cost=pl.CostEstimate(flops=2 * rows * width, bytes_accessed=12 * rows * width, transcendentals=0))
    return own, left_sum, right_sum


def exchange(arrays, steps):
    order = sorted(range(1, len(arrays)), key=lambda j: -min(j, len(arrays) - j))
    got = {0: arrays[0]}
    for j in order:
        got[j] = lax.ppermute(arrays[j], *steps[j - 1])
    return [got[j] for j in range(len(arrays))]


def assemble(pieces, slot, bands):
    per = pieces.shape[0] // bands
    return jnp.concatenate(
        [pieces[z * per + y, slot] for y in range(per) for z in range(bands)], axis=0
    )


def is_named(table, slot):
    named = table[0, 0] == slot
    for b in range(1, table.shape[1]):
        named = jnp.logical_or(named, table[0, b] == slot)
    return named


def clip_of(squares, entries):
    total = squares[0][...]
    for square in squares[1:]:
        total = total + square[...]
    total = jnp.sum(jnp.sum(total, axis=0, keepdims=True), axis=1, keepdims=True)
    return jnp.minimum(1.0, 1.0 / jnp.sqrt(total / entries + 1e-06))


def rotate(pieces, prepared, second, bands):
    slots, n, _ = second.shape

    def body(pieces, lt_src, l_src, r_src, rot_src, old_src, *refs):
        out, left, right, rot, old, lt, half, sems = refs
        pairs = ((lt_src, lt), (r_src, right), (rot_src, rot), (old_src, old), (l_src, left))
        copies = [
            pltpu.make_async_copy(src.at[s], dst.at[s], sems.at[s, i])
            for s in range(slots)
            for i, (src, dst) in enumerate(pairs)
        ]
        for c in copies:
            c.start()
        for s in range(slots):
            group = copies[s * len(pairs) : (s + 1) * len(pairs)]
            block = assemble(pieces, s, bands)
            group[0].wait()
            half[...] = mm(lt[s], block).astype(bf16)
            group[1].wait()
            out[s] = mm(half[...], right[s])
            for c in group[2:]:
                c.wait()

    whole = pl.BlockSpec(memory_space=VMEM)
    far = pl.BlockSpec(memory_space=HBM)
    return pl.pallas_call(
        body,
        in_specs=[whole] + [far] * 5,
        out_specs=[whole] * 5,
        out_shape=[
            VMEM((slots, n, n), f32),
            VMEM((slots, n, n), bf16),
            VMEM((slots, n, n), bf16),
            VMEM((slots, n, n), f32),
            VMEM((slots, n, n), f32),
        ],
        scratch_shapes=[
            pltpu.VMEM((slots, n, n), bf16),
            pltpu.VMEM((n, n), bf16),
            pltpu.SemaphoreType.DMA((slots, 5)),
        ],
        compiler_params=pltpu.CompilerParams(vmem_limit_bytes=12 << 20),
        name="rotate",
    )(pieces, *in_hbm(*prepared, second))


def direction(table, me, squares, rotated, bands, senders, entries):
    slots, n, _ = rotated[0].shape
    rows = n // senders
    per = senders // bands

    def body(table, me, *refs):
        squares, rest = refs[: len(refs) - 11], refs[len(refs) - 11 :]
        product, left, right, rot, old, out, second_out, new, step, half, sems = rest
        scale = clip_of(squares, entries)
        for s in range(slots):
            named = is_named(table, me[0] * slots + s)
            for r in tiles(n):
                turned = product[s, r] * scale
                before = old[s, r]
                value = 0.95 * before + 0.05 * turned * turned
                new[s, r] = jnp.where(named, value, before)
                ahead = rot[s, r] + 0.1 * turned
                step[r] = (ahead / (jnp.sqrt(value) + 1e-08)).astype(bf16)
            pltpu.make_async_copy(new.at[s], second_out.at[s], sems.at[s]).start()
            half[...] = mm(left[s], step[...]).astype(bf16)
            update = mm(half[...], right[s], ((1,), (1,))).astype(bf16)
            for y in range(per):
                for z in range(bands):
                    row = (y * bands + z) * rows
                    out[z * per + y, s] = update[row : row + rows]
        for s in range(slots):
            pltpu.make_async_copy(new.at[s], second_out.at[s], sems.at[s]).wait()

    scalar = pl.BlockSpec(memory_space=SMEM)
    whole = pl.BlockSpec(memory_space=VMEM)
    return pl.pallas_call(
        body,
        in_specs=[scalar] * 2 + [whole] * (len(squares) + 5),
        out_specs=[whole, pl.BlockSpec(memory_space=HBM)],
        out_shape=[
            jax.ShapeDtypeStruct((senders, slots, rows, n), bf16),
            HBM((slots, n, n), f32),
        ],
        scratch_shapes=[
            pltpu.VMEM((slots, n, n), f32),
            pltpu.VMEM((n, n), bf16),
            pltpu.VMEM((n, n), bf16),
            pltpu.SemaphoreType.DMA((slots,)),
        ],
        compiler_params=pltpu.CompilerParams(vmem_limit_bytes=16 << 20),
        name="direction",
    )(table, me, *squares, *rotated)


def factors_body(bands, entries, table, me, *refs):
    *squares, pieces = refs[:-14]
    sources, outs, (news, olds), sems = refs[-14:-11], refs[-11:-8], (refs[-8:-5], refs[-5:-2]), refs[-2:]
    slots, n, _ = news[0].shape
    copies = [
        [
            pltpu.make_async_copy(src.at[s], dst.at[s], sems[0].at[s, i])
            for i, (src, dst) in enumerate(zip(sources, olds))
        ]
        for s in range(slots)
    ]
    for group in copies:
        for c in group:
            c.start()
    scale = clip_of(squares, entries)
    square = 0.1 * scale * scale
    done = []
    for s in range(slots):
        named = is_named(table, me[0] * slots + s)
        block = assemble(pieces, s, bands)
        for i in range(3):
            if i == 0:
                more = square * mm(block, block, ((1,), (1,)))
            elif i == 1:
                more = square * mm(block.T, block)
            else:
                more = (0.1 * scale) * block.astype(f32)
            copies[s][i].wait()
            old = olds[i][s]
            news[i][s] = jnp.where(named, 0.9 * old + more, old)
            done.append(pltpu.make_async_copy(news[i].at[s], outs[i].at[s], sems[1].at[s, i]))
            done[-1].start()
    for c in done:
        c.wait()


def factors(table, me, squares, pieces, left, right, first, bands, entries):
    slots, n, _ = left.shape
    scalar = pl.BlockSpec(memory_space=SMEM)
    whole = pl.BlockSpec(memory_space=VMEM)
    far = pl.BlockSpec(memory_space=HBM)

    def body(*refs):
        factors_body(bands, entries, *refs)

    return pl.pallas_call(
        body,
        in_specs=[scalar] * 2 + [whole] * (len(squares) + 1) + [far] * 3,
        out_specs=[far] * 3,
        out_shape=[HBM(left.shape, f32)] * 3,
        scratch_shapes=[pltpu.VMEM((slots, n, n), f32)] * 6
        + [pltpu.SemaphoreType.DMA((slots, 3))] * 2,
        compiler_params=pltpu.CompilerParams(vmem_limit_bytes=24 << 20),
        cost_estimate=pl.CostEstimate(
            flops=slots * 4 * n**3, bytes_accessed=slots * 26 * n * n, transcendentals=0
        ),
        name="factors",
    )(table, me, *squares, pieces, *in_hbm(left, right, first))


def per_device(
    replica_grads,
    owners,
    left_factor,
    right_factor,
    left_basis,
    right_basis,
    first_moment,
    second_moment,
):
    rows_dev = replica_grads.shape[1]
    shards = lax.axis_size("fsdp")
    slots, n = left_factor.shape[1:3]
    per_band = n // rows_dev
    bands = shards // per_band
    dp = lax.axis_size("dp")
    dp_me = lax.axis_index("dp").astype(jnp.int32)
    me = lax.axis_index("fsdp").astype(jnp.int32)
    place = jnp.stack([dp_me // 2, dp_me % 2, me // per_band])
    table = jnp.concatenate([owners, (me // per_band).reshape(1, 1)], axis=1)
    me = me.reshape(1)
    core = [("dp", [(d, d ^ 1) for d in range(dp)])]
    along_x = [("dp", [(d, (d + 2 * h) % dp) for d in range(dp)]) for h in range(1, dp // 2)]
    along_y = [
        ("fsdp", [(i, i // per_band * per_band + (i + h) % per_band) for i in range(shards)])
        for h in range(1, per_band)
    ]
    along_z = [
        ("fsdp", [(i, (i + h * per_band) % shards) for i in range(shards)])
        for h in range(1, bands)
    ]
    parts = sum_over_replicas(place, replica_grads[0], bands)
    prepared = prepare(left_basis[0], right_basis[0], first_moment[0])
    parts, prepared = lax.optimization_barrier((parts, prepared))
    sums = finish(place, *parts, bands)
    rows, width = sums[0].shape[0], sums[0].shape[1] - LANES
    cols = width // n
    entries = rows_dev * shards * replica_grads.shape[2]
    spread = exchange(sums, along_z)
    one = jax.ShapeDtypeStruct((8, LANES), f32)
    out = [jax.ShapeDtypeStruct((shards * slots, rows, n), bf16), one]
    sent, square = local(dispatch_body, [table, *spread], out, "dispatch")
    sent = sent.reshape(shards, slots, rows, n)
    pieces = lax.all_to_all(sent, "fsdp", split_axis=0, concat_axis=0, tiled=True)
    for steps in (core, along_x):
        arrived = [lax.ppermute(square, *step) for step in steps]
        square = local(plus_body, [place, square, *arrived], one, "plus")
    squares = [square] + [lax.ppermute(square, *step) for step in along_y]
    rotated = rotate(pieces, prepared, second_moment[0], bands)
    update, second_new = direction(owners, me, squares, rotated, bands, shards, entries)
    back = lax.all_to_all(update, "fsdp", split_axis=0, concat_axis=0, tiled=True)
    back, pieces = lax.optimization_barrier((back, pieces))
    new = factors(
        owners, me, squares, pieces, left_factor[0], right_factor[0], first_moment[0], bands, entries
    )
    left_new, right_new, first_new = new
    out = [jax.ShapeDtypeStruct((rows, width), bf16)] * bands
    mine = local(collect_body, [table, back.reshape(shards * slots, rows, n)], out, "collect")
    out = jax.ShapeDtypeStruct((bands, rows, width), bf16)
    result = local(put_body, [table, *exchange(mine, along_z)], out, "put").reshape(rows_dev, width)
    return (result, left_new[None], right_new[None], first_new[None], second_new[None])


def solution(mesh):
    state = P("dp", "fsdp", None, None)
    return jax.shard_map(
        per_device,
        mesh=mesh,
        in_specs=(P("dp", "fsdp", None), P("dp", None)) + (state,) * 6,
        out_specs=(P("fsdp", "dp"),) + (state,) * 4,
        check_vma=False,
    )
```

time: 106 us -> 103 us (0.972)
  blocking collectives: 40.1 us -> 18.3 us
  starting transfers between devices: 24.6 us -> 35 us
  waiting for transfers between devices: 10.9 us -> 18.1 us
    all_to_all x1 -> x0, blocking collectives: 22.4 us -> none  [per_device(): lax.all_to_all(sent, 'fsdp', split_axis=0, concat_axis=0, tiled=True)]
    ppermute x6, waiting for transfers between devices: 0.02 us -> 6.28 us  [exchange(): got[j] = lax.ppermute(arrays[j], *steps[j - 1])]
    all_to_all x0 -> x1, starting transfers between devices: none -> 5.59 us  [per_device(): lax.all_to_all(sent, 'fsdp', split_axis=0, concat_axis=0, tiled=True)]
    ppermute x4 -> x7, starting transfers between devices: 4.16 us -> 9.44 us  [the longest x3 6.05 us: per_device(): squares = [square] + [lax.ppermute(square, *step) for step in along_y]]
    ppermute x1, waiting for transfers between devices: 2.92 us -> 0.01 us  [sum_over_replicas(): left_far = lax.ppermute(to_right, 'dp', up)]
    ppermute x1, waiting for transfers between devices: 0.01 us -> 2.38 us  [sum_over_replicas(): right_far = lax.ppermute(to_left, 'dp', down)]
    ppermute x1, waiting for transfers between devices: 0.01 us -> 2.35 us  [sum_over_replicas(): left_sum = lax.ppermute(relay(place, keep_right, left_far), 'dp', up)]
    ppermute x4 -> x7, waiting for transfers between devices: 6.07 us -> 3.87 us  [the longest x4 3.86 us: per_device(): arrived = [lax.ppermute(square, *step) for step in steps]]
  transfers between devices with their start and end apart: 18 -> 22, of which waited for: 6 -> 10; matrix products, arithmetic and copies ran while one was open for 0% -> 0% of each run, Pallas kernels for 14% -> 19%
where the time goes in v3:
time: 103 us; the launch traced here: 102 us
  starting transfers between devices  35 us (34%)
  Pallas kernels  29.7 us (29%)
  blocking collectives  18.3 us (18%)
  waiting for transfers between devices  18.1 us (18%)
    all_to_all x1, blocking collectives, per_device(): lax.all_to_all(update, 'fsdp', split_axis=0, concat_axis=0, tiled=True)  18.3 us
    ppermute x6, starting transfers between devices, exchange(): got[j] = lax.ppermute(arrays[j], *steps[j - 1])  9.62 us
    pallas_call x11, Pallas kernels, local(): pl.pallas_call(body, in_specs=[pl.BlockSpec(memory_space=SMEM)] + [pl.Blo...  8.75 us
    ppermute x6, waiting for transfers between devices, exchange(): got[j] = lax.ppermute(arrays[j], *steps[j - 1])  6.28 us
    ppermute x3, starting transfers between devices, per_device(): squares = [square] + [lax.ppermute(square, *step) for step in along_y]  6.05 us
    pallas_call x1, Pallas kernels, prepare(): pl.pallas_call(prepare_body, in_specs=[far] * 3, out_specs=[far] * 4, out...  6.02 us
    pallas_call x1, Pallas kernels, factors(): pl.pallas_call(body, in_specs=[scalar] * 2 + [whole] * (len(squares) + 1)...  5.87 us
    all_to_all x1, starting transfers between devices, per_device(): lax.all_to_all(sent, 'fsdp', split_axis=0, concat_axis=0, tiled=True)  5.59 us
  transfers between devices with their start and end apart: 22, of which 10 were waited for; matrix products, arithmetic and copies ran while one was open for 0% of the time, Pallas kernels for 19%

profile of v3, /device:TPU:0, one launch (start us, length us, event | category | flops | bytes accessed | tf_op | source)
XLA Modules:
  0.0 102.3 jit_solution(18360263057547492985)
XLA Ops:
  0.7 0.1 pad_add_fusion.1.place
  0.7 2.8 %load.1 = (bf16[1,128,2048]{2,1,0:T(8,128)(2,1)S(1)}, bf16[3,128,2048]{2,1,0:T(8,128)(2,1)S(1)}, bf16[1,128,2048]{2,1,0:T(8,128)(2,1)S(1)}, bf16[3,128,2048]{2,1,0:T(8,128)(2,1)S(1)}) custom-call(s32[3]{0:T(128)S(1)} %pad_add_fusion.1.place, bf16[128,16384]{1,0:T(8,128)(2,1)} %bitcast.20), custom_call_target="tpu_custom_call" | custom-call | tf_op jit(solution)/shard_map/load/pallas_call | solution.py:197
  3.5 0.1 collective-permute-start
  3.6 1.9 %collective-permute-done.far = bf16[1,128,2048]{2,1,0:T(8,128)(2,1)S(1)} collective-permute-done((bf16[1,128,2048]{2,1,0:T(8,128)(2,1)S(1)}, bf16[1,128,2048]{2,1,0:T(8,128)(2,1)S(1)}, u32[]{:S(2)}, u32[]{:S(2)}) %collective-permute-start) | collective-permute-done | bytes 524320 | tf_op jit(solution)/shard_map/ppermute | solution.py:292
  5.5 0.1 collective-permute-start.1
  5.7 0.7 pair_far.1
  6.3 2.9 %collective-permute-start.6 = (bf16[64,2048]{1,0:T(8,128)(2,1)S(1)}, bf16[64,2048]{1,0:T(8,128)(2,1)S(1)}, u32[]{:S(2)}, u32[]{:S(2)}) collective-permute-start(bf16[64,2048]{1,0:T(8,128)(2,1)S(1)} %get-tuple-element.63), channel_id=1, source_target_pairs={{0,96},{16,112},{32,0},{48,16},{64,32},{80,48},{96,64},{112,80},{1... | collective-permute-start | bytes 786440 | tf_op jit(solution)/shard_map/ppermute | solution.py:297
  9.2 0.9 pair_near.1
  10.1 1.3 %collective-permute-start.2 = (bf16[64,2048]{1,0:T(8,128)(2,1)S(1)}, bf16[64,2048]{1,0:T(8,128)(2,1)S(1)}, u32[]{:S(2)}, u32[]{:S(2)}) collective-permute-start(bf16[64,2048]{1,0:T(8,128)(2,1)S(1)} %get-tuple-element.56), channel_id=1, source_target_pairs={{0,32},{16,48},{32,64},{48,80},{64,96},{80,112},{96,0},{112,16},{1... | collective-permute-start | bytes 786440 | tf_op jit(solution)/shard_map/ppermute | solution.py:302
  11.4 2.1 %collective-permute-start.3 = (bf16[64,2048]{1,0:T(8,128)(2,1)S(1)}, bf16[64,2048]{1,0:T(8,128)(2,1)S(1)}, u32[]{:S(2)}, u32[]{:S(2)}) collective-permute-start(bf16[64,2048]{1,0:T(8,128)(2,1)S(1)} %get-tuple-element.57), channel_id=1, source_target_pairs={{0,96},{16,112},{32,0},{48,16},{64,32},{80,48},{96,64},{112,80},{1... | collective-permute-start | bytes 786440 | tf_op jit(solution)/shard_map/ppermute | solution.py:303
  13.5 2.4 %collective-permute-done.6.arrived = bf16[64,2048]{1,0:T(8,128)(2,1)S(1)} collective-permute-done((bf16[64,2048]{1,0:T(8,128)(2,1)S(1)}, bf16[64,2048]{1,0:T(8,128)(2,1)S(1)}, u32[]{:S(2)}, u32[]{:S(2)}) %collective-permute-start.6) | collective-permute-done | bytes 262176 | tf_op jit(solution)/shard_map/ppermute | solution.py:297
  15.9 0.6 relay.3
  16.5 3.8 %collective-permute-start.7 = (bf16[64,2048]{1,0:T(8,128)(2,1)S(1)}, bf16[64,2048]{1,0:T(8,128)(2,1)S(1)}, u32[]{:S(2)}, u32[]{:S(2)}) collective-permute-start(bf16[64,2048]{1,0:T(8,128)(2,1)S(1)} %relay.3), channel_id=1, source_target_pairs={{0,96},{16,112},{32,0},{48,16},{64,32},{80,48},{96,64},{112,80},{1... | collective-permute-start | bytes 786440 | tf_op jit(solution)/shard_map/ppermute | solution.py:305
  20.2 0.6 relay.2
  20.8 0.1 collective-permute-start.5
  20.9 6.0 %prepare.1 = (bf16[2,512,512]{2,1,0:T(8,128)(2,1)}, bf16[2,512,512]{2,1,0:T(8,128)(2,1)}, bf16[2,512,512]{2,1,0:T(8,128)(2,1)}, f32[2,512,512]{2,1,0:T(8,128)}) custom-call(f32[2,512,512]{2,1,0:T(8,128)} %bitcast.27, f32[2,512,512]{2,1,0:T(8,128)} %bitcast.28, f32[2,512,512]{2,1,0:T(8,128)} %bitcast.22), custom_call_target="tpu_custom_call" | custom-call | flops 2147483648 | bytes 11534336 | tf_op jit(solution)/shard_map/prepare/pallas_call | solution.py:93
  27.0 0.6 direct.1.own
  27.6 2.3 %collective-permute-done.5.left_sum = bf16[64,2048]{1,0:T(8,128)(2,1)S(1)} collective-permute-done((bf16[64,2048]{1,0:T(8,128)(2,1)S(1)}, bf16[64,2048]{1,0:T(8,128)(2,1)S(1)}, u32[]{:S(2)}, u32[]{:S(2)}) %collective-permute-start.5) | collective-permute-done | bytes 262176 | tf_op jit(solution)/shard_map/ppermute | solution.py:304
  30.0 0.8 finish.1
  30.8 4.1 %collective-permute-start.10 = (bf16[32,2176]{1,0:T(8,128)(2,1)S(1)}, bf16[32,2176]{1,0:T(8,128)(2,1)S(1)}, u32[]{:S(2)}, u32[]{:S(2)}) collective-permute-start(bf16[32,2176]{1,0:T(8,128)(2,1)S(1)} %get-tuple-element.74), channel_id=1, source_target_pairs={{0,12},{1,13},{2,14},{3,15},{4,0},{5,1},{6,2},{7,3},{8,4},{9,5},{1... | collective-permute-start | bytes 417800 | tf_op jit(solution)/shard_map/ppermute | solution.py:315
  34.9 1.9 %collective-permute-start.9 = (bf16[32,2176]{1,0:T(8,128)(2,1)S(1)}, bf16[32,2176]{1,0:T(8,128)(2,1)S(1)}, u32[]{:S(2)}, u32[]{:S(2)}) collective-permute-start(bf16[32,2176]{1,0:T(8,128)(2,1)S(1)} %get-tuple-element.73), channel_id=1, source_target_pairs={{0,8},{1,9},{2,10},{3,11},{4,12},{5,13},{6,14},{7,15},{8,0},{9,1},... | collective-permute-start | bytes 417800 | tf_op jit(solution)/shard_map/ppermute | solution.py:315
  36.8 2.2 %collective-permute-done.10.refs_3_ = bf16[32,2176]{1,0:T(8,128)(2,1)S(1)} collective-permute-done((bf16[32,2176]{1,0:T(8,128)(2,1)S(1)}, bf16[32,2176]{1,0:T(8,128)(2,1)S(1)}, u32[]{:S(2)}, u32[]{:S(2)}) %collective-permute-start.10) | collective-permute-done | bytes 139296 | tf_op jit(solution)/shard_map/ppermute | solution.py:315
  39.0 4.1 %collective-permute-done.8.refs_1_ = bf16[32,2176]{1,0:T(8,128)(2,1)S(1)} collective-permute-done((bf16[32,2176]{1,0:T(8,128)(2,1)S(1)}, bf16[32,2176]{1,0:T(8,128)(2,1)S(1)}, u32[]{:S(2)}, u32[]{:S(2)}) %collective-permute-start.8) | collective-permute-done | bytes 139296 | tf_op jit(solution)/shard_map/ppermute | solution.py:315
  43.1 1.6 %dispatch.1 = (bf16[32,32,512]{2,1,0:T(8,128)(2,1)}, f32[8,128]{1,0:T(8,128)S(1)}) custom-call(s32[1,17]{1,0:T(1,128)S(1)} %pad_add_fusion.table, bf16[32,2176]{1,0:T(8,128)(2,1)S(1)} %get-tuple-element.71.refs_0_, bf16[32,2176]{1,0:T(8,128)(2,1)S(1)} %collective-permute-done.8.refs_1_, bf16[32,2176]{1,0:T(8,128)(2,1)S(1)} %collective-permute-done.9.refs_2_, ...), custom_call_target="tpu_custom_call" | custom-call | tf_op jit(solution)/shard_map/dispatch/pallas_call | solution.py:118
  44.7 5.6 %all-to-all-start = ((bf16[16,2,32,512]{3,2,1,0:T(8,128)(2,1)}), bf16[16,2,32,512]{3,2,1,0:T(8,128)(2,1)S(1)}, u32[]{:S(2)}, u32[]{:S(2)}) async-start(bf16[16,2,32,512]{3,2,1,0:T(8,128)(2,1)} %bitcast.9), calls=%async_computation | async-start | bytes 2097152 | tf_op jit(solution)/shard_map/all_to_all | solution.py:539
  50.3 0.1 collective-permute-start.11
  50.4 1.2 %collective-permute-done.11.refs_1_ = f32[8,128]{1,0:T(8,128)S(1)} collective-permute-done((f32[8,128]{1,0:T(8,128)S(1)}, f32[8,128]{1,0:T(8,128)S(1)}, u32[]{:S(2)}, u32[]{:S(2)}) %collective-permute-start.11) | collective-permute-done | bytes 4128 | tf_op jit(solution)/shard_map/ppermute | solution.py:541
  51.5 0.5 plus.2.refs_0_
  52.1 0.1 collective-permute-start.12
  52.2 2.3 %collective-permute-start.13 = (f32[8,128]{1,0:T(8,128)S(1)}, f32[8,128]{1,0:T(8,128)S(1)}, u32[]{:S(2)}, u32[]{:S(2)}) collective-permute-start(f32[8,128]{1,0:T(8,128)S(1)} %plus.2.refs_0_), channel_id=1, source_target_pairs={{0,64},{16,80},{32,96},{48,112},{64,0},{80,16},{96,32},{112,48},{1... | collective-permute-start | bytes 12296 | tf_op jit(solution)/shard_map/ppermute | solution.py:541
  54.5 0.9 collective-permute-start.14
  55.4 1.6 %collective-permute-done.12.refs_1_ = f32[8,128]{1,0:T(8,128)S(1)} collective-permute-done((f32[8,128]{1,0:T(8,128)S(1)}, f32[8,128]{1,0:T(8,128)S(1)}, u32[]{:S(2)}, u32[]{:S(2)}) %collective-permute-start.12) | collective-permute-done | bytes 4128 | tf_op jit(solution)/shard_map/ppermute | solution.py:541
  57.0 0.4 collective-permute-done.13.refs_2_
  57.3 0.7 collective-permute-done.14.refs_3_
  58.1 0.5 plus.3.refs_0_.refs_2_
  58.6 1.9 %collective-permute-start.15 = (f32[8,128]{1,0:T(8,128)S(1)}, f32[8,128]{1,0:T(8,128)S(1)}, u32[]{:S(2)}, u32[]{:S(2)}) collective-permute-start(f32[8,128]{1,0:T(8,128)S(1)} %plus.3.refs_0_.refs_2_), channel_id=1, source_target_pairs={{0,1},{1,2},{2,3},{3,0},{4,5},{5,6},{6,7},{7,4},{8,9},{9,10},{10,1... | collective-permute-start | bytes 12296 | tf_op jit(solution)/shard_map/ppermute | solution.py:543
  60.6 2.7 %collective-permute-start.16 = (f32[8,128]{1,0:T(8,128)S(1)}, f32[8,128]{1,0:T(8,128)S(1)}, u32[]{:S(2)}, u32[]{:S(2)}) collective-permute-start(f32[8,128]{1,0:T(8,128)S(1)} %plus.3.refs_0_.refs_2_), channel_id=1, source_target_pairs={{0,2},{1,3},{2,0},{3,1},{4,6},{5,7},{6,4},{7,5},{8,10},{9,11},{10,... | collective-permute-start | bytes 12296 | tf_op jit(solution)/shard_map/ppermute | solution.py:543
  63.2 1.5 %collective-permute-start.17 = (f32[8,128]{1,0:T(8,128)S(1)}, f32[8,128]{1,0:T(8,128)S(1)}, u32[]{:S(2)}, u32[]{:S(2)}) collective-permute-start(f32[8,128]{1,0:T(8,128)S(1)} %plus.3.refs_0_.refs_2_), channel_id=1, source_target_pairs={{0,3},{1,0},{2,1},{3,2},{4,7},{5,4},{6,5},{7,6},{8,11},{9,8},{10,9... | collective-permute-start | bytes 12296 | tf_op jit(solution)/shard_map/ppermute | solution.py:543
  64.7 1.3 %all-to-all-done.pieces.refs_6_ = bf16[16,2,32,512]{3,2,1,0:T(8,128)(2,1)S(1)} async-done(((bf16[16,2,32,512]{3,2,1,0:T(8,128)(2,1)}), bf16[16,2,32,512]{3,2,1,0:T(8,128)(2,1)S(1)}, u32[]{:S(2)}, u32[]{:S(2)}) %all-to-all-start) | async-done | bytes 1048608 | tf_op jit(solution)/shard_map/all_to_all | solution.py:539
  66.0 3.2 %rotate.1 = (f32[2,512,512]{2,1,0:T(8,128)S(1)}, bf16[2,512,512]{2,1,0:T(8,128)(2,1)S(1)}, bf16[2,512,512]{2,1,0:T(8,128)(2,1)S(1)}, f32[2,512,512]{2,1,0:T(8,128)S(1)}, f32[2,512,512]{2,1,0:T(8,128)S(1)}) custom-call(bf16[16,2,32,512]{3,2,1,0:T(8,128)(2,1)S(1)} %all-to-all-done.pieces.refs_6_, bf16[2,512,512]{2,1,0:T(8,128)(2,1)} %get-tuple-element.77.lt_src, ...), custom_call_target="tpu_custom_call" | custom-call | tf_op jit(solution)/shard_map/rotate/pallas_call | solution.py:366
  69.2 3.2 %direction.1 = (bf16[16,2,32,512]{3,2,1,0:T(8,128)(2,1)S(1)}, f32[2,512,512]{2,1,0:T(8,128)}) custom-call(s32[1,16]{1,0:T(1,128)S(1)} %copy-done, s32[1]{0:T(128)} %bitcast.1.me.refs_1_, f32[8,128]{1,0:T(8,128)S(1)} %plus.3.refs_0_.refs_2_, f32[8,128]{1,0:T(8,128)S(1)} %collective-permute-done.15.refs_1_.refs_3_, ...), custom_call_target="tpu_custom_call" | custom-call | tf_op jit(solution)/shard_map/direction/pallas_call | solution.py:417
  72.4 18.3 %all_to_all.10 = bf16[16,2,32,512]{3,2,1,0:T(8,128)(2,1)S(1)} all-to-all(bf16[16,2,32,512]{3,2,1,0:T(8,128)(2,1)S(1)} %get-tuple-element.86), channel_id=1, replica_groups=mesh['dp'=8,'fsdp'=16] {'fsdp'}, dimensions={0} | all-to-all | bytes 2097152 | tf_op jit(solution)/shard_map/all_to_all | solution.py:546
  90.7 0.6 collect.1
  91.3 0.1 collective-permute-start.18
  91.4 2.4 %collective-permute-start.19 = (bf16[32,2048]{1,0:T(8,128)(2,1)S(1)}, bf16[32,2048]{1,0:T(8,128)(2,1)S(1)}, u32[]{:S(2)}, u32[]{:S(2)}) collective-permute-start(bf16[32,2048]{1,0:T(8,128)(2,1)S(1)} %get-tuple-element.90), channel_id=1, source_target_pairs={{0,8},{1,9},{2,10},{3,11},{4,12},{5,13},{6,14},{7,15},{8,0},{9,1},... | collective-permute-start | bytes 393224 | tf_op jit(solution)/shard_map/ppermute | solution.py:315
  93.8 1.2 %collective-permute-start.20 = (bf16[32,2048]{1,0:T(8,128)(2,1)S(1)}, bf16[32,2048]{1,0:T(8,128)(2,1)S(1)}, u32[]{:S(2)}, u32[]{:S(2)}) collective-permute-start(bf16[32,2048]{1,0:T(8,128)(2,1)S(1)} %get-tuple-element.91), channel_id=1, source_target_pairs={{0,12},{1,13},{2,14},{3,15},{4,0},{5,1},{6,2},{7,3},{8,4},{9,5},{1... | collective-permute-start | bytes 393224 | tf_op jit(solution)/shard_map/ppermute | solution.py:315
  95.0 5.9 %factors.1 = (f32[2,512,512]{2,1,0:T(8,128)}, f32[2,512,512]{2,1,0:T(8,128)}, f32[2,512,512]{2,1,0:T(8,128)}) custom-call(s32[1,16]{1,0:T(1,128)S(1)} %copy-done, s32[1]{0:T(128)} %bitcast.1.me.refs_1_, f32[8,128]{1,0:T(8,128)S(1)} %plus.3.refs_0_.refs_2_, f32[8,128]{1,0:T(8,128)S(1)} %collective-permute-done.15.refs_1_.refs_3_, ...), custom_call_target="tpu_custom_call" | custom-call | flops 1073741824 | bytes 13631488 | tf_op jit(solution)/shard_map/factors/pallas_call | solution.py:481
  100.9 1.4 %put.1 = bf16[4,32,2048]{2,1,0:T(8,128)(2,1)} custom-call(s32[1,17]{1,0:T(1,128)S(1)} %pad_add_fusion.table, bf16[32,2048]{1,0:T(8,128)(2,1)S(1)} %get-tuple-element.88.refs_0_, bf16[32,2048]{1,0:T(8,128)(2,1)S(1)} %collective-permute-done.18.refs_1_, bf16[32,2048]{1,0:T(8,128)(2,1)S(1)} %collective-permute-done.19.refs_2_, ...), custom_call_target="tpu_custom_call" | custom-call | tf_op jit(solution)/shard_map/put/pallas_call | solution.py:118
  (17 shorter events, 0.1 us)
Async XLA Ops:
  3.5 2.0 %collective-permute-start = (bf16[1,128,2048]{2,1,0:T(8,128)(2,1)S(1)}, bf16[1,128,2048]{2,1,0:T(8,128)(2,1)S(1)}, u32[]{:S(2)}, u32[]{:S(2)}) collective-permute-start(bf16[1,128,2048]{2,1,0:T(8,128)(2,1)S(1)} %get-tuple-element.52), channel_id=1, source_target_pairs={{0,16},{16,0},{32,48},{48,32},{64,80},{80,64},{96,112},{112,96},{1... | collective-permute-start | bytes 1572872 | tf_op jit(solution)/shard_map/ppermute | solution.py:292
  5.5 3.7 %collective-permute-start.1 = (bf16[3,128,2048]{2,1,0:T(8,128)(2,1)S(1)}, bf16[3,128,2048]{2,1,0:T(8,128)(2,1)S(1)}, u32[]{:S(2)}, u32[]{:S(2)}) collective-permute-start(bf16[3,128,2048]{2,1,0:T(8,128)(2,1)S(1)} %get-tuple-element.54), channel_id=1, source_target_pairs={{0,16},{16,0},{32,48},{48,32},{64,80},{80,64},{96,112},{112,96},{1... | collective-permute-start | bytes 4718600 | tf_op jit(solution)/shard_map/ppermute | solution.py:294
  6.3 9.6 %collective-permute-start.6 = (bf16[64,2048]{1,0:T(8,128)(2,1)S(1)}, bf16[64,2048]{1,0:T(8,128)(2,1)S(1)}, u32[]{:S(2)}, u32[]{:S(2)}) collective-permute-start(bf16[64,2048]{1,0:T(8,128)(2,1)S(1)} %get-tuple-element.63), channel_id=1, source_target_pairs={{0,96},{16,112},{32,0},{48,16},{64,32},{80,48},{96,64},{112,80},{1... | collective-permute-start | bytes 786440 | tf_op jit(solution)/shard_map/ppermute | solution.py:297
  9.2 11.0 %collective-permute-start.4 = (bf16[64,2048]{1,0:T(8,128)(2,1)S(1)}, bf16[64,2048]{1,0:T(8,128)(2,1)S(1)}, u32[]{:S(2)}, u32[]{:S(2)}) collective-permute-start(bf16[64,2048]{1,0:T(8,128)(2,1)S(1)} %get-tuple-element.61), channel_id=1, source_target_pairs={{0,32},{16,48},{32,64},{48,80},{64,96},{80,112},{96,0},{112,16},{1... | collective-permute-start | bytes 786440 | tf_op jit(solution)/shard_map/ppermute | solution.py:296
  10.1 16.8 %collective-permute-start.2 = (bf16[64,2048]{1,0:T(8,128)(2,1)S(1)}, bf16[64,2048]{1,0:T(8,128)(2,1)S(1)}, u32[]{:S(2)}, u32[]{:S(2)}) collective-permute-start(bf16[64,2048]{1,0:T(8,128)(2,1)S(1)} %get-tuple-element.56), channel_id=1, source_target_pairs={{0,32},{16,48},{32,64},{48,80},{64,96},{80,112},{96,0},{112,16},{1... | collective-permute-start | bytes 786440 | tf_op jit(solution)/shard_map/ppermute | solution.py:302
  11.4 15.5 %collective-permute-start.3 = (bf16[64,2048]{1,0:T(8,128)(2,1)S(1)}, bf16[64,2048]{1,0:T(8,128)(2,1)S(1)}, u32[]{:S(2)}, u32[]{:S(2)}) collective-permute-start(bf16[64,2048]{1,0:T(8,128)(2,1)S(1)} %get-tuple-element.57), channel_id=1, source_target_pairs={{0,96},{16,112},{32,0},{48,16},{64,32},{80,48},{96,64},{112,80},{1... | collective-permute-start | bytes 786440 | tf_op jit(solution)/shard_map/ppermute | solution.py:303
  16.5 11.1 %collective-permute-start.7 = (bf16[64,2048]{1,0:T(8,128)(2,1)S(1)}, bf16[64,2048]{1,0:T(8,128)(2,1)S(1)}, u32[]{:S(2)}, u32[]{:S(2)}) collective-permute-start(bf16[64,2048]{1,0:T(8,128)(2,1)S(1)} %relay.3), channel_id=1, source_target_pairs={{0,96},{16,112},{32,0},{48,16},{64,32},{80,48},{96,64},{112,80},{1... | collective-permute-start | bytes 786440 | tf_op jit(solution)/shard_map/ppermute | solution.py:305
  20.8 9.1 %collective-permute-start.5 = (bf16[64,2048]{1,0:T(8,128)(2,1)S(1)}, bf16[64,2048]{1,0:T(8,128)(2,1)S(1)}, u32[]{:S(2)}, u32[]{:S(2)}) collective-permute-start(bf16[64,2048]{1,0:T(8,128)(2,1)S(1)} %relay.2), channel_id=1, source_target_pairs={{0,32},{16,48},{32,64},{48,80},{64,96},{80,112},{96,0},{112,16},{1... | collective-permute-start | bytes 786440 | tf_op jit(solution)/shard_map/ppermute | solution.py:304
  27.0 9.8 %copy-start = (s32[1,16]{1,0:T(1,128)S(1)}, s32[1,16]{1,0:T(1,128)}, u32[]{:S(2)}) copy-start(s32[1,16]{1,0:T(1,128)} %refs_0_.1) | copy-start | bytes 196
  30.8 8.2 %collective-permute-start.10 = (bf16[32,2176]{1,0:T(8,128)(2,1)S(1)}, bf16[32,2176]{1,0:T(8,128)(2,1)S(1)}, u32[]{:S(2)}, u32[]{:S(2)}) collective-permute-start(bf16[32,2176]{1,0:T(8,128)(2,1)S(1)} %get-tuple-element.74), channel_id=1, source_target_pairs={{0,12},{1,13},{2,14},{3,15},{4,0},{5,1},{6,2},{7,3},{8,4},{9,5},{1... | collective-permute-start | bytes 417800 | tf_op jit(solution)/shard_map/ppermute | solution.py:315
  34.9 8.2 %collective-permute-start.8 = (bf16[32,2176]{1,0:T(8,128)(2,1)S(1)}, bf16[32,2176]{1,0:T(8,128)(2,1)S(1)}, u32[]{:S(2)}, u32[]{:S(2)}) collective-permute-start(bf16[32,2176]{1,0:T(8,128)(2,1)S(1)} %get-tuple-element.72), channel_id=1, source_target_pairs={{0,4},{1,5},{2,6},{3,7},{4,8},{5,9},{6,10},{7,11},{8,12},{9,13},{1... | collective-permute-start | bytes 417800 | tf_op jit(solution)/shard_map/ppermute | solution.py:315
  34.9 8.2 %collective-permute-start.9 = (bf16[32,2176]{1,0:T(8,128)(2,1)S(1)}, bf16[32,2176]{1,0:T(8,128)(2,1)S(1)}, u32[]{:S(2)}, u32[]{:S(2)}) collective-permute-start(bf16[32,2176]{1,0:T(8,128)(2,1)S(1)} %get-tuple-element.73), channel_id=1, source_target_pairs={{0,8},{1,9},{2,10},{3,11},{4,12},{5,13},{6,14},{7,15},{8,0},{9,1},... | collective-permute-start | bytes 417800 | tf_op jit(solution)/shard_map/ppermute | solution.py:315
  44.7 21.4 %all-to-all-start = ((bf16[16,2,32,512]{3,2,1,0:T(8,128)(2,1)}), bf16[16,2,32,512]{3,2,1,0:T(8,128)(2,1)S(1)}, u32[]{:S(2)}, u32[]{:S(2)}) async-start(bf16[16,2,32,512]{3,2,1,0:T(8,128)(2,1)} %bitcast.9), calls=%async_computation | async-start | bytes 2097152 | tf_op jit(solution)/shard_map/all_to_all | solution.py:539
  50.3 1.2 %collective-permute-start.11 = (f32[8,128]{1,0:T(8,128)S(1)}, f32[8,128]{1,0:T(8,128)S(1)}, u32[]{:S(2)}, u32[]{:S(2)}) collective-permute-start(f32[8,128]{1,0:T(8,128)S(1)} %get-tuple-element.75.refs_0_), channel_id=1, source_target_pairs={{0,16},{16,0},{32,48},{48,32},{64,80},{80,64},{96,112},{112,96},{1... | collective-permute-start | bytes 12296 | tf_op jit(solution)/shard_map/ppermute | solution.py:541
  52.1 4.9 %collective-permute-start.12 = (f32[8,128]{1,0:T(8,128)S(1)}, f32[8,128]{1,0:T(8,128)S(1)}, u32[]{:S(2)}, u32[]{:S(2)}) collective-permute-start(f32[8,128]{1,0:T(8,128)S(1)} %plus.2.refs_0_), channel_id=1, source_target_pairs={{0,32},{16,48},{32,64},{48,80},{64,96},{80,112},{96,0},{112,16},{1... | collective-permute-start | bytes 12296 | tf_op jit(solution)/shard_map/ppermute | solution.py:541
  52.2 5.2 %collective-permute-start.13 = (f32[8,128]{1,0:T(8,128)S(1)}, f32[8,128]{1,0:T(8,128)S(1)}, u32[]{:S(2)}, u32[]{:S(2)}) collective-permute-start(f32[8,128]{1,0:T(8,128)S(1)} %plus.2.refs_0_), channel_id=1, source_target_pairs={{0,64},{16,80},{32,96},{48,112},{64,0},{80,16},{96,32},{112,48},{1... | collective-permute-start | bytes 12296 | tf_op jit(solution)/shard_map/ppermute | solution.py:541
  54.5 3.6 %collective-permute-start.14 = (f32[8,128]{1,0:T(8,128)S(1)}, f32[8,128]{1,0:T(8,128)S(1)}, u32[]{:S(2)}, u32[]{:S(2)}) collective-permute-start(f32[8,128]{1,0:T(8,128)S(1)} %plus.2.refs_0_), channel_id=1, source_target_pairs={{0,96},{16,112},{32,0},{48,16},{64,32},{80,48},{96,64},{112,80},{1... | collective-permute-start | bytes 12296 | tf_op jit(solution)/shard_map/ppermute | solution.py:541
  58.6 10.6 %collective-permute-start.15 = (f32[8,128]{1,0:T(8,128)S(1)}, f32[8,128]{1,0:T(8,128)S(1)}, u32[]{:S(2)}, u32[]{:S(2)}) collective-permute-start(f32[8,128]{1,0:T(8,128)S(1)} %plus.3.refs_0_.refs_2_), channel_id=1, source_target_pairs={{0,1},{1,2},{2,3},{3,0},{4,5},{5,6},{6,7},{7,4},{8,9},{9,10},{10,1... | collective-permute-start | bytes 12296 | tf_op jit(solution)/shard_map/ppermute | solution.py:543
  60.6 8.7 %collective-permute-start.16 = (f32[8,128]{1,0:T(8,128)S(1)}, f32[8,128]{1,0:T(8,128)S(1)}, u32[]{:S(2)}, u32[]{:S(2)}) collective-permute-start(f32[8,128]{1,0:T(8,128)S(1)} %plus.3.refs_0_.refs_2_), channel_id=1, source_target_pairs={{0,2},{1,3},{2,0},{3,1},{4,6},{5,7},{6,4},{7,5},{8,10},{9,11},{10,... | collective-permute-start | bytes 12296 | tf_op jit(solution)/shard_map/ppermute | solution.py:543
  63.2 6.0 %collective-permute-start.17 = (f32[8,128]{1,0:T(8,128)S(1)}, f32[8,128]{1,0:T(8,128)S(1)}, u32[]{:S(2)}, u32[]{:S(2)}) collective-permute-start(f32[8,128]{1,0:T(8,128)S(1)} %plus.3.refs_0_.refs_2_), channel_id=1, source_target_pairs={{0,3},{1,0},{2,1},{3,2},{4,7},{5,4},{6,5},{7,6},{8,11},{9,8},{10,9... | collective-permute-start | bytes 12296 | tf_op jit(solution)/shard_map/ppermute | solution.py:543
  91.3 9.5 %collective-permute-start.18 = (bf16[32,2048]{1,0:T(8,128)(2,1)S(1)}, bf16[32,2048]{1,0:T(8,128)(2,1)S(1)}, u32[]{:S(2)}, u32[]{:S(2)}) collective-permute-start(bf16[32,2048]{1,0:T(8,128)(2,1)S(1)} %get-tuple-element.89), channel_id=1, source_target_pairs={{0,4},{1,5},{2,6},{3,7},{4,8},{5,9},{6,10},{7,11},{8,12},{9,13},{1... | collective-permute-start | bytes 393224 | tf_op jit(solution)/shard_map/ppermute | solution.py:315
  91.4 9.5 %collective-permute-start.19 = (bf16[32,2048]{1,0:T(8,128)(2,1)S(1)}, bf16[32,2048]{1,0:T(8,128)(2,1)S(1)}, u32[]{:S(2)}, u32[]{:S(2)}) collective-permute-start(bf16[32,2048]{1,0:T(8,128)(2,1)S(1)} %get-tuple-element.90), channel_id=1, source_target_pairs={{0,8},{1,9},{2,10},{3,11},{4,12},{5,13},{6,14},{7,15},{8,0},{9,1},... | collective-permute-start | bytes 393224 | tf_op jit(solution)/shard_map/ppermute | solution.py:315
  93.8 7.1 %collective-permute-start.20 = (bf16[32,2048]{1,0:T(8,128)(2,1)S(1)}, bf16[32,2048]{1,0:T(8,128)(2,1)S(1)}, u32[]{:S(2)}, u32[]{:S(2)}) collective-permute-start(bf16[32,2048]{1,0:T(8,128)(2,1)S(1)} %get-tuple-element.91), channel_id=1, source_target_pairs={{0,12},{1,13},{2,14},{3,15},{4,0},{5,1},{6,2},{7,3},{8,4},{9,5},{1... | collective-permute-start | bytes 393224 | tf_op jit(solution)/shard_map/ppermute | solution.py:315

commit v4 on v3

--- a/solution.py
+++ b/solution.py
@@ -401,7 +401,7 @@
                 value = 0.95 * before + 0.05 * turned * turned
                 new[s, r] = jnp.where(named, value, before)
                 ahead = rot[s, r] + 0.1 * turned
-                step[r] = (ahead / (jnp.sqrt(value) + 1e-08)).astype(bf16)
+                step[r] = (ahead * pl.reciprocal(jnp.sqrt(value) + 1e-08, approx=True)).astype(bf16)
             pltpu.make_async_copy(new.at[s], second_out.at[s], sems.at[s]).start()
             half[...] = mm(left[s], step[...]).astype(bf16)
             update = mm(half[...], right[s], ((1,), (1,))).astype(bf16)
@@ -434,8 +434,9 @@
 
 
 def factors_body(bands, entries, table, me, *refs):
-    *squares, pieces = refs[:-14]
-    sources, outs, (news, olds), sems = refs[-14:-11], refs[-11:-8], (refs[-8:-5], refs[-5:-2]), refs[-2:]
+    *squares, pieces = refs[:-16]
+    sources, outs, news, olds = (refs[i : i + 3] for i in range(-16, -4, 3))
+    block, product, *sems = refs[-4:]
     slots, n, _ = news[0].shape
     copies = [
         [
@@ -452,17 +453,17 @@
     done = []
     for s in range(slots):
         named = is_named(table, me[0] * slots + s)
-        block = assemble(pieces, s, bands)
+        block[...] = assemble(pieces, s, bands)
         for i in range(3):
             if i == 0:
-                more = square * mm(block, block, ((1,), (1,)))
+                product[...] = mm(block[...], block[...], ((1,), (1,)))
             elif i == 1:
-                more = square * mm(block.T, block)
-            else:
-                more = (0.1 * scale) * block.astype(f32)
+                product[...] = mm(block[...].T, block[...])
             copies[s][i].wait()
-            old = olds[i][s]
-            news[i][s] = jnp.where(named, 0.9 * old + more, old)
+            for r in tiles(n):
+                old = olds[i][s, r]
+                more = square * product[r] if i < 2 else (0.1 * scale) * block[r].astype(f32)
+                news[i][s, r] = jnp.where(named, 0.9 * old + more, old)
             done.append(pltpu.make_async_copy(news[i].at[s], outs[i].at[s], sems[1].at[s, i]))
             done[-1].start()
     for c in done:
@@ -484,6 +485,7 @@
         out_specs=[far] * 3,
         out_shape=[HBM(left.shape, f32)] * 3,
         scratch_shapes=[pltpu.VMEM((slots, n, n), f32)] * 6
+        + [pltpu.VMEM((n, n), bf16), pltpu.VMEM((n, n), f32)]
         + [pltpu.SemaphoreType.DMA((slots, 3))] * 2,
         compiler_params=pltpu.CompilerParams(vmem_limit_bytes=24 << 20),
         cost_estimate=pl.CostEstimate(

time: 103 us -> 102 us (level)
  no operation moved by 1% of the time
where the time goes in v4:
time: 102 us
  starting transfers between devices  35 us (34%)
  Pallas kernels  29.5 us (29%)
  blocking collectives  18.3 us (18%)
  waiting for transfers between devices  18.1 us (18%)
    all_to_all x1, blocking collectives, per_device(): lax.all_to_all(update, 'fsdp', split_axis=0, concat_axis=0, tiled=True)  18.3 us
    ppermute x6, starting transfers between devices, exchange(): got[j] = lax.ppermute(arrays[j], *steps[j - 1])  9.62 us
    pallas_call x11, Pallas kernels, local(): pl.pallas_call(body, in_specs=[pl.BlockSpec(memory_space=SMEM)] + [pl.Blo...  8.75 us
    ppermute x6, waiting for transfers between devices, exchange(): got[j] = lax.ppermute(arrays[j], *steps[j - 1])  6.28 us
    ppermute x3, starting transfers between devices, per_device(): squares = [square] + [lax.ppermute(square, *step) for step in along_y]  6.05 us
    pallas_call x1, Pallas kernels, prepare(): pl.pallas_call(prepare_body, in_specs=[far] * 3, out_specs=[far] * 4, out...  6.02 us
    all_to_all x1, starting transfers between devices, per_device(): lax.all_to_all(sent, 'fsdp', split_axis=0, concat_axis=0, tiled=True)  5.59 us
    pallas_call x1, Pallas kernels, factors(): pl.pallas_call(body, in_specs=[scalar] * 2 + [whole] * (len(squares) + 1)...  5.58 us
  transfers between devices with their start and end apart: 22, of which 10 were waited for; matrix products, arithmetic and copies ran while one was open for 0% of the time, Pallas kernels for 19%

profile of v4, /device:TPU:0, one launch (start us, length us, event | category | flops | bytes accessed | tf_op | source)
XLA Modules:
  0.0 102.0 jit_solution(10300399513701927272)
XLA Ops:
  0.7 0.1 pad_add_fusion.1.place
  0.7 2.8 %load.1 = (bf16[1,128,2048]{2,1,0:T(8,128)(2,1)S(1)}, bf16[3,128,2048]{2,1,0:T(8,128)(2,1)S(1)}, bf16[1,128,2048]{2,1,0:T(8,128)(2,1)S(1)}, bf16[3,128,2048]{2,1,0:T(8,128)(2,1)S(1)}) custom-call(s32[3]{0:T(128)S(1)} %pad_add_fusion.1.place, bf16[128,16384]{1,0:T(8,128)(2,1)} %bitcast.20), custom_call_target="tpu_custom_call" | custom-call | tf_op jit(solution)/shard_map/load/pallas_call | solution.py:197
  3.5 0.1 collective-permute-start
  3.6 1.9 %collective-permute-done.far = bf16[1,128,2048]{2,1,0:T(8,128)(2,1)S(1)} collective-permute-done((bf16[1,128,2048]{2,1,0:T(8,128)(2,1)S(1)}, bf16[1,128,2048]{2,1,0:T(8,128)(2,1)S(1)}, u32[]{:S(2)}, u32[]{:S(2)}) %collective-permute-start) | collective-permute-done | bytes 524320 | tf_op jit(solution)/shard_map/ppermute | solution.py:292
  5.5 0.1 collective-permute-start.1
  5.7 0.7 pair_far.1
  6.3 2.9 %collective-permute-start.6 = (bf16[64,2048]{1,0:T(8,128)(2,1)S(1)}, bf16[64,2048]{1,0:T(8,128)(2,1)S(1)}, u32[]{:S(2)}, u32[]{:S(2)}) collective-permute-start(bf16[64,2048]{1,0:T(8,128)(2,1)S(1)} %get-tuple-element.63), channel_id=1, source_target_pairs={{0,96},{16,112},{32,0},{48,16},{64,32},{80,48},{96,64},{112,80},{1... | collective-permute-start | bytes 786440 | tf_op jit(solution)/shard_map/ppermute | solution.py:297
  9.2 0.9 pair_near.1
  10.1 1.3 %collective-permute-start.2 = (bf16[64,2048]{1,0:T(8,128)(2,1)S(1)}, bf16[64,2048]{1,0:T(8,128)(2,1)S(1)}, u32[]{:S(2)}, u32[]{:S(2)}) collective-permute-start(bf16[64,2048]{1,0:T(8,128)(2,1)S(1)} %get-tuple-element.56), channel_id=1, source_target_pairs={{0,32},{16,48},{32,64},{48,80},{64,96},{80,112},{96,0},{112,16},{1... | collective-permute-start | bytes 786440 | tf_op jit(solution)/shard_map/ppermute | solution.py:302
  11.4 2.1 %collective-permute-start.3 = (bf16[64,2048]{1,0:T(8,128)(2,1)S(1)}, bf16[64,2048]{1,0:T(8,128)(2,1)S(1)}, u32[]{:S(2)}, u32[]{:S(2)}) collective-permute-start(bf16[64,2048]{1,0:T(8,128)(2,1)S(1)} %get-tuple-element.57), channel_id=1, source_target_pairs={{0,96},{16,112},{32,0},{48,16},{64,32},{80,48},{96,64},{112,80},{1... | collective-permute-start | bytes 786440 | tf_op jit(solution)/shard_map/ppermute | solution.py:303
  13.5 2.4 %collective-permute-done.6.arrived = bf16[64,2048]{1,0:T(8,128)(2,1)S(1)} collective-permute-done((bf16[64,2048]{1,0:T(8,128)(2,1)S(1)}, bf16[64,2048]{1,0:T(8,128)(2,1)S(1)}, u32[]{:S(2)}, u32[]{:S(2)}) %collective-permute-start.6) | collective-permute-done | bytes 262176 | tf_op jit(solution)/shard_map/ppermute | solution.py:297
  15.9 0.6 relay.3
  16.5 3.8 %collective-permute-start.7 = (bf16[64,2048]{1,0:T(8,128)(2,1)S(1)}, bf16[64,2048]{1,0:T(8,128)(2,1)S(1)}, u32[]{:S(2)}, u32[]{:S(2)}) collective-permute-start(bf16[64,2048]{1,0:T(8,128)(2,1)S(1)} %relay.3), channel_id=1, source_target_pairs={{0,96},{16,112},{32,0},{48,16},{64,32},{80,48},{96,64},{112,80},{1... | collective-permute-start | bytes 786440 | tf_op jit(solution)/shard_map/ppermute | solution.py:305
  20.2 0.6 relay.2
  20.8 0.1 collective-permute-start.5
  20.9 6.0 %prepare.1 = (bf16[2,512,512]{2,1,0:T(8,128)(2,1)}, bf16[2,512,512]{2,1,0:T(8,128)(2,1)}, bf16[2,512,512]{2,1,0:T(8,128)(2,1)}, f32[2,512,512]{2,1,0:T(8,128)}) custom-call(f32[2,512,512]{2,1,0:T(8,128)} %bitcast.27, f32[2,512,512]{2,1,0:T(8,128)} %bitcast.28, f32[2,512,512]{2,1,0:T(8,128)} %bitcast.22), custom_call_target="tpu_custom_call" | custom-call | flops 2147483648 | bytes 11534336 | tf_op jit(solution)/shard_map/prepare/pallas_call | solution.py:93
  27.0 0.6 direct.1.own
  27.6 2.3 %collective-permute-done.5.left_sum = bf16[64,2048]{1,0:T(8,128)(2,1)S(1)} collective-permute-done((bf16[64,2048]{1,0:T(8,128)(2,1)S(1)}, bf16[64,2048]{1,0:T(8,128)(2,1)S(1)}, u32[]{:S(2)}, u32[]{:S(2)}) %collective-permute-start.5) | collective-permute-done | bytes 262176 | tf_op jit(solution)/shard_map/ppermute | solution.py:304
  30.0 0.8 finish.1
  30.8 4.1 %collective-permute-start.10 = (bf16[32,2176]{1,0:T(8,128)(2,1)S(1)}, bf16[32,2176]{1,0:T(8,128)(2,1)S(1)}, u32[]{:S(2)}, u32[]{:S(2)}) collective-permute-start(bf16[32,2176]{1,0:T(8,128)(2,1)S(1)} %get-tuple-element.74), channel_id=1, source_target_pairs={{0,12},{1,13},{2,14},{3,15},{4,0},{5,1},{6,2},{7,3},{8,4},{9,5},{1... | collective-permute-start | bytes 417800 | tf_op jit(solution)/shard_map/ppermute | solution.py:315
  34.9 1.9 %collective-permute-start.9 = (bf16[32,2176]{1,0:T(8,128)(2,1)S(1)}, bf16[32,2176]{1,0:T(8,128)(2,1)S(1)}, u32[]{:S(2)}, u32[]{:S(2)}) collective-permute-start(bf16[32,2176]{1,0:T(8,128)(2,1)S(1)} %get-tuple-element.73), channel_id=1, source_target_pairs={{0,8},{1,9},{2,10},{3,11},{4,12},{5,13},{6,14},{7,15},{8,0},{9,1},... | collective-permute-start | bytes 417800 | tf_op jit(solution)/shard_map/ppermute | solution.py:315
  36.8 2.2 %collective-permute-done.10.refs_3_ = bf16[32,2176]{1,0:T(8,128)(2,1)S(1)} collective-permute-done((bf16[32,2176]{1,0:T(8,128)(2,1)S(1)}, bf16[32,2176]{1,0:T(8,128)(2,1)S(1)}, u32[]{:S(2)}, u32[]{:S(2)}) %collective-permute-start.10) | collective-permute-done | bytes 139296 | tf_op jit(solution)/shard_map/ppermute | solution.py:315
  39.0 4.1 %collective-permute-done.8.refs_1_ = bf16[32,2176]{1,0:T(8,128)(2,1)S(1)} collective-permute-done((bf16[32,2176]{1,0:T(8,128)(2,1)S(1)}, bf16[32,2176]{1,0:T(8,128)(2,1)S(1)}, u32[]{:S(2)}, u32[]{:S(2)}) %collective-permute-start.8) | collective-permute-done | bytes 139296 | tf_op jit(solution)/shard_map/ppermute | solution.py:315
  43.1 1.6 %dispatch.1 = (bf16[32,32,512]{2,1,0:T(8,128)(2,1)}, f32[8,128]{1,0:T(8,128)S(1)}) custom-call(s32[1,17]{1,0:T(1,128)S(1)} %pad_add_fusion.table, bf16[32,2176]{1,0:T(8,128)(2,1)S(1)} %get-tuple-element.71.refs_0_, bf16[32,2176]{1,0:T(8,128)(2,1)S(1)} %collective-permute-done.8.refs_1_, bf16[32,2176]{1,0:T(8,128)(2,1)S(1)} %collective-permute-done.9.refs_2_, ...), custom_call_target="tpu_custom_call" | custom-call | tf_op jit(solution)/shard_map/dispatch/pallas_call | solution.py:118
  44.7 5.6 %all-to-all-start = ((bf16[16,2,32,512]{3,2,1,0:T(8,128)(2,1)}), bf16[16,2,32,512]{3,2,1,0:T(8,128)(2,1)S(1)}, u32[]{:S(2)}, u32[]{:S(2)}) async-start(bf16[16,2,32,512]{3,2,1,0:T(8,128)(2,1)} %bitcast.9), calls=%async_computation | async-start | bytes 2097152 | tf_op jit(solution)/shard_map/all_to_all | solution.py:541
  50.3 0.1 collective-permute-start.11
  50.4 1.2 %collective-permute-done.11.refs_1_ = f32[8,128]{1,0:T(8,128)S(1)} collective-permute-done((f32[8,128]{1,0:T(8,128)S(1)}, f32[8,128]{1,0:T(8,128)S(1)}, u32[]{:S(2)}, u32[]{:S(2)}) %collective-permute-start.11) | collective-permute-done | bytes 4128 | tf_op jit(solution)/shard_map/ppermute | solution.py:543
  51.5 0.5 plus.2.refs_0_
  52.1 0.1 collective-permute-start.12
  52.2 2.3 %collective-permute-start.13 = (f32[8,128]{1,0:T(8,128)S(1)}, f32[8,128]{1,0:T(8,128)S(1)}, u32[]{:S(2)}, u32[]{:S(2)}) collective-permute-start(f32[8,128]{1,0:T(8,128)S(1)} %plus.2.refs_0_), channel_id=1, source_target_pairs={{0,64},{16,80},{32,96},{48,112},{64,0},{80,16},{96,32},{112,48},{1... | collective-permute-start | bytes 12296 | tf_op jit(solution)/shard_map/ppermute | solution.py:543
  54.5 0.9 collective-permute-start.14
  55.4 1.6 %collective-permute-done.12.refs_1_ = f32[8,128]{1,0:T(8,128)S(1)} collective-permute-done((f32[8,128]{1,0:T(8,128)S(1)}, f32[8,128]{1,0:T(8,128)S(1)}, u32[]{:S(2)}, u32[]{:S(2)}) %collective-permute-start.12) | collective-permute-done | bytes 4128 | tf_op jit(solution)/shard_map/ppermute | solution.py:543
  57.0 0.4 collective-permute-done.13.refs_2_
  57.3 0.7 collective-permute-done.14.refs_3_
  58.1 0.5 plus.3.refs_0_.refs_2_
  58.6 1.9 %collective-permute-start.15 = (f32[8,128]{1,0:T(8,128)S(1)}, f32[8,128]{1,0:T(8,128)S(1)}, u32[]{:S(2)}, u32[]{:S(2)}) collective-permute-start(f32[8,128]{1,0:T(8,128)S(1)} %plus.3.refs_0_.refs_2_), channel_id=1, source_target_pairs={{0,1},{1,2},{2,3},{3,0},{4,5},{5,6},{6,7},{7,4},{8,9},{9,10},{10,1... | collective-permute-start | bytes 12296 | tf_op jit(solution)/shard_map/ppermute | solution.py:545
  60.6 2.7 %collective-permute-start.16 = (f32[8,128]{1,0:T(8,128)S(1)}, f32[8,128]{1,0:T(8,128)S(1)}, u32[]{:S(2)}, u32[]{:S(2)}) collective-permute-start(f32[8,128]{1,0:T(8,128)S(1)} %plus.3.refs_0_.refs_2_), channel_id=1, source_target_pairs={{0,2},{1,3},{2,0},{3,1},{4,6},{5,7},{6,4},{7,5},{8,10},{9,11},{10,... | collective-permute-start | bytes 12296 | tf_op jit(solution)/shard_map/ppermute | solution.py:545
  63.2 1.5 %collective-permute-start.17 = (f32[8,128]{1,0:T(8,128)S(1)}, f32[8,128]{1,0:T(8,128)S(1)}, u32[]{:S(2)}, u32[]{:S(2)}) collective-permute-start(f32[8,128]{1,0:T(8,128)S(1)} %plus.3.refs_0_.refs_2_), channel_id=1, source_target_pairs={{0,3},{1,0},{2,1},{3,2},{4,7},{5,4},{6,5},{7,6},{8,11},{9,8},{10,9... | collective-permute-start | bytes 12296 | tf_op jit(solution)/shard_map/ppermute | solution.py:545
  64.7 1.3 %all-to-all-done.pieces.refs_6_ = bf16[16,2,32,512]{3,2,1,0:T(8,128)(2,1)S(1)} async-done(((bf16[16,2,32,512]{3,2,1,0:T(8,128)(2,1)}), bf16[16,2,32,512]{3,2,1,0:T(8,128)(2,1)S(1)}, u32[]{:S(2)}, u32[]{:S(2)}) %all-to-all-start) | async-done | bytes 1048608 | tf_op jit(solution)/shard_map/all_to_all | solution.py:541
  66.0 3.2 %rotate.1 = (f32[2,512,512]{2,1,0:T(8,128)S(1)}, bf16[2,512,512]{2,1,0:T(8,128)(2,1)S(1)}, bf16[2,512,512]{2,1,0:T(8,128)(2,1)S(1)}, f32[2,512,512]{2,1,0:T(8,128)S(1)}, f32[2,512,512]{2,1,0:T(8,128)S(1)}) custom-call(bf16[16,2,32,512]{3,2,1,0:T(8,128)(2,1)S(1)} %all-to-all-done.pieces.refs_6_, bf16[2,512,512]{2,1,0:T(8,128)(2,1)} %get-tuple-element.77.lt_src, ...), custom_call_target="tpu_custom_call" | custom-call | tf_op jit(solution)/shard_map/rotate/pallas_call | solution.py:366
  69.2 3.2 %direction.1 = (bf16[16,2,32,512]{3,2,1,0:T(8,128)(2,1)S(1)}, f32[2,512,512]{2,1,0:T(8,128)}) custom-call(s32[1,16]{1,0:T(1,128)S(1)} %copy-done, s32[1]{0:T(128)} %bitcast.1.me.refs_1_, f32[8,128]{1,0:T(8,128)S(1)} %plus.3.refs_0_.refs_2_, f32[8,128]{1,0:T(8,128)S(1)} %collective-permute-done.15.refs_1_.refs_3_, ...), custom_call_target="tpu_custom_call" | custom-call | tf_op jit(solution)/shard_map/direction/pallas_call | solution.py:417
  72.4 18.3 %all_to_all.10 = bf16[16,2,32,512]{3,2,1,0:T(8,128)(2,1)S(1)} all-to-all(bf16[16,2,32,512]{3,2,1,0:T(8,128)(2,1)S(1)} %get-tuple-element.86), channel_id=1, replica_groups=mesh['dp'=8,'fsdp'=16] {'fsdp'}, dimensions={0} | all-to-all | bytes 2097152 | tf_op jit(solution)/shard_map/all_to_all | solution.py:548
  90.7 0.6 collect.1
  91.3 0.1 collective-permute-start.18
  91.4 2.4 %collective-permute-start.19 = (bf16[32,2048]{1,0:T(8,128)(2,1)S(1)}, bf16[32,2048]{1,0:T(8,128)(2,1)S(1)}, u32[]{:S(2)}, u32[]{:S(2)}) collective-permute-start(bf16[32,2048]{1,0:T(8,128)(2,1)S(1)} %get-tuple-element.90), channel_id=1, source_target_pairs={{0,8},{1,9},{2,10},{3,11},{4,12},{5,13},{6,14},{7,15},{8,0},{9,1},... | collective-permute-start | bytes 393224 | tf_op jit(solution)/shard_map/ppermute | solution.py:315
  93.8 1.2 %collective-permute-start.20 = (bf16[32,2048]{1,0:T(8,128)(2,1)S(1)}, bf16[32,2048]{1,0:T(8,128)(2,1)S(1)}, u32[]{:S(2)}, u32[]{:S(2)}) collective-permute-start(bf16[32,2048]{1,0:T(8,128)(2,1)S(1)} %get-tuple-element.91), channel_id=1, source_target_pairs={{0,12},{1,13},{2,14},{3,15},{4,0},{5,1},{6,2},{7,3},{8,4},{9,5},{1... | collective-permute-start | bytes 393224 | tf_op jit(solution)/shard_map/ppermute | solution.py:315
  95.0 5.6 %factors.1 = (f32[2,512,512]{2,1,0:T(8,128)}, f32[2,512,512]{2,1,0:T(8,128)}, f32[2,512,512]{2,1,0:T(8,128)}) custom-call(s32[1,16]{1,0:T(1,128)S(1)} %copy-done, s32[1]{0:T(128)} %bitcast.1.me.refs_1_, f32[8,128]{1,0:T(8,128)S(1)} %plus.3.refs_0_.refs_2_, f32[8,128]{1,0:T(8,128)S(1)} %collective-permute-done.15.refs_1_.refs_3_, ...), custom_call_target="tpu_custom_call" | custom-call | flops 1073741824 | bytes 13631488 | tf_op jit(solution)/shard_map/factors/pallas_call | solution.py:482
  100.6 1.4 %put.1 = bf16[4,32,2048]{2,1,0:T(8,128)(2,1)} custom-call(s32[1,17]{1,0:T(1,128)S(1)} %pad_add_fusion.table, bf16[32,2048]{1,0:T(8,128)(2,1)S(1)} %get-tuple-element.88.refs_0_, bf16[32,2048]{1,0:T(8,128)(2,1)S(1)} %collective-permute-done.18.refs_1_, bf16[32,2048]{1,0:T(8,128)(2,1)S(1)} %collective-permute-done.19.refs_2_, ...), custom_call_target="tpu_custom_call" | custom-call | tf_op jit(solution)/shard_map/put/pallas_call | solution.py:118
  (17 shorter events, 0.1 us)
Async XLA Ops:
  3.5 2.0 %collective-permute-start = (bf16[1,128,2048]{2,1,0:T(8,128)(2,1)S(1)}, bf16[1,128,2048]{2,1,0:T(8,128)(2,1)S(1)}, u32[]{:S(2)}, u32[]{:S(2)}) collective-permute-start(bf16[1,128,2048]{2,1,0:T(8,128)(2,1)S(1)} %get-tuple-element.52), channel_id=1, source_target_pairs={{0,16},{16,0},{32,48},{48,32},{64,80},{80,64},{96,112},{112,96},{1... | collective-permute-start | bytes 1572872 | tf_op jit(solution)/shard_map/ppermute | solution.py:292
  5.5 3.7 %collective-permute-start.1 = (bf16[3,128,2048]{2,1,0:T(8,128)(2,1)S(1)}, bf16[3,128,2048]{2,1,0:T(8,128)(2,1)S(1)}, u32[]{:S(2)}, u32[]{:S(2)}) collective-permute-start(bf16[3,128,2048]{2,1,0:T(8,128)(2,1)S(1)} %get-tuple-element.54), channel_id=1, source_target_pairs={{0,16},{16,0},{32,48},{48,32},{64,80},{80,64},{96,112},{112,96},{1... | collective-permute-start | bytes 4718600 | tf_op jit(solution)/shard_map/ppermute | solution.py:294
  6.3 9.6 %collective-permute-start.6 = (bf16[64,2048]{1,0:T(8,128)(2,1)S(1)}, bf16[64,2048]{1,0:T(8,128)(2,1)S(1)}, u32[]{:S(2)}, u32[]{:S(2)}) collective-permute-start(bf16[64,2048]{1,0:T(8,128)(2,1)S(1)} %get-tuple-element.63), channel_id=1, source_target_pairs={{0,96},{16,112},{32,0},{48,16},{64,32},{80,48},{96,64},{112,80},{1... | collective-permute-start | bytes 786440 | tf_op jit(solution)/shard_map/ppermute | solution.py:297
  9.2 11.0 %collective-permute-start.4 = (bf16[64,2048]{1,0:T(8,128)(2,1)S(1)}, bf16[64,2048]{1,0:T(8,128)(2,1)S(1)}, u32[]{:S(2)}, u32[]{:S(2)}) collective-permute-start(bf16[64,2048]{1,0:T(8,128)(2,1)S(1)} %get-tuple-element.61), channel_id=1, source_target_pairs={{0,32},{16,48},{32,64},{48,80},{64,96},{80,112},{96,0},{112,16},{1... | collective-permute-start | bytes 786440 | tf_op jit(solution)/shard_map/ppermute | solution.py:296
  10.1 16.8 %collective-permute-start.2 = (bf16[64,2048]{1,0:T(8,128)(2,1)S(1)}, bf16[64,2048]{1,0:T(8,128)(2,1)S(1)}, u32[]{:S(2)}, u32[]{:S(2)}) collective-permute-start(bf16[64,2048]{1,0:T(8,128)(2,1)S(1)} %get-tuple-element.56), channel_id=1, source_target_pairs={{0,32},{16,48},{32,64},{48,80},{64,96},{80,112},{96,0},{112,16},{1... | collective-permute-start | bytes 786440 | tf_op jit(solution)/shard_map/ppermute | solution.py:302
  11.4 15.5 %collective-permute-start.3 = (bf16[64,2048]{1,0:T(8,128)(2,1)S(1)}, bf16[64,2048]{1,0:T(8,128)(2,1)S(1)}, u32[]{:S(2)}, u32[]{:S(2)}) collective-permute-start(bf16[64,2048]{1,0:T(8,128)(2,1)S(1)} %get-tuple-element.57), channel_id=1, source_target_pairs={{0,96},{16,112},{32,0},{48,16},{64,32},{80,48},{96,64},{112,80},{1... | collective-permute-start | bytes 786440 | tf_op jit(solution)/shard_map/ppermute | solution.py:303
  16.5 11.1 %collective-permute-start.7 = (bf16[64,2048]{1,0:T(8,128)(2,1)S(1)}, bf16[64,2048]{1,0:T(8,128)(2,1)S(1)}, u32[]{:S(2)}, u32[]{:S(2)}) collective-permute-start(bf16[64,2048]{1,0:T(8,128)(2,1)S(1)} %relay.3), channel_id=1, source_target_pairs={{0,96},{16,112},{32,0},{48,16},{64,32},{80,48},{96,64},{112,80},{1... | collective-permute-start | bytes 786440 | tf_op jit(solution)/shard_map/ppermute | solution.py:305
  20.8 9.1 %collective-permute-start.5 = (bf16[64,2048]{1,0:T(8,128)(2,1)S(1)}, bf16[64,2048]{1,0:T(8,128)(2,1)S(1)}, u32[]{:S(2)}, u32[]{:S(2)}) collective-permute-start(bf16[64,2048]{1,0:T(8,128)(2,1)S(1)} %relay.2), channel_id=1, source_target_pairs={{0,32},{16,48},{32,64},{48,80},{64,96},{80,112},{96,0},{112,16},{1... | collective-permute-start | bytes 786440 | tf_op jit(solution)/shard_map/ppermute | solution.py:304
  27.0 9.8 %copy-start = (s32[1,16]{1,0:T(1,128)S(1)}, s32[1,16]{1,0:T(1,128)}, u32[]{:S(2)}) copy-start(s32[1,16]{1,0:T(1,128)} %refs_0_.1) | copy-start | bytes 196
  30.8 8.2 %collective-permute-start.10 = (bf16[32,2176]{1,0:T(8,128)(2,1)S(1)}, bf16[32,2176]{1,0:T(8,128)(2,1)S(1)}, u32[]{:S(2)}, u32[]{:S(2)}) collective-permute-start(bf16[32,2176]{1,0:T(8,128)(2,1)S(1)} %get-tuple-element.74), channel_id=1, source_target_pairs={{0,12},{1,13},{2,14},{3,15},{4,0},{5,1},{6,2},{7,3},{8,4},{9,5},{1... | collective-permute-start | bytes 417800 | tf_op jit(solution)/shard_map/ppermute | solution.py:315
  34.9 8.2 %collective-permute-start.8 = (bf16[32,2176]{1,0:T(8,128)(2,1)S(1)}, bf16[32,2176]{1,0:T(8,128)(2,1)S(1)}, u32[]{:S(2)}, u32[]{:S(2)}) collective-permute-start(bf16[32,2176]{1,0:T(8,128)(2,1)S(1)} %get-tuple-element.72), channel_id=1, source_target_pairs={{0,4},{1,5},{2,6},{3,7},{4,8},{5,9},{6,10},{7,11},{8,12},{9,13},{1... | collective-permute-start | bytes 417800 | tf_op jit(solution)/shard_map/ppermute | solution.py:315
  34.9 8.2 %collective-permute-start.9 = (bf16[32,2176]{1,0:T(8,128)(2,1)S(1)}, bf16[32,2176]{1,0:T(8,128)(2,1)S(1)}, u32[]{:S(2)}, u32[]{:S(2)}) collective-permute-start(bf16[32,2176]{1,0:T(8,128)(2,1)S(1)} %get-tuple-element.73), channel_id=1, source_target_pairs={{0,8},{1,9},{2,10},{3,11},{4,12},{5,13},{6,14},{7,15},{8,0},{9,1},... | collective-permute-start | bytes 417800 | tf_op jit(solution)/shard_map/ppermute | solution.py:315
  44.7 21.4 %all-to-all-start = ((bf16[16,2,32,512]{3,2,1,0:T(8,128)(2,1)}), bf16[16,2,32,512]{3,2,1,0:T(8,128)(2,1)S(1)}, u32[]{:S(2)}, u32[]{:S(2)}) async-start(bf16[16,2,32,512]{3,2,1,0:T(8,128)(2,1)} %bitcast.9), calls=%async_computation | async-start | bytes 2097152 | tf_op jit(solution)/shard_map/all_to_all | solution.py:541
  50.3 1.2 %collective-permute-start.11 = (f32[8,128]{1,0:T(8,128)S(1)}, f32[8,128]{1,0:T(8,128)S(1)}, u32[]{:S(2)}, u32[]{:S(2)}) collective-permute-start(f32[8,128]{1,0:T(8,128)S(1)} %get-tuple-element.75.refs_0_), channel_id=1, source_target_pairs={{0,16},{16,0},{32,48},{48,32},{64,80},{80,64},{96,112},{112,96},{1... | collective-permute-start | bytes 12296 | tf_op jit(solution)/shard_map/ppermute | solution.py:543
  52.1 4.9 %collective-permute-start.12 = (f32[8,128]{1,0:T(8,128)S(1)}, f32[8,128]{1,0:T(8,128)S(1)}, u32[]{:S(2)}, u32[]{:S(2)}) collective-permute-start(f32[8,128]{1,0:T(8,128)S(1)} %plus.2.refs_0_), channel_id=1, source_target_pairs={{0,32},{16,48},{32,64},{48,80},{64,96},{80,112},{96,0},{112,16},{1... | collective-permute-start | bytes 12296 | tf_op jit(solution)/shard_map/ppermute | solution.py:543
  52.2 5.2 %collective-permute-start.13 = (f32[8,128]{1,0:T(8,128)S(1)}, f32[8,128]{1,0:T(8,128)S(1)}, u32[]{:S(2)}, u32[]{:S(2)}) collective-permute-start(f32[8,128]{1,0:T(8,128)S(1)} %plus.2.refs_0_), channel_id=1, source_target_pairs={{0,64},{16,80},{32,96},{48,112},{64,0},{80,16},{96,32},{112,48},{1... | collective-permute-start | bytes 12296 | tf_op jit(solution)/shard_map/ppermute | solution.py:543
  54.5 3.6 %collective-permute-start.14 = (f32[8,128]{1,0:T(8,128)S(1)}, f32[8,128]{1,0:T(8,128)S(1)}, u32[]{:S(2)}, u32[]{:S(2)}) collective-permute-start(f32[8,128]{1,0:T(8,128)S(1)} %plus.2.refs_0_), channel_id=1, source_target_pairs={{0,96},{16,112},{32,0},{48,16},{64,32},{80,48},{96,64},{112,80},{1... | collective-permute-start | bytes 12296 | tf_op jit(solution)/shard_map/ppermute | solution.py:543
  58.6 10.6 %collective-permute-start.15 = (f32[8,128]{1,0:T(8,128)S(1)}, f32[8,128]{1,0:T(8,128)S(1)}, u32[]{:S(2)}, u32[]{:S(2)}) collective-permute-start(f32[8,128]{1,0:T(8,128)S(1)} %plus.3.refs_0_.refs_2_), channel_id=1, source_target_pairs={{0,1},{1,2},{2,3},{3,0},{4,5},{5,6},{6,7},{7,4},{8,9},{9,10},{10,1... | collective-permute-start | bytes 12296 | tf_op jit(solution)/shard_map/ppermute | solution.py:545
  60.6 8.7 %collective-permute-start.16 = (f32[8,128]{1,0:T(8,128)S(1)}, f32[8,128]{1,0:T(8,128)S(1)}, u32[]{:S(2)}, u32[]{:S(2)}) collective-permute-start(f32[8,128]{1,0:T(8,128)S(1)} %plus.3.refs_0_.refs_2_), channel_id=1, source_target_pairs={{0,2},{1,3},{2,0},{3,1},{4,6},{5,7},{6,4},{7,5},{8,10},{9,11},{10,... | collective-permute-start | bytes 12296 | tf_op jit(solution)/shard_map/ppermute | solution.py:545
  63.2 6.0 %collective-permute-start.17 = (f32[8,128]{1,0:T(8,128)S(1)}, f32[8,128]{1,0:T(8,128)S(1)}, u32[]{:S(2)}, u32[]{:S(2)}) collective-permute-start(f32[8,128]{1,0:T(8,128)S(1)} %plus.3.refs_0_.refs_2_), channel_id=1, source_target_pairs={{0,3},{1,0},{2,1},{3,2},{4,7},{5,4},{6,5},{7,6},{8,11},{9,8},{10,9... | collective-permute-start | bytes 12296 | tf_op jit(solution)/shard_map/ppermute | solution.py:545
  91.3 9.3 %collective-permute-start.18 = (bf16[32,2048]{1,0:T(8,128)(2,1)S(1)}, bf16[32,2048]{1,0:T(8,128)(2,1)S(1)}, u32[]{:S(2)}, u32[]{:S(2)}) collective-permute-start(bf16[32,2048]{1,0:T(8,128)(2,1)S(1)} %get-tuple-element.89), channel_id=1, source_target_pairs={{0,4},{1,5},{2,6},{3,7},{4,8},{5,9},{6,10},{7,11},{8,12},{9,13},{1... | collective-permute-start | bytes 393224 | tf_op jit(solution)/shard_map/ppermute | solution.py:315
  91.4 9.2 %collective-permute-start.19 = (bf16[32,2048]{1,0:T(8,128)(2,1)S(1)}, bf16[32,2048]{1,0:T(8,128)(2,1)S(1)}, u32[]{:S(2)}, u32[]{:S(2)}) collective-permute-start(bf16[32,2048]{1,0:T(8,128)(2,1)S(1)} %get-tuple-element.90), channel_id=1, source_target_pairs={{0,8},{1,9},{2,10},{3,11},{4,12},{5,13},{6,14},{7,15},{8,0},{9,1},... | collective-permute-start | bytes 393224 | tf_op jit(solution)/shard_map/ppermute | solution.py:315
  93.8 6.8 %collective-permute-start.20 = (bf16[32,2048]{1,0:T(8,128)(2,1)S(1)}, bf16[32,2048]{1,0:T(8,128)(2,1)S(1)}, u32[]{:S(2)}, u32[]{:S(2)}) collective-permute-start(bf16[32,2048]{1,0:T(8,128)(2,1)S(1)} %get-tuple-element.91), channel_id=1, source_target_pairs={{0,12},{1,13},{2,14},{3,15},{4,0},{5,1},{6,2},{7,3},{8,4},{9,5},{1... | collective-permute-start | bytes 393224 | tf_op jit(solution)/shard_map/ppermute | solution.py:315

commit v5 on v4

--- a/solution.py
+++ b/solution.py
@@ -166,13 +166,6 @@
         dst[lax.rem(z + bands - j, bands)] = src[...]
 
 
-def plus_body(place, *refs):
-    total = refs[0][...]
-    for ref in refs[1:-1]:
-        total = total + ref[...]
-    refs[-1][...] = total
-
-
 def load(place, grads, width):
     rows, columns = grads.shape
     chips = columns // width // 2
@@ -342,24 +335,22 @@
     slots, n, _ = second.shape
 
     def body(pieces, lt_src, l_src, r_src, rot_src, old_src, *refs):
-        out, left, right, rot, old, lt, half, sems = refs
-        pairs = ((lt_src, lt), (r_src, right), (rot_src, rot), (old_src, old), (l_src, left))
+        out, right, left, rot, old, lt, half, sems = refs
+        pairs = [(src.at[s], dst.at[s]) for s in range(slots) for src, dst in ((lt_src, lt), (r_src, right))]
+        pairs += [(src.at[0], dst.at[0]) for src, dst in ((rot_src, rot), (old_src, old), (l_src, left))]
         copies = [
-            pltpu.make_async_copy(src.at[s], dst.at[s], sems.at[s, i])
-            for s in range(slots)
-            for i, (src, dst) in enumerate(pairs)
+            pltpu.make_async_copy(src, dst, sems.at[i]) for i, (src, dst) in enumerate(pairs)
         ]
         for c in copies:
             c.start()
         for s in range(slots):
-            group = copies[s * len(pairs) : (s + 1) * len(pairs)]
             block = assemble(pieces, s, bands)
-            group[0].wait()
+            copies[2 * s].wait()
             half[...] = mm(lt[s], block).astype(bf16)
-            group[1].wait()
+            copies[2 * s + 1].wait()
             out[s] = mm(half[...], right[s])
-            for c in group[2:]:
-                c.wait()
+        for c in copies[2 * slots :]:
+            c.wait()
 
     whole = pl.BlockSpec(memory_space=VMEM)
     far = pl.BlockSpec(memory_space=HBM)
@@ -370,40 +361,58 @@
         out_shape=[
             VMEM((slots, n, n), f32),
             VMEM((slots, n, n), bf16),
-            VMEM((slots, n, n), bf16),
-            VMEM((slots, n, n), f32),
-            VMEM((slots, n, n), f32),
+            VMEM((1, n, n), bf16),
+            VMEM((1, n, n), f32),
+            VMEM((1, n, n), f32),
         ],
         scratch_shapes=[
             pltpu.VMEM((slots, n, n), bf16),
             pltpu.VMEM((n, n), bf16),
-            pltpu.SemaphoreType.DMA((slots, 5)),
+            pltpu.SemaphoreType.DMA((2 * slots + 3,)),
         ],
         compiler_params=pltpu.CompilerParams(vmem_limit_bytes=12 << 20),
         name="rotate",
     )(pieces, *in_hbm(*prepared, second))
 
 
-def direction(table, me, squares, rotated, bands, senders, entries):
+def direction(table, me, squares, rotated, prepared, second, bands, senders, entries):
     slots, n, _ = rotated[0].shape
     rows = n // senders
     per = senders // bands
 
     def body(table, me, *refs):
-        squares, rest = refs[: len(refs) - 11], refs[len(refs) - 11 :]
-        product, left, right, rot, old, out, second_out, new, step, half, sems = rest
+        squares, rest = refs[: len(refs) - 18], refs[len(refs) - 18 :]
+        product, right, left, rot, old, l_src, rot_src, old_src, out, second_out = rest[:10]
+        left_more, rot_more, old_more, new, step, half, in_sems, sems = rest[10:]
+        pairs = ((rot_src, rot_more), (old_src, old_more), (l_src, left_more))
+        copies = [
+            [
+                pltpu.make_async_copy(src.at[s], dst.at[s - 1], in_sems.at[s, i])
+                for i, (src, dst) in enumerate(pairs)
+            ]
+            for s in range(1, slots)
+        ]
+        for group in copies:
+            for c in group:
+                c.start()
         scale = clip_of(squares, entries)
         for s in range(slots):
+            if s == 0:
+                states = rot.at[0], old.at[0], left.at[0]
+            else:
+                states = rot_more.at[s - 1], old_more.at[s - 1], left_more.at[s - 1]
+                for c in copies[s - 1]:
+                    c.wait()
             named = is_named(table, me[0] * slots + s)
             for r in tiles(n):
                 turned = product[s, r] * scale
-                before = old[s, r]
+                before = states[1][r]
                 value = 0.95 * before + 0.05 * turned * turned
                 new[s, r] = jnp.where(named, value, before)
-                ahead = rot[s, r] + 0.1 * turned
+                ahead = states[0][r] + 0.1 * turned
                 step[r] = (ahead * pl.reciprocal(jnp.sqrt(value) + 1e-08, approx=True)).astype(bf16)
             pltpu.make_async_copy(new.at[s], second_out.at[s], sems.at[s]).start()
-            half[...] = mm(left[s], step[...]).astype(bf16)
+            half[...] = mm(states[2][...], step[...]).astype(bf16)
             update = mm(half[...], right[s], ((1,), (1,))).astype(bf16)
             for y in range(per):
                 for z in range(bands):
@@ -414,23 +423,28 @@
 
     scalar = pl.BlockSpec(memory_space=SMEM)
     whole = pl.BlockSpec(memory_space=VMEM)
+    far = pl.BlockSpec(memory_space=HBM)
     return pl.pallas_call(
         body,
-        in_specs=[scalar] * 2 + [whole] * (len(squares) + 5),
-        out_specs=[whole, pl.BlockSpec(memory_space=HBM)],
+        in_specs=[scalar] * 2 + [whole] * (len(squares) + 5) + [far] * 3,
+        out_specs=[whole, far],
         out_shape=[
             jax.ShapeDtypeStruct((senders, slots, rows, n), bf16),
             HBM((slots, n, n), f32),
         ],
         scratch_shapes=[
+            pltpu.VMEM((slots - 1, n, n), bf16),
+            pltpu.VMEM((slots - 1, n, n), f32),
+            pltpu.VMEM((slots - 1, n, n), f32),
             pltpu.VMEM((slots, n, n), f32),
             pltpu.VMEM((n, n), bf16),
             pltpu.VMEM((n, n), bf16),
+            pltpu.SemaphoreType.DMA((slots, 3)),
             pltpu.SemaphoreType.DMA((slots,)),
         ],
         compiler_params=pltpu.CompilerParams(vmem_limit_bytes=16 << 20),
         name="direction",
-    )(table, me, *squares, *rotated)
+    )(table, me, *squares, *rotated, *in_hbm(prepared[1], prepared[3], second))
 
 
 def factors_body(bands, entries, table, me, *refs):
@@ -534,17 +548,20 @@
     cols = width // n
     entries = rows_dev * shards * replica_grads.shape[2]
     spread = exchange(sums, along_z)
-    one = jax.ShapeDtypeStruct((8, LANES), f32)
-    out = [jax.ShapeDtypeStruct((shards * slots, rows, n), bf16), one]
+    out = [
+        jax.ShapeDtypeStruct((shards * slots, rows, n), bf16),
+        jax.ShapeDtypeStruct((8, LANES), f32),
+    ]
     sent, square = local(dispatch_body, [table, *spread], out, "dispatch")
     sent = sent.reshape(shards, slots, rows, n)
     pieces = lax.all_to_all(sent, "fsdp", split_axis=0, concat_axis=0, tiled=True)
     for steps in (core, along_x):
-        arrived = [lax.ppermute(square, *step) for step in steps]
-        square = local(plus_body, [place, square, *arrived], one, "plus")
+        square = sum([lax.ppermute(square, *step) for step in steps], square)
     squares = [square] + [lax.ppermute(square, *step) for step in along_y]
     rotated = rotate(pieces, prepared, second_moment[0], bands)
-    update, second_new = direction(owners, me, squares, rotated, bands, shards, entries)
+    update, second_new = direction(
+        owners, me, squares, rotated, prepared, second_moment[0], bands, shards, entries
+    )
     back = lax.all_to_all(update, "fsdp", split_axis=0, concat_axis=0, tiled=True)
     back, pieces = lax.optimization_barrier((back, pieces))
     new = factors(

time: 102 us -> 102 us (level)
  waiting for transfers between devices: 18.1 us -> 16.5 us
  blocking collectives: 18.3 us -> 19.4 us
    ppermute x1, waiting for transfers between devices: 0.01 us -> 2.92 us  [sum_over_replicas(): left_far = lax.ppermute(to_right, 'dp', up)]
    ppermute x1, waiting for transfers between devices: 2.38 us -> 0.01 us  [sum_over_replicas(): right_far = lax.ppermute(to_left, 'dp', down)]
    ppermute x1, waiting for transfers between devices: 2.35 us -> 0.01 us  [sum_over_replicas(): left_sum = lax.ppermute(relay(place, keep_right, left_far), 'dp', up)]
    ppermute x6, waiting for transfers between devices: 6.28 us -> 4.42 us  [exchange(): got[j] = lax.ppermute(arrays[j], *steps[j - 1])]
    ppermute x1, starting transfers between devices: 0.01 us -> 1.66 us  [sum_over_replicas(): left_far = lax.ppermute(to_right, 'dp', up)]
    ppermute x4, waiting for transfers between devices: 3.86 us -> 5.38 us  [per_device(): square = sum([lax.ppermute(square, *step) for step in steps], square)]
    ppermute x3, starting transfers between devices: 6.05 us -> 4.77 us  [per_device(): squares = [square] + [lax.ppermute(square, *step) for step in along_y]]
    ppermute x1, starting transfers between devices: 2.92 us -> 1.66 us  [sum_over_replicas(): right_far = lax.ppermute(to_left, 'dp', down)]
  transfers between devices with their start and end apart: 22 -> 22, of which waited for: 10 -> 8; matrix products, arithmetic and copies ran while one was open for 0% -> 0% of each run, Pallas kernels for 19% -> 18%
where the time goes in v5:
time: 102 us; the launch traced here: 101 us
  starting transfers between devices  35.5 us (35%)
  Pallas kernels  29 us (28%)
  blocking collectives  19.4 us (19%)
  waiting for transfers between devices  16.5 us (16%)
    all_to_all x1, blocking collectives, per_device(): lax.all_to_all(update, 'fsdp', split_axis=0, concat_axis=0, tiled=True)  19.4 us
    ppermute x6, starting transfers between devices, exchange(): got[j] = lax.ppermute(arrays[j], *steps[j - 1])  10.3 us
    pallas_call x9, Pallas kernels, local(): pl.pallas_call(body, in_specs=[pl.BlockSpec(memory_space=SMEM)] + [pl.Blo...  7.66 us
    all_to_all x1, starting transfers between devices, per_device(): lax.all_to_all(sent, 'fsdp', split_axis=0, concat_axis=0, tiled=True)  6.25 us
    pallas_call x1, Pallas kernels, prepare(): pl.pallas_call(prepare_body, in_specs=[far] * 3, out_specs=[far] * 4, out...  6.01 us
    pallas_call x1, Pallas kernels, factors(): pl.pallas_call(body, in_specs=[scalar] * 2 + [whole] * (len(squares) + 1)...  5.58 us
    ppermute x4, waiting for transfers between devices, per_device(): square = sum([lax.ppermute(square, *step) for step in steps], square)  5.38 us
    ppermute x3, starting transfers between devices, per_device(): squares = [square] + [lax.ppermute(square, *step) for step in along_y]  4.77 us
  transfers between devices with their start and end apart: 22, of which 8 were waited for; matrix products, arithmetic and copies ran while one was open for 0% of the time, Pallas kernels for 18%

profile of v5, /device:TPU:0, one launch (start us, length us, event | category | flops | bytes accessed | tf_op | source)
XLA Modules:
  0.0 101.4 jit_solution(14696010813317120537)
XLA Ops:
  0.7 0.1 pad_add_fusion.1.place
  0.7 2.8 %load.1 = (bf16[1,128,2048]{2,1,0:T(8,128)(2,1)S(1)}, bf16[3,128,2048]{2,1,0:T(8,128)(2,1)S(1)}, bf16[1,128,2048]{2,1,0:T(8,128)(2,1)S(1)}, bf16[3,128,2048]{2,1,0:T(8,128)(2,1)S(1)}) custom-call(s32[3]{0:T(128)S(1)} %pad_add_fusion.1.place, bf16[128,16384]{1,0:T(8,128)(2,1)} %bitcast.22), custom_call_target="tpu_custom_call" | custom-call | tf_op jit(solution)/shard_map/load/pallas_call | solution.py:190
  3.5 0.1 collective-permute-start
  3.6 1.9 %collective-permute-done.far = bf16[1,128,2048]{2,1,0:T(8,128)(2,1)S(1)} collective-permute-done((bf16[1,128,2048]{2,1,0:T(8,128)(2,1)S(1)}, bf16[1,128,2048]{2,1,0:T(8,128)(2,1)S(1)}, u32[]{:S(2)}, u32[]{:S(2)}) %collective-permute-start) | collective-permute-done | bytes 524320 | tf_op jit(solution)/shard_map/ppermute | solution.py:285
  5.5 0.1 collective-permute-start.1
  5.7 0.7 pair_far.1
  6.3 1.7 %collective-permute-start.4 = (bf16[64,2048]{1,0:T(8,128)(2,1)S(1)}, bf16[64,2048]{1,0:T(8,128)(2,1)S(1)}, u32[]{:S(2)}, u32[]{:S(2)}) collective-permute-start(bf16[64,2048]{1,0:T(8,128)(2,1)S(1)} %get-tuple-element.61), channel_id=1, source_target_pairs={{0,32},{16,48},{32,64},{48,80},{64,96},{80,112},{96,0},{112,16},{1... | collective-permute-start | bytes 786440 | tf_op jit(solution)/shard_map/ppermute | solution.py:289
  8.0 1.7 %collective-permute-start.6 = (bf16[64,2048]{1,0:T(8,128)(2,1)S(1)}, bf16[64,2048]{1,0:T(8,128)(2,1)S(1)}, u32[]{:S(2)}, u32[]{:S(2)}) collective-permute-start(bf16[64,2048]{1,0:T(8,128)(2,1)S(1)} %get-tuple-element.63), channel_id=1, source_target_pairs={{0,96},{16,112},{32,0},{48,16},{64,32},{80,48},{96,64},{112,80},{1... | collective-permute-start | bytes 786440 | tf_op jit(solution)/shard_map/ppermute | solution.py:290
  9.6 0.9 pair_near.1
  10.5 0.9 collective-permute-start.2
  11.4 2.4 %collective-permute-start.3 = (bf16[64,2048]{1,0:T(8,128)(2,1)S(1)}, bf16[64,2048]{1,0:T(8,128)(2,1)S(1)}, u32[]{:S(2)}, u32[]{:S(2)}) collective-permute-start(bf16[64,2048]{1,0:T(8,128)(2,1)S(1)} %get-tuple-element.57), channel_id=1, source_target_pairs={{0,96},{16,112},{32,0},{48,16},{64,32},{80,48},{96,64},{112,80},{1... | collective-permute-start | bytes 786440 | tf_op jit(solution)/shard_map/ppermute | solution.py:296
  13.8 2.9 %collective-permute-done.4.arrived = bf16[64,2048]{1,0:T(8,128)(2,1)S(1)} collective-permute-done((bf16[64,2048]{1,0:T(8,128)(2,1)S(1)}, bf16[64,2048]{1,0:T(8,128)(2,1)S(1)}, u32[]{:S(2)}, u32[]{:S(2)}) %collective-permute-start.4) | collective-permute-done | bytes 262176 | tf_op jit(solution)/shard_map/ppermute | solution.py:289
  16.7 0.6 relay.2
  17.3 0.4 collective-permute-start.5
  17.8 0.6 relay.3
  18.4 2.9 %collective-permute-start.7 = (bf16[64,2048]{1,0:T(8,128)(2,1)S(1)}, bf16[64,2048]{1,0:T(8,128)(2,1)S(1)}, u32[]{:S(2)}, u32[]{:S(2)}) collective-permute-start(bf16[64,2048]{1,0:T(8,128)(2,1)S(1)} %relay.3), channel_id=1, source_target_pairs={{0,96},{16,112},{32,0},{48,16},{64,32},{80,48},{96,64},{112,80},{1... | collective-permute-start | bytes 786440 | tf_op jit(solution)/shard_map/ppermute | solution.py:298
  21.3 6.0 %prepare.1 = (bf16[2,512,512]{2,1,0:T(8,128)(2,1)}, bf16[2,512,512]{2,1,0:T(8,128)(2,1)}, bf16[2,512,512]{2,1,0:T(8,128)(2,1)}, f32[2,512,512]{2,1,0:T(8,128)}) custom-call(f32[2,512,512]{2,1,0:T(8,128)} %bitcast.28, f32[2,512,512]{2,1,0:T(8,128)} %bitcast.29, f32[2,512,512]{2,1,0:T(8,128)} %bitcast.23), custom_call_target="tpu_custom_call" | custom-call | flops 2147483648 | bytes 11534336 | tf_op jit(solution)/shard_map/prepare/pallas_call | solution.py:93
  27.3 0.0 copy-start
  27.4 0.6 direct.1.own
  28.0 0.8 finish.1
  28.8 2.1 %collective-permute-start.8 = (bf16[32,2176]{1,0:T(8,128)(2,1)S(1)}, bf16[32,2176]{1,0:T(8,128)(2,1)S(1)}, u32[]{:S(2)}, u32[]{:S(2)}) collective-permute-start(bf16[32,2176]{1,0:T(8,128)(2,1)S(1)} %get-tuple-element.72), channel_id=1, source_target_pairs={{0,4},{1,5},{2,6},{3,7},{4,8},{5,9},{6,10},{7,11},{8,12},{9,13},{1... | collective-permute-start | bytes 417800 | tf_op jit(solution)/shard_map/ppermute | solution.py:308
  30.9 3.6 %collective-permute-start.9 = (bf16[32,2176]{1,0:T(8,128)(2,1)S(1)}, bf16[32,2176]{1,0:T(8,128)(2,1)S(1)}, u32[]{:S(2)}, u32[]{:S(2)}) collective-permute-start(bf16[32,2176]{1,0:T(8,128)(2,1)S(1)} %get-tuple-element.73), channel_id=1, source_target_pairs={{0,8},{1,9},{2,10},{3,11},{4,12},{5,13},{6,14},{7,15},{8,0},{9,1},... | collective-permute-start | bytes 417800 | tf_op jit(solution)/shard_map/ppermute | solution.py:308
  34.5 1.0 collective-permute-start.10
  35.5 0.1 pad_add_fusion.table
  35.6 1.6 %collective-permute-done.8.refs_1_ = bf16[32,2176]{1,0:T(8,128)(2,1)S(1)} collective-permute-done((bf16[32,2176]{1,0:T(8,128)(2,1)S(1)}, bf16[32,2176]{1,0:T(8,128)(2,1)S(1)}, u32[]{:S(2)}, u32[]{:S(2)}) %collective-permute-start.8) | collective-permute-done | bytes 139296 | tf_op jit(solution)/shard_map/ppermute | solution.py:308
  37.2 2.8 %collective-permute-done.9.refs_2_ = bf16[32,2176]{1,0:T(8,128)(2,1)S(1)} collective-permute-done((bf16[32,2176]{1,0:T(8,128)(2,1)S(1)}, bf16[32,2176]{1,0:T(8,128)(2,1)S(1)}, u32[]{:S(2)}, u32[]{:S(2)}) %collective-permute-start.9) | collective-permute-done | bytes 139296 | tf_op jit(solution)/shard_map/ppermute | solution.py:308
  40.0 1.6 %dispatch.1 = (bf16[32,32,512]{2,1,0:T(8,128)(2,1)}, f32[8,128]{1,0:T(8,128)S(1)}) custom-call(s32[1,17]{1,0:T(1,128)S(1)} %pad_add_fusion.table, bf16[32,2176]{1,0:T(8,128)(2,1)S(1)} %get-tuple-element.71.refs_0_, bf16[32,2176]{1,0:T(8,128)(2,1)S(1)} %collective-permute-done.8.refs_1_, bf16[32,2176]{1,0:T(8,128)(2,1)S(1)} %collective-permute-done.9.refs_2_, ...), custom_call_target="tpu_custom_call" | custom-call | tf_op jit(solution)/shard_map/dispatch/pallas_call | solution.py:118
  41.5 6.2 %all-to-all-start = ((bf16[16,2,32,512]{3,2,1,0:T(8,128)(2,1)}), bf16[16,2,32,512]{3,2,1,0:T(8,128)(2,1)S(1)}, u32[]{:S(2)}, u32[]{:S(2)}) async-start(bf16[16,2,32,512]{3,2,1,0:T(8,128)(2,1)} %bitcast.9), calls=%async_computation | async-start | bytes 2097152 | tf_op jit(solution)/shard_map/all_to_all | solution.py:557
  47.8 0.1 collective-permute-start.11
  47.9 1.2 %collective-permute-done.11 = f32[8,128]{1,0:T(8,128)S(1)} collective-permute-done((f32[8,128]{1,0:T(8,128)S(1)}, f32[8,128]{1,0:T(8,128)S(1)}, u32[]{:S(2)}, u32[]{:S(2)}) %collective-permute-start.11) | collective-permute-done | bytes 4128 | tf_op jit(solution)/shard_map/ppermute | solution.py:559
  49.0 2.3 %collective-permute-start.14 = (f32[8,128]{1,0:T(8,128)S(1)}, f32[8,128]{1,0:T(8,128)S(1)}, u32[]{:S(2)}, u32[]{:S(2)}) collective-permute-start(f32[8,128]{1,0:T(8,128)S(1)} %add.19), channel_id=1, source_target_pairs={{0,96},{16,112},{32,0},{48,16},{64,32},{80,48},{96,64},{112,80},{1... | collective-permute-start | bytes 12296 | tf_op jit(solution)/shard_map/ppermute | solution.py:559
  51.4 0.9 collective-permute-start.13
  52.3 0.6 collective-permute-start.12
  52.9 3.6 %collective-permute-done.13 = f32[8,128]{1,0:T(8,128)S(1)} collective-permute-done((f32[8,128]{1,0:T(8,128)S(1)}, f32[8,128]{1,0:T(8,128)S(1)}, u32[]{:S(2)}, u32[]{:S(2)}) %collective-permute-start.13) | collective-permute-done | bytes 4128 | tf_op jit(solution)/shard_map/ppermute | solution.py:559
  56.5 0.6 collective-permute-done.12
  57.1 3.1 %collective-permute-start.17 = (f32[8,128]{1,0:T(8,128)S(1)}, f32[8,128]{1,0:T(8,128)S(1)}, u32[]{:S(2)}, u32[]{:S(2)}) collective-permute-start(f32[8,128]{1,0:T(8,128)S(1)} %add_add_fusion.refs_0_.refs_2_), channel_id=1, source_target_pairs={{0,3},{1,0},{2,1},{3,2},{4,7},{5,4},{6,5},{7,6},{8,11},{9,8},{10,9... | collective-permute-start | bytes 12296 | tf_op jit(solution)/shard_map/ppermute | solution.py:560
  60.2 0.9 collective-permute-start.16
  61.0 0.9 collective-permute-start.15
  61.9 1.9 %all-to-all-done.pieces.refs_6_ = bf16[16,2,32,512]{3,2,1,0:T(8,128)(2,1)S(1)} async-done(((bf16[16,2,32,512]{3,2,1,0:T(8,128)(2,1)}), bf16[16,2,32,512]{3,2,1,0:T(8,128)(2,1)S(1)}, u32[]{:S(2)}, u32[]{:S(2)}) %all-to-all-start) | async-done | bytes 1048608 | tf_op jit(solution)/shard_map/all_to_all | solution.py:557
  63.8 2.9 %rotate.1 = (f32[2,512,512]{2,1,0:T(8,128)S(1)}, bf16[2,512,512]{2,1,0:T(8,128)(2,1)S(1)}, bf16[1,512,512]{2,1,0:T(8,128)(2,1)S(1)}, f32[1,512,512]{2,1,0:T(8,128)S(1)}, f32[1,512,512]{2,1,0:T(8,128)S(1)}) custom-call(bf16[16,2,32,512]{3,2,1,0:T(8,128)(2,1)S(1)} %all-to-all-done.pieces.refs_6_, bf16[2,512,512]{2,1,0:T(8,128)(2,1)} %get-tuple-element.77.lt_src, ...), custom_call_target="tpu_custom_call" | custom-call | tf_op jit(solution)/shard_map/rotate/pallas_call | solution.py:357
  66.7 4.0 %direction.1 = (bf16[16,2,32,512]{3,2,1,0:T(8,128)(2,1)S(1)}, f32[2,512,512]{2,1,0:T(8,128)}) custom-call(s32[1,16]{1,0:T(1,128)S(1)} %copy-done, s32[1]{0:T(128)} %bitcast.1.me.refs_1_, f32[8,128]{1,0:T(8,128)S(1)} %add_add_fusion.refs_0_.refs_2_, f32[8,128]{1,0:T(8,128)S(1)} %collective-permute-done.15.refs_1_.refs_3_, ...), custom_call_target="tpu_custom_call" | custom-call | tf_op jit(solution)/shard_map/direction/pallas_call | solution.py:427
  70.7 19.4 %all_to_all.10 = bf16[16,2,32,512]{3,2,1,0:T(8,128)(2,1)S(1)} all-to-all(bf16[16,2,32,512]{3,2,1,0:T(8,128)(2,1)S(1)} %get-tuple-element.86), channel_id=1, replica_groups=mesh['dp'=8,'fsdp'=16] {'fsdp'}, dimensions={0} | all-to-all | bytes 2097152 | tf_op jit(solution)/shard_map/all_to_all | solution.py:565
  90.1 0.6 collect.1
  90.7 0.1 collective-permute-start.18
  90.8 2.4 %collective-permute-start.19 = (bf16[32,2048]{1,0:T(8,128)(2,1)S(1)}, bf16[32,2048]{1,0:T(8,128)(2,1)S(1)}, u32[]{:S(2)}, u32[]{:S(2)}) collective-permute-start(bf16[32,2048]{1,0:T(8,128)(2,1)S(1)} %get-tuple-element.90), channel_id=1, source_target_pairs={{0,8},{1,9},{2,10},{3,11},{4,12},{5,13},{6,14},{7,15},{8,0},{9,1},... | collective-permute-start | bytes 393224 | tf_op jit(solution)/shard_map/ppermute | solution.py:308
  93.2 1.2 %collective-permute-start.20 = (bf16[32,2048]{1,0:T(8,128)(2,1)S(1)}, bf16[32,2048]{1,0:T(8,128)(2,1)S(1)}, u32[]{:S(2)}, u32[]{:S(2)}) collective-permute-start(bf16[32,2048]{1,0:T(8,128)(2,1)S(1)} %get-tuple-element.91), channel_id=1, source_target_pairs={{0,12},{1,13},{2,14},{3,15},{4,0},{5,1},{6,2},{7,3},{8,4},{9,5},{1... | collective-permute-start | bytes 393224 | tf_op jit(solution)/shard_map/ppermute | solution.py:308
  94.4 5.6 %factors.1 = (f32[2,512,512]{2,1,0:T(8,128)}, f32[2,512,512]{2,1,0:T(8,128)}, f32[2,512,512]{2,1,0:T(8,128)}) custom-call(s32[1,16]{1,0:T(1,128)S(1)} %copy-done, s32[1]{0:T(128)} %bitcast.1.me.refs_1_, f32[8,128]{1,0:T(8,128)S(1)} %add_add_fusion.refs_0_.refs_2_, f32[8,128]{1,0:T(8,128)S(1)} %collective-permute-done.15.refs_1_.refs_3_, ...), custom_call_target="tpu_custom_call" | custom-call | flops 1073741824 | bytes 13631488 | tf_op jit(solution)/shard_map/factors/pallas_call | solution.py:496
  100.0 1.4 %put.1 = bf16[4,32,2048]{2,1,0:T(8,128)(2,1)} custom-call(s32[1,17]{1,0:T(1,128)S(1)} %pad_add_fusion.table, bf16[32,2048]{1,0:T(8,128)(2,1)S(1)} %get-tuple-element.88.refs_0_, bf16[32,2048]{1,0:T(8,128)(2,1)S(1)} %collective-permute-done.18.refs_1_, bf16[32,2048]{1,0:T(8,128)(2,1)S(1)} %collective-permute-done.19.refs_2_, ...), custom_call_target="tpu_custom_call" | custom-call | tf_op jit(solution)/shard_map/put/pallas_call | solution.py:118
  (17 shorter events, 0.0 us)
Async XLA Ops:
  3.5 2.0 %collective-permute-start = (bf16[1,128,2048]{2,1,0:T(8,128)(2,1)S(1)}, bf16[1,128,2048]{2,1,0:T(8,128)(2,1)S(1)}, u32[]{:S(2)}, u32[]{:S(2)}) collective-permute-start(bf16[1,128,2048]{2,1,0:T(8,128)(2,1)S(1)} %get-tuple-element.52), channel_id=1, source_target_pairs={{0,16},{16,0},{32,48},{48,32},{64,80},{80,64},{96,112},{112,96},{1... | collective-permute-start | bytes 1572872 | tf_op jit(solution)/shard_map/ppermute | solution.py:285
  5.5 4.1 %collective-permute-start.1 = (bf16[3,128,2048]{2,1,0:T(8,128)(2,1)S(1)}, bf16[3,128,2048]{2,1,0:T(8,128)(2,1)S(1)}, u32[]{:S(2)}, u32[]{:S(2)}) collective-permute-start(bf16[3,128,2048]{2,1,0:T(8,128)(2,1)S(1)} %get-tuple-element.54), channel_id=1, source_target_pairs={{0,16},{16,0},{32,48},{48,32},{64,80},{80,64},{96,112},{112,96},{1... | collective-permute-start | bytes 4718600 | tf_op jit(solution)/shard_map/ppermute | solution.py:287
  6.3 10.4 %collective-permute-start.4 = (bf16[64,2048]{1,0:T(8,128)(2,1)S(1)}, bf16[64,2048]{1,0:T(8,128)(2,1)S(1)}, u32[]{:S(2)}, u32[]{:S(2)}) collective-permute-start(bf16[64,2048]{1,0:T(8,128)(2,1)S(1)} %get-tuple-element.61), channel_id=1, source_target_pairs={{0,32},{16,48},{32,64},{48,80},{64,96},{80,112},{96,0},{112,16},{1... | collective-permute-start | bytes 786440 | tf_op jit(solution)/shard_map/ppermute | solution.py:289
  8.0 9.8 %collective-permute-start.6 = (bf16[64,2048]{1,0:T(8,128)(2,1)S(1)}, bf16[64,2048]{1,0:T(8,128)(2,1)S(1)}, u32[]{:S(2)}, u32[]{:S(2)}) collective-permute-start(bf16[64,2048]{1,0:T(8,128)(2,1)S(1)} %get-tuple-element.63), channel_id=1, source_target_pairs={{0,96},{16,112},{32,0},{48,16},{64,32},{80,48},{96,64},{112,80},{1... | collective-permute-start | bytes 786440 | tf_op jit(solution)/shard_map/ppermute | solution.py:290
  10.5 16.8 %collective-permute-start.2 = (bf16[64,2048]{1,0:T(8,128)(2,1)S(1)}, bf16[64,2048]{1,0:T(8,128)(2,1)S(1)}, u32[]{:S(2)}, u32[]{:S(2)}) collective-permute-start(bf16[64,2048]{1,0:T(8,128)(2,1)S(1)} %get-tuple-element.56), channel_id=1, source_target_pairs={{0,32},{16,48},{32,64},{48,80},{64,96},{80,112},{96,0},{112,16},{1... | collective-permute-start | bytes 786440 | tf_op jit(solution)/shard_map/ppermute | solution.py:295
  11.4 15.9 %collective-permute-start.3 = (bf16[64,2048]{1,0:T(8,128)(2,1)S(1)}, bf16[64,2048]{1,0:T(8,128)(2,1)S(1)}, u32[]{:S(2)}, u32[]{:S(2)}) collective-permute-start(bf16[64,2048]{1,0:T(8,128)(2,1)S(1)} %get-tuple-element.57), channel_id=1, source_target_pairs={{0,96},{16,112},{32,0},{48,16},{64,32},{80,48},{96,64},{112,80},{1... | collective-permute-start | bytes 786440 | tf_op jit(solution)/shard_map/ppermute | solution.py:296
  17.3 10.7 %collective-permute-start.5 = (bf16[64,2048]{1,0:T(8,128)(2,1)S(1)}, bf16[64,2048]{1,0:T(8,128)(2,1)S(1)}, u32[]{:S(2)}, u32[]{:S(2)}) collective-permute-start(bf16[64,2048]{1,0:T(8,128)(2,1)S(1)} %relay.2), channel_id=1, source_target_pairs={{0,32},{16,48},{32,64},{48,80},{64,96},{80,112},{96,0},{112,16},{1... | collective-permute-start | bytes 786440 | tf_op jit(solution)/shard_map/ppermute | solution.py:297
  18.4 9.6 %collective-permute-start.7 = (bf16[64,2048]{1,0:T(8,128)(2,1)S(1)}, bf16[64,2048]{1,0:T(8,128)(2,1)S(1)}, u32[]{:S(2)}, u32[]{:S(2)}) collective-permute-start(bf16[64,2048]{1,0:T(8,128)(2,1)S(1)} %relay.3), channel_id=1, source_target_pairs={{0,96},{16,112},{32,0},{48,16},{64,32},{80,48},{96,64},{112,80},{1... | collective-permute-start | bytes 786440 | tf_op jit(solution)/shard_map/ppermute | solution.py:298
  27.3 8.2 %copy-start = (s32[1,16]{1,0:T(1,128)S(1)}, s32[1,16]{1,0:T(1,128)}, u32[]{:S(2)}) copy-start(s32[1,16]{1,0:T(1,128)} %refs_0_.1) | copy-start | bytes 196
  28.8 8.3 %collective-permute-start.8 = (bf16[32,2176]{1,0:T(8,128)(2,1)S(1)}, bf16[32,2176]{1,0:T(8,128)(2,1)S(1)}, u32[]{:S(2)}, u32[]{:S(2)}) collective-permute-start(bf16[32,2176]{1,0:T(8,128)(2,1)S(1)} %get-tuple-element.72), channel_id=1, source_target_pairs={{0,4},{1,5},{2,6},{3,7},{4,8},{5,9},{6,10},{7,11},{8,12},{9,13},{1... | collective-permute-start | bytes 417800 | tf_op jit(solution)/shard_map/ppermute | solution.py:308
  30.9 9.1 %collective-permute-start.9 = (bf16[32,2176]{1,0:T(8,128)(2,1)S(1)}, bf16[32,2176]{1,0:T(8,128)(2,1)S(1)}, u32[]{:S(2)}, u32[]{:S(2)}) collective-permute-start(bf16[32,2176]{1,0:T(8,128)(2,1)S(1)} %get-tuple-element.73), channel_id=1, source_target_pairs={{0,8},{1,9},{2,10},{3,11},{4,12},{5,13},{6,14},{7,15},{8,0},{9,1},... | collective-permute-start | bytes 417800 | tf_op jit(solution)/shard_map/ppermute | solution.py:308
  34.5 5.5 %collective-permute-start.10 = (bf16[32,2176]{1,0:T(8,128)(2,1)S(1)}, bf16[32,2176]{1,0:T(8,128)(2,1)S(1)}, u32[]{:S(2)}, u32[]{:S(2)}) collective-permute-start(bf16[32,2176]{1,0:T(8,128)(2,1)S(1)} %get-tuple-element.74), channel_id=1, source_target_pairs={{0,12},{1,13},{2,14},{3,15},{4,0},{5,1},{6,2},{7,3},{8,4},{9,5},{1... | collective-permute-start | bytes 417800 | tf_op jit(solution)/shard_map/ppermute | solution.py:308
  41.5 22.2 %all-to-all-start = ((bf16[16,2,32,512]{3,2,1,0:T(8,128)(2,1)}), bf16[16,2,32,512]{3,2,1,0:T(8,128)(2,1)S(1)}, u32[]{:S(2)}, u32[]{:S(2)}) async-start(bf16[16,2,32,512]{3,2,1,0:T(8,128)(2,1)} %bitcast.9), calls=%async_computation | async-start | bytes 2097152 | tf_op jit(solution)/shard_map/all_to_all | solution.py:557
  47.8 1.2 %collective-permute-start.11 = (f32[8,128]{1,0:T(8,128)S(1)}, f32[8,128]{1,0:T(8,128)S(1)}, u32[]{:S(2)}, u32[]{:S(2)}) collective-permute-start(f32[8,128]{1,0:T(8,128)S(1)} %get-tuple-element.75), channel_id=1, source_target_pairs={{0,16},{16,0},{32,48},{48,32},{64,80},{80,64},{96,112},{112,96},{1... | collective-permute-start | bytes 12296 | tf_op jit(solution)/shard_map/ppermute | solution.py:559
  49.0 3.8 %collective-permute-start.14 = (f32[8,128]{1,0:T(8,128)S(1)}, f32[8,128]{1,0:T(8,128)S(1)}, u32[]{:S(2)}, u32[]{:S(2)}) collective-permute-start(f32[8,128]{1,0:T(8,128)S(1)} %add.19), channel_id=1, source_target_pairs={{0,96},{16,112},{32,0},{48,16},{64,32},{80,48},{96,64},{112,80},{1... | collective-permute-start | bytes 12296 | tf_op jit(solution)/shard_map/ppermute | solution.py:559
  51.4 5.1 %collective-permute-start.13 = (f32[8,128]{1,0:T(8,128)S(1)}, f32[8,128]{1,0:T(8,128)S(1)}, u32[]{:S(2)}, u32[]{:S(2)}) collective-permute-start(f32[8,128]{1,0:T(8,128)S(1)} %add.19), channel_id=1, source_target_pairs={{0,64},{16,80},{32,96},{48,112},{64,0},{80,16},{96,32},{112,48},{1... | collective-permute-start | bytes 12296 | tf_op jit(solution)/shard_map/ppermute | solution.py:559
  52.3 4.8 %collective-permute-start.12 = (f32[8,128]{1,0:T(8,128)S(1)}, f32[8,128]{1,0:T(8,128)S(1)}, u32[]{:S(2)}, u32[]{:S(2)}) collective-permute-start(f32[8,128]{1,0:T(8,128)S(1)} %add.19), channel_id=1, source_target_pairs={{0,32},{16,48},{32,64},{48,80},{64,96},{80,112},{96,0},{112,16},{1... | collective-permute-start | bytes 12296 | tf_op jit(solution)/shard_map/ppermute | solution.py:559
  57.1 9.6 %collective-permute-start.17 = (f32[8,128]{1,0:T(8,128)S(1)}, f32[8,128]{1,0:T(8,128)S(1)}, u32[]{:S(2)}, u32[]{:S(2)}) collective-permute-start(f32[8,128]{1,0:T(8,128)S(1)} %add_add_fusion.refs_0_.refs_2_), channel_id=1, source_target_pairs={{0,3},{1,0},{2,1},{3,2},{4,7},{5,4},{6,5},{7,6},{8,11},{9,8},{10,9... | collective-permute-start | bytes 12296 | tf_op jit(solution)/shard_map/ppermute | solution.py:560
  60.2 6.5 %collective-permute-start.16 = (f32[8,128]{1,0:T(8,128)S(1)}, f32[8,128]{1,0:T(8,128)S(1)}, u32[]{:S(2)}, u32[]{:S(2)}) collective-permute-start(f32[8,128]{1,0:T(8,128)S(1)} %add_add_fusion.refs_0_.refs_2_), channel_id=1, source_target_pairs={{0,2},{1,3},{2,0},{3,1},{4,6},{5,7},{6,4},{7,5},{8,10},{9,11},{10,... | collective-permute-start | bytes 12296 | tf_op jit(solution)/shard_map/ppermute | solution.py:560
  61.0 5.7 %collective-permute-start.15 = (f32[8,128]{1,0:T(8,128)S(1)}, f32[8,128]{1,0:T(8,128)S(1)}, u32[]{:S(2)}, u32[]{:S(2)}) collective-permute-start(f32[8,128]{1,0:T(8,128)S(1)} %add_add_fusion.refs_0_.refs_2_), channel_id=1, source_target_pairs={{0,1},{1,2},{2,3},{3,0},{4,5},{5,6},{6,7},{7,4},{8,9},{9,10},{10,1... | collective-permute-start | bytes 12296 | tf_op jit(solution)/shard_map/ppermute | solution.py:560
  90.7 9.3 %collective-permute-start.18 = (bf16[32,2048]{1,0:T(8,128)(2,1)S(1)}, bf16[32,2048]{1,0:T(8,128)(2,1)S(1)}, u32[]{:S(2)}, u32[]{:S(2)}) collective-permute-start(bf16[32,2048]{1,0:T(8,128)(2,1)S(1)} %get-tuple-element.89), channel_id=1, source_target_pairs={{0,4},{1,5},{2,6},{3,7},{4,8},{5,9},{6,10},{7,11},{8,12},{9,13},{1... | collective-permute-start | bytes 393224 | tf_op jit(solution)/shard_map/ppermute | solution.py:308
  90.8 9.2 %collective-permute-start.19 = (bf16[32,2048]{1,0:T(8,128)(2,1)S(1)}, bf16[32,2048]{1,0:T(8,128)(2,1)S(1)}, u32[]{:S(2)}, u32[]{:S(2)}) collective-permute-start(bf16[32,2048]{1,0:T(8,128)(2,1)S(1)} %get-tuple-element.90), channel_id=1, source_target_pairs={{0,8},{1,9},{2,10},{3,11},{4,12},{5,13},{6,14},{7,15},{8,0},{9,1},... | collective-permute-start | bytes 393224 | tf_op jit(solution)/shard_map/ppermute | solution.py:308
  93.2 6.8 %collective-permute-start.20 = (bf16[32,2048]{1,0:T(8,128)(2,1)S(1)}, bf16[32,2048]{1,0:T(8,128)(2,1)S(1)}, u32[]{:S(2)}, u32[]{:S(2)}) collective-permute-start(bf16[32,2048]{1,0:T(8,128)(2,1)S(1)} %get-tuple-element.91), channel_id=1, source_target_pairs={{0,12},{1,13},{2,14},{3,15},{4,0},{5,1},{6,2},{7,3},{8,4},{9,5},{1... | collective-permute-start | bytes 393224 | tf_op jit(solution)/shard_map/ppermute | solution.py:308

commit v6 on v4

--- a/solution.py
+++ b/solution.py
@@ -166,13 +166,6 @@
         dst[lax.rem(z + bands - j, bands)] = src[...]
 
 
-def plus_body(place, *refs):
-    total = refs[0][...]
-    for ref in refs[1:-1]:
-        total = total + ref[...]
-    refs[-1][...] = total
-
-
 def load(place, grads, width):
     rows, columns = grads.shape
     chips = columns // width // 2
@@ -534,14 +527,15 @@
     cols = width // n
     entries = rows_dev * shards * replica_grads.shape[2]
     spread = exchange(sums, along_z)
-    one = jax.ShapeDtypeStruct((8, LANES), f32)
-    out = [jax.ShapeDtypeStruct((shards * slots, rows, n), bf16), one]
+    out = [
+        jax.ShapeDtypeStruct((shards * slots, rows, n), bf16),
+        jax.ShapeDtypeStruct((8, LANES), f32),
+    ]
     sent, square = local(dispatch_body, [table, *spread], out, "dispatch")
     sent = sent.reshape(shards, slots, rows, n)
     pieces = lax.all_to_all(sent, "fsdp", split_axis=0, concat_axis=0, tiled=True)
     for steps in (core, along_x):
-        arrived = [lax.ppermute(square, *step) for step in steps]
-        square = local(plus_body, [place, square, *arrived], one, "plus")
+        square = sum([lax.ppermute(square, *step) for step in steps], square)
     squares = [square] + [lax.ppermute(square, *step) for step in along_y]
     rotated = rotate(pieces, prepared, second_moment[0], bands)
     update, second_new = direction(owners, me, squares, rotated, bands, shards, entries)

time: 102 us -> 102 us (level)
  Pallas kernels: 29.5 us -> 28.3 us
  waiting for transfers between devices: 18.1 us -> 19.3 us
    all_to_all x1, waiting for transfers between devices: 1.33 us -> 2.56 us  [per_device(): lax.all_to_all(sent, 'fsdp', split_axis=0, concat_axis=0, tiled=True)]
    pallas_call x11 -> x9, Pallas kernels: 8.75 us -> 7.67 us  [local(): pl.pallas_call(body, in_specs=[pl.BlockSpec(memory_space=SMEM)] + [pl.Blo...]
  transfers between devices with their start and end apart: 22 -> 22, of which waited for: 10 -> 10; matrix products, arithmetic and copies ran while one was open for 0% -> 0% of each run, Pallas kernels for 19% -> 18%
where the time goes in v6:
time: 102 us; the launch traced here: 101 us
  starting transfers between devices  34.9 us (34%)
  Pallas kernels  28.3 us (28%)
  waiting for transfers between devices  19.3 us (19%)
  blocking collectives  17.7 us (17%)
    all_to_all x1, blocking collectives, per_device(): lax.all_to_all(update, 'fsdp', split_axis=0, concat_axis=0, tiled=True)  17.7 us
    ppermute x6, starting transfers between devices, exchange(): got[j] = lax.ppermute(arrays[j], *steps[j - 1])  9.63 us
    pallas_call x9, Pallas kernels, local(): pl.pallas_call(body, in_specs=[pl.BlockSpec(memory_space=SMEM)] + [pl.Blo...  7.67 us
    ppermute x6, waiting for transfers between devices, exchange(): got[j] = lax.ppermute(arrays[j], *steps[j - 1])  6.28 us
    pallas_call x1, Pallas kernels, prepare(): pl.pallas_call(prepare_body, in_specs=[far] * 3, out_specs=[far] * 4, out...  6.02 us
    ppermute x3, starting transfers between devices, per_device(): squares = [square] + [lax.ppermute(square, *step) for step in along_y]  5.98 us
    all_to_all x1, starting transfers between devices, per_device(): lax.all_to_all(sent, 'fsdp', split_axis=0, concat_axis=0, tiled=True)  5.59 us
    pallas_call x1, Pallas kernels, factors(): pl.pallas_call(body, in_specs=[scalar] * 2 + [whole] * (len(squares) + 1)...  5.58 us
  transfers between devices with their start and end apart: 22, of which 10 were waited for; matrix products, arithmetic and copies ran while one was open for 0% of the time, Pallas kernels for 18%

profile of v6, /device:TPU:0, one launch (start us, length us, event | category | flops | bytes accessed | tf_op | source)
XLA Modules:
  0.0 101.3 jit_solution(2252109850469362860)
XLA Ops:
  0.7 0.1 pad_add_fusion.1.place
  0.7 2.8 %load.1 = (bf16[1,128,2048]{2,1,0:T(8,128)(2,1)S(1)}, bf16[3,128,2048]{2,1,0:T(8,128)(2,1)S(1)}, bf16[1,128,2048]{2,1,0:T(8,128)(2,1)S(1)}, bf16[3,128,2048]{2,1,0:T(8,128)(2,1)S(1)}) custom-call(s32[3]{0:T(128)S(1)} %pad_add_fusion.1.place, bf16[128,16384]{1,0:T(8,128)(2,1)} %bitcast.20), custom_call_target="tpu_custom_call" | custom-call | tf_op jit(solution)/shard_map/load/pallas_call | solution.py:190
  3.5 0.1 collective-permute-start
  3.6 1.9 %collective-permute-done.far = bf16[1,128,2048]{2,1,0:T(8,128)(2,1)S(1)} collective-permute-done((bf16[1,128,2048]{2,1,0:T(8,128)(2,1)S(1)}, bf16[1,128,2048]{2,1,0:T(8,128)(2,1)S(1)}, u32[]{:S(2)}, u32[]{:S(2)}) %collective-permute-start) | collective-permute-done | bytes 524320 | tf_op jit(solution)/shard_map/ppermute | solution.py:285
  5.5 0.1 collective-permute-start.1
  5.7 0.7 pair_far.1
  6.3 2.9 %collective-permute-start.6 = (bf16[64,2048]{1,0:T(8,128)(2,1)S(1)}, bf16[64,2048]{1,0:T(8,128)(2,1)S(1)}, u32[]{:S(2)}, u32[]{:S(2)}) collective-permute-start(bf16[64,2048]{1,0:T(8,128)(2,1)S(1)} %get-tuple-element.63), channel_id=1, source_target_pairs={{0,96},{16,112},{32,0},{48,16},{64,32},{80,48},{96,64},{112,80},{1... | collective-permute-start | bytes 786440 | tf_op jit(solution)/shard_map/ppermute | solution.py:290
  9.2 0.0 collective-permute-start.4
  9.2 0.9 pair_near.1
  10.1 1.3 %collective-permute-start.2 = (bf16[64,2048]{1,0:T(8,128)(2,1)S(1)}, bf16[64,2048]{1,0:T(8,128)(2,1)S(1)}, u32[]{:S(2)}, u32[]{:S(2)}) collective-permute-start(bf16[64,2048]{1,0:T(8,128)(2,1)S(1)} %get-tuple-element.56), channel_id=1, source_target_pairs={{0,32},{16,48},{32,64},{48,80},{64,96},{80,112},{96,0},{112,16},{1... | collective-permute-start | bytes 786440 | tf_op jit(solution)/shard_map/ppermute | solution.py:295
  11.4 2.1 %collective-permute-start.3 = (bf16[64,2048]{1,0:T(8,128)(2,1)S(1)}, bf16[64,2048]{1,0:T(8,128)(2,1)S(1)}, u32[]{:S(2)}, u32[]{:S(2)}) collective-permute-start(bf16[64,2048]{1,0:T(8,128)(2,1)S(1)} %get-tuple-element.57), channel_id=1, source_target_pairs={{0,96},{16,112},{32,0},{48,16},{64,32},{80,48},{96,64},{112,80},{1... | collective-permute-start | bytes 786440 | tf_op jit(solution)/shard_map/ppermute | solution.py:296
  13.5 2.4 %collective-permute-done.6.arrived = bf16[64,2048]{1,0:T(8,128)(2,1)S(1)} collective-permute-done((bf16[64,2048]{1,0:T(8,128)(2,1)S(1)}, bf16[64,2048]{1,0:T(8,128)(2,1)S(1)}, u32[]{:S(2)}, u32[]{:S(2)}) %collective-permute-start.6) | collective-permute-done | bytes 262176 | tf_op jit(solution)/shard_map/ppermute | solution.py:290
  15.9 0.6 relay.3
  16.5 3.8 %collective-permute-start.7 = (bf16[64,2048]{1,0:T(8,128)(2,1)S(1)}, bf16[64,2048]{1,0:T(8,128)(2,1)S(1)}, u32[]{:S(2)}, u32[]{:S(2)}) collective-permute-start(bf16[64,2048]{1,0:T(8,128)(2,1)S(1)} %relay.3), channel_id=1, source_target_pairs={{0,96},{16,112},{32,0},{48,16},{64,32},{80,48},{96,64},{112,80},{1... | collective-permute-start | bytes 786440 | tf_op jit(solution)/shard_map/ppermute | solution.py:298
  20.2 0.6 relay.2
  20.8 0.1 collective-permute-start.5
  20.9 6.0 %prepare.1 = (bf16[2,512,512]{2,1,0:T(8,128)(2,1)}, bf16[2,512,512]{2,1,0:T(8,128)(2,1)}, bf16[2,512,512]{2,1,0:T(8,128)(2,1)}, f32[2,512,512]{2,1,0:T(8,128)}) custom-call(f32[2,512,512]{2,1,0:T(8,128)} %bitcast.27, f32[2,512,512]{2,1,0:T(8,128)} %bitcast.28, f32[2,512,512]{2,1,0:T(8,128)} %bitcast.22), custom_call_target="tpu_custom_call" | custom-call | flops 2147483648 | bytes 11534336 | tf_op jit(solution)/shard_map/prepare/pallas_call | solution.py:93
  27.0 0.0 copy-start
  27.0 0.6 direct.1.own
  27.6 2.3 %collective-permute-done.5.left_sum = bf16[64,2048]{1,0:T(8,128)(2,1)S(1)} collective-permute-done((bf16[64,2048]{1,0:T(8,128)(2,1)S(1)}, bf16[64,2048]{1,0:T(8,128)(2,1)S(1)}, u32[]{:S(2)}, u32[]{:S(2)}) %collective-permute-start.5) | collective-permute-done | bytes 262176 | tf_op jit(solution)/shard_map/ppermute | solution.py:297
  30.0 0.8 finish.1
  30.8 4.1 %collective-permute-start.10 = (bf16[32,2176]{1,0:T(8,128)(2,1)S(1)}, bf16[32,2176]{1,0:T(8,128)(2,1)S(1)}, u32[]{:S(2)}, u32[]{:S(2)}) collective-permute-start(bf16[32,2176]{1,0:T(8,128)(2,1)S(1)} %get-tuple-element.74), channel_id=1, source_target_pairs={{0,12},{1,13},{2,14},{3,15},{4,0},{5,1},{6,2},{7,3},{8,4},{9,5},{1... | collective-permute-start | bytes 417800 | tf_op jit(solution)/shard_map/ppermute | solution.py:308
  34.9 1.9 %collective-permute-start.9 = (bf16[32,2176]{1,0:T(8,128)(2,1)S(1)}, bf16[32,2176]{1,0:T(8,128)(2,1)S(1)}, u32[]{:S(2)}, u32[]{:S(2)}) collective-permute-start(bf16[32,2176]{1,0:T(8,128)(2,1)S(1)} %get-tuple-element.73), channel_id=1, source_target_pairs={{0,8},{1,9},{2,10},{3,11},{4,12},{5,13},{6,14},{7,15},{8,0},{9,1},... | collective-permute-start | bytes 417800 | tf_op jit(solution)/shard_map/ppermute | solution.py:308
  36.8 0.1 pad_add_fusion.table
  36.8 2.2 %collective-permute-done.10.refs_3_ = bf16[32,2176]{1,0:T(8,128)(2,1)S(1)} collective-permute-done((bf16[32,2176]{1,0:T(8,128)(2,1)S(1)}, bf16[32,2176]{1,0:T(8,128)(2,1)S(1)}, u32[]{:S(2)}, u32[]{:S(2)}) %collective-permute-start.10) | collective-permute-done | bytes 139296 | tf_op jit(solution)/shard_map/ppermute | solution.py:308
  39.0 4.1 %collective-permute-done.8.refs_1_ = bf16[32,2176]{1,0:T(8,128)(2,1)S(1)} collective-permute-done((bf16[32,2176]{1,0:T(8,128)(2,1)S(1)}, bf16[32,2176]{1,0:T(8,128)(2,1)S(1)}, u32[]{:S(2)}, u32[]{:S(2)}) %collective-permute-start.8) | collective-permute-done | bytes 139296 | tf_op jit(solution)/shard_map/ppermute | solution.py:308
  43.1 1.6 %dispatch.1 = (bf16[32,32,512]{2,1,0:T(8,128)(2,1)}, f32[8,128]{1,0:T(8,128)S(1)}) custom-call(s32[1,17]{1,0:T(1,128)S(1)} %pad_add_fusion.table, bf16[32,2176]{1,0:T(8,128)(2,1)S(1)} %get-tuple-element.71.refs_0_, bf16[32,2176]{1,0:T(8,128)(2,1)S(1)} %collective-permute-done.8.refs_1_, bf16[32,2176]{1,0:T(8,128)(2,1)S(1)} %collective-permute-done.9.refs_2_, ...), custom_call_target="tpu_custom_call" | custom-call | tf_op jit(solution)/shard_map/dispatch/pallas_call | solution.py:118
  44.7 5.6 %all-to-all-start = ((bf16[16,2,32,512]{3,2,1,0:T(8,128)(2,1)}), bf16[16,2,32,512]{3,2,1,0:T(8,128)(2,1)S(1)}, u32[]{:S(2)}, u32[]{:S(2)}) async-start(bf16[16,2,32,512]{3,2,1,0:T(8,128)(2,1)} %bitcast.9), calls=%async_computation | async-start | bytes 2097152 | tf_op jit(solution)/shard_map/all_to_all | solution.py:536
  50.3 0.1 collective-permute-start.11
  50.4 1.2 %collective-permute-done.11 = f32[8,128]{1,0:T(8,128)S(1)} collective-permute-done((f32[8,128]{1,0:T(8,128)S(1)}, f32[8,128]{1,0:T(8,128)S(1)}, u32[]{:S(2)}, u32[]{:S(2)}) %collective-permute-start.11) | collective-permute-done | bytes 4128 | tf_op jit(solution)/shard_map/ppermute | solution.py:538
  51.5 2.3 %collective-permute-start.13 = (f32[8,128]{1,0:T(8,128)S(1)}, f32[8,128]{1,0:T(8,128)S(1)}, u32[]{:S(2)}, u32[]{:S(2)}) collective-permute-start(f32[8,128]{1,0:T(8,128)S(1)} %add.19), channel_id=1, source_target_pairs={{0,64},{16,80},{32,96},{48,112},{64,0},{80,16},{96,32},{112,48},{1... | collective-permute-start | bytes 12296 | tf_op jit(solution)/shard_map/ppermute | solution.py:538
  53.9 0.9 collective-permute-start.14
  54.8 1.6 %collective-permute-done.12 = f32[8,128]{1,0:T(8,128)S(1)} collective-permute-done((f32[8,128]{1,0:T(8,128)S(1)}, f32[8,128]{1,0:T(8,128)S(1)}, u32[]{:S(2)}, u32[]{:S(2)}) %collective-permute-start.12) | collective-permute-done | bytes 4128 | tf_op jit(solution)/shard_map/ppermute | solution.py:538
  56.3 0.3 collective-permute-done.13
  56.6 0.8 collective-permute-done.14
  57.5 1.8 %collective-permute-start.15 = (f32[8,128]{1,0:T(8,128)S(1)}, f32[8,128]{1,0:T(8,128)S(1)}, u32[]{:S(2)}, u32[]{:S(2)}) collective-permute-start(f32[8,128]{1,0:T(8,128)S(1)} %add_add_fusion.refs_0_.refs_2_), channel_id=1, source_target_pairs={{0,1},{1,2},{2,3},{3,0},{4,5},{5,6},{6,7},{7,4},{8,9},{9,10},{10,1... | collective-permute-start | bytes 12296 | tf_op jit(solution)/shard_map/ppermute | solution.py:539
  59.3 2.7 %collective-permute-start.16 = (f32[8,128]{1,0:T(8,128)S(1)}, f32[8,128]{1,0:T(8,128)S(1)}, u32[]{:S(2)}, u32[]{:S(2)}) collective-permute-start(f32[8,128]{1,0:T(8,128)S(1)} %add_add_fusion.refs_0_.refs_2_), channel_id=1, source_target_pairs={{0,2},{1,3},{2,0},{3,1},{4,6},{5,7},{6,4},{7,5},{8,10},{9,11},{10,... | collective-permute-start | bytes 12296 | tf_op jit(solution)/shard_map/ppermute | solution.py:539
  62.0 1.5 %collective-permute-start.17 = (f32[8,128]{1,0:T(8,128)S(1)}, f32[8,128]{1,0:T(8,128)S(1)}, u32[]{:S(2)}, u32[]{:S(2)}) collective-permute-start(f32[8,128]{1,0:T(8,128)S(1)} %add_add_fusion.refs_0_.refs_2_), channel_id=1, source_target_pairs={{0,3},{1,0},{2,1},{3,2},{4,7},{5,4},{6,5},{7,6},{8,11},{9,8},{10,9... | collective-permute-start | bytes 12296 | tf_op jit(solution)/shard_map/ppermute | solution.py:539
  63.5 2.6 %all-to-all-done.pieces.refs_6_ = bf16[16,2,32,512]{3,2,1,0:T(8,128)(2,1)S(1)} async-done(((bf16[16,2,32,512]{3,2,1,0:T(8,128)(2,1)}), bf16[16,2,32,512]{3,2,1,0:T(8,128)(2,1)S(1)}, u32[]{:S(2)}, u32[]{:S(2)}) %all-to-all-start) | async-done | bytes 1048608 | tf_op jit(solution)/shard_map/all_to_all | solution.py:536
  66.0 3.2 %rotate.1 = (f32[2,512,512]{2,1,0:T(8,128)S(1)}, bf16[2,512,512]{2,1,0:T(8,128)(2,1)S(1)}, bf16[2,512,512]{2,1,0:T(8,128)(2,1)S(1)}, f32[2,512,512]{2,1,0:T(8,128)S(1)}, f32[2,512,512]{2,1,0:T(8,128)S(1)}) custom-call(bf16[16,2,32,512]{3,2,1,0:T(8,128)(2,1)S(1)} %all-to-all-done.pieces.refs_6_, bf16[2,512,512]{2,1,0:T(8,128)(2,1)} %get-tuple-element.77.lt_src, ...), custom_call_target="tpu_custom_call" | custom-call | tf_op jit(solution)/shard_map/rotate/pallas_call | solution.py:359
  69.2 3.1 %direction.1 = (bf16[16,2,32,512]{3,2,1,0:T(8,128)(2,1)S(1)}, f32[2,512,512]{2,1,0:T(8,128)}) custom-call(s32[1,16]{1,0:T(1,128)S(1)} %copy-done, s32[1]{0:T(128)} %bitcast.1.me.refs_1_, f32[8,128]{1,0:T(8,128)S(1)} %add_add_fusion.refs_0_.refs_2_, f32[8,128]{1,0:T(8,128)S(1)} %collective-permute-done.15.refs_1_.refs_3_, ...), custom_call_target="tpu_custom_call" | custom-call | tf_op jit(solution)/shard_map/direction/pallas_call | solution.py:410
  72.4 17.7 %all_to_all.10 = bf16[16,2,32,512]{3,2,1,0:T(8,128)(2,1)S(1)} all-to-all(bf16[16,2,32,512]{3,2,1,0:T(8,128)(2,1)S(1)} %get-tuple-element.86), channel_id=1, replica_groups=mesh['dp'=8,'fsdp'=16] {'fsdp'}, dimensions={0} | all-to-all | bytes 2097152 | tf_op jit(solution)/shard_map/all_to_all | solution.py:542
  90.1 0.6 collect.1
  90.7 0.1 collective-permute-start.18
  90.8 2.4 %collective-permute-start.19 = (bf16[32,2048]{1,0:T(8,128)(2,1)S(1)}, bf16[32,2048]{1,0:T(8,128)(2,1)S(1)}, u32[]{:S(2)}, u32[]{:S(2)}) collective-permute-start(bf16[32,2048]{1,0:T(8,128)(2,1)S(1)} %get-tuple-element.90), channel_id=1, source_target_pairs={{0,8},{1,9},{2,10},{3,11},{4,12},{5,13},{6,14},{7,15},{8,0},{9,1},... | collective-permute-start | bytes 393224 | tf_op jit(solution)/shard_map/ppermute | solution.py:308
  93.2 1.2 %collective-permute-start.20 = (bf16[32,2048]{1,0:T(8,128)(2,1)S(1)}, bf16[32,2048]{1,0:T(8,128)(2,1)S(1)}, u32[]{:S(2)}, u32[]{:S(2)}) collective-permute-start(bf16[32,2048]{1,0:T(8,128)(2,1)S(1)} %get-tuple-element.91), channel_id=1, source_target_pairs={{0,12},{1,13},{2,14},{3,15},{4,0},{5,1},{6,2},{7,3},{8,4},{9,5},{1... | collective-permute-start | bytes 393224 | tf_op jit(solution)/shard_map/ppermute | solution.py:308
  94.3 5.6 %factors.1 = (f32[2,512,512]{2,1,0:T(8,128)}, f32[2,512,512]{2,1,0:T(8,128)}, f32[2,512,512]{2,1,0:T(8,128)}) custom-call(s32[1,16]{1,0:T(1,128)S(1)} %copy-done, s32[1]{0:T(128)} %bitcast.1.me.refs_1_, f32[8,128]{1,0:T(8,128)S(1)} %add_add_fusion.refs_0_.refs_2_, f32[8,128]{1,0:T(8,128)S(1)} %collective-permute-done.15.refs_1_.refs_3_, ...), custom_call_target="tpu_custom_call" | custom-call | flops 1073741824 | bytes 13631488 | tf_op jit(solution)/shard_map/factors/pallas_call | solution.py:475
  100.0 1.4 %put.1 = bf16[4,32,2048]{2,1,0:T(8,128)(2,1)} custom-call(s32[1,17]{1,0:T(1,128)S(1)} %pad_add_fusion.table, bf16[32,2048]{1,0:T(8,128)(2,1)S(1)} %get-tuple-element.88.refs_0_, bf16[32,2048]{1,0:T(8,128)(2,1)S(1)} %collective-permute-done.18.refs_1_, bf16[32,2048]{1,0:T(8,128)(2,1)S(1)} %collective-permute-done.19.refs_2_, ...), custom_call_target="tpu_custom_call" | custom-call | tf_op jit(solution)/shard_map/put/pallas_call | solution.py:118
  (17 shorter events, 0.0 us)
Async XLA Ops:
  3.5 2.0 %collective-permute-start = (bf16[1,128,2048]{2,1,0:T(8,128)(2,1)S(1)}, bf16[1,128,2048]{2,1,0:T(8,128)(2,1)S(1)}, u32[]{:S(2)}, u32[]{:S(2)}) collective-permute-start(bf16[1,128,2048]{2,1,0:T(8,128)(2,1)S(1)} %get-tuple-element.52), channel_id=1, source_target_pairs={{0,16},{16,0},{32,48},{48,32},{64,80},{80,64},{96,112},{112,96},{1... | collective-permute-start | bytes 1572872 | tf_op jit(solution)/shard_map/ppermute | solution.py:285
  5.5 3.7 %collective-permute-start.1 = (bf16[3,128,2048]{2,1,0:T(8,128)(2,1)S(1)}, bf16[3,128,2048]{2,1,0:T(8,128)(2,1)S(1)}, u32[]{:S(2)}, u32[]{:S(2)}) collective-permute-start(bf16[3,128,2048]{2,1,0:T(8,128)(2,1)S(1)} %get-tuple-element.54), channel_id=1, source_target_pairs={{0,16},{16,0},{32,48},{48,32},{64,80},{80,64},{96,112},{112,96},{1... | collective-permute-start | bytes 4718600 | tf_op jit(solution)/shard_map/ppermute | solution.py:287
  6.3 9.6 %collective-permute-start.6 = (bf16[64,2048]{1,0:T(8,128)(2,1)S(1)}, bf16[64,2048]{1,0:T(8,128)(2,1)S(1)}, u32[]{:S(2)}, u32[]{:S(2)}) collective-permute-start(bf16[64,2048]{1,0:T(8,128)(2,1)S(1)} %get-tuple-element.63), channel_id=1, source_target_pairs={{0,96},{16,112},{32,0},{48,16},{64,32},{80,48},{96,64},{112,80},{1... | collective-permute-start | bytes 786440 | tf_op jit(solution)/shard_map/ppermute | solution.py:290
  9.2 11.0 %collective-permute-start.4 = (bf16[64,2048]{1,0:T(8,128)(2,1)S(1)}, bf16[64,2048]{1,0:T(8,128)(2,1)S(1)}, u32[]{:S(2)}, u32[]{:S(2)}) collective-permute-start(bf16[64,2048]{1,0:T(8,128)(2,1)S(1)} %get-tuple-element.61), channel_id=1, source_target_pairs={{0,32},{16,48},{32,64},{48,80},{64,96},{80,112},{96,0},{112,16},{1... | collective-permute-start | bytes 786440 | tf_op jit(solution)/shard_map/ppermute | solution.py:289
  10.1 16.8 %collective-permute-start.2 = (bf16[64,2048]{1,0:T(8,128)(2,1)S(1)}, bf16[64,2048]{1,0:T(8,128)(2,1)S(1)}, u32[]{:S(2)}, u32[]{:S(2)}) collective-permute-start(bf16[64,2048]{1,0:T(8,128)(2,1)S(1)} %get-tuple-element.56), channel_id=1, source_target_pairs={{0,32},{16,48},{32,64},{48,80},{64,96},{80,112},{96,0},{112,16},{1... | collective-permute-start | bytes 786440 | tf_op jit(solution)/shard_map/ppermute | solution.py:295
  11.4 15.5 %collective-permute-start.3 = (bf16[64,2048]{1,0:T(8,128)(2,1)S(1)}, bf16[64,2048]{1,0:T(8,128)(2,1)S(1)}, u32[]{:S(2)}, u32[]{:S(2)}) collective-permute-start(bf16[64,2048]{1,0:T(8,128)(2,1)S(1)} %get-tuple-element.57), channel_id=1, source_target_pairs={{0,96},{16,112},{32,0},{48,16},{64,32},{80,48},{96,64},{112,80},{1... | collective-permute-start | bytes 786440 | tf_op jit(solution)/shard_map/ppermute | solution.py:296
  16.5 11.1 %collective-permute-start.7 = (bf16[64,2048]{1,0:T(8,128)(2,1)S(1)}, bf16[64,2048]{1,0:T(8,128)(2,1)S(1)}, u32[]{:S(2)}, u32[]{:S(2)}) collective-permute-start(bf16[64,2048]{1,0:T(8,128)(2,1)S(1)} %relay.3), channel_id=1, source_target_pairs={{0,96},{16,112},{32,0},{48,16},{64,32},{80,48},{96,64},{112,80},{1... | collective-permute-start | bytes 786440 | tf_op jit(solution)/shard_map/ppermute | solution.py:298
  20.8 9.1 %collective-permute-start.5 = (bf16[64,2048]{1,0:T(8,128)(2,1)S(1)}, bf16[64,2048]{1,0:T(8,128)(2,1)S(1)}, u32[]{:S(2)}, u32[]{:S(2)}) collective-permute-start(bf16[64,2048]{1,0:T(8,128)(2,1)S(1)} %relay.2), channel_id=1, source_target_pairs={{0,32},{16,48},{32,64},{48,80},{64,96},{80,112},{96,0},{112,16},{1... | collective-permute-start | bytes 786440 | tf_op jit(solution)/shard_map/ppermute | solution.py:297
  27.0 9.8 %copy-start = (s32[1,16]{1,0:T(1,128)S(1)}, s32[1,16]{1,0:T(1,128)}, u32[]{:S(2)}) copy-start(s32[1,16]{1,0:T(1,128)} %refs_0_.1) | copy-start | bytes 196
  30.8 8.2 %collective-permute-start.10 = (bf16[32,2176]{1,0:T(8,128)(2,1)S(1)}, bf16[32,2176]{1,0:T(8,128)(2,1)S(1)}, u32[]{:S(2)}, u32[]{:S(2)}) collective-permute-start(bf16[32,2176]{1,0:T(8,128)(2,1)S(1)} %get-tuple-element.74), channel_id=1, source_target_pairs={{0,12},{1,13},{2,14},{3,15},{4,0},{5,1},{6,2},{7,3},{8,4},{9,5},{1... | collective-permute-start | bytes 417800 | tf_op jit(solution)/shard_map/ppermute | solution.py:308
  34.9 8.2 %collective-permute-start.8 = (bf16[32,2176]{1,0:T(8,128)(2,1)S(1)}, bf16[32,2176]{1,0:T(8,128)(2,1)S(1)}, u32[]{:S(2)}, u32[]{:S(2)}) collective-permute-start(bf16[32,2176]{1,0:T(8,128)(2,1)S(1)} %get-tuple-element.72), channel_id=1, source_target_pairs={{0,4},{1,5},{2,6},{3,7},{4,8},{5,9},{6,10},{7,11},{8,12},{9,13},{1... | collective-permute-start | bytes 417800 | tf_op jit(solution)/shard_map/ppermute | solution.py:308
  34.9 8.2 %collective-permute-start.9 = (bf16[32,2176]{1,0:T(8,128)(2,1)S(1)}, bf16[32,2176]{1,0:T(8,128)(2,1)S(1)}, u32[]{:S(2)}, u32[]{:S(2)}) collective-permute-start(bf16[32,2176]{1,0:T(8,128)(2,1)S(1)} %get-tuple-element.73), channel_id=1, source_target_pairs={{0,8},{1,9},{2,10},{3,11},{4,12},{5,13},{6,14},{7,15},{8,0},{9,1},... | collective-permute-start | bytes 417800 | tf_op jit(solution)/shard_map/ppermute | solution.py:308
  44.7 21.4 %all-to-all-start = ((bf16[16,2,32,512]{3,2,1,0:T(8,128)(2,1)}), bf16[16,2,32,512]{3,2,1,0:T(8,128)(2,1)S(1)}, u32[]{:S(2)}, u32[]{:S(2)}) async-start(bf16[16,2,32,512]{3,2,1,0:T(8,128)(2,1)} %bitcast.9), calls=%async_computation | async-start | bytes 2097152 | tf_op jit(solution)/shard_map/all_to_all | solution.py:536
  50.3 1.2 %collective-permute-start.11 = (f32[8,128]{1,0:T(8,128)S(1)}, f32[8,128]{1,0:T(8,128)S(1)}, u32[]{:S(2)}, u32[]{:S(2)}) collective-permute-start(f32[8,128]{1,0:T(8,128)S(1)} %get-tuple-element.75), channel_id=1, source_target_pairs={{0,16},{16,0},{32,48},{48,32},{64,80},{80,64},{96,112},{112,96},{1... | collective-permute-start | bytes 12296 | tf_op jit(solution)/shard_map/ppermute | solution.py:538
  51.5 4.8 %collective-permute-start.12 = (f32[8,128]{1,0:T(8,128)S(1)}, f32[8,128]{1,0:T(8,128)S(1)}, u32[]{:S(2)}, u32[]{:S(2)}) collective-permute-start(f32[8,128]{1,0:T(8,128)S(1)} %add.19), channel_id=1, source_target_pairs={{0,32},{16,48},{32,64},{48,80},{64,96},{80,112},{96,0},{112,16},{1... | collective-permute-start | bytes 12296 | tf_op jit(solution)/shard_map/ppermute | solution.py:538
  51.5 5.1 %collective-permute-start.13 = (f32[8,128]{1,0:T(8,128)S(1)}, f32[8,128]{1,0:T(8,128)S(1)}, u32[]{:S(2)}, u32[]{:S(2)}) collective-permute-start(f32[8,128]{1,0:T(8,128)S(1)} %add.19), channel_id=1, source_target_pairs={{0,64},{16,80},{32,96},{48,112},{64,0},{80,16},{96,32},{112,48},{1... | collective-permute-start | bytes 12296 | tf_op jit(solution)/shard_map/ppermute | solution.py:538
  53.9 3.6 %collective-permute-start.14 = (f32[8,128]{1,0:T(8,128)S(1)}, f32[8,128]{1,0:T(8,128)S(1)}, u32[]{:S(2)}, u32[]{:S(2)}) collective-permute-start(f32[8,128]{1,0:T(8,128)S(1)} %add.19), channel_id=1, source_target_pairs={{0,96},{16,112},{32,0},{48,16},{64,32},{80,48},{96,64},{112,80},{1... | collective-permute-start | bytes 12296 | tf_op jit(solution)/shard_map/ppermute | solution.py:538
  57.5 11.7 %collective-permute-start.15 = (f32[8,128]{1,0:T(8,128)S(1)}, f32[8,128]{1,0:T(8,128)S(1)}, u32[]{:S(2)}, u32[]{:S(2)}) collective-permute-start(f32[8,128]{1,0:T(8,128)S(1)} %add_add_fusion.refs_0_.refs_2_), channel_id=1, source_target_pairs={{0,1},{1,2},{2,3},{3,0},{4,5},{5,6},{6,7},{7,4},{8,9},{9,10},{10,1... | collective-permute-start | bytes 12296 | tf_op jit(solution)/shard_map/ppermute | solution.py:539
  59.3 9.9 %collective-permute-start.16 = (f32[8,128]{1,0:T(8,128)S(1)}, f32[8,128]{1,0:T(8,128)S(1)}, u32[]{:S(2)}, u32[]{:S(2)}) collective-permute-start(f32[8,128]{1,0:T(8,128)S(1)} %add_add_fusion.refs_0_.refs_2_), channel_id=1, source_target_pairs={{0,2},{1,3},{2,0},{3,1},{4,6},{5,7},{6,4},{7,5},{8,10},{9,11},{10,... | collective-permute-start | bytes 12296 | tf_op jit(solution)/shard_map/ppermute | solution.py:539
  62.0 7.2 %collective-permute-start.17 = (f32[8,128]{1,0:T(8,128)S(1)}, f32[8,128]{1,0:T(8,128)S(1)}, u32[]{:S(2)}, u32[]{:S(2)}) collective-permute-start(f32[8,128]{1,0:T(8,128)S(1)} %add_add_fusion.refs_0_.refs_2_), channel_id=1, source_target_pairs={{0,3},{1,0},{2,1},{3,2},{4,7},{5,4},{6,5},{7,6},{8,11},{9,8},{10,9... | collective-permute-start | bytes 12296 | tf_op jit(solution)/shard_map/ppermute | solution.py:539
  90.7 9.3 %collective-permute-start.18 = (bf16[32,2048]{1,0:T(8,128)(2,1)S(1)}, bf16[32,2048]{1,0:T(8,128)(2,1)S(1)}, u32[]{:S(2)}, u32[]{:S(2)}) collective-permute-start(bf16[32,2048]{1,0:T(8,128)(2,1)S(1)} %get-tuple-element.89), channel_id=1, source_target_pairs={{0,4},{1,5},{2,6},{3,7},{4,8},{5,9},{6,10},{7,11},{8,12},{9,13},{1... | collective-permute-start | bytes 393224 | tf_op jit(solution)/shard_map/ppermute | solution.py:308
  90.8 9.2 %collective-permute-start.19 = (bf16[32,2048]{1,0:T(8,128)(2,1)S(1)}, bf16[32,2048]{1,0:T(8,128)(2,1)S(1)}, u32[]{:S(2)}, u32[]{:S(2)}) collective-permute-start(bf16[32,2048]{1,0:T(8,128)(2,1)S(1)} %get-tuple-element.90), channel_id=1, source_target_pairs={{0,8},{1,9},{2,10},{3,11},{4,12},{5,13},{6,14},{7,15},{8,0},{9,1},... | collective-permute-start | bytes 393224 | tf_op jit(solution)/shard_map/ppermute | solution.py:308
  93.2 6.8 %collective-permute-start.20 = (bf16[32,2048]{1,0:T(8,128)(2,1)S(1)}, bf16[32,2048]{1,0:T(8,128)(2,1)S(1)}, u32[]{:S(2)}, u32[]{:S(2)}) collective-permute-start(bf16[32,2048]{1,0:T(8,128)(2,1)S(1)} %get-tuple-element.91), channel_id=1, source_target_pairs={{0,12},{1,13},{2,14},{3,15},{4,0},{5,1},{6,2},{7,3},{8,4},{9,5},{1... | collective-permute-start | bytes 393224 | tf_op jit(solution)/shard_map/ppermute | solution.py:308

commit v7 on v5

--- a/solution.py
+++ b/solution.py
@@ -336,8 +336,10 @@
 
     def body(pieces, lt_src, l_src, r_src, rot_src, old_src, *refs):
         out, right, left, rot, old, lt, half, sems = refs
-        pairs = [(src.at[s], dst.at[s]) for s in range(slots) for src, dst in ((lt_src, lt), (r_src, right))]
-        pairs += [(src.at[0], dst.at[0]) for src, dst in ((rot_src, rot), (old_src, old), (l_src, left))]
+        first = ((lt_src, lt), (r_src, right))
+        pairs = [(src.at[s], dst.at[s]) for s in range(slots) for src, dst in first]
+        pairs += [(src.at[0], dst.at[0]) for src, dst in ((rot_src, rot), (old_src, old))]
+        pairs.append((l_src, left))
         copies = [
             pltpu.make_async_copy(src, dst, sems.at[i]) for i, (src, dst) in enumerate(pairs)
         ]
@@ -361,7 +363,7 @@
         out_shape=[
             VMEM((slots, n, n), f32),
             VMEM((slots, n, n), bf16),
-            VMEM((1, n, n), bf16),
+            VMEM((slots, n, n), bf16),
             VMEM((1, n, n), f32),
             VMEM((1, n, n), f32),
         ],
@@ -381,10 +383,10 @@
     per = senders // bands
 
     def body(table, me, *refs):
-        squares, rest = refs[: len(refs) - 18], refs[len(refs) - 18 :]
-        product, right, left, rot, old, l_src, rot_src, old_src, out, second_out = rest[:10]
-        left_more, rot_more, old_more, new, step, half, in_sems, sems = rest[10:]
-        pairs = ((rot_src, rot_more), (old_src, old_more), (l_src, left_more))
+        squares, rest = refs[: len(refs) - 16], refs[len(refs) - 16 :]
+        product, right, left, rot, old, rot_src, old_src, out, second_out = rest[:9]
+        rot_more, old_more, new, step, half, in_sems, sems = rest[9:]
+        pairs = ((old_src, old_more), (rot_src, rot_more))
         copies = [
             [
                 pltpu.make_async_copy(src.at[s], dst.at[s - 1], in_sems.at[s, i])
@@ -398,9 +400,9 @@
         scale = clip_of(squares, entries)
         for s in range(slots):
             if s == 0:
-                states = rot.at[0], old.at[0], left.at[0]
+                states = rot.at[0], old.at[0]
             else:
-                states = rot_more.at[s - 1], old_more.at[s - 1], left_more.at[s - 1]
+                states = rot_more.at[s - 1], old_more.at[s - 1]
                 for c in copies[s - 1]:
                     c.wait()
             named = is_named(table, me[0] * slots + s)
@@ -412,7 +414,7 @@
                 ahead = states[0][r] + 0.1 * turned
                 step[r] = (ahead * pl.reciprocal(jnp.sqrt(value) + 1e-08, approx=True)).astype(bf16)
             pltpu.make_async_copy(new.at[s], second_out.at[s], sems.at[s]).start()
-            half[...] = mm(states[2][...], step[...]).astype(bf16)
+            half[...] = mm(left[s], step[...]).astype(bf16)
             update = mm(half[...], right[s], ((1,), (1,))).astype(bf16)
             for y in range(per):
                 for z in range(bands):
@@ -426,25 +428,24 @@
     far = pl.BlockSpec(memory_space=HBM)
     return pl.pallas_call(
         body,
-        in_specs=[scalar] * 2 + [whole] * (len(squares) + 5) + [far] * 3,
+        in_specs=[scalar] * 2 + [whole] * (len(squares) + 5) + [far] * 2,
         out_specs=[whole, far],
         out_shape=[
             jax.ShapeDtypeStruct((senders, slots, rows, n), bf16),
             HBM((slots, n, n), f32),
         ],
         scratch_shapes=[
-            pltpu.VMEM((slots - 1, n, n), bf16),
             pltpu.VMEM((slots - 1, n, n), f32),
             pltpu.VMEM((slots - 1, n, n), f32),
             pltpu.VMEM((slots, n, n), f32),
             pltpu.VMEM((n, n), bf16),
             pltpu.VMEM((n, n), bf16),
-            pltpu.SemaphoreType.DMA((slots, 3)),
+            pltpu.SemaphoreType.DMA((slots, 2)),
             pltpu.SemaphoreType.DMA((slots,)),
         ],
         compiler_params=pltpu.CompilerParams(vmem_limit_bytes=16 << 20),
         name="direction",
-    )(table, me, *squares, *rotated, *in_hbm(prepared[1], prepared[3], second))
+    )(table, me, *squares, *rotated, *in_hbm(prepared[3], second))
 
 
 def factors_body(bands, entries, table, me, *refs):

time: 102 us -> 103 us (level)
  transfers between devices with their start and end apart: 22 -> 22, of which waited for: 8 -> 8; matrix products, arithmetic and copies ran while one was open for 0% -> 0% of each run, Pallas kernels for 18% -> 17%
where the time goes in v7:
time: 103 us; the launch traced here: 102 us
  starting transfers between devices  35.5 us (34%)
  Pallas kernels  29.6 us (29%)
  blocking collectives  19.4 us (19%)
  waiting for transfers between devices  16.5 us (16%)
    all_to_all x1, blocking collectives, per_device(): lax.all_to_all(update, 'fsdp', split_axis=0, concat_axis=0, tiled=True)  19.4 us
    ppermute x6, starting transfers between devices, exchange(): got[j] = lax.ppermute(arrays[j], *steps[j - 1])  10.3 us
    pallas_call x9, Pallas kernels, local(): pl.pallas_call(body, in_specs=[pl.BlockSpec(memory_space=SMEM)] + [pl.Blo...  7.66 us
    all_to_all x1, starting transfers between devices, per_device(): lax.all_to_all(sent, 'fsdp', split_axis=0, concat_axis=0, tiled=True)  6.25 us
    pallas_call x1, Pallas kernels, prepare(): pl.pallas_call(prepare_body, in_specs=[far] * 3, out_specs=[far] * 4, out...  6.01 us
    pallas_call x1, Pallas kernels, factors(): pl.pallas_call(body, in_specs=[scalar] * 2 + [whole] * (len(squares) + 1)...  5.58 us
    ppermute x4, waiting for transfers between devices, per_device(): square = sum([lax.ppermute(square, *step) for step in steps], square)  5.38 us
    ppermute x3, starting transfers between devices, per_device(): squares = [square] + [lax.ppermute(square, *step) for step in along_y]  4.77 us
  transfers between devices with their start and end apart: 22, of which 8 were waited for; matrix products, arithmetic and copies ran while one was open for 0% of the time, Pallas kernels for 17%

profile of v7, /device:TPU:0, one launch (start us, length us, event | category | flops | bytes accessed | tf_op | source)
XLA Modules:
  0.0 102.1 jit_solution(11214192633130317140)
XLA Ops:
  0.7 0.1 pad_add_fusion.1.place
  0.7 2.8 %load.1 = (bf16[1,128,2048]{2,1,0:T(8,128)(2,1)S(1)}, bf16[3,128,2048]{2,1,0:T(8,128)(2,1)S(1)}, bf16[1,128,2048]{2,1,0:T(8,128)(2,1)S(1)}, bf16[3,128,2048]{2,1,0:T(8,128)(2,1)S(1)}) custom-call(s32[3]{0:T(128)S(1)} %pad_add_fusion.1.place, bf16[128,16384]{1,0:T(8,128)(2,1)} %bitcast.22), custom_call_target="tpu_custom_call" | custom-call | tf_op jit(solution)/shard_map/load/pallas_call | solution.py:190
  3.5 0.1 collective-permute-start
  3.6 1.9 %collective-permute-done.far = bf16[1,128,2048]{2,1,0:T(8,128)(2,1)S(1)} collective-permute-done((bf16[1,128,2048]{2,1,0:T(8,128)(2,1)S(1)}, bf16[1,128,2048]{2,1,0:T(8,128)(2,1)S(1)}, u32[]{:S(2)}, u32[]{:S(2)}) %collective-permute-start) | collective-permute-done | bytes 524320 | tf_op jit(solution)/shard_map/ppermute | solution.py:285
  5.5 0.1 collective-permute-start.1
  5.7 0.7 pair_far.1
  6.3 1.7 %collective-permute-start.4 = (bf16[64,2048]{1,0:T(8,128)(2,1)S(1)}, bf16[64,2048]{1,0:T(8,128)(2,1)S(1)}, u32[]{:S(2)}, u32[]{:S(2)}) collective-permute-start(bf16[64,2048]{1,0:T(8,128)(2,1)S(1)} %get-tuple-element.61), channel_id=1, source_target_pairs={{0,32},{16,48},{32,64},{48,80},{64,96},{80,112},{96,0},{112,16},{1... | collective-permute-start | bytes 786440 | tf_op jit(solution)/shard_map/ppermute | solution.py:289
  8.0 1.7 %collective-permute-start.6 = (bf16[64,2048]{1,0:T(8,128)(2,1)S(1)}, bf16[64,2048]{1,0:T(8,128)(2,1)S(1)}, u32[]{:S(2)}, u32[]{:S(2)}) collective-permute-start(bf16[64,2048]{1,0:T(8,128)(2,1)S(1)} %get-tuple-element.63), channel_id=1, source_target_pairs={{0,96},{16,112},{32,0},{48,16},{64,32},{80,48},{96,64},{112,80},{1... | collective-permute-start | bytes 786440 | tf_op jit(solution)/shard_map/ppermute | solution.py:290
  9.6 0.9 pair_near.1
  10.5 0.9 collective-permute-start.2
  11.4 2.4 %collective-permute-start.3 = (bf16[64,2048]{1,0:T(8,128)(2,1)S(1)}, bf16[64,2048]{1,0:T(8,128)(2,1)S(1)}, u32[]{:S(2)}, u32[]{:S(2)}) collective-permute-start(bf16[64,2048]{1,0:T(8,128)(2,1)S(1)} %get-tuple-element.57), channel_id=1, source_target_pairs={{0,96},{16,112},{32,0},{48,16},{64,32},{80,48},{96,64},{112,80},{1... | collective-permute-start | bytes 786440 | tf_op jit(solution)/shard_map/ppermute | solution.py:296
  13.8 2.9 %collective-permute-done.4.arrived = bf16[64,2048]{1,0:T(8,128)(2,1)S(1)} collective-permute-done((bf16[64,2048]{1,0:T(8,128)(2,1)S(1)}, bf16[64,2048]{1,0:T(8,128)(2,1)S(1)}, u32[]{:S(2)}, u32[]{:S(2)}) %collective-permute-start.4) | collective-permute-done | bytes 262176 | tf_op jit(solution)/shard_map/ppermute | solution.py:289
  16.7 0.6 relay.2
  17.3 0.4 collective-permute-start.5
  17.8 0.6 relay.3
  18.4 2.9 %collective-permute-start.7 = (bf16[64,2048]{1,0:T(8,128)(2,1)S(1)}, bf16[64,2048]{1,0:T(8,128)(2,1)S(1)}, u32[]{:S(2)}, u32[]{:S(2)}) collective-permute-start(bf16[64,2048]{1,0:T(8,128)(2,1)S(1)} %relay.3), channel_id=1, source_target_pairs={{0,96},{16,112},{32,0},{48,16},{64,32},{80,48},{96,64},{112,80},{1... | collective-permute-start | bytes 786440 | tf_op jit(solution)/shard_map/ppermute | solution.py:298
  21.3 6.0 %prepare.1 = (bf16[2,512,512]{2,1,0:T(8,128)(2,1)}, bf16[2,512,512]{2,1,0:T(8,128)(2,1)}, bf16[2,512,512]{2,1,0:T(8,128)(2,1)}, f32[2,512,512]{2,1,0:T(8,128)}) custom-call(f32[2,512,512]{2,1,0:T(8,128)} %bitcast.28, f32[2,512,512]{2,1,0:T(8,128)} %bitcast.29, f32[2,512,512]{2,1,0:T(8,128)} %bitcast.23), custom_call_target="tpu_custom_call" | custom-call | flops 2147483648 | bytes 11534336 | tf_op jit(solution)/shard_map/prepare/pallas_call | solution.py:93
  27.3 0.0 copy-start
  27.4 0.6 direct.1.own
  28.0 0.8 finish.1
  28.8 2.1 %collective-permute-start.8 = (bf16[32,2176]{1,0:T(8,128)(2,1)S(1)}, bf16[32,2176]{1,0:T(8,128)(2,1)S(1)}, u32[]{:S(2)}, u32[]{:S(2)}) collective-permute-start(bf16[32,2176]{1,0:T(8,128)(2,1)S(1)} %get-tuple-element.72), channel_id=1, source_target_pairs={{0,4},{1,5},{2,6},{3,7},{4,8},{5,9},{6,10},{7,11},{8,12},{9,13},{1... | collective-permute-start | bytes 417800 | tf_op jit(solution)/shard_map/ppermute | solution.py:308
  30.9 3.6 %collective-permute-start.9 = (bf16[32,2176]{1,0:T(8,128)(2,1)S(1)}, bf16[32,2176]{1,0:T(8,128)(2,1)S(1)}, u32[]{:S(2)}, u32[]{:S(2)}) collective-permute-start(bf16[32,2176]{1,0:T(8,128)(2,1)S(1)} %get-tuple-element.73), channel_id=1, source_target_pairs={{0,8},{1,9},{2,10},{3,11},{4,12},{5,13},{6,14},{7,15},{8,0},{9,1},... | collective-permute-start | bytes 417800 | tf_op jit(solution)/shard_map/ppermute | solution.py:308
  34.5 1.0 collective-permute-start.10
  35.5 0.1 pad_add_fusion.table
  35.6 1.6 %collective-permute-done.8.refs_1_ = bf16[32,2176]{1,0:T(8,128)(2,1)S(1)} collective-permute-done((bf16[32,2176]{1,0:T(8,128)(2,1)S(1)}, bf16[32,2176]{1,0:T(8,128)(2,1)S(1)}, u32[]{:S(2)}, u32[]{:S(2)}) %collective-permute-start.8) | collective-permute-done | bytes 139296 | tf_op jit(solution)/shard_map/ppermute | solution.py:308
  37.2 2.8 %collective-permute-done.9.refs_2_ = bf16[32,2176]{1,0:T(8,128)(2,1)S(1)} collective-permute-done((bf16[32,2176]{1,0:T(8,128)(2,1)S(1)}, bf16[32,2176]{1,0:T(8,128)(2,1)S(1)}, u32[]{:S(2)}, u32[]{:S(2)}) %collective-permute-start.9) | collective-permute-done | bytes 139296 | tf_op jit(solution)/shard_map/ppermute | solution.py:308
  40.0 1.6 %dispatch.1 = (bf16[32,32,512]{2,1,0:T(8,128)(2,1)}, f32[8,128]{1,0:T(8,128)S(1)}) custom-call(s32[1,17]{1,0:T(1,128)S(1)} %pad_add_fusion.table, bf16[32,2176]{1,0:T(8,128)(2,1)S(1)} %get-tuple-element.71.refs_0_, bf16[32,2176]{1,0:T(8,128)(2,1)S(1)} %collective-permute-done.8.refs_1_, bf16[32,2176]{1,0:T(8,128)(2,1)S(1)} %collective-permute-done.9.refs_2_, ...), custom_call_target="tpu_custom_call" | custom-call | tf_op jit(solution)/shard_map/dispatch/pallas_call | solution.py:118
  41.5 6.2 %all-to-all-start = ((bf16[16,2,32,512]{3,2,1,0:T(8,128)(2,1)}), bf16[16,2,32,512]{3,2,1,0:T(8,128)(2,1)S(1)}, u32[]{:S(2)}, u32[]{:S(2)}) async-start(bf16[16,2,32,512]{3,2,1,0:T(8,128)(2,1)} %bitcast.9), calls=%async_computation | async-start | bytes 2097152 | tf_op jit(solution)/shard_map/all_to_all | solution.py:558
  47.8 0.1 collective-permute-start.11
  47.9 1.2 %collective-permute-done.11 = f32[8,128]{1,0:T(8,128)S(1)} collective-permute-done((f32[8,128]{1,0:T(8,128)S(1)}, f32[8,128]{1,0:T(8,128)S(1)}, u32[]{:S(2)}, u32[]{:S(2)}) %collective-permute-start.11) | collective-permute-done | bytes 4128 | tf_op jit(solution)/shard_map/ppermute | solution.py:560
  49.0 2.3 %collective-permute-start.14 = (f32[8,128]{1,0:T(8,128)S(1)}, f32[8,128]{1,0:T(8,128)S(1)}, u32[]{:S(2)}, u32[]{:S(2)}) collective-permute-start(f32[8,128]{1,0:T(8,128)S(1)} %add.19), channel_id=1, source_target_pairs={{0,96},{16,112},{32,0},{48,16},{64,32},{80,48},{96,64},{112,80},{1... | collective-permute-start | bytes 12296 | tf_op jit(solution)/shard_map/ppermute | solution.py:560
  51.4 0.9 collective-permute-start.13
  52.3 0.6 collective-permute-start.12
  52.9 3.6 %collective-permute-done.13 = f32[8,128]{1,0:T(8,128)S(1)} collective-permute-done((f32[8,128]{1,0:T(8,128)S(1)}, f32[8,128]{1,0:T(8,128)S(1)}, u32[]{:S(2)}, u32[]{:S(2)}) %collective-permute-start.13) | collective-permute-done | bytes 4128 | tf_op jit(solution)/shard_map/ppermute | solution.py:560
  56.5 0.6 collective-permute-done.12
  57.1 3.1 %collective-permute-start.17 = (f32[8,128]{1,0:T(8,128)S(1)}, f32[8,128]{1,0:T(8,128)S(1)}, u32[]{:S(2)}, u32[]{:S(2)}) collective-permute-start(f32[8,128]{1,0:T(8,128)S(1)} %add_add_fusion.refs_0_.refs_2_), channel_id=1, source_target_pairs={{0,3},{1,0},{2,1},{3,2},{4,7},{5,4},{6,5},{7,6},{8,11},{9,8},{10,9... | collective-permute-start | bytes 12296 | tf_op jit(solution)/shard_map/ppermute | solution.py:561
  60.2 0.9 collective-permute-start.16
  61.0 0.9 collective-permute-start.15
  61.9 1.9 %all-to-all-done.pieces.refs_6_ = bf16[16,2,32,512]{3,2,1,0:T(8,128)(2,1)S(1)} async-done(((bf16[16,2,32,512]{3,2,1,0:T(8,128)(2,1)}), bf16[16,2,32,512]{3,2,1,0:T(8,128)(2,1)S(1)}, u32[]{:S(2)}, u32[]{:S(2)}) %all-to-all-start) | async-done | bytes 1048608 | tf_op jit(solution)/shard_map/all_to_all | solution.py:558
  63.8 2.9 %rotate.1 = (f32[2,512,512]{2,1,0:T(8,128)S(1)}, bf16[2,512,512]{2,1,0:T(8,128)(2,1)S(1)}, bf16[2,512,512]{2,1,0:T(8,128)(2,1)S(1)}, f32[1,512,512]{2,1,0:T(8,128)S(1)}, f32[1,512,512]{2,1,0:T(8,128)S(1)}) custom-call(bf16[16,2,32,512]{3,2,1,0:T(8,128)(2,1)S(1)} %all-to-all-done.pieces.refs_6_, bf16[2,512,512]{2,1,0:T(8,128)(2,1)} %get-tuple-element.77.lt_src, ...), custom_call_target="tpu_custom_call" | custom-call | tf_op jit(solution)/shard_map/rotate/pallas_call | solution.py:359
  66.7 4.7 %direction.1 = (bf16[16,2,32,512]{3,2,1,0:T(8,128)(2,1)S(1)}, f32[2,512,512]{2,1,0:T(8,128)}) custom-call(s32[1,16]{1,0:T(1,128)S(1)} %copy-done, s32[1]{0:T(128)} %bitcast.1.me.refs_1_, f32[8,128]{1,0:T(8,128)S(1)} %add_add_fusion.refs_0_.refs_2_, f32[8,128]{1,0:T(8,128)S(1)} %collective-permute-done.15.refs_1_.refs_3_, ...), custom_call_target="tpu_custom_call" | custom-call | tf_op jit(solution)/shard_map/direction/pallas_call | solution.py:429
  71.4 19.4 %all_to_all.10 = bf16[16,2,32,512]{3,2,1,0:T(8,128)(2,1)S(1)} all-to-all(bf16[16,2,32,512]{3,2,1,0:T(8,128)(2,1)S(1)} %get-tuple-element.86), channel_id=1, replica_groups=mesh['dp'=8,'fsdp'=16] {'fsdp'}, dimensions={0} | all-to-all | bytes 2097152 | tf_op jit(solution)/shard_map/all_to_all | solution.py:566
  90.8 0.6 collect.1
  91.4 0.1 collective-permute-start.18
  91.5 2.4 %collective-permute-start.19 = (bf16[32,2048]{1,0:T(8,128)(2,1)S(1)}, bf16[32,2048]{1,0:T(8,128)(2,1)S(1)}, u32[]{:S(2)}, u32[]{:S(2)}) collective-permute-start(bf16[32,2048]{1,0:T(8,128)(2,1)S(1)} %get-tuple-element.90), channel_id=1, source_target_pairs={{0,8},{1,9},{2,10},{3,11},{4,12},{5,13},{6,14},{7,15},{8,0},{9,1},... | collective-permute-start | bytes 393224 | tf_op jit(solution)/shard_map/ppermute | solution.py:308
  93.9 1.2 %collective-permute-start.20 = (bf16[32,2048]{1,0:T(8,128)(2,1)S(1)}, bf16[32,2048]{1,0:T(8,128)(2,1)S(1)}, u32[]{:S(2)}, u32[]{:S(2)}) collective-permute-start(bf16[32,2048]{1,0:T(8,128)(2,1)S(1)} %get-tuple-element.91), channel_id=1, source_target_pairs={{0,12},{1,13},{2,14},{3,15},{4,0},{5,1},{6,2},{7,3},{8,4},{9,5},{1... | collective-permute-start | bytes 393224 | tf_op jit(solution)/shard_map/ppermute | solution.py:308
  95.1 5.6 %factors.1 = (f32[2,512,512]{2,1,0:T(8,128)}, f32[2,512,512]{2,1,0:T(8,128)}, f32[2,512,512]{2,1,0:T(8,128)}) custom-call(s32[1,16]{1,0:T(1,128)S(1)} %copy-done, s32[1]{0:T(128)} %bitcast.1.me.refs_1_, f32[8,128]{1,0:T(8,128)S(1)} %add_add_fusion.refs_0_.refs_2_, f32[8,128]{1,0:T(8,128)S(1)} %collective-permute-done.15.refs_1_.refs_3_, ...), custom_call_target="tpu_custom_call" | custom-call | flops 1073741824 | bytes 13631488 | tf_op jit(solution)/shard_map/factors/pallas_call | solution.py:497
  100.7 1.4 %put.1 = bf16[4,32,2048]{2,1,0:T(8,128)(2,1)} custom-call(s32[1,17]{1,0:T(1,128)S(1)} %pad_add_fusion.table, bf16[32,2048]{1,0:T(8,128)(2,1)S(1)} %get-tuple-element.88.refs_0_, bf16[32,2048]{1,0:T(8,128)(2,1)S(1)} %collective-permute-done.18.refs_1_, bf16[32,2048]{1,0:T(8,128)(2,1)S(1)} %collective-permute-done.19.refs_2_, ...), custom_call_target="tpu_custom_call" | custom-call | tf_op jit(solution)/shard_map/put/pallas_call | solution.py:118
  (17 shorter events, 0.0 us)
Async XLA Ops:
  3.5 2.0 %collective-permute-start = (bf16[1,128,2048]{2,1,0:T(8,128)(2,1)S(1)}, bf16[1,128,2048]{2,1,0:T(8,128)(2,1)S(1)}, u32[]{:S(2)}, u32[]{:S(2)}) collective-permute-start(bf16[1,128,2048]{2,1,0:T(8,128)(2,1)S(1)} %get-tuple-element.52), channel_id=1, source_target_pairs={{0,16},{16,0},{32,48},{48,32},{64,80},{80,64},{96,112},{112,96},{1... | collective-permute-start | bytes 1572872 | tf_op jit(solution)/shard_map/ppermute | solution.py:285
  5.5 4.1 %collective-permute-start.1 = (bf16[3,128,2048]{2,1,0:T(8,128)(2,1)S(1)}, bf16[3,128,2048]{2,1,0:T(8,128)(2,1)S(1)}, u32[]{:S(2)}, u32[]{:S(2)}) collective-permute-start(bf16[3,128,2048]{2,1,0:T(8,128)(2,1)S(1)} %get-tuple-element.54), channel_id=1, source_target_pairs={{0,16},{16,0},{32,48},{48,32},{64,80},{80,64},{96,112},{112,96},{1... | collective-permute-start | bytes 4718600 | tf_op jit(solution)/shard_map/ppermute | solution.py:287
  6.3 10.4 %collective-permute-start.4 = (bf16[64,2048]{1,0:T(8,128)(2,1)S(1)}, bf16[64,2048]{1,0:T(8,128)(2,1)S(1)}, u32[]{:S(2)}, u32[]{:S(2)}) collective-permute-start(bf16[64,2048]{1,0:T(8,128)(2,1)S(1)} %get-tuple-element.61), channel_id=1, source_target_pairs={{0,32},{16,48},{32,64},{48,80},{64,96},{80,112},{96,0},{112,16},{1... | collective-permute-start | bytes 786440 | tf_op jit(solution)/shard_map/ppermute | solution.py:289
  8.0 9.8 %collective-permute-start.6 = (bf16[64,2048]{1,0:T(8,128)(2,1)S(1)}, bf16[64,2048]{1,0:T(8,128)(2,1)S(1)}, u32[]{:S(2)}, u32[]{:S(2)}) collective-permute-start(bf16[64,2048]{1,0:T(8,128)(2,1)S(1)} %get-tuple-element.63), channel_id=1, source_target_pairs={{0,96},{16,112},{32,0},{48,16},{64,32},{80,48},{96,64},{112,80},{1... | collective-permute-start | bytes 786440 | tf_op jit(solution)/shard_map/ppermute | solution.py:290
  10.5 16.8 %collective-permute-start.2 = (bf16[64,2048]{1,0:T(8,128)(2,1)S(1)}, bf16[64,2048]{1,0:T(8,128)(2,1)S(1)}, u32[]{:S(2)}, u32[]{:S(2)}) collective-permute-start(bf16[64,2048]{1,0:T(8,128)(2,1)S(1)} %get-tuple-element.56), channel_id=1, source_target_pairs={{0,32},{16,48},{32,64},{48,80},{64,96},{80,112},{96,0},{112,16},{1... | collective-permute-start | bytes 786440 | tf_op jit(solution)/shard_map/ppermute | solution.py:295
  11.4 15.9 %collective-permute-start.3 = (bf16[64,2048]{1,0:T(8,128)(2,1)S(1)}, bf16[64,2048]{1,0:T(8,128)(2,1)S(1)}, u32[]{:S(2)}, u32[]{:S(2)}) collective-permute-start(bf16[64,2048]{1,0:T(8,128)(2,1)S(1)} %get-tuple-element.57), channel_id=1, source_target_pairs={{0,96},{16,112},{32,0},{48,16},{64,32},{80,48},{96,64},{112,80},{1... | collective-permute-start | bytes 786440 | tf_op jit(solution)/shard_map/ppermute | solution.py:296
  17.3 10.7 %collective-permute-start.5 = (bf16[64,2048]{1,0:T(8,128)(2,1)S(1)}, bf16[64,2048]{1,0:T(8,128)(2,1)S(1)}, u32[]{:S(2)}, u32[]{:S(2)}) collective-permute-start(bf16[64,2048]{1,0:T(8,128)(2,1)S(1)} %relay.2), channel_id=1, source_target_pairs={{0,32},{16,48},{32,64},{48,80},{64,96},{80,112},{96,0},{112,16},{1... | collective-permute-start | bytes 786440 | tf_op jit(solution)/shard_map/ppermute | solution.py:297
  18.4 9.6 %collective-permute-start.7 = (bf16[64,2048]{1,0:T(8,128)(2,1)S(1)}, bf16[64,2048]{1,0:T(8,128)(2,1)S(1)}, u32[]{:S(2)}, u32[]{:S(2)}) collective-permute-start(bf16[64,2048]{1,0:T(8,128)(2,1)S(1)} %relay.3), channel_id=1, source_target_pairs={{0,96},{16,112},{32,0},{48,16},{64,32},{80,48},{96,64},{112,80},{1... | collective-permute-start | bytes 786440 | tf_op jit(solution)/shard_map/ppermute | solution.py:298
  27.3 8.2 %copy-start = (s32[1,16]{1,0:T(1,128)S(1)}, s32[1,16]{1,0:T(1,128)}, u32[]{:S(2)}) copy-start(s32[1,16]{1,0:T(1,128)} %refs_0_.1) | copy-start | bytes 196
  28.8 8.3 %collective-permute-start.8 = (bf16[32,2176]{1,0:T(8,128)(2,1)S(1)}, bf16[32,2176]{1,0:T(8,128)(2,1)S(1)}, u32[]{:S(2)}, u32[]{:S(2)}) collective-permute-start(bf16[32,2176]{1,0:T(8,128)(2,1)S(1)} %get-tuple-element.72), channel_id=1, source_target_pairs={{0,4},{1,5},{2,6},{3,7},{4,8},{5,9},{6,10},{7,11},{8,12},{9,13},{1... | collective-permute-start | bytes 417800 | tf_op jit(solution)/shard_map/ppermute | solution.py:308
  30.9 9.1 %collective-permute-start.9 = (bf16[32,2176]{1,0:T(8,128)(2,1)S(1)}, bf16[32,2176]{1,0:T(8,128)(2,1)S(1)}, u32[]{:S(2)}, u32[]{:S(2)}) collective-permute-start(bf16[32,2176]{1,0:T(8,128)(2,1)S(1)} %get-tuple-element.73), channel_id=1, source_target_pairs={{0,8},{1,9},{2,10},{3,11},{4,12},{5,13},{6,14},{7,15},{8,0},{9,1},... | collective-permute-start | bytes 417800 | tf_op jit(solution)/shard_map/ppermute | solution.py:308
  34.5 5.5 %collective-permute-start.10 = (bf16[32,2176]{1,0:T(8,128)(2,1)S(1)}, bf16[32,2176]{1,0:T(8,128)(2,1)S(1)}, u32[]{:S(2)}, u32[]{:S(2)}) collective-permute-start(bf16[32,2176]{1,0:T(8,128)(2,1)S(1)} %get-tuple-element.74), channel_id=1, source_target_pairs={{0,12},{1,13},{2,14},{3,15},{4,0},{5,1},{6,2},{7,3},{8,4},{9,5},{1... | collective-permute-start | bytes 417800 | tf_op jit(solution)/shard_map/ppermute | solution.py:308
  41.5 22.2 %all-to-all-start = ((bf16[16,2,32,512]{3,2,1,0:T(8,128)(2,1)}), bf16[16,2,32,512]{3,2,1,0:T(8,128)(2,1)S(1)}, u32[]{:S(2)}, u32[]{:S(2)}) async-start(bf16[16,2,32,512]{3,2,1,0:T(8,128)(2,1)} %bitcast.9), calls=%async_computation | async-start | bytes 2097152 | tf_op jit(solution)/shard_map/all_to_all | solution.py:558
  47.8 1.2 %collective-permute-start.11 = (f32[8,128]{1,0:T(8,128)S(1)}, f32[8,128]{1,0:T(8,128)S(1)}, u32[]{:S(2)}, u32[]{:S(2)}) collective-permute-start(f32[8,128]{1,0:T(8,128)S(1)} %get-tuple-element.75), channel_id=1, source_target_pairs={{0,16},{16,0},{32,48},{48,32},{64,80},{80,64},{96,112},{112,96},{1... | collective-permute-start | bytes 12296 | tf_op jit(solution)/shard_map/ppermute | solution.py:560
  49.0 3.8 %collective-permute-start.14 = (f32[8,128]{1,0:T(8,128)S(1)}, f32[8,128]{1,0:T(8,128)S(1)}, u32[]{:S(2)}, u32[]{:S(2)}) collective-permute-start(f32[8,128]{1,0:T(8,128)S(1)} %add.19), channel_id=1, source_target_pairs={{0,96},{16,112},{32,0},{48,16},{64,32},{80,48},{96,64},{112,80},{1... | collective-permute-start | bytes 12296 | tf_op jit(solution)/shard_map/ppermute | solution.py:560
  51.4 5.1 %collective-permute-start.13 = (f32[8,128]{1,0:T(8,128)S(1)}, f32[8,128]{1,0:T(8,128)S(1)}, u32[]{:S(2)}, u32[]{:S(2)}) collective-permute-start(f32[8,128]{1,0:T(8,128)S(1)} %add.19), channel_id=1, source_target_pairs={{0,64},{16,80},{32,96},{48,112},{64,0},{80,16},{96,32},{112,48},{1... | collective-permute-start | bytes 12296 | tf_op jit(solution)/shard_map/ppermute | solution.py:560
  52.3 4.8 %collective-permute-start.12 = (f32[8,128]{1,0:T(8,128)S(1)}, f32[8,128]{1,0:T(8,128)S(1)}, u32[]{:S(2)}, u32[]{:S(2)}) collective-permute-start(f32[8,128]{1,0:T(8,128)S(1)} %add.19), channel_id=1, source_target_pairs={{0,32},{16,48},{32,64},{48,80},{64,96},{80,112},{96,0},{112,16},{1... | collective-permute-start | bytes 12296 | tf_op jit(solution)/shard_map/ppermute | solution.py:560
  57.1 9.6 %collective-permute-start.17 = (f32[8,128]{1,0:T(8,128)S(1)}, f32[8,128]{1,0:T(8,128)S(1)}, u32[]{:S(2)}, u32[]{:S(2)}) collective-permute-start(f32[8,128]{1,0:T(8,128)S(1)} %add_add_fusion.refs_0_.refs_2_), channel_id=1, source_target_pairs={{0,3},{1,0},{2,1},{3,2},{4,7},{5,4},{6,5},{7,6},{8,11},{9,8},{10,9... | collective-permute-start | bytes 12296 | tf_op jit(solution)/shard_map/ppermute | solution.py:561
  60.2 6.5 %collective-permute-start.16 = (f32[8,128]{1,0:T(8,128)S(1)}, f32[8,128]{1,0:T(8,128)S(1)}, u32[]{:S(2)}, u32[]{:S(2)}) collective-permute-start(f32[8,128]{1,0:T(8,128)S(1)} %add_add_fusion.refs_0_.refs_2_), channel_id=1, source_target_pairs={{0,2},{1,3},{2,0},{3,1},{4,6},{5,7},{6,4},{7,5},{8,10},{9,11},{10,... | collective-permute-start | bytes 12296 | tf_op jit(solution)/shard_map/ppermute | solution.py:561
  61.0 5.7 %collective-permute-start.15 = (f32[8,128]{1,0:T(8,128)S(1)}, f32[8,128]{1,0:T(8,128)S(1)}, u32[]{:S(2)}, u32[]{:S(2)}) collective-permute-start(f32[8,128]{1,0:T(8,128)S(1)} %add_add_fusion.refs_0_.refs_2_), channel_id=1, source_target_pairs={{0,1},{1,2},{2,3},{3,0},{4,5},{5,6},{6,7},{7,4},{8,9},{9,10},{10,1... | collective-permute-start | bytes 12296 | tf_op jit(solution)/shard_map/ppermute | solution.py:561
  91.4 9.3 %collective-permute-start.18 = (bf16[32,2048]{1,0:T(8,128)(2,1)S(1)}, bf16[32,2048]{1,0:T(8,128)(2,1)S(1)}, u32[]{:S(2)}, u32[]{:S(2)}) collective-permute-start(bf16[32,2048]{1,0:T(8,128)(2,1)S(1)} %get-tuple-element.89), channel_id=1, source_target_pairs={{0,4},{1,5},{2,6},{3,7},{4,8},{5,9},{6,10},{7,11},{8,12},{9,13},{1... | collective-permute-start | bytes 393224 | tf_op jit(solution)/shard_map/ppermute | solution.py:308
  91.5 9.2 %collective-permute-start.19 = (bf16[32,2048]{1,0:T(8,128)(2,1)S(1)}, bf16[32,2048]{1,0:T(8,128)(2,1)S(1)}, u32[]{:S(2)}, u32[]{:S(2)}) collective-permute-start(bf16[32,2048]{1,0:T(8,128)(2,1)S(1)} %get-tuple-element.90), channel_id=1, source_target_pairs={{0,8},{1,9},{2,10},{3,11},{4,12},{5,13},{6,14},{7,15},{8,0},{9,1},... | collective-permute-start | bytes 393224 | tf_op jit(solution)/shard_map/ppermute | solution.py:308
  93.9 6.8 %collective-permute-start.20 = (bf16[32,2048]{1,0:T(8,128)(2,1)S(1)}, bf16[32,2048]{1,0:T(8,128)(2,1)S(1)}, u32[]{:S(2)}, u32[]{:S(2)}) collective-permute-start(bf16[32,2048]{1,0:T(8,128)(2,1)S(1)} %get-tuple-element.91), channel_id=1, source_target_pairs={{0,12},{1,13},{2,14},{3,15},{4,0},{5,1},{6,2},{7,3},{8,4},{9,5},{1... | collective-permute-start | bytes 393224 | tf_op jit(solution)/shard_map/ppermute | solution.py:308

commit v8 on v5

--- a/solution.py
+++ b/solution.py
@@ -80,7 +80,8 @@
             half[rows] = (product[rows] + product[more]).astype(bf16)
             head[s, rows], tail[rows] = split(right[s, rows])
         outs[s][2].start()
-        rot[s] = 0.9 * (mm(half[...], head[s]) + mm(half[...], tail[...]))
+        turned = mm(half[...], head[s]) + mm(half[...], tail[...])
+        rot[s] = (0.9 * turned).astype(bf16)
         outs[s][3].start()
     for group in outs:
         for c in group:
@@ -94,11 +95,10 @@
         prepare_body,
         in_specs=[far] * 3,
         out_specs=[far] * 4,
-        out_shape=[HBM((slots, n, n), bf16)] * 3 + [HBM((slots, n, n), f32)],
+        out_shape=[HBM((slots, n, n), bf16)] * 4,
         scratch_shapes=[pltpu.VMEM((slots, n, n), f32)] * 3
-        + [pltpu.VMEM((slots, n, n), bf16)] * 3
+        + [pltpu.VMEM((slots, n, n), bf16)] * 4
         + [
-            pltpu.VMEM((slots, n, n), f32),
             pltpu.VMEM((2 * n, n), bf16),
             pltpu.VMEM((n, n), bf16),
             pltpu.VMEM((n, n), bf16),
@@ -362,7 +362,7 @@
             VMEM((slots, n, n), f32),
             VMEM((slots, n, n), bf16),
             VMEM((1, n, n), bf16),
-            VMEM((1, n, n), f32),
+            VMEM((1, n, n), bf16),
             VMEM((1, n, n), f32),
         ],
         scratch_shapes=[
@@ -401,7 +401,7 @@
                 states = rot.at[0], old.at[0], left.at[0]
             else:
                 states = rot_more.at[s - 1], old_more.at[s - 1], left_more.at[s - 1]
-                for c in copies[s - 1]:
+                for c in copies[s - 1][:2]:
                     c.wait()
             named = is_named(table, me[0] * slots + s)
             for r in tiles(n):
@@ -409,9 +409,11 @@
                 before = states[1][r]
                 value = 0.95 * before + 0.05 * turned * turned
                 new[s, r] = jnp.where(named, value, before)
-                ahead = states[0][r] + 0.1 * turned
+                ahead = states[0][r].astype(f32) + 0.1 * turned
                 step[r] = (ahead * pl.reciprocal(jnp.sqrt(value) + 1e-08, approx=True)).astype(bf16)
             pltpu.make_async_copy(new.at[s], second_out.at[s], sems.at[s]).start()
+            if s > 0:
+                copies[s - 1][2].wait()
             half[...] = mm(states[2][...], step[...]).astype(bf16)
             update = mm(half[...], right[s], ((1,), (1,))).astype(bf16)
             for y in range(per):
@@ -434,7 +436,7 @@
         ],
         scratch_shapes=[
             pltpu.VMEM((slots - 1, n, n), bf16),
-            pltpu.VMEM((slots - 1, n, n), f32),
+            pltpu.VMEM((slots - 1, n, n), bf16),
             pltpu.VMEM((slots - 1, n, n), f32),
             pltpu.VMEM((slots, n, n), f32),
             pltpu.VMEM((n, n), bf16),
@@ -460,15 +462,15 @@
         for s in range(slots)
     ]
     for group in copies:
-        for c in group:
-            c.start()
+        for i in (2, 0, 1):
+            group[i].start()
     scale = clip_of(squares, entries)
     square = 0.1 * scale * scale
     done = []
     for s in range(slots):
         named = is_named(table, me[0] * slots + s)
         block[...] = assemble(pieces, s, bands)
-        for i in range(3):
+        for i in (2, 0, 1):
             if i == 0:
                 product[...] = mm(block[...], block[...], ((1,), (1,)))
             elif i == 1:

time: 102 us -> 102 us (level)
  no operation moved by 1% of the time
where the time goes in v8:
time: 102 us; the launch traced here: 101 us
  starting transfers between devices  35.5 us (35%)
  Pallas kernels  28.5 us (28%)
  blocking collectives  19.1 us (19%)
  waiting for transfers between devices  17 us (17%)
    all_to_all x1, blocking collectives, per_device(): lax.all_to_all(update, 'fsdp', split_axis=0, concat_axis=0, tiled=True)  19.1 us
    ppermute x6, starting transfers between devices, exchange(): got[j] = lax.ppermute(arrays[j], *steps[j - 1])  10.3 us
    pallas_call x9, Pallas kernels, local(): pl.pallas_call(body, in_specs=[pl.BlockSpec(memory_space=SMEM)] + [pl.Blo...  7.66 us
    all_to_all x1, starting transfers between devices, per_device(): lax.all_to_all(sent, 'fsdp', split_axis=0, concat_axis=0, tiled=True)  6.25 us
    pallas_call x1, Pallas kernels, prepare(): pl.pallas_call(prepare_body, in_specs=[far] * 3, out_specs=[far] * 4, out...  5.85 us
    pallas_call x1, Pallas kernels, factors(): pl.pallas_call(body, in_specs=[scalar] * 2 + [whole] * (len(squares) + 1)...  5.67 us
    ppermute x4, waiting for transfers between devices, per_device(): square = sum([lax.ppermute(square, *step) for step in steps], square)  5.38 us
    ppermute x3, starting transfers between devices, per_device(): squares = [square] + [lax.ppermute(square, *step) for step in along_y]  4.77 us
  transfers between devices with their start and end apart: 22, of which 8 were waited for; matrix products, arithmetic and copies ran while one was open for 0% of the time, Pallas kernels for 18%

profile of v8, /device:TPU:0, one launch (start us, length us, event | category | flops | bytes accessed | tf_op | source)
XLA Modules:
  0.0 101.1 jit_solution(6882189165457904328)
XLA Ops:
  0.7 0.1 pad_add_fusion.1.place
  0.7 2.8 %load.1 = (bf16[1,128,2048]{2,1,0:T(8,128)(2,1)S(1)}, bf16[3,128,2048]{2,1,0:T(8,128)(2,1)S(1)}, bf16[1,128,2048]{2,1,0:T(8,128)(2,1)S(1)}, bf16[3,128,2048]{2,1,0:T(8,128)(2,1)S(1)}) custom-call(s32[3]{0:T(128)S(1)} %pad_add_fusion.1.place, bf16[128,16384]{1,0:T(8,128)(2,1)} %bitcast.22), custom_call_target="tpu_custom_call" | custom-call | tf_op jit(solution)/shard_map/load/pallas_call | solution.py:190
  3.5 0.1 collective-permute-start
  3.6 1.9 %collective-permute-done.far = bf16[1,128,2048]{2,1,0:T(8,128)(2,1)S(1)} collective-permute-done((bf16[1,128,2048]{2,1,0:T(8,128)(2,1)S(1)}, bf16[1,128,2048]{2,1,0:T(8,128)(2,1)S(1)}, u32[]{:S(2)}, u32[]{:S(2)}) %collective-permute-start) | collective-permute-done | bytes 524320 | tf_op jit(solution)/shard_map/ppermute | solution.py:285
  5.5 0.1 collective-permute-start.1
  5.7 0.7 pair_far.1
  6.3 1.7 %collective-permute-start.4 = (bf16[64,2048]{1,0:T(8,128)(2,1)S(1)}, bf16[64,2048]{1,0:T(8,128)(2,1)S(1)}, u32[]{:S(2)}, u32[]{:S(2)}) collective-permute-start(bf16[64,2048]{1,0:T(8,128)(2,1)S(1)} %get-tuple-element.61), channel_id=1, source_target_pairs={{0,32},{16,48},{32,64},{48,80},{64,96},{80,112},{96,0},{112,16},{1... | collective-permute-start | bytes 786440 | tf_op jit(solution)/shard_map/ppermute | solution.py:289
  8.0 1.7 %collective-permute-start.6 = (bf16[64,2048]{1,0:T(8,128)(2,1)S(1)}, bf16[64,2048]{1,0:T(8,128)(2,1)S(1)}, u32[]{:S(2)}, u32[]{:S(2)}) collective-permute-start(bf16[64,2048]{1,0:T(8,128)(2,1)S(1)} %get-tuple-element.63), channel_id=1, source_target_pairs={{0,96},{16,112},{32,0},{48,16},{64,32},{80,48},{96,64},{112,80},{1... | collective-permute-start | bytes 786440 | tf_op jit(solution)/shard_map/ppermute | solution.py:290
  9.6 0.9 pair_near.1
  10.5 0.9 collective-permute-start.2
  11.4 2.4 %collective-permute-start.3 = (bf16[64,2048]{1,0:T(8,128)(2,1)S(1)}, bf16[64,2048]{1,0:T(8,128)(2,1)S(1)}, u32[]{:S(2)}, u32[]{:S(2)}) collective-permute-start(bf16[64,2048]{1,0:T(8,128)(2,1)S(1)} %get-tuple-element.57), channel_id=1, source_target_pairs={{0,96},{16,112},{32,0},{48,16},{64,32},{80,48},{96,64},{112,80},{1... | collective-permute-start | bytes 786440 | tf_op jit(solution)/shard_map/ppermute | solution.py:296
  13.8 2.9 %collective-permute-done.4.arrived = bf16[64,2048]{1,0:T(8,128)(2,1)S(1)} collective-permute-done((bf16[64,2048]{1,0:T(8,128)(2,1)S(1)}, bf16[64,2048]{1,0:T(8,128)(2,1)S(1)}, u32[]{:S(2)}, u32[]{:S(2)}) %collective-permute-start.4) | collective-permute-done | bytes 262176 | tf_op jit(solution)/shard_map/ppermute | solution.py:289
  16.7 0.6 relay.2
  17.3 0.4 collective-permute-start.5
  17.8 0.6 relay.3
  18.4 2.9 %collective-permute-start.7 = (bf16[64,2048]{1,0:T(8,128)(2,1)S(1)}, bf16[64,2048]{1,0:T(8,128)(2,1)S(1)}, u32[]{:S(2)}, u32[]{:S(2)}) collective-permute-start(bf16[64,2048]{1,0:T(8,128)(2,1)S(1)} %relay.3), channel_id=1, source_target_pairs={{0,96},{16,112},{32,0},{48,16},{64,32},{80,48},{96,64},{112,80},{1... | collective-permute-start | bytes 786440 | tf_op jit(solution)/shard_map/ppermute | solution.py:298
  21.3 5.8 %prepare.1 = (bf16[2,512,512]{2,1,0:T(8,128)(2,1)}, bf16[2,512,512]{2,1,0:T(8,128)(2,1)}, bf16[2,512,512]{2,1,0:T(8,128)(2,1)}, bf16[2,512,512]{2,1,0:T(8,128)(2,1)}) custom-call(f32[2,512,512]{2,1,0:T(8,128)} %bitcast.28, f32[2,512,512]{2,1,0:T(8,128)} %bitcast.29, f32[2,512,512]{2,1,0:T(8,128)} %bitcast.23), custom_call_target="tpu_custom_call" | custom-call | flops 2147483648 | bytes 11534336 | tf_op jit(solution)/shard_map/prepare/pallas_call | solution.py:94
  27.2 0.0 copy-start
  27.2 0.6 direct.1.own
  27.8 0.8 finish.1
  28.7 2.1 %collective-permute-start.8 = (bf16[32,2176]{1,0:T(8,128)(2,1)S(1)}, bf16[32,2176]{1,0:T(8,128)(2,1)S(1)}, u32[]{:S(2)}, u32[]{:S(2)}) collective-permute-start(bf16[32,2176]{1,0:T(8,128)(2,1)S(1)} %get-tuple-element.72), channel_id=1, source_target_pairs={{0,4},{1,5},{2,6},{3,7},{4,8},{5,9},{6,10},{7,11},{8,12},{9,13},{1... | collective-permute-start | bytes 417800 | tf_op jit(solution)/shard_map/ppermute | solution.py:308
  30.7 3.6 %collective-permute-start.9 = (bf16[32,2176]{1,0:T(8,128)(2,1)S(1)}, bf16[32,2176]{1,0:T(8,128)(2,1)S(1)}, u32[]{:S(2)}, u32[]{:S(2)}) collective-permute-start(bf16[32,2176]{1,0:T(8,128)(2,1)S(1)} %get-tuple-element.73), channel_id=1, source_target_pairs={{0,8},{1,9},{2,10},{3,11},{4,12},{5,13},{6,14},{7,15},{8,0},{9,1},... | collective-permute-start | bytes 417800 | tf_op jit(solution)/shard_map/ppermute | solution.py:308
  34.3 1.0 collective-permute-start.10
  35.3 0.1 pad_add_fusion.table
  35.4 1.3 %collective-permute-done.8.refs_1_ = bf16[32,2176]{1,0:T(8,128)(2,1)S(1)} collective-permute-done((bf16[32,2176]{1,0:T(8,128)(2,1)S(1)}, bf16[32,2176]{1,0:T(8,128)(2,1)S(1)}, u32[]{:S(2)}, u32[]{:S(2)}) %collective-permute-start.8) | collective-permute-done | bytes 139296 | tf_op jit(solution)/shard_map/ppermute | solution.py:308
  36.7 3.3 %collective-permute-done.9.refs_2_ = bf16[32,2176]{1,0:T(8,128)(2,1)S(1)} collective-permute-done((bf16[32,2176]{1,0:T(8,128)(2,1)S(1)}, bf16[32,2176]{1,0:T(8,128)(2,1)S(1)}, u32[]{:S(2)}, u32[]{:S(2)}) %collective-permute-start.9) | collective-permute-done | bytes 139296 | tf_op jit(solution)/shard_map/ppermute | solution.py:308
  40.0 1.6 %dispatch.1 = (bf16[32,32,512]{2,1,0:T(8,128)(2,1)}, f32[8,128]{1,0:T(8,128)S(1)}) custom-call(s32[1,17]{1,0:T(1,128)S(1)} %pad_add_fusion.table, bf16[32,2176]{1,0:T(8,128)(2,1)S(1)} %get-tuple-element.71.refs_0_, bf16[32,2176]{1,0:T(8,128)(2,1)S(1)} %collective-permute-done.8.refs_1_, bf16[32,2176]{1,0:T(8,128)(2,1)S(1)} %collective-permute-done.9.refs_2_, ...), custom_call_target="tpu_custom_call" | custom-call | tf_op jit(solution)/shard_map/dispatch/pallas_call | solution.py:118
  41.5 6.2 %all-to-all-start = ((bf16[16,2,32,512]{3,2,1,0:T(8,128)(2,1)}), bf16[16,2,32,512]{3,2,1,0:T(8,128)(2,1)S(1)}, u32[]{:S(2)}, u32[]{:S(2)}) async-start(bf16[16,2,32,512]{3,2,1,0:T(8,128)(2,1)} %bitcast.9), calls=%async_computation | async-start | bytes 2097152 | tf_op jit(solution)/shard_map/all_to_all | solution.py:559
  47.8 0.1 collective-permute-start.11
  47.9 1.2 %collective-permute-done.11 = f32[8,128]{1,0:T(8,128)S(1)} collective-permute-done((f32[8,128]{1,0:T(8,128)S(1)}, f32[8,128]{1,0:T(8,128)S(1)}, u32[]{:S(2)}, u32[]{:S(2)}) %collective-permute-start.11) | collective-permute-done | bytes 4128 | tf_op jit(solution)/shard_map/ppermute | solution.py:561
  49.0 2.3 %collective-permute-start.14 = (f32[8,128]{1,0:T(8,128)S(1)}, f32[8,128]{1,0:T(8,128)S(1)}, u32[]{:S(2)}, u32[]{:S(2)}) collective-permute-start(f32[8,128]{1,0:T(8,128)S(1)} %add.19), channel_id=1, source_target_pairs={{0,96},{16,112},{32,0},{48,16},{64,32},{80,48},{96,64},{112,80},{1... | collective-permute-start | bytes 12296 | tf_op jit(solution)/shard_map/ppermute | solution.py:561
  51.4 0.9 collective-permute-start.13
  52.3 0.6 collective-permute-start.12
  52.9 3.6 %collective-permute-done.13 = f32[8,128]{1,0:T(8,128)S(1)} collective-permute-done((f32[8,128]{1,0:T(8,128)S(1)}, f32[8,128]{1,0:T(8,128)S(1)}, u32[]{:S(2)}, u32[]{:S(2)}) %collective-permute-start.13) | collective-permute-done | bytes 4128 | tf_op jit(solution)/shard_map/ppermute | solution.py:561
  56.5 0.6 collective-permute-done.12
  57.1 3.1 %collective-permute-start.17 = (f32[8,128]{1,0:T(8,128)S(1)}, f32[8,128]{1,0:T(8,128)S(1)}, u32[]{:S(2)}, u32[]{:S(2)}) collective-permute-start(f32[8,128]{1,0:T(8,128)S(1)} %add_add_fusion.refs_0_.refs_2_), channel_id=1, source_target_pairs={{0,3},{1,0},{2,1},{3,2},{4,7},{5,4},{6,5},{7,6},{8,11},{9,8},{10,9... | collective-permute-start | bytes 12296 | tf_op jit(solution)/shard_map/ppermute | solution.py:562
  60.2 0.9 collective-permute-start.16
  61.0 0.9 collective-permute-start.15
  61.9 2.2 %all-to-all-done.pieces.refs_6_ = bf16[16,2,32,512]{3,2,1,0:T(8,128)(2,1)S(1)} async-done(((bf16[16,2,32,512]{3,2,1,0:T(8,128)(2,1)}), bf16[16,2,32,512]{3,2,1,0:T(8,128)(2,1)S(1)}, u32[]{:S(2)}, u32[]{:S(2)}) %all-to-all-start) | async-done | bytes 1048608 | tf_op jit(solution)/shard_map/all_to_all | solution.py:559
  64.1 2.9 %rotate.1 = (f32[2,512,512]{2,1,0:T(8,128)S(1)}, bf16[2,512,512]{2,1,0:T(8,128)(2,1)S(1)}, bf16[1,512,512]{2,1,0:T(8,128)(2,1)S(1)}, bf16[1,512,512]{2,1,0:T(8,128)(2,1)S(1)}, f32[1,512,512]{2,1,0:T(8,128)S(1)}) custom-call(bf16[16,2,32,512]{3,2,1,0:T(8,128)(2,1)S(1)} %all-to-all-done.pieces.refs_6_, bf16[2,512,512]{2,1,0:T(8,128)(2,1)} %get-tuple-element.77.lt_src, ...), custom_call_target="tpu_custom_call" | custom-call | tf_op jit(solution)/shard_map/rotate/pallas_call | solution.py:357
  67.0 3.6 %direction.1 = (bf16[16,2,32,512]{3,2,1,0:T(8,128)(2,1)S(1)}, f32[2,512,512]{2,1,0:T(8,128)}) custom-call(s32[1,16]{1,0:T(1,128)S(1)} %copy-done, s32[1]{0:T(128)} %bitcast.1.me.refs_1_, f32[8,128]{1,0:T(8,128)S(1)} %add_add_fusion.refs_0_.refs_2_, f32[8,128]{1,0:T(8,128)S(1)} %collective-permute-done.15.refs_1_.refs_3_, ...), custom_call_target="tpu_custom_call" | custom-call | tf_op jit(solution)/shard_map/direction/pallas_call | solution.py:429
  70.7 19.1 %all_to_all.10 = bf16[16,2,32,512]{3,2,1,0:T(8,128)(2,1)S(1)} all-to-all(bf16[16,2,32,512]{3,2,1,0:T(8,128)(2,1)S(1)} %get-tuple-element.86), channel_id=1, replica_groups=mesh['dp'=8,'fsdp'=16] {'fsdp'}, dimensions={0} | all-to-all | bytes 2097152 | tf_op jit(solution)/shard_map/all_to_all | solution.py:567
  89.7 0.6 collect.1
  90.3 0.1 collective-permute-start.18
  90.4 2.4 %collective-permute-start.19 = (bf16[32,2048]{1,0:T(8,128)(2,1)S(1)}, bf16[32,2048]{1,0:T(8,128)(2,1)S(1)}, u32[]{:S(2)}, u32[]{:S(2)}) collective-permute-start(bf16[32,2048]{1,0:T(8,128)(2,1)S(1)} %get-tuple-element.90), channel_id=1, source_target_pairs={{0,8},{1,9},{2,10},{3,11},{4,12},{5,13},{6,14},{7,15},{8,0},{9,1},... | collective-permute-start | bytes 393224 | tf_op jit(solution)/shard_map/ppermute | solution.py:308
  92.8 1.2 %collective-permute-start.20 = (bf16[32,2048]{1,0:T(8,128)(2,1)S(1)}, bf16[32,2048]{1,0:T(8,128)(2,1)S(1)}, u32[]{:S(2)}, u32[]{:S(2)}) collective-permute-start(bf16[32,2048]{1,0:T(8,128)(2,1)S(1)} %get-tuple-element.91), channel_id=1, source_target_pairs={{0,12},{1,13},{2,14},{3,15},{4,0},{5,1},{6,2},{7,3},{8,4},{9,5},{1... | collective-permute-start | bytes 393224 | tf_op jit(solution)/shard_map/ppermute | solution.py:308
  94.0 5.7 %factors.1 = (f32[2,512,512]{2,1,0:T(8,128)}, f32[2,512,512]{2,1,0:T(8,128)}, f32[2,512,512]{2,1,0:T(8,128)}) custom-call(s32[1,16]{1,0:T(1,128)S(1)} %copy-done, s32[1]{0:T(128)} %bitcast.1.me.refs_1_, f32[8,128]{1,0:T(8,128)S(1)} %add_add_fusion.refs_0_.refs_2_, f32[8,128]{1,0:T(8,128)S(1)} %collective-permute-done.15.refs_1_.refs_3_, ...), custom_call_target="tpu_custom_call" | custom-call | flops 1073741824 | bytes 13631488 | tf_op jit(solution)/shard_map/factors/pallas_call | solution.py:498
  99.7 1.4 %put.1 = bf16[4,32,2048]{2,1,0:T(8,128)(2,1)} custom-call(s32[1,17]{1,0:T(1,128)S(1)} %pad_add_fusion.table, bf16[32,2048]{1,0:T(8,128)(2,1)S(1)} %get-tuple-element.88.refs_0_, bf16[32,2048]{1,0:T(8,128)(2,1)S(1)} %collective-permute-done.18.refs_1_, bf16[32,2048]{1,0:T(8,128)(2,1)S(1)} %collective-permute-done.19.refs_2_, ...), custom_call_target="tpu_custom_call" | custom-call | tf_op jit(solution)/shard_map/put/pallas_call | solution.py:118
  (17 shorter events, 0.0 us)
Async XLA Ops:
  3.5 2.0 %collective-permute-start = (bf16[1,128,2048]{2,1,0:T(8,128)(2,1)S(1)}, bf16[1,128,2048]{2,1,0:T(8,128)(2,1)S(1)}, u32[]{:S(2)}, u32[]{:S(2)}) collective-permute-start(bf16[1,128,2048]{2,1,0:T(8,128)(2,1)S(1)} %get-tuple-element.52), channel_id=1, source_target_pairs={{0,16},{16,0},{32,48},{48,32},{64,80},{80,64},{96,112},{112,96},{1... | collective-permute-start | bytes 1572872 | tf_op jit(solution)/shard_map/ppermute | solution.py:285
  5.5 4.1 %collective-permute-start.1 = (bf16[3,128,2048]{2,1,0:T(8,128)(2,1)S(1)}, bf16[3,128,2048]{2,1,0:T(8,128)(2,1)S(1)}, u32[]{:S(2)}, u32[]{:S(2)}) collective-permute-start(bf16[3,128,2048]{2,1,0:T(8,128)(2,1)S(1)} %get-tuple-element.54), channel_id=1, source_target_pairs={{0,16},{16,0},{32,48},{48,32},{64,80},{80,64},{96,112},{112,96},{1... | collective-permute-start | bytes 4718600 | tf_op jit(solution)/shard_map/ppermute | solution.py:287
  6.3 10.4 %collective-permute-start.4 = (bf16[64,2048]{1,0:T(8,128)(2,1)S(1)}, bf16[64,2048]{1,0:T(8,128)(2,1)S(1)}, u32[]{:S(2)}, u32[]{:S(2)}) collective-permute-start(bf16[64,2048]{1,0:T(8,128)(2,1)S(1)} %get-tuple-element.61), channel_id=1, source_target_pairs={{0,32},{16,48},{32,64},{48,80},{64,96},{80,112},{96,0},{112,16},{1... | collective-permute-start | bytes 786440 | tf_op jit(solution)/shard_map/ppermute | solution.py:289
  8.0 9.8 %collective-permute-start.6 = (bf16[64,2048]{1,0:T(8,128)(2,1)S(1)}, bf16[64,2048]{1,0:T(8,128)(2,1)S(1)}, u32[]{:S(2)}, u32[]{:S(2)}) collective-permute-start(bf16[64,2048]{1,0:T(8,128)(2,1)S(1)} %get-tuple-element.63), channel_id=1, source_target_pairs={{0,96},{16,112},{32,0},{48,16},{64,32},{80,48},{96,64},{112,80},{1... | collective-permute-start | bytes 786440 | tf_op jit(solution)/shard_map/ppermute | solution.py:290
  10.5 16.6 %collective-permute-start.2 = (bf16[64,2048]{1,0:T(8,128)(2,1)S(1)}, bf16[64,2048]{1,0:T(8,128)(2,1)S(1)}, u32[]{:S(2)}, u32[]{:S(2)}) collective-permute-start(bf16[64,2048]{1,0:T(8,128)(2,1)S(1)} %get-tuple-element.56), channel_id=1, source_target_pairs={{0,32},{16,48},{32,64},{48,80},{64,96},{80,112},{96,0},{112,16},{1... | collective-permute-start | bytes 786440 | tf_op jit(solution)/shard_map/ppermute | solution.py:295
  11.4 15.7 %collective-permute-start.3 = (bf16[64,2048]{1,0:T(8,128)(2,1)S(1)}, bf16[64,2048]{1,0:T(8,128)(2,1)S(1)}, u32[]{:S(2)}, u32[]{:S(2)}) collective-permute-start(bf16[64,2048]{1,0:T(8,128)(2,1)S(1)} %get-tuple-element.57), channel_id=1, source_target_pairs={{0,96},{16,112},{32,0},{48,16},{64,32},{80,48},{96,64},{112,80},{1... | collective-permute-start | bytes 786440 | tf_op jit(solution)/shard_map/ppermute | solution.py:296
  17.3 10.5 %collective-permute-start.5 = (bf16[64,2048]{1,0:T(8,128)(2,1)S(1)}, bf16[64,2048]{1,0:T(8,128)(2,1)S(1)}, u32[]{:S(2)}, u32[]{:S(2)}) collective-permute-start(bf16[64,2048]{1,0:T(8,128)(2,1)S(1)} %relay.2), channel_id=1, source_target_pairs={{0,32},{16,48},{32,64},{48,80},{64,96},{80,112},{96,0},{112,16},{1... | collective-permute-start | bytes 786440 | tf_op jit(solution)/shard_map/ppermute | solution.py:297
  18.4 9.5 %collective-permute-start.7 = (bf16[64,2048]{1,0:T(8,128)(2,1)S(1)}, bf16[64,2048]{1,0:T(8,128)(2,1)S(1)}, u32[]{:S(2)}, u32[]{:S(2)}) collective-permute-start(bf16[64,2048]{1,0:T(8,128)(2,1)S(1)} %relay.3), channel_id=1, source_target_pairs={{0,96},{16,112},{32,0},{48,16},{64,32},{80,48},{96,64},{112,80},{1... | collective-permute-start | bytes 786440 | tf_op jit(solution)/shard_map/ppermute | solution.py:298
  27.2 8.2 %copy-start = (s32[1,16]{1,0:T(1,128)S(1)}, s32[1,16]{1,0:T(1,128)}, u32[]{:S(2)}) copy-start(s32[1,16]{1,0:T(1,128)} %refs_0_.1) | copy-start | bytes 196
  28.7 8.0 %collective-permute-start.8 = (bf16[32,2176]{1,0:T(8,128)(2,1)S(1)}, bf16[32,2176]{1,0:T(8,128)(2,1)S(1)}, u32[]{:S(2)}, u32[]{:S(2)}) collective-permute-start(bf16[32,2176]{1,0:T(8,128)(2,1)S(1)} %get-tuple-element.72), channel_id=1, source_target_pairs={{0,4},{1,5},{2,6},{3,7},{4,8},{5,9},{6,10},{7,11},{8,12},{9,13},{1... | collective-permute-start | bytes 417800 | tf_op jit(solution)/shard_map/ppermute | solution.py:308
  30.7 9.2 %collective-permute-start.9 = (bf16[32,2176]{1,0:T(8,128)(2,1)S(1)}, bf16[32,2176]{1,0:T(8,128)(2,1)S(1)}, u32[]{:S(2)}, u32[]{:S(2)}) collective-permute-start(bf16[32,2176]{1,0:T(8,128)(2,1)S(1)} %get-tuple-element.73), channel_id=1, source_target_pairs={{0,8},{1,9},{2,10},{3,11},{4,12},{5,13},{6,14},{7,15},{8,0},{9,1},... | collective-permute-start | bytes 417800 | tf_op jit(solution)/shard_map/ppermute | solution.py:308
  34.3 5.7 %collective-permute-start.10 = (bf16[32,2176]{1,0:T(8,128)(2,1)S(1)}, bf16[32,2176]{1,0:T(8,128)(2,1)S(1)}, u32[]{:S(2)}, u32[]{:S(2)}) collective-permute-start(bf16[32,2176]{1,0:T(8,128)(2,1)S(1)} %get-tuple-element.74), channel_id=1, source_target_pairs={{0,12},{1,13},{2,14},{3,15},{4,0},{5,1},{6,2},{7,3},{8,4},{9,5},{1... | collective-permute-start | bytes 417800 | tf_op jit(solution)/shard_map/ppermute | solution.py:308
  41.5 22.6 %all-to-all-start = ((bf16[16,2,32,512]{3,2,1,0:T(8,128)(2,1)}), bf16[16,2,32,512]{3,2,1,0:T(8,128)(2,1)S(1)}, u32[]{:S(2)}, u32[]{:S(2)}) async-start(bf16[16,2,32,512]{3,2,1,0:T(8,128)(2,1)} %bitcast.9), calls=%async_computation | async-start | bytes 2097152 | tf_op jit(solution)/shard_map/all_to_all | solution.py:559
  47.8 1.2 %collective-permute-start.11 = (f32[8,128]{1,0:T(8,128)S(1)}, f32[8,128]{1,0:T(8,128)S(1)}, u32[]{:S(2)}, u32[]{:S(2)}) collective-permute-start(f32[8,128]{1,0:T(8,128)S(1)} %get-tuple-element.75), channel_id=1, source_target_pairs={{0,16},{16,0},{32,48},{48,32},{64,80},{80,64},{96,112},{112,96},{1... | collective-permute-start | bytes 12296 | tf_op jit(solution)/shard_map/ppermute | solution.py:561
  49.0 3.8 %collective-permute-start.14 = (f32[8,128]{1,0:T(8,128)S(1)}, f32[8,128]{1,0:T(8,128)S(1)}, u32[]{:S(2)}, u32[]{:S(2)}) collective-permute-start(f32[8,128]{1,0:T(8,128)S(1)} %add.19), channel_id=1, source_target_pairs={{0,96},{16,112},{32,0},{48,16},{64,32},{80,48},{96,64},{112,80},{1... | collective-permute-start | bytes 12296 | tf_op jit(solution)/shard_map/ppermute | solution.py:561
  51.4 5.1 %collective-permute-start.13 = (f32[8,128]{1,0:T(8,128)S(1)}, f32[8,128]{1,0:T(8,128)S(1)}, u32[]{:S(2)}, u32[]{:S(2)}) collective-permute-start(f32[8,128]{1,0:T(8,128)S(1)} %add.19), channel_id=1, source_target_pairs={{0,64},{16,80},{32,96},{48,112},{64,0},{80,16},{96,32},{112,48},{1... | collective-permute-start | bytes 12296 | tf_op jit(solution)/shard_map/ppermute | solution.py:561
  52.3 4.8 %collective-permute-start.12 = (f32[8,128]{1,0:T(8,128)S(1)}, f32[8,128]{1,0:T(8,128)S(1)}, u32[]{:S(2)}, u32[]{:S(2)}) collective-permute-start(f32[8,128]{1,0:T(8,128)S(1)} %add.19), channel_id=1, source_target_pairs={{0,32},{16,48},{32,64},{48,80},{64,96},{80,112},{96,0},{112,16},{1... | collective-permute-start | bytes 12296 | tf_op jit(solution)/shard_map/ppermute | solution.py:561
  57.1 9.9 %collective-permute-start.17 = (f32[8,128]{1,0:T(8,128)S(1)}, f32[8,128]{1,0:T(8,128)S(1)}, u32[]{:S(2)}, u32[]{:S(2)}) collective-permute-start(f32[8,128]{1,0:T(8,128)S(1)} %add_add_fusion.refs_0_.refs_2_), channel_id=1, source_target_pairs={{0,3},{1,0},{2,1},{3,2},{4,7},{5,4},{6,5},{7,6},{8,11},{9,8},{10,9... | collective-permute-start | bytes 12296 | tf_op jit(solution)/shard_map/ppermute | solution.py:562
  60.2 6.8 %collective-permute-start.16 = (f32[8,128]{1,0:T(8,128)S(1)}, f32[8,128]{1,0:T(8,128)S(1)}, u32[]{:S(2)}, u32[]{:S(2)}) collective-permute-start(f32[8,128]{1,0:T(8,128)S(1)} %add_add_fusion.refs_0_.refs_2_), channel_id=1, source_target_pairs={{0,2},{1,3},{2,0},{3,1},{4,6},{5,7},{6,4},{7,5},{8,10},{9,11},{10,... | collective-permute-start | bytes 12296 | tf_op jit(solution)/shard_map/ppermute | solution.py:562
  61.0 6.0 %collective-permute-start.15 = (f32[8,128]{1,0:T(8,128)S(1)}, f32[8,128]{1,0:T(8,128)S(1)}, u32[]{:S(2)}, u32[]{:S(2)}) collective-permute-start(f32[8,128]{1,0:T(8,128)S(1)} %add_add_fusion.refs_0_.refs_2_), channel_id=1, source_target_pairs={{0,1},{1,2},{2,3},{3,0},{4,5},{5,6},{6,7},{7,4},{8,9},{9,10},{10,1... | collective-permute-start | bytes 12296 | tf_op jit(solution)/shard_map/ppermute | solution.py:562
  90.3 9.3 %collective-permute-start.18 = (bf16[32,2048]{1,0:T(8,128)(2,1)S(1)}, bf16[32,2048]{1,0:T(8,128)(2,1)S(1)}, u32[]{:S(2)}, u32[]{:S(2)}) collective-permute-start(bf16[32,2048]{1,0:T(8,128)(2,1)S(1)} %get-tuple-element.89), channel_id=1, source_target_pairs={{0,4},{1,5},{2,6},{3,7},{4,8},{5,9},{6,10},{7,11},{8,12},{9,13},{1... | collective-permute-start | bytes 393224 | tf_op jit(solution)/shard_map/ppermute | solution.py:308
  90.4 9.3 %collective-permute-start.19 = (bf16[32,2048]{1,0:T(8,128)(2,1)S(1)}, bf16[32,2048]{1,0:T(8,128)(2,1)S(1)}, u32[]{:S(2)}, u32[]{:S(2)}) collective-permute-start(bf16[32,2048]{1,0:T(8,128)(2,1)S(1)} %get-tuple-element.90), channel_id=1, source_target_pairs={{0,8},{1,9},{2,10},{3,11},{4,12},{5,13},{6,14},{7,15},{8,0},{9,1},... | collective-permute-start | bytes 393224 | tf_op jit(solution)/shard_map/ppermute | solution.py:308
  92.8 6.9 %collective-permute-start.20 = (bf16[32,2048]{1,0:T(8,128)(2,1)S(1)}, bf16[32,2048]{1,0:T(8,128)(2,1)S(1)}, u32[]{:S(2)}, u32[]{:S(2)}) collective-permute-start(bf16[32,2048]{1,0:T(8,128)(2,1)S(1)} %get-tuple-element.91), channel_id=1, source_target_pairs={{0,12},{1,13},{2,14},{3,15},{4,0},{5,1},{6,2},{7,3},{8,4},{9,5},{1... | collective-permute-start | bytes 393224 | tf_op jit(solution)/shard_map/ppermute | solution.py:308

commit v9 on v6

--- a/solution.py
+++ b/solution.py
@@ -80,7 +80,8 @@
             half[rows] = (product[rows] + product[more]).astype(bf16)
             head[s, rows], tail[rows] = split(right[s, rows])
         outs[s][2].start()
-        rot[s] = 0.9 * (mm(half[...], head[s]) + mm(half[...], tail[...]))
+        turned = mm(half[...], head[s]) + mm(half[...], tail[...])
+        rot[s] = (0.9 * turned).astype(bf16)
         outs[s][3].start()
     for group in outs:
         for c in group:
@@ -94,11 +95,10 @@
         prepare_body,
         in_specs=[far] * 3,
         out_specs=[far] * 4,
-        out_shape=[HBM((slots, n, n), bf16)] * 3 + [HBM((slots, n, n), f32)],
+        out_shape=[HBM((slots, n, n), bf16)] * 4,
         scratch_shapes=[pltpu.VMEM((slots, n, n), f32)] * 3
-        + [pltpu.VMEM((slots, n, n), bf16)] * 3
+        + [pltpu.VMEM((slots, n, n), bf16)] * 4
         + [
-            pltpu.VMEM((slots, n, n), f32),
             pltpu.VMEM((2 * n, n), bf16),
             pltpu.VMEM((n, n), bf16),
             pltpu.VMEM((n, n), bf16),
@@ -364,7 +364,7 @@
             VMEM((slots, n, n), f32),
             VMEM((slots, n, n), bf16),
             VMEM((slots, n, n), bf16),
-            VMEM((slots, n, n), f32),
+            VMEM((slots, n, n), bf16),
             VMEM((slots, n, n), f32),
         ],
         scratch_shapes=[
@@ -393,7 +393,7 @@
                 before = old[s, r]
                 value = 0.95 * before + 0.05 * turned * turned
                 new[s, r] = jnp.where(named, value, before)
-                ahead = rot[s, r] + 0.1 * turned
+                ahead = rot[s, r].astype(f32) + 0.1 * turned
                 step[r] = (ahead * pl.reciprocal(jnp.sqrt(value) + 1e-08, approx=True)).astype(bf16)
             pltpu.make_async_copy(new.at[s], second_out.at[s], sems.at[s]).start()
             half[...] = mm(left[s], step[...]).astype(bf16)

time: 102 us -> 101 us (level)
  no operation moved by 1% of the time
where the time goes in v9:
time: 101 us
  starting transfers between devices  34.9 us (35%)
  Pallas kernels  28 us (28%)
  waiting for transfers between devices  19.5 us (19%)
  blocking collectives  17.7 us (18%)
    all_to_all x1, blocking collectives, per_device(): lax.all_to_all(update, 'fsdp', split_axis=0, concat_axis=0, tiled=True)  17.7 us
    ppermute x6, starting transfers between devices, exchange(): got[j] = lax.ppermute(arrays[j], *steps[j - 1])  9.63 us
    pallas_call x9, Pallas kernels, local(): pl.pallas_call(body, in_specs=[pl.BlockSpec(memory_space=SMEM)] + [pl.Blo...  7.67 us
    ppermute x6, waiting for transfers between devices, exchange(): got[j] = lax.ppermute(arrays[j], *steps[j - 1])  6.28 us
    ppermute x3, starting transfers between devices, per_device(): squares = [square] + [lax.ppermute(square, *step) for step in along_y]  5.98 us
    pallas_call x1, Pallas kernels, prepare(): pl.pallas_call(prepare_body, in_specs=[far] * 3, out_specs=[far] * 4, out...  5.86 us
    all_to_all x1, starting transfers between devices, per_device(): lax.all_to_all(sent, 'fsdp', split_axis=0, concat_axis=0, tiled=True)  5.59 us
    pallas_call x1, Pallas kernels, factors(): pl.pallas_call(body, in_specs=[scalar] * 2 + [whole] * (len(squares) + 1)...  5.58 us
  transfers between devices with their start and end apart: 22, of which 10 were waited for; matrix products, arithmetic and copies ran while one was open for 0% of the time, Pallas kernels for 18%

profile of v9, /device:TPU:0, one launch (start us, length us, event | category | flops | bytes accessed | tf_op | source)
XLA Modules:
  0.0 101.1 jit_solution(15917888518489579234)
XLA Ops:
  0.7 0.1 pad_add_fusion.1.place
  0.7 2.8 %load.1 = (bf16[1,128,2048]{2,1,0:T(8,128)(2,1)S(1)}, bf16[3,128,2048]{2,1,0:T(8,128)(2,1)S(1)}, bf16[1,128,2048]{2,1,0:T(8,128)(2,1)S(1)}, bf16[3,128,2048]{2,1,0:T(8,128)(2,1)S(1)}) custom-call(s32[3]{0:T(128)S(1)} %pad_add_fusion.1.place, bf16[128,16384]{1,0:T(8,128)(2,1)} %bitcast.20), custom_call_target="tpu_custom_call" | custom-call | tf_op jit(solution)/shard_map/load/pallas_call | solution.py:190
  3.5 0.1 collective-permute-start
  3.6 1.9 %collective-permute-done.far = bf16[1,128,2048]{2,1,0:T(8,128)(2,1)S(1)} collective-permute-done((bf16[1,128,2048]{2,1,0:T(8,128)(2,1)S(1)}, bf16[1,128,2048]{2,1,0:T(8,128)(2,1)S(1)}, u32[]{:S(2)}, u32[]{:S(2)}) %collective-permute-start) | collective-permute-done | bytes 524320 | tf_op jit(solution)/shard_map/ppermute | solution.py:285
  5.5 0.1 collective-permute-start.1
  5.7 0.7 pair_far.1
  6.3 2.9 %collective-permute-start.6 = (bf16[64,2048]{1,0:T(8,128)(2,1)S(1)}, bf16[64,2048]{1,0:T(8,128)(2,1)S(1)}, u32[]{:S(2)}, u32[]{:S(2)}) collective-permute-start(bf16[64,2048]{1,0:T(8,128)(2,1)S(1)} %get-tuple-element.63), channel_id=1, source_target_pairs={{0,96},{16,112},{32,0},{48,16},{64,32},{80,48},{96,64},{112,80},{1... | collective-permute-start | bytes 786440 | tf_op jit(solution)/shard_map/ppermute | solution.py:290
  9.2 0.0 collective-permute-start.4
  9.2 0.9 pair_near.1
  10.1 1.3 %collective-permute-start.2 = (bf16[64,2048]{1,0:T(8,128)(2,1)S(1)}, bf16[64,2048]{1,0:T(8,128)(2,1)S(1)}, u32[]{:S(2)}, u32[]{:S(2)}) collective-permute-start(bf16[64,2048]{1,0:T(8,128)(2,1)S(1)} %get-tuple-element.56), channel_id=1, source_target_pairs={{0,32},{16,48},{32,64},{48,80},{64,96},{80,112},{96,0},{112,16},{1... | collective-permute-start | bytes 786440 | tf_op jit(solution)/shard_map/ppermute | solution.py:295
  11.4 2.1 %collective-permute-start.3 = (bf16[64,2048]{1,0:T(8,128)(2,1)S(1)}, bf16[64,2048]{1,0:T(8,128)(2,1)S(1)}, u32[]{:S(2)}, u32[]{:S(2)}) collective-permute-start(bf16[64,2048]{1,0:T(8,128)(2,1)S(1)} %get-tuple-element.57), channel_id=1, source_target_pairs={{0,96},{16,112},{32,0},{48,16},{64,32},{80,48},{96,64},{112,80},{1... | collective-permute-start | bytes 786440 | tf_op jit(solution)/shard_map/ppermute | solution.py:296
  13.5 2.4 %collective-permute-done.6.arrived = bf16[64,2048]{1,0:T(8,128)(2,1)S(1)} collective-permute-done((bf16[64,2048]{1,0:T(8,128)(2,1)S(1)}, bf16[64,2048]{1,0:T(8,128)(2,1)S(1)}, u32[]{:S(2)}, u32[]{:S(2)}) %collective-permute-start.6) | collective-permute-done | bytes 262176 | tf_op jit(solution)/shard_map/ppermute | solution.py:290
  15.9 0.6 relay.3
  16.5 3.8 %collective-permute-start.7 = (bf16[64,2048]{1,0:T(8,128)(2,1)S(1)}, bf16[64,2048]{1,0:T(8,128)(2,1)S(1)}, u32[]{:S(2)}, u32[]{:S(2)}) collective-permute-start(bf16[64,2048]{1,0:T(8,128)(2,1)S(1)} %relay.3), channel_id=1, source_target_pairs={{0,96},{16,112},{32,0},{48,16},{64,32},{80,48},{96,64},{112,80},{1... | collective-permute-start | bytes 786440 | tf_op jit(solution)/shard_map/ppermute | solution.py:298
  20.2 0.6 relay.2
  20.8 0.1 collective-permute-start.5
  20.9 5.9 %prepare.1 = (bf16[2,512,512]{2,1,0:T(8,128)(2,1)}, bf16[2,512,512]{2,1,0:T(8,128)(2,1)}, bf16[2,512,512]{2,1,0:T(8,128)(2,1)}, bf16[2,512,512]{2,1,0:T(8,128)(2,1)}) custom-call(f32[2,512,512]{2,1,0:T(8,128)} %bitcast.27, f32[2,512,512]{2,1,0:T(8,128)} %bitcast.28, f32[2,512,512]{2,1,0:T(8,128)} %bitcast.22), custom_call_target="tpu_custom_call" | custom-call | flops 2147483648 | bytes 11534336 | tf_op jit(solution)/shard_map/prepare/pallas_call | solution.py:94
  26.8 0.0 copy-start
  26.8 0.6 direct.1.own
  27.5 2.5 %collective-permute-done.5.left_sum = bf16[64,2048]{1,0:T(8,128)(2,1)S(1)} collective-permute-done((bf16[64,2048]{1,0:T(8,128)(2,1)S(1)}, bf16[64,2048]{1,0:T(8,128)(2,1)S(1)}, u32[]{:S(2)}, u32[]{:S(2)}) %collective-permute-start.5) | collective-permute-done | bytes 262176 | tf_op jit(solution)/shard_map/ppermute | solution.py:297
  30.0 0.8 finish.1
  30.8 4.1 %collective-permute-start.10 = (bf16[32,2176]{1,0:T(8,128)(2,1)S(1)}, bf16[32,2176]{1,0:T(8,128)(2,1)S(1)}, u32[]{:S(2)}, u32[]{:S(2)}) collective-permute-start(bf16[32,2176]{1,0:T(8,128)(2,1)S(1)} %get-tuple-element.74), channel_id=1, source_target_pairs={{0,12},{1,13},{2,14},{3,15},{4,0},{5,1},{6,2},{7,3},{8,4},{9,5},{1... | collective-permute-start | bytes 417800 | tf_op jit(solution)/shard_map/ppermute | solution.py:308
  34.9 1.9 %collective-permute-start.9 = (bf16[32,2176]{1,0:T(8,128)(2,1)S(1)}, bf16[32,2176]{1,0:T(8,128)(2,1)S(1)}, u32[]{:S(2)}, u32[]{:S(2)}) collective-permute-start(bf16[32,2176]{1,0:T(8,128)(2,1)S(1)} %get-tuple-element.73), channel_id=1, source_target_pairs={{0,8},{1,9},{2,10},{3,11},{4,12},{5,13},{6,14},{7,15},{8,0},{9,1},... | collective-permute-start | bytes 417800 | tf_op jit(solution)/shard_map/ppermute | solution.py:308
  36.8 0.1 pad_add_fusion.table
  36.8 2.2 %collective-permute-done.10.refs_3_ = bf16[32,2176]{1,0:T(8,128)(2,1)S(1)} collective-permute-done((bf16[32,2176]{1,0:T(8,128)(2,1)S(1)}, bf16[32,2176]{1,0:T(8,128)(2,1)S(1)}, u32[]{:S(2)}, u32[]{:S(2)}) %collective-permute-start.10) | collective-permute-done | bytes 139296 | tf_op jit(solution)/shard_map/ppermute | solution.py:308
  39.0 4.1 %collective-permute-done.8.refs_1_ = bf16[32,2176]{1,0:T(8,128)(2,1)S(1)} collective-permute-done((bf16[32,2176]{1,0:T(8,128)(2,1)S(1)}, bf16[32,2176]{1,0:T(8,128)(2,1)S(1)}, u32[]{:S(2)}, u32[]{:S(2)}) %collective-permute-start.8) | collective-permute-done | bytes 139296 | tf_op jit(solution)/shard_map/ppermute | solution.py:308
  43.1 1.6 %dispatch.1 = (bf16[32,32,512]{2,1,0:T(8,128)(2,1)}, f32[8,128]{1,0:T(8,128)S(1)}) custom-call(s32[1,17]{1,0:T(1,128)S(1)} %pad_add_fusion.table, bf16[32,2176]{1,0:T(8,128)(2,1)S(1)} %get-tuple-element.71.refs_0_, bf16[32,2176]{1,0:T(8,128)(2,1)S(1)} %collective-permute-done.8.refs_1_, bf16[32,2176]{1,0:T(8,128)(2,1)S(1)} %collective-permute-done.9.refs_2_, ...), custom_call_target="tpu_custom_call" | custom-call | tf_op jit(solution)/shard_map/dispatch/pallas_call | solution.py:118
  44.7 5.6 %all-to-all-start = ((bf16[16,2,32,512]{3,2,1,0:T(8,128)(2,1)}), bf16[16,2,32,512]{3,2,1,0:T(8,128)(2,1)S(1)}, u32[]{:S(2)}, u32[]{:S(2)}) async-start(bf16[16,2,32,512]{3,2,1,0:T(8,128)(2,1)} %bitcast.9), calls=%async_computation | async-start | bytes 2097152 | tf_op jit(solution)/shard_map/all_to_all | solution.py:536
  50.3 0.1 collective-permute-start.11
  50.4 1.2 %collective-permute-done.11 = f32[8,128]{1,0:T(8,128)S(1)} collective-permute-done((f32[8,128]{1,0:T(8,128)S(1)}, f32[8,128]{1,0:T(8,128)S(1)}, u32[]{:S(2)}, u32[]{:S(2)}) %collective-permute-start.11) | collective-permute-done | bytes 4128 | tf_op jit(solution)/shard_map/ppermute | solution.py:538
  51.5 2.2 %collective-permute-start.13 = (f32[8,128]{1,0:T(8,128)S(1)}, f32[8,128]{1,0:T(8,128)S(1)}, u32[]{:S(2)}, u32[]{:S(2)}) collective-permute-start(f32[8,128]{1,0:T(8,128)S(1)} %add.19), channel_id=1, source_target_pairs={{0,64},{16,80},{32,96},{48,112},{64,0},{80,16},{96,32},{112,48},{1... | collective-permute-start | bytes 12296 | tf_op jit(solution)/shard_map/ppermute | solution.py:538
  53.7 1.1 %collective-permute-start.14 = (f32[8,128]{1,0:T(8,128)S(1)}, f32[8,128]{1,0:T(8,128)S(1)}, u32[]{:S(2)}, u32[]{:S(2)}) collective-permute-start(f32[8,128]{1,0:T(8,128)S(1)} %add.19), channel_id=1, source_target_pairs={{0,96},{16,112},{32,0},{48,16},{64,32},{80,48},{96,64},{112,80},{1... | collective-permute-start | bytes 12296 | tf_op jit(solution)/shard_map/ppermute | solution.py:538
  54.8 1.6 %collective-permute-done.12 = f32[8,128]{1,0:T(8,128)S(1)} collective-permute-done((f32[8,128]{1,0:T(8,128)S(1)}, f32[8,128]{1,0:T(8,128)S(1)}, u32[]{:S(2)}, u32[]{:S(2)}) %collective-permute-start.12) | collective-permute-done | bytes 4128 | tf_op jit(solution)/shard_map/ppermute | solution.py:538
  56.3 0.3 collective-permute-done.13
  56.6 0.7 collective-permute-done.14
  57.3 1.8 %collective-permute-start.15 = (f32[8,128]{1,0:T(8,128)S(1)}, f32[8,128]{1,0:T(8,128)S(1)}, u32[]{:S(2)}, u32[]{:S(2)}) collective-permute-start(f32[8,128]{1,0:T(8,128)S(1)} %add_add_fusion.refs_0_.refs_2_), channel_id=1, source_target_pairs={{0,1},{1,2},{2,3},{3,0},{4,5},{5,6},{6,7},{7,4},{8,9},{9,10},{10,1... | collective-permute-start | bytes 12296 | tf_op jit(solution)/shard_map/ppermute | solution.py:539
  59.2 2.7 %collective-permute-start.16 = (f32[8,128]{1,0:T(8,128)S(1)}, f32[8,128]{1,0:T(8,128)S(1)}, u32[]{:S(2)}, u32[]{:S(2)}) collective-permute-start(f32[8,128]{1,0:T(8,128)S(1)} %add_add_fusion.refs_0_.refs_2_), channel_id=1, source_target_pairs={{0,2},{1,3},{2,0},{3,1},{4,6},{5,7},{6,4},{7,5},{8,10},{9,11},{10,... | collective-permute-start | bytes 12296 | tf_op jit(solution)/shard_map/ppermute | solution.py:539
  61.8 1.5 %collective-permute-start.17 = (f32[8,128]{1,0:T(8,128)S(1)}, f32[8,128]{1,0:T(8,128)S(1)}, u32[]{:S(2)}, u32[]{:S(2)}) collective-permute-start(f32[8,128]{1,0:T(8,128)S(1)} %add_add_fusion.refs_0_.refs_2_), channel_id=1, source_target_pairs={{0,3},{1,0},{2,1},{3,2},{4,7},{5,4},{6,5},{7,6},{8,11},{9,8},{10,9... | collective-permute-start | bytes 12296 | tf_op jit(solution)/shard_map/ppermute | solution.py:539
  63.3 2.7 %all-to-all-done.pieces.refs_6_ = bf16[16,2,32,512]{3,2,1,0:T(8,128)(2,1)S(1)} async-done(((bf16[16,2,32,512]{3,2,1,0:T(8,128)(2,1)}), bf16[16,2,32,512]{3,2,1,0:T(8,128)(2,1)S(1)}, u32[]{:S(2)}, u32[]{:S(2)}) %all-to-all-start) | async-done | bytes 1048608 | tf_op jit(solution)/shard_map/all_to_all | solution.py:536
  66.0 3.0 %rotate.1 = (f32[2,512,512]{2,1,0:T(8,128)S(1)}, bf16[2,512,512]{2,1,0:T(8,128)(2,1)S(1)}, bf16[2,512,512]{2,1,0:T(8,128)(2,1)S(1)}, bf16[2,512,512]{2,1,0:T(8,128)(2,1)S(1)}, f32[2,512,512]{2,1,0:T(8,128)S(1)}) custom-call(bf16[16,2,32,512]{3,2,1,0:T(8,128)(2,1)S(1)} %all-to-all-done.pieces.refs_6_, bf16[2,512,512]{2,1,0:T(8,128)(2,1)} %get-tuple-element.77.lt_src, ...), custom_call_target="tpu_custom_call" | custom-call | tf_op jit(solution)/shard_map/rotate/pallas_call | solution.py:359
  69.0 3.2 %direction.1 = (bf16[16,2,32,512]{3,2,1,0:T(8,128)(2,1)S(1)}, f32[2,512,512]{2,1,0:T(8,128)}) custom-call(s32[1,16]{1,0:T(1,128)S(1)} %copy-done, s32[1]{0:T(128)} %bitcast.1.me.refs_1_, f32[8,128]{1,0:T(8,128)S(1)} %add_add_fusion.refs_0_.refs_2_, f32[8,128]{1,0:T(8,128)S(1)} %collective-permute-done.15.refs_1_.refs_3_, ...), custom_call_target="tpu_custom_call" | custom-call | tf_op jit(solution)/shard_map/direction/pallas_call | solution.py:410
  72.2 17.7 %all_to_all.10 = bf16[16,2,32,512]{3,2,1,0:T(8,128)(2,1)S(1)} all-to-all(bf16[16,2,32,512]{3,2,1,0:T(8,128)(2,1)S(1)} %get-tuple-element.86), channel_id=1, replica_groups=mesh['dp'=8,'fsdp'=16] {'fsdp'}, dimensions={0} | all-to-all | bytes 2097152 | tf_op jit(solution)/shard_map/all_to_all | solution.py:542
  89.9 0.6 collect.1
  90.5 0.1 collective-permute-start.18
  90.6 2.4 %collective-permute-start.19 = (bf16[32,2048]{1,0:T(8,128)(2,1)S(1)}, bf16[32,2048]{1,0:T(8,128)(2,1)S(1)}, u32[]{:S(2)}, u32[]{:S(2)}) collective-permute-start(bf16[32,2048]{1,0:T(8,128)(2,1)S(1)} %get-tuple-element.90), channel_id=1, source_target_pairs={{0,8},{1,9},{2,10},{3,11},{4,12},{5,13},{6,14},{7,15},{8,0},{9,1},... | collective-permute-start | bytes 393224 | tf_op jit(solution)/shard_map/ppermute | solution.py:308
  93.0 1.2 %collective-permute-start.20 = (bf16[32,2048]{1,0:T(8,128)(2,1)S(1)}, bf16[32,2048]{1,0:T(8,128)(2,1)S(1)}, u32[]{:S(2)}, u32[]{:S(2)}) collective-permute-start(bf16[32,2048]{1,0:T(8,128)(2,1)S(1)} %get-tuple-element.91), channel_id=1, source_target_pairs={{0,12},{1,13},{2,14},{3,15},{4,0},{5,1},{6,2},{7,3},{8,4},{9,5},{1... | collective-permute-start | bytes 393224 | tf_op jit(solution)/shard_map/ppermute | solution.py:308
  94.2 5.6 %factors.1 = (f32[2,512,512]{2,1,0:T(8,128)}, f32[2,512,512]{2,1,0:T(8,128)}, f32[2,512,512]{2,1,0:T(8,128)}) custom-call(s32[1,16]{1,0:T(1,128)S(1)} %copy-done, s32[1]{0:T(128)} %bitcast.1.me.refs_1_, f32[8,128]{1,0:T(8,128)S(1)} %add_add_fusion.refs_0_.refs_2_, f32[8,128]{1,0:T(8,128)S(1)} %collective-permute-done.15.refs_1_.refs_3_, ...), custom_call_target="tpu_custom_call" | custom-call | flops 1073741824 | bytes 13631488 | tf_op jit(solution)/shard_map/factors/pallas_call | solution.py:475
  99.8 1.4 %put.1 = bf16[4,32,2048]{2,1,0:T(8,128)(2,1)} custom-call(s32[1,17]{1,0:T(1,128)S(1)} %pad_add_fusion.table, bf16[32,2048]{1,0:T(8,128)(2,1)S(1)} %get-tuple-element.88.refs_0_, bf16[32,2048]{1,0:T(8,128)(2,1)S(1)} %collective-permute-done.18.refs_1_, bf16[32,2048]{1,0:T(8,128)(2,1)S(1)} %collective-permute-done.19.refs_2_, ...), custom_call_target="tpu_custom_call" | custom-call | tf_op jit(solution)/shard_map/put/pallas_call | solution.py:118
  (17 shorter events, 0.0 us)
Async XLA Ops:
  3.5 2.0 %collective-permute-start = (bf16[1,128,2048]{2,1,0:T(8,128)(2,1)S(1)}, bf16[1,128,2048]{2,1,0:T(8,128)(2,1)S(1)}, u32[]{:S(2)}, u32[]{:S(2)}) collective-permute-start(bf16[1,128,2048]{2,1,0:T(8,128)(2,1)S(1)} %get-tuple-element.52), channel_id=1, source_target_pairs={{0,16},{16,0},{32,48},{48,32},{64,80},{80,64},{96,112},{112,96},{1... | collective-permute-start | bytes 1572872 | tf_op jit(solution)/shard_map/ppermute | solution.py:285
  5.5 3.7 %collective-permute-start.1 = (bf16[3,128,2048]{2,1,0:T(8,128)(2,1)S(1)}, bf16[3,128,2048]{2,1,0:T(8,128)(2,1)S(1)}, u32[]{:S(2)}, u32[]{:S(2)}) collective-permute-start(bf16[3,128,2048]{2,1,0:T(8,128)(2,1)S(1)} %get-tuple-element.54), channel_id=1, source_target_pairs={{0,16},{16,0},{32,48},{48,32},{64,80},{80,64},{96,112},{112,96},{1... | collective-permute-start | bytes 4718600 | tf_op jit(solution)/shard_map/ppermute | solution.py:287
  6.3 9.6 %collective-permute-start.6 = (bf16[64,2048]{1,0:T(8,128)(2,1)S(1)}, bf16[64,2048]{1,0:T(8,128)(2,1)S(1)}, u32[]{:S(2)}, u32[]{:S(2)}) collective-permute-start(bf16[64,2048]{1,0:T(8,128)(2,1)S(1)} %get-tuple-element.63), channel_id=1, source_target_pairs={{0,96},{16,112},{32,0},{48,16},{64,32},{80,48},{96,64},{112,80},{1... | collective-permute-start | bytes 786440 | tf_op jit(solution)/shard_map/ppermute | solution.py:290
  9.2 11.0 %collective-permute-start.4 = (bf16[64,2048]{1,0:T(8,128)(2,1)S(1)}, bf16[64,2048]{1,0:T(8,128)(2,1)S(1)}, u32[]{:S(2)}, u32[]{:S(2)}) collective-permute-start(bf16[64,2048]{1,0:T(8,128)(2,1)S(1)} %get-tuple-element.61), channel_id=1, source_target_pairs={{0,32},{16,48},{32,64},{48,80},{64,96},{80,112},{96,0},{112,16},{1... | collective-permute-start | bytes 786440 | tf_op jit(solution)/shard_map/ppermute | solution.py:289
  10.1 16.7 %collective-permute-start.2 = (bf16[64,2048]{1,0:T(8,128)(2,1)S(1)}, bf16[64,2048]{1,0:T(8,128)(2,1)S(1)}, u32[]{:S(2)}, u32[]{:S(2)}) collective-permute-start(bf16[64,2048]{1,0:T(8,128)(2,1)S(1)} %get-tuple-element.56), channel_id=1, source_target_pairs={{0,32},{16,48},{32,64},{48,80},{64,96},{80,112},{96,0},{112,16},{1... | collective-permute-start | bytes 786440 | tf_op jit(solution)/shard_map/ppermute | solution.py:295
  11.4 15.4 %collective-permute-start.3 = (bf16[64,2048]{1,0:T(8,128)(2,1)S(1)}, bf16[64,2048]{1,0:T(8,128)(2,1)S(1)}, u32[]{:S(2)}, u32[]{:S(2)}) collective-permute-start(bf16[64,2048]{1,0:T(8,128)(2,1)S(1)} %get-tuple-element.57), channel_id=1, source_target_pairs={{0,96},{16,112},{32,0},{48,16},{64,32},{80,48},{96,64},{112,80},{1... | collective-permute-start | bytes 786440 | tf_op jit(solution)/shard_map/ppermute | solution.py:296
  16.5 11.0 %collective-permute-start.7 = (bf16[64,2048]{1,0:T(8,128)(2,1)S(1)}, bf16[64,2048]{1,0:T(8,128)(2,1)S(1)}, u32[]{:S(2)}, u32[]{:S(2)}) collective-permute-start(bf16[64,2048]{1,0:T(8,128)(2,1)S(1)} %relay.3), channel_id=1, source_target_pairs={{0,96},{16,112},{32,0},{48,16},{64,32},{80,48},{96,64},{112,80},{1... | collective-permute-start | bytes 786440 | tf_op jit(solution)/shard_map/ppermute | solution.py:298
  20.8 9.1 %collective-permute-start.5 = (bf16[64,2048]{1,0:T(8,128)(2,1)S(1)}, bf16[64,2048]{1,0:T(8,128)(2,1)S(1)}, u32[]{:S(2)}, u32[]{:S(2)}) collective-permute-start(bf16[64,2048]{1,0:T(8,128)(2,1)S(1)} %relay.2), channel_id=1, source_target_pairs={{0,32},{16,48},{32,64},{48,80},{64,96},{80,112},{96,0},{112,16},{1... | collective-permute-start | bytes 786440 | tf_op jit(solution)/shard_map/ppermute | solution.py:297
  26.8 10.0 %copy-start = (s32[1,16]{1,0:T(1,128)S(1)}, s32[1,16]{1,0:T(1,128)}, u32[]{:S(2)}) copy-start(s32[1,16]{1,0:T(1,128)} %refs_0_.1) | copy-start | bytes 196
  30.8 8.2 %collective-permute-start.10 = (bf16[32,2176]{1,0:T(8,128)(2,1)S(1)}, bf16[32,2176]{1,0:T(8,128)(2,1)S(1)}, u32[]{:S(2)}, u32[]{:S(2)}) collective-permute-start(bf16[32,2176]{1,0:T(8,128)(2,1)S(1)} %get-tuple-element.74), channel_id=1, source_target_pairs={{0,12},{1,13},{2,14},{3,15},{4,0},{5,1},{6,2},{7,3},{8,4},{9,5},{1... | collective-permute-start | bytes 417800 | tf_op jit(solution)/shard_map/ppermute | solution.py:308
  34.9 8.2 %collective-permute-start.8 = (bf16[32,2176]{1,0:T(8,128)(2,1)S(1)}, bf16[32,2176]{1,0:T(8,128)(2,1)S(1)}, u32[]{:S(2)}, u32[]{:S(2)}) collective-permute-start(bf16[32,2176]{1,0:T(8,128)(2,1)S(1)} %get-tuple-element.72), channel_id=1, source_target_pairs={{0,4},{1,5},{2,6},{3,7},{4,8},{5,9},{6,10},{7,11},{8,12},{9,13},{1... | collective-permute-start | bytes 417800 | tf_op jit(solution)/shard_map/ppermute | solution.py:308
  34.9 8.2 %collective-permute-start.9 = (bf16[32,2176]{1,0:T(8,128)(2,1)S(1)}, bf16[32,2176]{1,0:T(8,128)(2,1)S(1)}, u32[]{:S(2)}, u32[]{:S(2)}) collective-permute-start(bf16[32,2176]{1,0:T(8,128)(2,1)S(1)} %get-tuple-element.73), channel_id=1, source_target_pairs={{0,8},{1,9},{2,10},{3,11},{4,12},{5,13},{6,14},{7,15},{8,0},{9,1},... | collective-permute-start | bytes 417800 | tf_op jit(solution)/shard_map/ppermute | solution.py:308
  44.7 21.4 %all-to-all-start = ((bf16[16,2,32,512]{3,2,1,0:T(8,128)(2,1)}), bf16[16,2,32,512]{3,2,1,0:T(8,128)(2,1)S(1)}, u32[]{:S(2)}, u32[]{:S(2)}) async-start(bf16[16,2,32,512]{3,2,1,0:T(8,128)(2,1)} %bitcast.9), calls=%async_computation | async-start | bytes 2097152 | tf_op jit(solution)/shard_map/all_to_all | solution.py:536
  50.3 1.2 %collective-permute-start.11 = (f32[8,128]{1,0:T(8,128)S(1)}, f32[8,128]{1,0:T(8,128)S(1)}, u32[]{:S(2)}, u32[]{:S(2)}) collective-permute-start(f32[8,128]{1,0:T(8,128)S(1)} %get-tuple-element.75), channel_id=1, source_target_pairs={{0,16},{16,0},{32,48},{48,32},{64,80},{80,64},{96,112},{112,96},{1... | collective-permute-start | bytes 12296 | tf_op jit(solution)/shard_map/ppermute | solution.py:538
  51.5 4.8 %collective-permute-start.12 = (f32[8,128]{1,0:T(8,128)S(1)}, f32[8,128]{1,0:T(8,128)S(1)}, u32[]{:S(2)}, u32[]{:S(2)}) collective-permute-start(f32[8,128]{1,0:T(8,128)S(1)} %add.19), channel_id=1, source_target_pairs={{0,32},{16,48},{32,64},{48,80},{64,96},{80,112},{96,0},{112,16},{1... | collective-permute-start | bytes 12296 | tf_op jit(solution)/shard_map/ppermute | solution.py:538
  51.5 5.1 %collective-permute-start.13 = (f32[8,128]{1,0:T(8,128)S(1)}, f32[8,128]{1,0:T(8,128)S(1)}, u32[]{:S(2)}, u32[]{:S(2)}) collective-permute-start(f32[8,128]{1,0:T(8,128)S(1)} %add.19), channel_id=1, source_target_pairs={{0,64},{16,80},{32,96},{48,112},{64,0},{80,16},{96,32},{112,48},{1... | collective-permute-start | bytes 12296 | tf_op jit(solution)/shard_map/ppermute | solution.py:538
  53.7 3.6 %collective-permute-start.14 = (f32[8,128]{1,0:T(8,128)S(1)}, f32[8,128]{1,0:T(8,128)S(1)}, u32[]{:S(2)}, u32[]{:S(2)}) collective-permute-start(f32[8,128]{1,0:T(8,128)S(1)} %add.19), channel_id=1, source_target_pairs={{0,96},{16,112},{32,0},{48,16},{64,32},{80,48},{96,64},{112,80},{1... | collective-permute-start | bytes 12296 | tf_op jit(solution)/shard_map/ppermute | solution.py:538
  57.3 11.7 %collective-permute-start.15 = (f32[8,128]{1,0:T(8,128)S(1)}, f32[8,128]{1,0:T(8,128)S(1)}, u32[]{:S(2)}, u32[]{:S(2)}) collective-permute-start(f32[8,128]{1,0:T(8,128)S(1)} %add_add_fusion.refs_0_.refs_2_), channel_id=1, source_target_pairs={{0,1},{1,2},{2,3},{3,0},{4,5},{5,6},{6,7},{7,4},{8,9},{9,10},{10,1... | collective-permute-start | bytes 12296 | tf_op jit(solution)/shard_map/ppermute | solution.py:539
  59.2 9.8 %collective-permute-start.16 = (f32[8,128]{1,0:T(8,128)S(1)}, f32[8,128]{1,0:T(8,128)S(1)}, u32[]{:S(2)}, u32[]{:S(2)}) collective-permute-start(f32[8,128]{1,0:T(8,128)S(1)} %add_add_fusion.refs_0_.refs_2_), channel_id=1, source_target_pairs={{0,2},{1,3},{2,0},{3,1},{4,6},{5,7},{6,4},{7,5},{8,10},{9,11},{10,... | collective-permute-start | bytes 12296 | tf_op jit(solution)/shard_map/ppermute | solution.py:539
  61.8 7.2 %collective-permute-start.17 = (f32[8,128]{1,0:T(8,128)S(1)}, f32[8,128]{1,0:T(8,128)S(1)}, u32[]{:S(2)}, u32[]{:S(2)}) collective-permute-start(f32[8,128]{1,0:T(8,128)S(1)} %add_add_fusion.refs_0_.refs_2_), channel_id=1, source_target_pairs={{0,3},{1,0},{2,1},{3,2},{4,7},{5,4},{6,5},{7,6},{8,11},{9,8},{10,9... | collective-permute-start | bytes 12296 | tf_op jit(solution)/shard_map/ppermute | solution.py:539
  90.5 9.3 %collective-permute-start.18 = (bf16[32,2048]{1,0:T(8,128)(2,1)S(1)}, bf16[32,2048]{1,0:T(8,128)(2,1)S(1)}, u32[]{:S(2)}, u32[]{:S(2)}) collective-permute-start(bf16[32,2048]{1,0:T(8,128)(2,1)S(1)} %get-tuple-element.89), channel_id=1, source_target_pairs={{0,4},{1,5},{2,6},{3,7},{4,8},{5,9},{6,10},{7,11},{8,12},{9,13},{1... | collective-permute-start | bytes 393224 | tf_op jit(solution)/shard_map/ppermute | solution.py:308
  90.6 9.2 %collective-permute-start.19 = (bf16[32,2048]{1,0:T(8,128)(2,1)S(1)}, bf16[32,2048]{1,0:T(8,128)(2,1)S(1)}, u32[]{:S(2)}, u32[]{:S(2)}) collective-permute-start(bf16[32,2048]{1,0:T(8,128)(2,1)S(1)} %get-tuple-element.90), channel_id=1, source_target_pairs={{0,8},{1,9},{2,10},{3,11},{4,12},{5,13},{6,14},{7,15},{8,0},{9,1},... | collective-permute-start | bytes 393224 | tf_op jit(solution)/shard_map/ppermute | solution.py:308
  93.0 6.8 %collective-permute-start.20 = (bf16[32,2048]{1,0:T(8,128)(2,1)S(1)}, bf16[32,2048]{1,0:T(8,128)(2,1)S(1)}, u32[]{:S(2)}, u32[]{:S(2)}) collective-permute-start(bf16[32,2048]{1,0:T(8,128)(2,1)S(1)} %get-tuple-element.91), channel_id=1, source_target_pairs={{0,12},{1,13},{2,14},{3,15},{4,0},{5,1},{6,2},{7,3},{8,4},{9,5},{1... | collective-permute-start | bytes 393224 | tf_op jit(solution)/shard_map/ppermute | solution.py:308
